TPU v7x, 32 devices: a whole 2x2x4 slice. The times are simulated.
32 devices in a mesh: dp: 2 (over x), blk: 16 (over z, y, core).
Axes of the slice: x: 2, y: 2, z: 4, core: 2. Of those that a mesh axis runs over, the one named last changes fastest.
Arguments:
- byte_embeds: bfloat16 [2, 8192, 768], P('dp', 'blk'), may hold values from -6 to 6
- segments: int32 [2, 8192], P('dp', 'blk'), may hold values from 0 to 7, as said below
- score_weight: bfloat16 [768], replicated, may hold values from -0.4375 to 0.4375
- norm_gain1: bfloat16 [768], replicated, may hold values from 0.5 to 1.5
- w_query: bfloat16 [768, 768], replicated, may hold values from -0.21875 to 0.21875
- w_key: bfloat16 [768, 768], replicated, may hold values from -0.21875 to 0.21875
- w_value: bfloat16 [768, 768], replicated, may hold values from -0.21875 to 0.21875
- w_out: bfloat16 [768, 768], replicated, may hold values from -0.875 to 0.875
- rel_bias: bfloat16 [32, 12], replicated, may hold values from -4 to 4
- norm_gain2: bfloat16 [768], replicated, may hold values from 0.5 to 1.5
- w_gate: bfloat16 [768, 2048], replicated, may hold values from -0.21875 to 0.21875
- w_up: bfloat16 [768, 2048], replicated, may hold values from -0.21875 to 0.21875
- w_down: bfloat16 [2048, 768], replicated, may hold values from -0.1875 to 0.1875
- cotangent: bfloat16 [2, 4096, 768], P('dp', 'blk'), may hold values from -6 to 6
Outputs:
- block_out: bfloat16 [2, 4096, 768], P('dp', 'blk')
- grad_bytes: bfloat16 [2, 8192, 768], P('dp', 'blk')
- grad_score: float32 [768], replicated
- grad_gain1: float32 [768], replicated
- grad_query: float32 [768, 768], P(('dp', 'blk'))
- grad_key: float32 [768, 768], P(('dp', 'blk'))
- grad_value: float32 [768, 768], P(('dp', 'blk'))
- grad_out: float32 [768, 768], P(('dp', 'blk'))
- grad_bias: float32 [32, 12], replicated
- grad_gain2: float32 [768], replicated
- grad_gate: float32 [768, 2048], P(('dp', 'blk'))
- grad_up: float32 [768, 2048], P(('dp', 'blk'))
- grad_down: float32 [2048, 768], P(('dp', 'blk'))
- block_share: float32 [4], replicated
Inputs may be any that keep to these rules, and one draw needn't show every extreme that they name: `segments`: segment ids are 0 at each row's first byte and never fall along a row, by steps of one; of rows 2k and 2k + 1, one, chosen by the seed, is a single document and the other holds exactly 8 documents.
All inputs are finite; a program needn't handle non-finite values.
Results may differ from a plain program's by a relative error of at most 0.019.
Values may be sent and summed in bfloat16 or wider, within the bound.
A program may use at most 256 MiB of HBM per device.

v0:
```python
import math

import jax
import jax.numpy as jnp
from jax import lax
from jax.sharding import PartitionSpec as P

BUCKETS = 32
MAX_BLOCK = 4


BIG_NEG = -1e30
PRECISE = lax.Precision.HIGHEST


def extended(shard, sides, width):
    for axis, dim in sides:
        peers, length = (lax.axis_size(axis), shard.shape[dim])
        up = [(i, (i + 1) % peers) for i in range(peers - 1)]
        down = [(j, i) for i, j in up]
        last = lax.slice_in_dim(shard, length - width, length, axis=dim)
        leading = lax.slice_in_dim(shard, 0, width, axis=dim)
        before = lax.ppermute(last, axis, up)
        after = lax.ppermute(leading, axis, down)
        shard = jnp.concatenate([before, shard, after], axis=dim)
    return shard


def buckets_of(relative):
    distance = jnp.abs(relative)
    beyond = jnp.zeros_like(distance)
    for border in (12, 16, 23, 32, 46, 64, 91):
        beyond = beyond + (distance >= border).astype(jnp.int32)
    nearer = jnp.where(distance < 8, distance, 8 + beyond)
    return nearer + BUCKETS // 2 * (relative > 0).astype(jnp.int32)


def rms_norm(values, gain):
    return values * lax.rsqrt(jnp.mean(values * values, axis=-1, keepdims=True) + 1e-06) * gain


def geglu(gate_proj, up_proj):
    return jax.nn.gelu(gate_proj, approximate=True) * up_proj


def toeplitz(band_values, query_count, key_count):
    band_len = band_values.shape[1]
    repeated = jnp.tile(band_values, (1, query_count))
    flattened = repeated[:, query_count - 1 : query_count - 1 + query_count * (band_len - 1)]
    return flattened.reshape(band_values.shape[0], query_count, band_len - 1)[:, :, :key_count]


def diagonal_sums(grid):
    head_count, query_count, key_count = grid.shape
    band_len = query_count + key_count - 1
    widened = jnp.pad(grid, ((0, 0), (0, 0), (0, band_len - 1 - key_count)))
    flattened = widened.reshape(head_count, query_count * (band_len - 1))
    flattened = jnp.pad(flattened, ((0, 0), (query_count - 1, 1)))
    return jnp.sum(flattened.reshape(head_count, query_count, band_len), axis=1)


def pool_masks(labels, base, length):
    positions = jnp.arange(length + 6, dtype=jnp.int32) + base - 3
    centre = labels[:, 3 : 3 + length]
    centre_pos = positions[3 : 3 + length]
    result = []
    for block_width in range(1, MAX_BLOCK + 1):
        pool_terms = []
        for offset in range(1 - block_width, block_width):
            near_labels = labels[:, 3 + offset : 3 + offset + length]
            near_pos = positions[3 + offset : 3 + offset + length]
            same_block = near_pos // block_width == centre_pos // block_width
            keep_mask = jnp.logical_and(near_labels == centre, same_block[None, :])
            pool_terms.append((offset, keep_mask.astype(jnp.float32)))
        counts = sum((entry[1] for entry in pool_terms))
        result.append((pool_terms, counts))
    return result


def in_blocks(step_fn, state_now, pieces, start_row, along):
    row_total = pieces[0].shape[along]
    block_size = math.gcd(row_total, 512)

    def one_turn(turn_index, state_inner):
        sub_block = tuple(
            (
                lax.dynamic_slice_in_dim(operand, turn_index * block_size, block_size, along)
                for operand in pieces
            )
        )
        return step_fn(state_inner, sub_block, start_row + turn_index * block_size)

    return lax.fori_loop(0, row_total // block_size, one_turn, state_now)


def body(
    byte_embeds,
    segments,
    score_weight,
    norm_gain1,
    w_query,
    w_key,
    w_value,
    w_out,
    rel_bias,
    norm_gain2,
    w_gate,
    w_up,
    w_down,
    cotangent,
):
    row_count, length, width_d = byte_embeds.shape
    tokens = length // 2
    shards = lax.axis_size("blk")
    devices_all = shards * lax.axis_size("dp")
    position = lax.axis_index("blk")
    base = position * length
    head_count = rel_bias.shape[1]
    head_dim = width_d // head_count
    score_scale = 1.0 / math.sqrt(head_dim)
    bias_table = rel_bias.astype(jnp.float32)
    score_vec = score_weight.astype(jnp.float32)
    rim_bytes = extended(byte_embeds, (("blk", 1),), 2)
    padded = jnp.pad(rim_bytes.astype(jnp.float32), ((0, 0), (1, 1), (0, 0)))
    rim_labels = extended(segments + 1, (("blk", 1),), 2)
    labels_pad = jnp.pad(rim_labels, ((0, 0), (1, 1)))
    masks_all = pool_masks(labels_pad, base, length)
    pools = []
    for pool_terms, counts in masks_all:
        summed = sum(
            (
                keep_mask[:, :, None] * padded[:, 3 + offset : 3 + offset + length]
                for offset, keep_mask in pool_terms
            )
        )
        pools.append(summed / counts[:, :, None])
    stacked = jnp.stack(pools, axis=2)
    block_scores = jnp.sum(stacked * score_vec, axis=-1)
    block_probs = jax.nn.softmax(block_scores, axis=-1)
    mixed = jnp.sum(block_probs[..., None] * stacked, axis=2)
    hidden = 0.5 * (mixed[:, 0::2] + mixed[:, 1::2])
    tok_labels = segments[:, 0::2]
    gain_one = norm_gain1.astype(jnp.float32)
    normed1, norm1_back = jax.vjp(rms_norm, hidden, gain_one)
    n1_low = normed1.astype(jnp.bfloat16)
    query_low = jnp.dot(n1_low, w_query, preferred_element_type=jnp.float32).astype(jnp.bfloat16)
    key_low = jnp.dot(n1_low, w_key, preferred_element_type=jnp.float32).astype(jnp.bfloat16)
    value_low = jnp.dot(n1_low, w_value, preferred_element_type=jnp.float32).astype(jnp.bfloat16)
    query_heads = query_low.reshape(row_count, tokens, head_count, head_dim)
    key_t = jnp.transpose(key_low, (1, 0, 2))
    value_t = jnp.transpose(value_low, (1, 0, 2))
    label_t = jnp.transpose(tok_labels, (1, 0))
    query_pos = position * tokens + jnp.arange(tokens, dtype=jnp.int32)

    def pair_scores(query_part, query_places, query_labels, key_block, key_labels, key_pos):
        key_count = key_block.shape[0]
        query_count = query_places.shape[0]
        key_heads = key_block.reshape(key_count, row_count, head_count, head_dim)
        raw_scores = jnp.einsum(
            "rqhd,krhd->rhqk", query_part, key_heads, preferred_element_type=jnp.float32
        )
        relative = (
            key_pos[0]
            - query_places[0]
            - (query_count - 1)
            + jnp.arange(query_count + key_count - 1, dtype=jnp.int32)
        )
        onehot = (
            buckets_of(relative)[:, None] == jnp.arange(BUCKETS, dtype=jnp.int32)[None, :]
        ).astype(jnp.float32)
        bias_band = jnp.einsum("lb,bh->hl", onehot, bias_table, precision=PRECISE)
        bias_block = toeplitz(bias_band, query_count, key_count)
        allowed = (
            query_labels[:, None, :, None] == jnp.transpose(key_labels, (1, 0))[:, None, None, :]
        )
        return (raw_scores * score_scale + bias_block[None], allowed, onehot)

    def absorb(state_now, pieces, start_row):
        key_block, value_block, key_labels = pieces
        running_max, denominator, accumulated = state_now
        key_pos = start_row + jnp.arange(key_block.shape[0], dtype=jnp.int32)
        scores, allowed, unused = pair_scores(
            query_heads, query_pos, tok_labels, key_block, key_labels, key_pos
        )
        masked = jnp.where(allowed, scores, BIG_NEG)
        new_max = jnp.maximum(running_max, jnp.max(masked, axis=-1))
        weights = jnp.where(allowed, jnp.exp(masked - new_max[..., None]), 0.0)
        shrink = jnp.exp(running_max - new_max)
        value_heads = value_block.reshape(value_block.shape[0], row_count, head_count, head_dim)
        added = jnp.einsum(
            "rhqk,krhd->rhqd",
            weights.astype(jnp.bfloat16),
            value_heads,
            preferred_element_type=jnp.float32,
        )
        return (
            new_max,
            denominator * shrink + jnp.sum(weights, axis=-1),
            accumulated * shrink[..., None] + added,
        )

    initial = (
        jnp.full((row_count, head_count, tokens), BIG_NEG, jnp.float32),
        jnp.zeros((row_count, head_count, tokens), jnp.float32),
        jnp.zeros((row_count, head_count, tokens, head_dim), jnp.float32),
    )
    running = in_blocks(
        absorb,
        initial,
        (
            lax.all_gather(key_t, "blk", axis=0, tiled=True),
            lax.all_gather(value_t, "blk", axis=0, tiled=True),
            lax.all_gather(label_t, "blk", axis=0, tiled=True),
        ),
        jnp.int32(0),
        0,
    )
    running_max, denominator, accumulated = running
    log_total = running_max + jnp.log(denominator)
    attended_f = accumulated / denominator[..., None]
    attended_low = (
        jnp.transpose(attended_f, (0, 2, 1, 3))
        .reshape(row_count, tokens, width_d)
        .astype(jnp.bfloat16)
    )
    residual = hidden + jnp.dot(attended_low, w_out, preferred_element_type=jnp.float32)
    gain_two = norm_gain2.astype(jnp.float32)
    normed2, norm2_back = jax.vjp(rms_norm, residual, gain_two)
    n2_low = normed2.astype(jnp.bfloat16)
    gate_proj = jnp.dot(n2_low, w_gate, preferred_element_type=jnp.float32)
    up_proj = jnp.dot(n2_low, w_up, preferred_element_type=jnp.float32)
    activated, geglu_back = jax.vjp(geglu, gate_proj, up_proj)
    act_low = activated.astype(jnp.bfloat16)
    block_out = (residual + jnp.dot(act_low, w_down, preferred_element_type=jnp.float32)).astype(
        jnp.bfloat16
    )
    grad_down = jnp.einsum("rtf,rtd->fd", act_low, cotangent, preferred_element_type=jnp.float32)
    d_act = jnp.einsum("rtd,fd->rtf", cotangent, w_down, preferred_element_type=jnp.float32)
    d_gate, d_up = geglu_back(d_act)
    d_gate_low = d_gate.astype(jnp.bfloat16)
    d_up_low = d_up.astype(jnp.bfloat16)
    grad_gate = jnp.einsum("rtd,rtf->df", n2_low, d_gate_low, preferred_element_type=jnp.float32)
    grad_up = jnp.einsum("rtd,rtf->df", n2_low, d_up_low, preferred_element_type=jnp.float32)
    d_normed2 = jnp.einsum(
        "rtf,df->rtd", d_gate_low, w_gate, preferred_element_type=jnp.float32
    ) + jnp.einsum("rtf,df->rtd", d_up_low, w_up, preferred_element_type=jnp.float32)
    d_res_part, d_gain_two = norm2_back(d_normed2)
    d_residual = cotangent.astype(jnp.float32) + d_res_part
    d_branch = d_residual.astype(jnp.bfloat16)
    grad_out = jnp.einsum("rtd,rte->de", attended_low, d_branch, preferred_element_type=jnp.float32)
    d_attended = jnp.einsum(
        "rte,de->rtd", d_branch, w_out, preferred_element_type=jnp.float32
    ).astype(jnp.bfloat16)
    d_att_tokens = d_attended.reshape(row_count, tokens, head_count, head_dim)
    d_att_heads = jnp.transpose(d_att_tokens, (0, 2, 1, 3))
    row_delta = jnp.sum(d_att_heads.astype(jnp.float32) * attended_f, axis=-1)
    kv_rows = (
        lax.all_gather(key_t, "blk", axis=0, tiled=True),
        lax.all_gather(value_t, "blk", axis=0, tiled=True),
        lax.all_gather(label_t, "blk", axis=0, tiled=True),
    )

    def score_grads(key_block, value_block, key_labels, key_pos):
        scores, allowed, onehot = pair_scores(
            query_heads, query_pos, tok_labels, key_block, key_labels, key_pos
        )
        chances = jnp.where(allowed, jnp.exp(scores - log_total[..., None]), 0.0)
        value_heads = value_block.reshape(value_block.shape[0], row_count, head_count, head_dim)
        d_chances = jnp.einsum(
            "rhqd,krhd->rhqk", d_att_heads, value_heads, preferred_element_type=jnp.float32
        )
        d_scores = (chances * (d_chances - row_delta[..., None])).astype(jnp.bfloat16)
        return (chances, d_scores, onehot)

    def query_step(state_now, pieces, start_row):
        key_block, value_block, key_labels = pieces
        key_pos = start_row + jnp.arange(key_block.shape[0], dtype=jnp.int32)
        chances, d_scores, onehot = score_grads(key_block, value_block, key_labels, key_pos)
        d_query_acc, d_table_acc = state_now
        key_heads = key_block.reshape(key_block.shape[0], row_count, head_count, head_dim)
        d_query_acc = d_query_acc + score_scale * jnp.einsum(
            "rhqk,krhd->rhqd", d_scores, key_heads, preferred_element_type=jnp.float32
        )
        grid = jnp.sum(d_scores.astype(jnp.float32), axis=0)
        d_table_acc = d_table_acc + jnp.einsum(
            "hl,lb->bh", diagonal_sums(grid), onehot, precision=PRECISE
        )
        return (d_query_acc, d_table_acc)

    d_query_acc, d_table = in_blocks(
        query_step,
        (
            jnp.zeros((row_count, head_count, tokens, head_dim), jnp.float32),
            jnp.zeros((BUCKETS, head_count), jnp.float32),
        ),
        kv_rows,
        0,
        0,
    )

    def block_terms(pieces, first_pos):
        key_block, value_block, key_labels = pieces
        key_pos = first_pos + jnp.arange(key_block.shape[0], dtype=jnp.int32)
        chances, d_scores, unused = score_grads(key_block, value_block, key_labels, key_pos)
        d_key_part = score_scale * jnp.einsum(
            "rhqk,rqhd->krhd", d_scores, query_heads, preferred_element_type=jnp.float32
        )
        d_value_part = jnp.einsum(
            "rhqk,rqhd->krhd",
            chances.astype(jnp.bfloat16),
            d_att_tokens,
            preferred_element_type=jnp.float32,
        )
        block_rows = key_block.shape[0]
        return jnp.concatenate(
            [
                d_key_part.reshape(block_rows, row_count, width_d),
                d_value_part.reshape(block_rows, row_count, width_d),
            ],
            axis=-1,
        )

    sliced = tuple((operand for operand in kv_rows))
    block_size = math.gcd(tokens * lax.axis_size("blk"), 512)

    def one_block(turn_index):
        sub_block = tuple(
            (
                lax.dynamic_slice_in_dim(operand, turn_index * block_size, block_size, 0)
                for operand in sliced
            )
        )
        return block_terms(sub_block, turn_index * block_size)

    stacked_terms = lax.map(
        one_block, jnp.arange(tokens * lax.axis_size("blk") // block_size, dtype=jnp.int32)
    )
    key_sums = lax.psum_scatter(
        stacked_terms.reshape(tokens * lax.axis_size("blk"), row_count, 2 * width_d).astype(
            jnp.bfloat16
        ),
        "blk",
        scatter_dimension=0,
        tiled=True,
    ).astype(jnp.float32)
    d_key_f = key_sums[:, :, :width_d]
    d_value_f = key_sums[:, :, width_d:]
    d_key_low = jnp.transpose(d_key_f, (1, 0, 2)).astype(jnp.bfloat16)
    d_value_low = jnp.transpose(d_value_f, (1, 0, 2)).astype(jnp.bfloat16)
    d_query_low = (
        jnp.transpose(d_query_acc, (0, 2, 1, 3))
        .reshape(row_count, tokens, width_d)
        .astype(jnp.bfloat16)
    )
    grad_query = jnp.einsum("rtd,rte->de", n1_low, d_query_low, preferred_element_type=jnp.float32)
    grad_key = jnp.einsum("rtd,rte->de", n1_low, d_key_low, preferred_element_type=jnp.float32)
    grad_value = jnp.einsum("rtd,rte->de", n1_low, d_value_low, preferred_element_type=jnp.float32)
    d_normed1 = (
        jnp.einsum("rte,de->rtd", d_query_low, w_query, preferred_element_type=jnp.float32)
        + jnp.einsum("rte,de->rtd", d_key_low, w_key, preferred_element_type=jnp.float32)
        + jnp.einsum("rte,de->rtd", d_value_low, w_value, preferred_element_type=jnp.float32)
    )
    d_hid_part, d_gain_one = norm1_back(d_normed1)
    d_hidden = d_residual + d_hid_part
    d_mixed = 0.5 * jnp.repeat(d_hidden, 2, axis=1)
    d_block = jnp.sum(d_mixed[:, :, None, :] * stacked, axis=-1)
    d_block_scores = block_probs * (
        d_block - jnp.sum(block_probs * d_block, axis=-1, keepdims=True)
    )
    grad_score_local = jnp.sum(d_block_scores[..., None] * stacked, axis=(0, 1, 2))
    d_pools = (
        block_probs[..., None] * d_mixed[:, :, None, :] + d_block_scores[..., None] * score_vec
    )
    spread = jnp.stack(
        [
            d_pools[:, :, width_index] / masks_all[width_index][1][:, :, None]
            for width_index in range(MAX_BLOCK)
        ],
        axis=2,
    ).reshape(row_count, length, MAX_BLOCK * width_d)
    rim_spread = extended(spread.astype(jnp.bfloat16), (("blk", 1),), 2).astype(spread.dtype)
    spread_pad = jnp.pad(rim_spread, ((0, 0), (1, 1), (0, 0))).reshape(
        row_count, length + 6, MAX_BLOCK, width_d
    )
    d_bytes = jnp.zeros((row_count, length, width_d), jnp.float32)
    for width_index in range(MAX_BLOCK):
        for offset, keep_mask in masks_all[width_index][0]:
            d_bytes = (
                d_bytes
                + keep_mask[:, :, None]
                * spread_pad[:, 3 + offset : 3 + offset + length, width_index]
            )
    share_local = jnp.sum(block_probs, axis=(0, 1)) / (row_count * length * devices_all)
    summed_weights = (
        lax.psum_scatter(grad_query, ("dp", "blk"), scatter_dimension=0, tiled=True),
        lax.psum_scatter(grad_key, ("dp", "blk"), scatter_dimension=0, tiled=True),
        lax.psum_scatter(grad_value, ("dp", "blk"), scatter_dimension=0, tiled=True),
        lax.psum_scatter(grad_out, ("dp", "blk"), scatter_dimension=0, tiled=True),
        lax.psum_scatter(grad_gate, ("dp", "blk"), scatter_dimension=0, tiled=True),
        lax.psum_scatter(grad_up, ("dp", "blk"), scatter_dimension=0, tiled=True),
        lax.psum_scatter(grad_down, ("dp", "blk"), scatter_dimension=0, tiled=True),
    )
    summed_small = lax.psum(
        (grad_score_local, d_gain_one, d_gain_two, d_table, share_local), ("dp", "blk")
    )
    return (
        block_out,
        d_bytes.astype(jnp.bfloat16),
        summed_small[0],
        summed_small[1],
        summed_weights[0],
        summed_weights[1],
        summed_weights[2],
        summed_weights[3],
        summed_small[3],
        summed_small[2],
        summed_weights[4],
        summed_weights[5],
        summed_weights[6],
        summed_small[4],
    )


def solution(mesh):
    placed = (
        P("dp", "blk", None),
        P("dp", "blk"),
        P(),
        P(),
        P(),
        P(),
        P(),
        P(),
        P(),
        P(),
        P(),
        P(),
        P(),
        P("dp", "blk", None),
    )
    return jax.shard_map(
        body,
        mesh=mesh,
        in_specs=placed,
        out_specs=(
            P("dp", "blk", None),
            P("dp", "blk", None),
            P(),
            P(),
            P(("dp", "blk"), None),
            P(("dp", "blk"), None),
            P(("dp", "blk"), None),
            P(("dp", "blk"), None),
            P(),
            P(),
            P(("dp", "blk"), None),
            P(("dp", "blk"), None),
            P(("dp", "blk"), None),
            P(),
        ),
        check_vma=False,
    )
```

profile of v0, /device:TPU:0, one launch (start us, length us, event | category | flops | bytes accessed | tf_op | source)
XLA Modules:
  0.0 3660.0 jit_solution(134144845234778780)
XLA Ops:
  65.1 23.5 all-gather
  92.9 31.6 all-gather.8.cloned.1.call-done
  133.1 54.7 %all-gather.6.cloned.1.call-done = bf16[4096,768]{1,0:T(8,128)(2,1)} async-done(((bf16[256,768]{1,0:T(8,128)(2,1)}), bf16[4096,768]{1,0:T(8,128)(2,1)}) %all-gather.6.cloned.1.call-update) | async-done | bytes 6291472 | tf_op jit(solution)/shard_map/all_gather | solution.py:211
  196.5 656.0 %while.51 = (s32[]{:T(128)}, f32[1,12,256]{2,1,0:T(8,128)S(1)}, f32[1,12,256]{2,1,0:T(8,128)}, f32[1,12,256,64]{2,3,1,0:T(8,128)}, s32[1,256]{1,0:T(1,128)}, /*i...) while((s32[]{:T(128)}, f32[1,12,256]{2,1,0:T(8,128)S(1)}, ...), condition=%wide.region_8.9_spmd.clone, body=%wide.region_5.8_spmd.clone.sunk | while | flops 422702016 | bytes 133813072 | solution.py:93
  238.0 20.3 reshape.2063
  320.0 20.3 reshape.2063
  401.9 20.3 reshape.2063
  483.8 20.3 reshape.2063
  565.7 20.3 reshape.2063
  647.6 20.3 reshape.2063
  729.6 20.3 reshape.2063
  811.5 20.3 reshape.2063
  873.7 801.2 %while.50 = (s32[]{:T(128)}, bf16[8,512,1,1536]{3,1,0,2:T(8,128)(2,1)}, s32[1,256]{1,0:T(1,128)}, s32[8]{0:T(128)}, s32[4096,1]{0,1:T(1,128)}, /*index=5*/bf16[4...) while((s32[]{:T(128)}, ...), condition=%wide.region_16.17_spmd, body=%wide.region_15.16_spmd.sunk | while | flops 825533376 | bytes 137081552 | solution.py:335
  917.1 20.3 reshape.2062
  1017.2 20.3 reshape.2062
  1117.3 20.3 reshape.2062
  1217.5 20.3 reshape.2062
  1317.6 20.3 reshape.2062
  1417.8 20.3 reshape.2062
  1517.9 20.3 reshape.2062
  1618.0 20.3 reshape.2062
  1675.1 1199.9 %while.52 = (s32[]{:T(128)}, f32[1,12,256,64]{2,3,1,0:T(8,128)}, f32[32,12]{0,1:T(8,128)}, s32[1,256]{1,0:T(1,128)}, s32[4096,1]{0,1:T(1,128)}, /*index=5*/bf16[...) while((s32[]{:T(128)}, f32[1,12,256,64]{2,3,1,0:T(8,128)}, ...), condition=%wide.region_14.15_spmd.clone, body=%wide.region_12.14_spmd.clone.sunk | while | flops 627554432 | bytes 209427152 | solution.py:93
  1743.8 20.3 reshape.2065
  1889.4 20.3 reshape.2065
  2035.5 20.3 reshape.2065
  2947.2 41.7 %all-reduce.5 = (f32[768]{0:T(1024)}, f32[768]{0:T(1024)}, f32[32,12]{0,1:T(8,128)}, f32[768]{0:T(1024)}, f32[4]{0:T(128)}) all-reduce(f32[768]{0:T(1024)S(1)} %get-tuple-element.1183, f32[768]{0:T(1024)S(1)} %copy-done.86, f32[32,12]{0,1:T(8,128)S(1)} %copy-done.92, ...), channel_id=1, replica_groups=mesh['dp'=2,'blk'=16] {'dp','blk'}, use_global_device_ids=true, to_apply=%region_22.23 | all-reduce | flops 2692 | bytes 21536 | tf_op jit(solution)/shard_map/psum | solution.py:403
  3006.8 76.4 %reduce-scatter.17.cloned.1.call-done = f32[24,768]{1,0:T(8,128)} async-done(((f32[768,768]{1,0:T(8,128)}), f32[24,768]{1,0:T(8,128)}) %reduce-scatter.17.cloned.1.call-update) | async-done | bytes 73744 | tf_op jit(solution)/shard_map/reduce_scatter | solution.py:398
  3083.2 119.7 %reduce-scatter.21.cloned.1.call-done = f32[24,2048]{1,0:T(8,128)} async-done(((f32[768,2048]{1,0:T(8,128)}), f32[24,2048]{1,0:T(8,128)}) %reduce-scatter.21.cloned.1.call-update) | async-done | bytes 196624 | tf_op jit(solution)/shard_map/reduce_scatter | solution.py:400
  3202.9 121.0 %reduce-scatter.19.cloned.1.call-done = f32[24,2048]{1,0:T(8,128)} async-done(((f32[768,2048]{1,0:T(8,128)}), f32[24,2048]{1,0:T(8,128)}) %reduce-scatter.19.cloned.1.call-update) | async-done | bytes 196624 | tf_op jit(solution)/shard_map/reduce_scatter | solution.py:399
  3323.9 120.1 %reduce-scatter.23.cloned.1.call-done = f32[64,768]{1,0:T(8,128)} async-done(((f32[2048,768]{1,0:T(8,128)}), f32[64,768]{1,0:T(8,128)}) %reduce-scatter.23.cloned.1.call-update) | async-done | bytes 196624 | tf_op jit(solution)/shard_map/reduce_scatter | solution.py:401
  3444.0 105.2 %reduce-scatter.15.cloned.1.call-done = f32[24,768]{1,0:T(8,128)} async-done(((f32[768,768]{1,0:T(8,128)}), f32[24,768]{1,0:T(8,128)}) %reduce-scatter.15.cloned.1.call-update) | async-done | bytes 73744 | tf_op jit(solution)/shard_map/reduce_scatter | solution.py:397
  3549.2 103.8 %reduce-scatter.13.cloned.1.call-done = f32[24,768]{1,0:T(8,128)} async-done(((f32[768,768]{1,0:T(8,128)}), f32[24,768]{1,0:T(8,128)}) %reduce-scatter.13.cloned.1.call-update) | async-done | bytes 73744 | tf_op jit(solution)/shard_map/reduce_scatter | solution.py:396
  (977 shorter events, 2390.7 us)
Async XLA Ops:
  7.2 853.5 %copy-start = (bf16[2048,768]{1,0:T(8,128)(2,1)S(1)}, bf16[2048,768]{1,0:T(8,128)(2,1)}, u32[]{:S(2)}) copy-start(bf16[2048,768]{1,0:T(8,128)(2,1)} %param.32) | copy-start | bytes 9437188
  7.2 20.1 copy-start.87
  7.2 117.3 %all-gather.8.cloned.1.call-start = ((), (), s32[]{:S(2)}) async-start(), calls=%async_computation.17 | async-start | bytes 6684672 | tf_op jit(solution)/shard_map/all_gather | solution.py:212
  8.7 17.3 collective-permute-start.3
  10.0 16.0 collective-permute-start.2
  15.0 13.7 collective-permute-start.1
  17.2 11.6 collective-permute-start
  25.2 32.1 copy-start.47
  25.9 8.9 copy-start.53
  57.8 31.3 copy-start.16
  59.1 128.7 %all-gather.6.cloned.1.call-start = ((), (), s32[]{:S(2)}) async-start(), calls=%async_computation.16 | async-start | bytes 6684672 | tf_op jit(solution)/shard_map/all_gather | solution.py:211
  61.7 2838.7 %reduce-scatter.9.cloned.1.call-start = ((), (), s32[]{:S(2)}) async-start(), calls=%async_computation.8 | async-start | bytes 13369344 | tf_op jit(solution)/shard_map/reduce_scatter | solution.py:338
  857.3 9.9 copy-start.21
  1675.0 1331.7 %reduce-scatter.11.cloned.1.call-start = ((), (), s32[]{:S(2)}) async-start(), calls=%async_computation.9 | async-start | bytes 2433024 | tf_op jit(solution)/shard_map/reduce_scatter | solution.py:395
  1776.8 9.4 copy-start.3
  1922.4 8.8 copy-start.3
  2068.5 8.8 copy-start.3
  2214.6 8.8 copy-start.3
  2360.7 8.8 copy-start.3
  2506.8 8.8 copy-start.3
  2652.9 8.8 copy-start.3
  2799.0 8.8 copy-start.3
  2879.8 203.3 %reduce-scatter.17.cloned.1.call-start = ((), (), s32[]{:S(2)}) async-start(), calls=%async_computation.12 | async-start | bytes 2433024 | tf_op jit(solution)/shard_map/reduce_scatter | solution.py:398
  2883.1 319.8 %reduce-scatter.21.cloned.1.call-start = ((), (), s32[]{:S(2)}) async-start(), calls=%async_computation.14 | async-start | bytes 6488064 | tf_op jit(solution)/shard_map/reduce_scatter | solution.py:400
  2888.0 435.9 %reduce-scatter.19.cloned.1.call-start = ((), (), s32[]{:S(2)}) async-start(), calls=%async_computation.13 | async-start | bytes 6488064 | tf_op jit(solution)/shard_map/reduce_scatter | solution.py:399
  2893.0 551.0 %reduce-scatter.23.cloned.1.call-start = ((), (), s32[]{:S(2)}) async-start(), calls=%async_computation.15 | async-start | bytes 6488064 | tf_op jit(solution)/shard_map/reduce_scatter | solution.py:401
  2899.0 650.2 %reduce-scatter.15.cloned.1.call-start = ((), (), s32[]{:S(2)}) async-start(), calls=%async_computation.11 | async-start | bytes 2433024 | tf_op jit(solution)/shard_map/reduce_scatter | solution.py:397
  2903.3 749.7 %reduce-scatter.13.cloned.1.call-start = ((), (), s32[]{:S(2)}) async-start(), calls=%async_computation.10 | async-start | bytes 2433024 | tf_op jit(solution)/shard_map/reduce_scatter | solution.py:396
  2939.3 7.9 copy-start.86
  2939.3 7.9 copy-start.92
  2939.3 50.8 %collective-permute-start.5 = (bf16[1,2,3072]{2,1,0:T(2,128)(2,1)S(1)}, bf16[1,2,3072]{2,1,0:T(2,128)(2,1)S(1)}, u32[]{:S(2)}, u32[]{:S(2)}) collective-permute-start(bf16[1,2,3072]{2,1,0:T(2,128)(2,1)S(1)} %copy.146), channel_id=1, source_target_pairs={{1,0},{2,1},{3,2},{4,3},{5,4},{6,5},{7,6},{8,7},{9,8},{10,9},{11,1... | collective-permute-start | bytes 36872 | tf_op jit(solution)/shard_map/ppermute | solution.py:24
  2940.8 48.1 %collective-permute-start.4 = (bf16[1,2,3072]{2,1,0:T(2,128)(2,1)S(1)}, bf16[1,2,3072]{2,1,0:T(2,128)(2,1)S(1)}, u32[]{:S(2)}, u32[]{:S(2)}) collective-permute-start(bf16[1,2,3072]{2,1,0:T(2,128)(2,1)S(1)} %copy.145), channel_id=1, source_target_pairs={{0,1},{1,2},{2,3},{3,4},{4,5},{5,6},{6,7},{7,8},{8,9},{9,10},{10,1... | collective-permute-start | bytes 36872 | tf_op jit(solution)/shard_map/ppermute | solution.py:23
  (156 other events, 378.3 us)
Sparse Core Ops, SparseCore 0:
  59.2 65.2 all-gather.7
  127.3 60.4 all-gather.5
  1675.1 133.3 reduce-scatter.8
  2880.0 98.5 reduce-scatter.10
  2985.1 98.0 reduce-scatter.16
  3089.2 113.6 reduce-scatter.20
  3210.0 113.8 reduce-scatter.18
  3330.1 113.8 reduce-scatter.22
  3450.7 98.3 reduce-scatter.14
  3554.9 98.0 reduce-scatter.12
where the time goes:
time: 3680 us; the launch traced here: 3660 us
  local copies, waits for them, and re-layouts  2160 us (59%)
  waiting for transfers between devices  733 us (20%)
  matrix products  383 us (10%)
  other arithmetic  214 us (6%)
  loops' own time  70 us (2%)
  blocking collectives  65.2 us (2%)
    another operation x48, local copies, waits for them, and re-layouts, toeplitz(): repeated = jnp.tile(band_values, (1, query_count))  499 us
    reshape x24, local copies, waits for them, and re-layouts, toeplitz(): flattened.reshape(band_values.shape[0], query_count, band_len - 1)  488 us
    slice x24, local copies, waits for them, and re-layouts, toeplitz(): repeated[:, query_count - 1:query_count - 1 + query_count * (band_len - 1)]  279 us
    while x216, local copies, waits for them, and re-layouts  219 us
    reshape x8, local copies, waits for them, and re-layouts, diagonal_sums(): return jnp.sum(flattened.reshape(head_count, query_count, band_len), axis=1)  160 us
    slice x24, local copies, waits for them, and re-layouts, toeplitz(): flattened.reshape(band_values.shape[0], query_count, band_len - 1)  147 us
    dot_general x24, matrix products, pair_scores(): jnp.einsum('rqhd,krhd->rhqk', query_part, key_heads, preferred_element_ty...  123 us
    reduce_scatter x1, waiting for transfers between devices, body(): lax.psum_scatter(grad_gate, ('dp', 'blk'), scatter_dimension=0, tiled=True)  121 us
  transfers between devices with their start and end apart: 16, of which 8 were waited for; matrix products, arithmetic and copies ran while one was open for 34% of the time, Pallas kernels for 0%

commit v1 on v0

v1 whole, which is shorter than its diff:
```python
import functools
import math

import jax
import jax.numpy as jnp
from jax import lax
from jax.experimental import pallas as pl
from jax.experimental.pallas import tpu as pltpu
from jax.sharding import PartitionSpec as P

BUCKETS = 32
MAX_BLOCK = 4
VMEM_BYTES = 60 * 2**20


def extended(shard, sides, width):
    for axis, dim in sides:
        peers, length = (lax.axis_size(axis), shard.shape[dim])
        up = [(i, (i + 1) % peers) for i in range(peers - 1)]
        down = [(j, i) for i, j in up]
        last = lax.slice_in_dim(shard, length - width, length, axis=dim)
        leading = lax.slice_in_dim(shard, 0, width, axis=dim)
        before = lax.ppermute(last, axis, up)
        after = lax.ppermute(leading, axis, down)
        shard = jnp.concatenate([before, shard, after], axis=dim)
    return shard


def buckets_of(relative):
    distance = jnp.abs(relative)
    beyond = jnp.zeros_like(distance)
    for border in (12, 16, 23, 32, 46, 64, 91):
        beyond = beyond + (distance >= border).astype(jnp.int32)
    nearer = jnp.where(distance < 8, distance, 8 + beyond)
    return nearer + BUCKETS // 2 * (relative > 0).astype(jnp.int32)


def rms_norm(values, gain):
    return values * lax.rsqrt(jnp.mean(values * values, axis=-1, keepdims=True) + 1e-06) * gain


def geglu(gate_proj, up_proj):
    return jax.nn.gelu(gate_proj, approximate=True) * up_proj


def pool_masks(labels, base, length):
    positions = jnp.arange(length + 6, dtype=jnp.int32) + base - 3
    centre = labels[:, 3 : 3 + length]
    centre_pos = positions[3 : 3 + length]
    result = []
    for block_width in range(1, MAX_BLOCK + 1):
        pool_terms = []
        for offset in range(1 - block_width, block_width):
            near_labels = labels[:, 3 + offset : 3 + offset + length]
            near_pos = positions[3 + offset : 3 + offset + length]
            same_block = near_pos // block_width == centre_pos // block_width
            keep_mask = jnp.logical_and(near_labels == centre, same_block[None, :])
            pool_terms.append((offset, keep_mask.astype(jnp.float32)))
        counts = sum((entry[1] for entry in pool_terms))
        result.append((pool_terms, counts))
    return result


MESH_ID = pl.DeviceIdType.MESH
GROUPS = 4


def bits_of(size):
    return [1 << p for p in reversed(range(size.bit_length() - 1))]


def bit(value, mask):
    return (value // mask) % 2


def flipped(value, mask):
    return value + mask * (1 - 2 * bit(value, mask))


class Place:
    def __init__(self, shards):
        self.shards = shards
        self.rest_size = shards // GROUPS
        self.dp = lax.axis_index("dp")
        self.blk = lax.axis_index("blk")
        self.row = self.dp % 2
        self.group = self.blk // self.rest_size
        self.rest = self.blk % self.rest_size

    def at(self, row, group, rest):
        return (self.dp - self.row + row, group * self.rest_size + rest)

    def chunk(self, group, rest):
        return group * self.rest_size + rest

    def other_row(self):
        return self.at(1 - self.row, self.group, self.rest)

    def other_rest(self, mask):
        return self.at(self.row, self.group, flipped(self.rest, mask))

    def other_group(self, step):
        return self.at(self.row, (self.group + step) % GROUPS, self.rest)


def greet(targets):
    barrier = pltpu.get_barrier_semaphore()
    for target in targets:
        pl.semaphore_signal(barrier, inc=1, device_id=target, device_id_type=MESH_ID)
    pl.semaphore_wait(barrier, len(targets))


def remote(src, dst, send_sem, recv_sem, target):
    return pltpu.make_async_remote_copy(
        src_ref=src,
        dst_ref=dst,
        send_sem=send_sem,
        recv_sem=recv_sem,
        device_id=target,
        device_id_type=MESH_ID,
    )


def line_and_row(place):
    found = []
    for step in range(GROUPS):
        for flip in range(2):
            if step or flip:
                row = 1 - place.row if flip else place.row
                found.append(place.at(row, (place.group + step) % GROUPS, place.rest))
    return found


def spread_heads(place, q_ref, out_ref, send_sem, recv_sem):
    row_to = place.group // 2
    slot = place.group % 2
    dst = out_ref.at[place.row, slot]
    mine = recv_sem.at[place.row * 2 + slot]
    at_home = row_to == place.row
    for step in range(GROUPS):
        group = (place.group + step) % GROUPS
        src = q_ref.at[group]
        copy = remote(src, dst, send_sem.at[step], mine, place.at(row_to, group, place.rest))
        if step:
            copy.start()
        else:
            pl.when(jnp.logical_not(at_home))(copy.start)
            pl.when(at_home)(pltpu.make_async_copy(src, dst, mine).start)


def spread_heads_wait(place, q_ref, out_ref, send_sem, recv_sem):
    at_home = place.group // 2 == place.row
    for row in range(2):
        for slot in range(2):
            pltpu.make_async_copy(q_ref.at[0], out_ref.at[row, slot], recv_sem.at[row * 2 + slot]).wait()
    for step in range(GROUPS):
        copy = remote(q_ref.at[0], out_ref.at[0, 0], send_sem.at[step], recv_sem.at[0], place.other_row())
        if step:
            copy.wait_send()
        else:
            pl.when(jnp.logical_not(at_home))(copy.wait_send)


def return_heads(place, o_ref, out_ref, send_sem, recv_sem):
    for row in range(2):
        for slot in range(2):
            group = place.row * 2 + slot
            src = o_ref.at[row, slot]
            dst = out_ref.at[place.group]
            mine = recv_sem.at[place.group]
            at_home = jnp.logical_and(place.row == row, place.group == group)
            copy = remote(src, dst, send_sem.at[row * 2 + slot], mine, place.at(row, group, place.rest))
            pl.when(jnp.logical_not(at_home))(copy.start)
            pl.when(at_home)(pltpu.make_async_copy(src, dst, mine).start)


def return_heads_wait(place, o_ref, out_ref, send_sem, recv_sem):
    for group in range(GROUPS):
        pltpu.make_async_copy(o_ref.at[0, 0], out_ref.at[group], recv_sem.at[group]).wait()
    for row in range(2):
        for slot in range(2):
            group = place.row * 2 + slot
            at_home = jnp.logical_and(place.row == row, place.group == group)
            copy = remote(o_ref.at[0, 0], out_ref.at[0], send_sem.at[row * 2 + slot], recv_sem.at[0], place.other_row())
            pl.when(jnp.logical_not(at_home))(copy.wait_send)


def spread_kernel(shards, q_ref, out_ref, send_sem, recv_sem):
    place = Place(shards)
    greet(line_and_row(place))
    spread_heads(place, q_ref, out_ref, send_sem, recv_sem)
    spread_heads_wait(place, q_ref, out_ref, send_sem, recv_sem)


def return_kernel(shards, o_ref, out_ref, send_sem, recv_sem):
    place = Place(shards)
    greet(line_and_row(place))
    return_heads(place, o_ref, out_ref, send_sem, recv_sem)
    return_heads_wait(place, o_ref, out_ref, send_sem, recv_sem)


def move_heads(kernel, lead, shards, ident, packed):
    rows, lanes = packed.shape[-2:]
    return pl.pallas_call(
        functools.partial(kernel, shards),
        out_shape=jax.ShapeDtypeStruct(lead + (rows, lanes), packed.dtype),
        in_specs=[pl.BlockSpec(memory_space=pltpu.VMEM)],
        out_specs=pl.BlockSpec(memory_space=pltpu.VMEM),
        scratch_shapes=[pltpu.SemaphoreType.DMA((4,)), pltpu.SemaphoreType.DMA((4,))],
        compiler_params=pltpu.CompilerParams(collective_id=ident, has_side_effects=True, vmem_limit_bytes=VMEM_BYTES),
        name="move_heads_%d" % ident,
    )(packed)


def gather_kernel(shards, q_ref, kv_ref, label_ref, qo_ref, kvo_ref, labo_ref, q_send, q_recv, z_send, far_send, core_send, kv_recv, own_sem, lab_send, lab_recv):
    place = Place(shards)
    tokens = kv_ref.shape[1]
    rest_bits = bits_of(place.rest_size)
    core, far = rest_bits[-1], ["row"] + rest_bits[:-1]
    greet(line_and_row(place) + [place.other_rest(mask) for mask in rest_bits])

    dims = [("row", 1)] + [("blk", m) for m in bits_of(shards)]
    lab_index = [place.row] + [bit(place.blk, m) for _, m in dims[1:]]
    lab_order = list(range(len(dims)))

    def lab_copy(stage):
        index = tuple(slice(None) if p in lab_order[:stage] else lab_index[p] for p in range(len(dims)))
        axis, mask = dims[lab_order[stage]]
        target = place.other_row() if axis == "row" else (place.dp, flipped(place.blk, mask))
        there = labo_ref.at[index]
        return remote(there, there, lab_send.at[stage], lab_recv.at[stage], target)

    labo_ref[tuple(lab_index)] = label_ref[...]
    lab_copy(0).start()
    lab_stage = 0

    def slot(row, group, rest):
        start = pl.multiple_of(place.chunk(group, rest) * tokens, tokens)
        return kvo_ref.at[row, pl.ds(start, tokens)]

    def held(dz, offset, core_off):
        row = 1 - place.row if offset & 1 else place.row
        rest = place.rest
        for p, mask in enumerate(far[1:]):
            if offset >> (p + 1) & 1:
                rest = flipped(rest, mask)
        if core_off:
            rest = flipped(rest, core)
        return slot(row, (place.group + dz) % GROUPS, rest)

    count = 1 << len(far)

    def sem_of(dz, offset, core_off):
        return kv_recv.at[(core_off * count + offset) * GROUPS + dz]

    own = pltpu.make_async_copy(kv_ref.at[place.group], held(0, 0, 0), own_sem)
    own.start()
    waits = []
    for step in (1, 3, 2):
        copy = remote(kv_ref.at[(place.group + step) % GROUPS], held(0, 0, 0), z_send.at[step], sem_of((GROUPS - step) % GROUPS, 0, 0), place.other_group(step))
        copy.start()
        waits.append(copy)
    spread_heads(place, q_ref, qo_ref, q_send, q_recv)

    used = 0
    events = sorted(((dz, off) for dz in range(GROUPS) for off in range(count)), key=lambda e: (bin(e[1]).count("1"), (0, 1, 3, 2).index(e[0])))
    core_target = place.other_rest(core)
    for dz, off in events:
        here = held(dz, off, 0)
        if dz == 0 and off == 0:
            src = kv_ref.at[place.group]
        else:
            remote(here, here, z_send.at[0], sem_of(dz, off, 0), core_target).wait_recv()
            src = here
        order = [(p + dz) % len(far) for p in range(len(far))]
        last = max([order.index(p) for p in range(len(far)) if off >> p & 1], default=-1)
        for p in order[last + 1 :]:
            target = place.other_row() if p == 0 else place.other_rest(far[p])
            copy = remote(src, here, far_send.at[used], sem_of(dz, off | 1 << p, 0), target)
            copy.start()
            waits.append(copy)
            used += 1
        copy = remote(src, here, core_send.at[off * GROUPS + dz], sem_of(dz, off, 1), core_target)
        copy.start()
        waits.append(copy)
        if lab_stage < len(dims):
            lab_copy(lab_stage).wait()
            lab_stage += 1
            if lab_stage < len(dims):
                lab_copy(lab_stage).start()
    for dz, off in events:
        here = held(dz, off, 1)
        remote(here, here, z_send.at[0], sem_of(dz, off, 1), core_target).wait_recv()
    own.wait()
    for copy in waits:
        copy.wait_send()
    spread_heads_wait(place, q_ref, qo_ref, q_send, q_recv)


def gather_all(shards, q_packed, kv_parts, labels):
    tokens, width = kv_parts.shape[1:]
    far = 1 + len(bits_of(shards // GROUPS)) - 1
    count = 1 << far
    nbits = 1 + len(bits_of(shards))
    sem = pltpu.SemaphoreType.DMA
    return pl.pallas_call(
        functools.partial(gather_kernel, shards),
        out_shape=(
            jax.ShapeDtypeStruct((2, 2) + q_packed.shape[1:], q_packed.dtype),
            jax.ShapeDtypeStruct((2, shards * tokens, width), kv_parts.dtype),
            jax.ShapeDtypeStruct((2,) * nbits + labels.shape, labels.dtype),
        ),
        in_specs=[pl.BlockSpec(memory_space=pltpu.VMEM)] * 3,
        out_specs=(pl.BlockSpec(memory_space=pltpu.VMEM),) * 3,
        scratch_shapes=[
            sem((4,)), sem((4,)), sem((GROUPS,)), sem((GROUPS * (count - 1),)), sem((GROUPS * count,)), sem((GROUPS * count * 2,)),
            sem, sem((nbits,)), sem((nbits,)),
        ],
        compiler_params=pltpu.CompilerParams(collective_id=1, has_side_effects=True, vmem_limit_bytes=VMEM_BYTES),
        name="gather_keys",
    )(q_packed, kv_parts, labels)


def add_blocks(dst_ref, src_ref, index, shape):
    lead = shape[:-2]
    total = math.prod(lead)

    def one(step, _):
        place, left = [], step
        for size in reversed(lead):
            place.append(left % size)
            left = left // size
        place = tuple(reversed(place))
        full, k = [], 0
        for entry in index:
            if entry is None:
                full.append(place[k])
                k += 1
            else:
                full.append(entry)
        mine = src_ref[tuple(full)].astype(jnp.float32)
        dst_ref[place] = (dst_ref[place].astype(jnp.float32) + mine).astype(dst_ref.dtype)
        return 0

    lax.fori_loop(0, total, one, 0)


def reduce_kernel(shards, q_ref, kv_ref, qo_ref, kvo_ref, q_send, q_recv, send_sem, recv_sem, z_send, z_recv, *bufs):
    place = Place(shards)
    rest_bits = bits_of(place.rest_size)
    greet(line_and_row(place) + [place.other_rest(mask) for mask in rest_bits])
    return_heads(place, q_ref, qo_ref, q_send, q_recv)
    ndim = 1 + len(rest_bits)
    own = [place.row] + [bit(place.rest, m) for m in rest_bits]
    targets = [place.other_row()] + [place.other_rest(m) for m in rest_bits]
    state = {}

    def plan(group_step):
        far = list(range(ndim - 1))
        turn = group_step % len(far)
        return [ndim - 1] + far[turn:] + far[:turn]

    def copy_of(step, stage):
        order = plan(step)
        group = (place.group + step) % GROUPS
        done = order[:stage]
        p_now = order[stage]
        buf = bufs[stage].at[step]
        if stage == 0:
            index = (p_index(group, done, p_now))
            src = kv_ref.at[index]
        else:
            kept = [p for p in range(ndim) if p not in done]
            src = bufs[stage - 1].at[(step,) + tuple(1 - own[p] if p == p_now else slice(None) for p in kept)]
        return remote(src, buf, send_sem.at[stage, step], recv_sem.at[stage, step], targets[p_now])

    def p_index(group, done, p_now):
        index = [slice(None)] * ndim
        index[p_now] = 1 - own[p_now]
        return (index[0], group) + tuple(index[1:])

    def absorb(step, stage):
        order = plan(step)
        done, p_now = order[:stage], order[stage]
        buf = bufs[stage].at[step]
        group = (place.group + step) % GROUPS
        if stage == 0:
            index = [None] * ndim
            index[p_now] = own[p_now]
            add_blocks(buf, kv_ref, (index[0], group) + tuple(index[1:]), buf.shape)
        else:
            kept = [p for p in range(ndim) if p not in done]
            index = tuple(own[p] if p == p_now else None for p in kept)
            add_blocks(buf, bufs[stage - 1].at[step], index, buf.shape)

    steps = (2, 1, 3, 0)
    for step in steps:
        copy_of(step, 0).start()
    for stage in range(ndim):
        for step in steps:
            copy_of(step, stage).wait()
            absorb(step, stage)
            if stage < ndim - 1:
                copy_of(step, stage + 1).start()
            elif step:
                remote(bufs[stage].at[step], kvo_ref.at[place.group], z_send.at[step], z_recv.at[(GROUPS - step) % GROUPS], place.other_group(step)).start()
            else:
                kvo_ref[place.group] = bufs[stage][step]
    for step in (1, 3, 2):
        there = kvo_ref.at[(place.group + step) % GROUPS]
        remote(bufs[ndim - 1].at[step], there, z_send.at[step], z_recv.at[step], place.other_group(step)).wait()
    return_heads_wait(place, q_ref, qo_ref, q_send, q_recv)


def reduce_all(shards, q_packed, kv_sums):
    tokens_all, width = kv_sums.shape[1:]
    tokens = tokens_all // shards
    rest_bits = bits_of(shards // GROUPS)
    ndim = 1 + len(rest_bits)
    sem = pltpu.SemaphoreType.DMA
    return pl.pallas_call(
        functools.partial(reduce_kernel, shards),
        out_shape=(
            jax.ShapeDtypeStruct((GROUPS,) + q_packed.shape[2:], q_packed.dtype),
            jax.ShapeDtypeStruct((GROUPS, tokens, width), kv_sums.dtype),
        ),
        in_specs=[pl.BlockSpec(memory_space=pltpu.VMEM)] * 2,
        out_specs=(pl.BlockSpec(memory_space=pltpu.VMEM),) * 2,
        scratch_shapes=[sem((4,)), sem((4,)), sem((ndim, GROUPS)), sem((ndim, GROUPS)), sem((GROUPS,)), sem((GROUPS,))]
        + [pltpu.VMEM((GROUPS,) + (2,) * (ndim - 1 - s) + (tokens, width), kv_sums.dtype) for s in range(ndim)],
        compiler_params=pltpu.CompilerParams(collective_id=2, has_side_effects=True, vmem_limit_bytes=VMEM_BYTES),
        name="reduce_keys",
    )(q_packed, kv_sums.reshape((2, GROUPS) + (2,) * len(rest_bits) + (tokens, width)))


def weights_kernel(orders, axes, *refs):
    streams = len(orders) - 1
    ins, small_ref = refs[:streams], refs[streams]
    outs, small_out = refs[streams + 1 : 2 * streams + 1], refs[2 * streams + 1]
    send_sem, recv_sem = refs[2 * streams + 2 : 2 * streams + 4]
    bufs = refs[2 * streams + 4 :]
    ndim = len(axes)
    at = {"dp": lax.axis_index("dp"), "blk": lax.axis_index("blk")}
    own = [bit(at[axis], mask) for axis, mask in axes]

    def target(p):
        axis, mask = axes[p]
        moved = dict(at)
        moved[axis] = flipped(at[axis], mask)
        return (moved["dp"], moved["blk"])

    greet([target(p) for p in range(ndim)])
    small_bufs = bufs[streams * ndim]
    small_out[...] = small_ref[...]

    def parts(s, stage):
        order = orders[s]
        if s == streams:
            src = small_ref if stage == 0 else small_bufs.at[1, stage - 1]
            return src, small_bufs.at[0, stage], None
        kept = [p for p in range(ndim) if p not in order[:stage]]
        src = ins[s] if stage == 0 else bufs[s * ndim + stage - 1]
        return src, bufs[s * ndim + stage], kept

    def copy_of(s, stage):
        src, buf, kept = parts(s, stage)
        p_now = orders[s][stage]
        if kept is not None:
            src = src.at[tuple(1 - own[p] if p == p_now else slice(None) for p in kept)]
        return remote(src, buf, send_sem.at[s, stage], recv_sem.at[s, stage], target(p_now))

    def absorb(s, stage):
        src, buf, kept = parts(s, stage)
        if kept is None:
            total = src[...] + buf[...]
            if stage == ndim - 1:
                small_out[...] = total
            else:
                small_bufs[1, stage] = total
            return
        p_now = orders[s][stage]
        index = tuple(own[p] if p == p_now else None for p in kept)
        if stage == ndim - 1:
            outs[s][...] = buf[...].astype(jnp.float32) + src[index[0]].astype(jnp.float32)
        else:
            add_blocks(buf, src, index, buf.shape)

    for s in range(streams + 1):
        copy_of(s, 0).start()
    for stage in range(ndim):
        for s in range(streams + 1):
            copy_of(s, stage).wait()
            absorb(s, stage)
            if stage < ndim - 1:
                copy_of(s, stage + 1).start()


def reduce_weights(shape, blocks, small):
    axes = [("dp", m) for m in bits_of(shape["dp"])] + [("blk", m) for m in bits_of(shape["blk"])]
    ndim = len(axes)
    rest_bits = bits_of(shape["blk"] // GROUPS)
    core = ndim - 1
    across = list(range(len(bits_of(shape["dp"]))))
    up = [ndim - len(rest_bits) + p for p in range(len(rest_bits) - 1)]
    along = [ndim - len(rest_bits) - 1, ndim - len(rest_bits) - 2]
    first = [core] + across + up + along
    second = [core] + up + across + along
    orders = [first if s % 2 == 0 else second for s in range(len(blocks))] + [first]
    sem = pltpu.SemaphoreType.DMA
    scratch = []
    for block in blocks:
        rows, cols = block.shape[-2:]
        scratch += [pltpu.VMEM((2,) * (ndim - 1 - s) + (rows, cols), block.dtype) for s in range(ndim)]
    scratch.append(pltpu.VMEM((2, ndim) + small.shape, small.dtype))
    wide = [block.reshape((2,) * ndim + block.shape[-2:]) for block in blocks]
    found = pl.pallas_call(
        functools.partial(weights_kernel, orders, axes),
        out_shape=tuple(jax.ShapeDtypeStruct(b.shape[-2:], jnp.float32) for b in blocks) + (jax.ShapeDtypeStruct(small.shape, small.dtype),),
        in_specs=[pl.BlockSpec(memory_space=pltpu.VMEM)] * (len(blocks) + 1),
        out_specs=(pl.BlockSpec(memory_space=pltpu.VMEM),) * (len(blocks) + 1),
        scratch_shapes=[sem((len(blocks) + 1, ndim)), sem((len(blocks) + 1, ndim))] + scratch,
        compiler_params=pltpu.CompilerParams(collective_id=3, has_side_effects=True, vmem_limit_bytes=VMEM_BYTES),
        name="reduce_weights",
    )(*wide, small)
    return found[:-1], found[-1]


TQ = 256
TK = 512
NEAR_ROWS = 448
NEG = -1e30
FIRST_MAX = -1e29
NT = (((1,), (1,)), ((), ()))
NN = (((1,), (0,)), ((), ()))
BORDERS = (12, 16, 23, 32, 46, 64, 91)


def mxu(left, right, dims=NN):
    return lax.dot_general(left, right, dims, preferred_element_type=jnp.float32)


def turned(tile):
    return jnp.concatenate([tile[:, 64:], tile[:, :64]], axis=1)


def spread_lanes(packed, high):
    lane = lax.broadcasted_iota(jnp.int32, (1, 128), 1)
    keep = lane >= 64 if high else lane < 64
    zero = jnp.zeros((), packed.dtype)
    pair, last = packed[0:TQ], packed[TQ:]
    pick = lambda tile: jnp.where(keep, tile, zero)
    if high:
        return [pick(turned(pair)), pick(pair), jnp.concatenate([pick(turned(last)), pick(last)], axis=0)]
    return [pick(pair), pick(turned(pair)), jnp.concatenate([pick(last), pick(turned(last))], axis=0)]


def join_heads(parts):
    half = TQ // 2
    top = jnp.concatenate([parts[0], parts[1]], axis=1)
    low = jnp.concatenate([parts[2][:half], parts[2][half:]], axis=1)
    return jnp.concatenate([top, low], axis=0)


def valid_mask(se_ref, r, i, k0):
    kpos = k0 + lax.broadcasted_iota(jnp.int32, (TK, TQ), 0)
    return jnp.logical_and(kpos >= se_ref[r, i, 0:1, :], kpos < se_ref[r, i, 1:2, :])


def near_buckets(first, rows, parity):
    relative = (
        first - TK + TQ * parity
        + lax.broadcasted_iota(jnp.int32, (rows, TQ), 0)
        - lax.broadcasted_iota(jnp.int32, (rows, TQ), 1)
    )
    return buckets_of(relative)


def make_bias(table, parity, bias_ref):
    heads = bias_ref.shape[0]
    for h in range(heads):
        bias_ref[h, 0] = jnp.full((TK, TQ), table[h, 15], jnp.float32).astype(jnp.bfloat16)
        bias_ref[h, 3] = jnp.full((TK, TQ), table[h, 31], jnp.float32).astype(jnp.bfloat16)
    for tile in range(2):
        def rows(step, _):
            start = pl.multiple_of(step * 32, 32)
            which = near_buckets(tile * TK + start, 32, parity)
            for h in range(heads):
                value = jnp.zeros((32, TQ), jnp.float32)
                for b in range(BUCKETS):
                    value = jnp.where(which == b, table[h, b], value)
                bias_ref[h, tile + 1, pl.ds(start, 32)] = value.astype(jnp.bfloat16)
            return 0
        lax.fori_loop(0, TK // 32, rows, 0)


def tile_kind(bounds, r, i, t):
    slot = jnp.clip(t - bounds[r, i, 2] + 1, 0, 3)
    away = jnp.logical_or(slot == 0, slot == 3)
    inside = jnp.logical_and(t >= bounds[r, i, 3], t < bounds[r, i, 4])
    return slot, jnp.logical_and(away, inside)


def fwd_kernel(bounds, table, q_ref, kv_ref, se_ref, o_ref, keep_ref, lse_ref, bias_ref, vt, acc, mx, qp):
    heads = lse_ref.shape[2]
    make_bias(table, bounds[0, 0, 5], bias_ref)
    for r in range(2):
        for i in range(2):
            for h, tile in enumerate(spread_lanes(q_ref[r, i], False)):
                qp[r, i, h] = tile

    def row_body(r, _):
        lo_all = jnp.minimum(bounds[r, 0, 0], bounds[r, 1, 0])
        hi_all = jnp.maximum(bounds[r, 0, 1], bounds[r, 1, 1])

        def turn(t, _):
            k0 = pl.multiple_of(t * TK, TK)
            for h in range(heads):
                tile = kv_ref[r, pl.ds(k0, TK), h * 128 : h * 128 + 128]
                vt[h, 0:64, pl.ds(k0, TK)] = tile.T[64:128, :]
                vt[h, 64:80, pl.ds(k0, TK)] = jnp.ones((16, TK), jnp.bfloat16)
            return 0

        lax.fori_loop(lo_all, hi_all, turn, 0)

        def q_body(i, _):
            acc[...] = jnp.zeros_like(acc)
            mx[...] = jnp.full_like(mx, FIRST_MAX)

            def tile_body(t, _):
                k0 = pl.multiple_of(t * TK, TK)
                slot, plain = tile_kind(bounds, r, i, t)

                def scores(h):
                    return mxu(kv_ref[r, pl.ds(k0, TK), h * 128 : h * 128 + 128], qp[r, i, h], NT)

                def finish(h, s, b):
                    m_old = mx[h]
                    m_new = jnp.maximum(m_old, jnp.max(s, axis=0, keepdims=True) + b)
                    p = jnp.exp(s - (m_new - b)).astype(jnp.bfloat16)
                    mx[h] = m_new
                    acc[h] = acc[h] * jnp.exp(m_old - m_new) + mxu(vt[h, :, pl.ds(k0, TK)], p)

                @pl.when(plain)
                def _():
                    found = [scores(h) for h in range(heads)]
                    for h in range(heads):
                        finish(h, found[h], jnp.where(slot == 0, table[h, 15], table[h, 31]))

                @pl.when(jnp.logical_not(plain))
                def _():
                    ok = valid_mask(se_ref, r, i, k0)
                    for h in range(heads):
                        s = scores(h) + bias_ref[h, slot].astype(jnp.float32)
                        finish(h, jnp.where(ok, s, NEG), 0.0)

                return 0

            lax.fori_loop(bounds[r, i, 0], bounds[r, i, 1], tile_body, 0)
            parts = []
            for h in range(heads):
                total = acc[h, 64:65, :]
                parts.append((acc[h, 0:64, :] / total).T)
                lse_ref[r, i, h] = mx[h] + jnp.log(total)
            joined = join_heads(parts)
            o_ref[r, i] = joined.astype(jnp.bfloat16)
            keep_ref[r, i] = joined
            return 0

        lax.fori_loop(0, 2, q_body, 0)
        return 0

    lax.fori_loop(0, 2, row_body, 0)


SMEM_SPEC = pl.BlockSpec(memory_space=pltpu.SMEM)
VMEM_SPEC = pl.BlockSpec(memory_space=pltpu.VMEM)


def attention(bounds, table, q, kv, se):
    heads, n = kv.shape[2] // 128, kv.shape[1]
    packed = q.shape
    return pl.pallas_call(
        fwd_kernel,
        out_shape=(
            jax.ShapeDtypeStruct(packed, jnp.bfloat16),
            jax.ShapeDtypeStruct(packed, jnp.float32),
            jax.ShapeDtypeStruct((2, 2, heads, 1, TQ), jnp.float32),
            jax.ShapeDtypeStruct((heads, 4, TK, TQ), jnp.bfloat16),
        ),
        in_specs=[SMEM_SPEC] * 2 + [VMEM_SPEC] * 3,
        out_specs=(VMEM_SPEC,) * 4,
        scratch_shapes=[
            pltpu.VMEM((heads, 80, n), jnp.bfloat16),
            pltpu.VMEM((heads, 80, TQ), jnp.float32),
            pltpu.VMEM((heads, 1, TQ), jnp.float32),
            pltpu.VMEM((2, 2, heads, TQ, 128), jnp.bfloat16),
        ],
        compiler_params=pltpu.CompilerParams(vmem_limit_bytes=VMEM_BYTES),
        name="attention",
    )(bounds, table, q, kv, se)


def bwd_kernel(bounds, table, q_ref, do_ref, keep_ref, kv_ref, bias_ref, se_ref, lse_ref,
               dq_ref, dkv_ref, tab_ref, kt, dqt, dkv, grid, side, qp, dp_ref, delta):
    heads = lse_ref.shape[2]
    n = kv_ref.shape[1]
    grid[...] = jnp.zeros_like(grid)
    side[...] = jnp.zeros_like(side)
    for r in range(2):
        for i in range(2):
            for h, tile in enumerate(spread_lanes(q_ref[r, i], False)):
                qp[r, i, h] = tile
            for h, tile in enumerate(spread_lanes(do_ref[r, i], True)):
                dp_ref[r, i, h] = tile
            prod = (do_ref[r, i].astype(jnp.float32) * keep_ref[r, i]).T
            top, low = prod[:, 0:TQ], prod[:, TQ:]
            delta[r, i, 0] = jnp.sum(top[0:64], axis=0, keepdims=True)
            delta[r, i, 1] = jnp.sum(top[64:128], axis=0, keepdims=True)
            delta[r, i, 2] = jnp.concatenate(
                [jnp.sum(low[0:64], axis=0, keepdims=True), jnp.sum(low[64:128], axis=0, keepdims=True)], axis=1
            )

    def row_body(r, _):
        lo_all = jnp.minimum(bounds[r, 0, 0], bounds[r, 1, 0])
        hi_all = jnp.maximum(bounds[r, 0, 1], bounds[r, 1, 1])

        def clear(t, _):
            k0 = pl.multiple_of(t * TK, TK)
            for h in range(heads):
                dkv[h, pl.ds(k0, TK), :] = jnp.zeros((TK, 128), jnp.float32)
            return 0

        lax.fori_loop(0, n // TK, clear, 0)

        def turn(t, _):
            k0 = pl.multiple_of(t * TK, TK)
            for h in range(heads):
                tile = kv_ref[r, pl.ds(k0, TK), h * 128 : h * 128 + 128]
                kt[h, 0:64, pl.ds(k0, TK)] = tile.T[0:64, :]
                kt[h, 64:80, pl.ds(k0, TK)] = jnp.ones((16, TK), jnp.bfloat16)
            return 0

        lax.fori_loop(lo_all, hi_all, turn, 0)

        def q_body(i, _):
            dqt[...] = jnp.zeros_like(dqt)

            def tile_body(t, _):
                k0 = pl.multiple_of(t * TK, TK)
                slot, plain = tile_kind(bounds, r, i, t)

                def finish(h, p, ds, where):
                    ds_low = ds.astype(jnp.bfloat16)
                    two = jnp.concatenate([ds_low, p.astype(jnp.bfloat16)], axis=1)
                    both = jnp.concatenate([qp[r, i, h], dp_ref[r, i, h]], axis=0)
                    dkv[h, pl.ds(k0, TK), :] += mxu(two, both)
                    dqt[h, where] += mxu(kt[h, :, pl.ds(k0, TK)], ds_low)

                def products(h):
                    tile = kv_ref[r, pl.ds(k0, TK), h * 128 : h * 128 + 128]
                    return mxu(tile, qp[r, i, h], NT), mxu(tile, dp_ref[r, i, h], NT)

                @pl.when(plain)
                def _():
                    for h in range(heads):
                        s, d_probs = products(h)
                        p = jnp.exp(s - (lse_ref[r, i, h] - jnp.where(slot == 0, table[h, 15], table[h, 31])))
                        finish(h, p, p * (d_probs - delta[r, i, h]), jnp.where(slot == 0, 0, 2))

                @pl.when(jnp.logical_not(plain))
                def _():
                    ok = valid_mask(se_ref, r, i, k0)
                    for h in range(heads):
                        s, d_probs = products(h)
                        s = s + bias_ref[h, slot].astype(jnp.float32)
                        p = jnp.where(ok, jnp.exp(jnp.where(ok, s, NEG) - lse_ref[r, i, h]), 0.0)
                        ds = p * (d_probs - delta[r, i, h])
                        grid[h, slot] += ds
                        finish(h, p, ds, 1)

                return 0

            lax.fori_loop(bounds[r, i, 0], bounds[r, i, 1], tile_body, 0)
            parts = []
            for h in range(heads):
                parts.append((dqt[h, 0, 0:64] + dqt[h, 1, 0:64] + dqt[h, 2, 0:64]).T * 0.125)
                side[h, 0:1] += dqt[h, 0, 64:65]
                side[h, 1:2] += dqt[h, 2, 64:65]
            dq_ref[r, i] = join_heads(parts).astype(jnp.bfloat16)
            return 0

        lax.fori_loop(0, 2, q_body, 0)

        def put(t, _):
            k0 = pl.multiple_of(t * TK, TK)
            for h in range(heads):
                dkv_ref[r, pl.ds(k0, TK), h * 128 : h * 128 + 128] = dkv[h, pl.ds(k0, TK), :].astype(jnp.bfloat16)
            return 0

        lax.fori_loop(0, n // TK, put, 0)
        return 0

    lax.fori_loop(0, 2, row_body, 0)

    parity = bounds[0, 0, 5]
    tab_ref[...] = jnp.zeros_like(tab_ref)
    for h in range(heads):
        tab_ref[h, 15:16] = side[h, 0:1] + jnp.sum(grid[h, 0], axis=0, keepdims=True)
        tab_ref[h, 31:32] = side[h, 1:2] + jnp.sum(grid[h, 3], axis=0, keepdims=True)

    first = 13 - 8 * parity
    count = NEAR_ROWS // 32

    def block(h, step):
        tile = step // (TK // 32)
        start = pl.multiple_of((step % (TK // 32)) * 32, 32)
        return grid[h, tile + 1, pl.ds(start, 32)]

    def outer(bucket):
        def one(step, _):
            for h in range(heads):
                tab_ref[h, bucket : bucket + 1] += jnp.sum(block(h, step), axis=0, keepdims=True)
            return 0
        return one

    lax.fori_loop(0, first, outer(15), 0)
    lax.fori_loop(first + count, 2 * TK // 32, outer(31), 0)

    def inner(step, _):
        which = near_buckets(step * 32, 32, parity)
        for b in range(BUCKETS):
            here = which == b
            for h in range(heads):
                tab_ref[h, b : b + 1] += jnp.sum(jnp.where(here, block(h, step), 0.0), axis=0, keepdims=True)
        return 0

    lax.fori_loop(first, first + count, inner, 0)


def attention_back(bounds, table, q, do, keep, kv, bias, se, lse):
    heads, n = kv.shape[2] // 128, kv.shape[1]
    return pl.pallas_call(
        bwd_kernel,
        out_shape=(
            jax.ShapeDtypeStruct(q.shape, jnp.bfloat16),
            jax.ShapeDtypeStruct(kv.shape, jnp.bfloat16),
            jax.ShapeDtypeStruct((heads, BUCKETS, TQ), jnp.float32),
        ),
        in_specs=[SMEM_SPEC] * 2 + [VMEM_SPEC] * 7,
        out_specs=(VMEM_SPEC,) * 3,
        scratch_shapes=[
            pltpu.VMEM((heads, 80, n), jnp.bfloat16),
            pltpu.VMEM((heads, 3, 80, TQ), jnp.float32),
            pltpu.VMEM((heads, n, 128), jnp.float32),
            pltpu.VMEM((heads, 4, TK, TQ), jnp.float32),
            pltpu.VMEM((heads, 2, TQ), jnp.float32),
            pltpu.VMEM((2, 2, heads, TQ, 128), jnp.bfloat16),
            pltpu.VMEM((2, 2, heads, TQ, 128), jnp.bfloat16),
            pltpu.VMEM((2, 2, heads, 1, TQ), jnp.float32),
        ],
        compiler_params=pltpu.CompilerParams(vmem_limit_bytes=VMEM_BYTES),
        name="attention_back",
    )(bounds, table, q, do, keep, kv, bias, se, lse)


def pack_heads(array):
    tokens, width = array.shape
    parts = jnp.transpose(array.reshape(tokens, GROUPS, width // GROUPS), (1, 0, 2))
    half = tokens // 2
    last = jnp.concatenate([parts[:, :half, 128:], parts[:, half:, 128:]], axis=2)
    return jnp.concatenate([parts[:, :, :128], last], axis=1)


def unpack_heads(packed):
    rows = packed.shape[1]
    tokens = rows * 2 // 3
    last = packed[:, tokens:]
    last = jnp.concatenate([last[:, :, :64], last[:, :, 64:]], axis=1)
    parts = jnp.concatenate([packed[:, :tokens], last], axis=2)
    return jnp.transpose(parts, (1, 0, 2)).reshape(tokens, -1)


def body(
    byte_embeds,
    segments,
    score_weight,
    norm_gain1,
    w_query,
    w_key,
    w_value,
    w_out,
    rel_bias,
    norm_gain2,
    w_gate,
    w_up,
    w_down,
    cotangent,
):
    row_count, length, width_d = byte_embeds.shape
    tokens = length // 2
    shards = lax.axis_size("blk")
    devices_all = shards * lax.axis_size("dp")
    position = lax.axis_index("blk")
    base = position * length
    head_count = rel_bias.shape[1]
    head_dim = width_d // head_count
    score_scale = 1.0 / math.sqrt(head_dim)
    bias_table = rel_bias.astype(jnp.float32)
    score_vec = score_weight.astype(jnp.float32)
    rim_bytes = extended(byte_embeds, (("blk", 1),), 2)
    padded = jnp.pad(rim_bytes.astype(jnp.float32), ((0, 0), (1, 1), (0, 0)))
    rim_labels = extended(segments + 1, (("blk", 1),), 2)
    labels_pad = jnp.pad(rim_labels, ((0, 0), (1, 1)))
    masks_all = pool_masks(labels_pad, base, length)
    pools = []
    for pool_terms, counts in masks_all:
        summed = sum(
            (
                keep_mask[:, :, None] * padded[:, 3 + offset : 3 + offset + length]
                for offset, keep_mask in pool_terms
            )
        )
        pools.append(summed / counts[:, :, None])
    stacked = jnp.stack(pools, axis=2)
    block_scores = jnp.sum(stacked * score_vec, axis=-1)
    block_probs = jax.nn.softmax(block_scores, axis=-1)
    mixed = jnp.sum(block_probs[..., None] * stacked, axis=2)
    hidden = 0.5 * (mixed[:, 0::2] + mixed[:, 1::2])
    tok_labels = segments[:, 0::2]
    gain_one = norm_gain1.astype(jnp.float32)
    normed1, norm1_back = jax.vjp(rms_norm, hidden, gain_one)
    n1_low = normed1.astype(jnp.bfloat16)
    query_low = jnp.dot(n1_low, w_query, preferred_element_type=jnp.float32).astype(jnp.bfloat16)
    key_low = jnp.dot(n1_low, w_key, preferred_element_type=jnp.float32).astype(jnp.bfloat16)
    value_low = jnp.dot(n1_low, w_value, preferred_element_type=jnp.float32).astype(jnp.bfloat16)
    shape = {"dp": lax.axis_size("dp"), "blk": shards}
    group = position // (shards // GROUPS)
    rest = position % (shards // GROUPS)
    row = lax.axis_index("dp") % 2
    group_heads = head_count // GROUPS
    q_packed = pack_heads(query_low[0] * jnp.bfloat16(score_scale))
    kv_parts = jnp.stack([key_low.reshape(tokens, head_count, head_dim), value_low.reshape(tokens, head_count, head_dim)], axis=2)
    kv_parts = jnp.transpose(kv_parts.reshape(tokens, GROUPS, group_heads * 2 * head_dim), (1, 0, 2))
    label_block = jnp.pad(tok_labels.reshape(tokens // 128, 128), ((0, 8 - tokens // 128), (0, 0)))
    q_all, kv_all, labels_all = gather_all(shards, q_packed, kv_parts, label_block)
    labels_all = labels_all.reshape(2, shards, 8, 128)[:, :, : tokens // 128].reshape(2, shards * tokens)
    ids = jnp.arange(8, dtype=jnp.int32)
    counts = jnp.sum((labels_all[:, None, :] == ids[None, :, None]).astype(jnp.int32), axis=2)
    ends = jnp.sum(jnp.where(ids[None, :] <= ids[:, None], counts[:, None, :], 0), axis=2)
    begins = ends - counts
    rest_size = shards // GROUPS
    query_labels = jnp.stack(
        [lax.dynamic_slice_in_dim(labels_all, ((2 * row + i) * rest_size + rest) * tokens, tokens, 1) for i in range(2)],
        axis=1,
    )
    chosen = query_labels[:, :, None, :] == ids[None, None, :, None]
    span = jnp.stack(
        [jnp.sum(jnp.where(chosen, edge[:, None, :, None], 0), axis=2) for edge in (begins, ends)], axis=2
    )
    parity = rest % 2
    firsts = jnp.stack([((2 * row + i) * rest_size + rest) * tokens for i in range(2)])
    near = jnp.broadcast_to((firsts // TK - 1 + parity)[None], (2, 2))
    bounds = jnp.stack(
        [
            jnp.min(span[:, :, 0], axis=-1) // TK,
            -(-jnp.max(span[:, :, 1], axis=-1) // TK),
            near,
            -(-jnp.max(span[:, :, 0], axis=-1) // TK),
            jnp.min(span[:, :, 1], axis=-1) // TK,
            jnp.broadcast_to(parity, (2, 2)),
        ],
        axis=-1,
    ).astype(jnp.int32)
    table = lax.dynamic_slice_in_dim(bias_table.T, group * group_heads, group_heads, 0)
    o_packed, o_kept, log_total, bias_tiles = attention(bounds, table, q_all, kv_all, span)
    o_home = move_heads(return_kernel, (GROUPS,), shards, 4, o_packed)
    attended_low = unpack_heads(o_home)[None]
    residual = hidden + jnp.dot(attended_low, w_out, preferred_element_type=jnp.float32)
    gain_two = norm_gain2.astype(jnp.float32)
    normed2, norm2_back = jax.vjp(rms_norm, residual, gain_two)
    n2_low = normed2.astype(jnp.bfloat16)
    gate_proj = jnp.dot(n2_low, w_gate, preferred_element_type=jnp.float32)
    up_proj = jnp.dot(n2_low, w_up, preferred_element_type=jnp.float32)
    activated, geglu_back = jax.vjp(geglu, gate_proj, up_proj)
    act_low = activated.astype(jnp.bfloat16)
    block_out = (residual + jnp.dot(act_low, w_down, preferred_element_type=jnp.float32)).astype(
        jnp.bfloat16
    )
    grad_down = jnp.einsum("rtf,rtd->fd", act_low, cotangent, preferred_element_type=jnp.float32)
    d_act = jnp.einsum("rtd,fd->rtf", cotangent, w_down, preferred_element_type=jnp.float32)
    d_gate, d_up = geglu_back(d_act)
    d_gate_low = d_gate.astype(jnp.bfloat16)
    d_up_low = d_up.astype(jnp.bfloat16)
    grad_gate = jnp.einsum("rtd,rtf->df", n2_low, d_gate_low, preferred_element_type=jnp.float32)
    grad_up = jnp.einsum("rtd,rtf->df", n2_low, d_up_low, preferred_element_type=jnp.float32)
    d_normed2 = jnp.einsum(
        "rtf,df->rtd", d_gate_low, w_gate, preferred_element_type=jnp.float32
    ) + jnp.einsum("rtf,df->rtd", d_up_low, w_up, preferred_element_type=jnp.float32)
    d_res_part, d_gain_two = norm2_back(d_normed2)
    d_residual = cotangent.astype(jnp.float32) + d_res_part
    d_branch = d_residual.astype(jnp.bfloat16)
    grad_out = jnp.einsum("rtd,rte->de", attended_low, d_branch, preferred_element_type=jnp.float32)
    d_attended = jnp.einsum(
        "rte,de->rtd", d_branch, w_out, preferred_element_type=jnp.float32
    ).astype(jnp.bfloat16)
    do_all = move_heads(spread_kernel, (2, 2), shards, 5, pack_heads(d_attended[0]))
    dq_packed, dkv_all, d_table_lanes = attention_back(
        bounds, table, q_all, do_all, o_kept, kv_all, bias_tiles, span, log_total
    )
    dq_home, dkv_home = reduce_all(shards, dq_packed, dkv_all)
    d_query_low = unpack_heads(dq_home)[None]
    dkv_home = jnp.transpose(dkv_home, (1, 0, 2)).reshape(1, tokens, head_count, 2, head_dim)
    d_key_low = dkv_home[:, :, :, 0].reshape(1, tokens, width_d)
    d_value_low = dkv_home[:, :, :, 1].reshape(1, tokens, width_d)
    d_table = jnp.zeros((head_count, BUCKETS), jnp.float32)
    d_table = lax.dynamic_update_slice_in_dim(d_table, jnp.sum(d_table_lanes, axis=-1), group * group_heads, 0).T
    grad_query = jnp.einsum("rtd,rte->de", n1_low, d_query_low, preferred_element_type=jnp.float32)
    grad_key = jnp.einsum("rtd,rte->de", n1_low, d_key_low, preferred_element_type=jnp.float32)
    grad_value = jnp.einsum("rtd,rte->de", n1_low, d_value_low, preferred_element_type=jnp.float32)
    d_normed1 = (
        jnp.einsum("rte,de->rtd", d_query_low, w_query, preferred_element_type=jnp.float32)
        + jnp.einsum("rte,de->rtd", d_key_low, w_key, preferred_element_type=jnp.float32)
        + jnp.einsum("rte,de->rtd", d_value_low, w_value, preferred_element_type=jnp.float32)
    )
    d_hid_part, d_gain_one = norm1_back(d_normed1)
    d_hidden = d_residual + d_hid_part
    d_mixed = 0.5 * jnp.repeat(d_hidden, 2, axis=1)
    d_block = jnp.sum(d_mixed[:, :, None, :] * stacked, axis=-1)
    d_block_scores = block_probs * (
        d_block - jnp.sum(block_probs * d_block, axis=-1, keepdims=True)
    )
    grad_score_local = jnp.sum(d_block_scores[..., None] * stacked, axis=(0, 1, 2))
    d_pools = (
        block_probs[..., None] * d_mixed[:, :, None, :] + d_block_scores[..., None] * score_vec
    )
    spread = jnp.stack(
        [
            d_pools[:, :, width_index] / masks_all[width_index][1][:, :, None]
            for width_index in range(MAX_BLOCK)
        ],
        axis=2,
    ).reshape(row_count, length, MAX_BLOCK * width_d)
    rim_spread = extended(spread.astype(jnp.bfloat16), (("blk", 1),), 2).astype(spread.dtype)
    spread_pad = jnp.pad(rim_spread, ((0, 0), (1, 1), (0, 0))).reshape(
        row_count, length + 6, MAX_BLOCK, width_d
    )
    d_bytes = jnp.zeros((row_count, length, width_d), jnp.float32)
    for width_index in range(MAX_BLOCK):
        for offset, keep_mask in masks_all[width_index][0]:
            d_bytes = (
                d_bytes
                + keep_mask[:, :, None]
                * spread_pad[:, 3 + offset : 3 + offset + length, width_index]
            )
    share_local = jnp.sum(block_probs, axis=(0, 1)) / (row_count * length * devices_all)
    small = (grad_score_local, d_gain_one, d_gain_two, d_table, share_local)
    if devices_all <= 32:
        def blocks(grad):
            return grad.reshape(devices_all, grad.shape[0] // devices_all, grad.shape[1]).astype(jnp.bfloat16)

        wide = jnp.concatenate([blocks(grad_gate), blocks(grad_up)], axis=1)
        slim = jnp.concatenate([blocks(g) for g in (grad_query, grad_key, grad_value, grad_out, grad_down)], axis=1)
        flat = jnp.concatenate([part.reshape(-1) for part in small])
        flat = jnp.pad(flat, (0, -flat.shape[0] % 1024)).reshape(-1, 128)
        (wide, slim), flat = reduce_weights(shape, (wide, slim), flat)
        per = width_d // devices_all
        summed_weights = [slim[p * per : (p + 1) * per] for p in range(4)]
        summed_weights += [wide[:per], wide[per:], slim[4 * per :]]
        flat, summed_small = flat.reshape(-1), []
        for part in small:
            summed_small.append(flat[: part.size].reshape(part.shape))
            flat = flat[part.size :]
    else:
        summed_weights = [
            lax.psum_scatter(grad, ("dp", "blk"), scatter_dimension=0, tiled=True)
            for grad in (grad_query, grad_key, grad_value, grad_out, grad_gate, grad_up, grad_down)
        ]
        summed_small = lax.psum(small, ("dp", "blk"))
    return (
        block_out,
        d_bytes.astype(jnp.bfloat16),
        summed_small[0],
        summed_small[1],
        summed_weights[0],
        summed_weights[1],
        summed_weights[2],
        summed_weights[3],
        summed_small[3],
        summed_small[2],
        summed_weights[4],
        summed_weights[5],
        summed_weights[6],
        summed_small[4],
    )


def solution(mesh):
    placed = (
        P("dp", "blk", None),
        P("dp", "blk"),
        P(),
        P(),
        P(),
        P(),
        P(),
        P(),
        P(),
        P(),
        P(),
        P(),
        P(),
        P("dp", "blk", None),
    )
    return jax.shard_map(
        body,
        mesh=mesh,
        in_specs=placed,
        out_specs=(
            P("dp", "blk", None),
            P("dp", "blk", None),
            P(),
            P(),
            P(("dp", "blk"), None),
            P(("dp", "blk"), None),
            P(("dp", "blk"), None),
            P(("dp", "blk"), None),
            P(),
            P(),
            P(("dp", "blk"), None),
            P(("dp", "blk"), None),
            P(("dp", "blk"), None),
            P(),
        ),
        check_vma=False,
    )
```

time: 3680 us -> 587 us (0.16)
  local copies, waits for them, and re-layouts: 2160 us -> 95.2 us
  waiting for transfers between devices: 733 us -> 0.02 us
  Pallas kernels: 0 us -> 362 us
  matrix products: 383 us -> 38.3 us
  other arithmetic: 214 us -> 63.6 us
  loops' own time: 70 us -> 0 us
  blocking collectives: 65.2 us -> 0 us
    reshape x40 -> x5, local copies, waits for them, and re-layouts: 746 us -> 4.54 us  [the longest x1 2.28 us: body(): kv_parts.reshape(tokens, GROUPS, group_heads * 2 * head_dim)]
    reduce_scatter x8 -> x0, waiting for transfers between devices: 646 us -> none  [the longest x1 121 us: body(): lax.psum_scatter(grad_gate, ('dp', 'blk'), scatter_dimension=0, tiled=True)]
    another operation x48 -> x9, local copies, waits for them, and re-layouts: 499 us -> 2.58 us  [the longest x3 1.4 us: body(): jnp.stack([jnp.min(span[:, :, 0], axis=-1) // TK, -(-jnp.max(span[:, :, 1...]
    slice x96 -> x16, local copies, waits for them, and re-layouts: 466 us -> 19 us  [the longest x2 3.4 us: body(): summed_weights += [wide[:per], wide[per:], slim[4 * per:]]]
    pallas_call x0 -> x7, Pallas kernels: none -> 362 us  [the longest x1 119 us: reduce_weights(): pl.pallas_call(functools.partial(weights_kernel, orders, axes), out_shape...]
    dot_general x96 -> x0, matrix products: 332 us -> none  [the longest x24 123 us: pair_scores(): jnp.einsum('rqhd,krhd->rhqk', query_part, key_heads, preferred_element_ty...]
    while x216 -> x0, local copies, waits for them, and re-layouts: 219 us -> none
    dynamic_slice x56 -> x1, local copies, waits for them, and re-layouts: 87.6 us -> 0.01 us  [body(): lax.dynamic_slice_in_dim(labels_all, ((2 * row + i) * rest_size + rest) *...]
  transfers between devices with their start and end apart: 16 -> 6, of which waited for: 8 -> 0; matrix products, arithmetic and copies ran while one was open for 34% -> 11% of each run, Pallas kernels for 0% -> 21%
where the time goes in v1:
time: 587 us; the launch traced here: 577 us
  Pallas kernels  362 us (62%)
  local copies, waits for them, and re-layouts  95.2 us (16%)
  other arithmetic  63.6 us (11%)
  matrix products  38.3 us (7%)
  starting transfers between devices  15.7 us (3%)
    pallas_call x1, Pallas kernels, reduce_weights(): pl.pallas_call(functools.partial(weights_kernel, orders, axes), out_shape...  119 us
    pallas_call x1, Pallas kernels, gather_all(): pl.pallas_call(functools.partial(gather_kernel, shards), out_shape=(jax.S...  57.2 us
    pallas_call x1, Pallas kernels, reduce_all(): pl.pallas_call(functools.partial(reduce_kernel, shards), out_shape=(jax.S...  56.2 us
    pallas_call x1, Pallas kernels, attention_back(): pl.pallas_call(bwd_kernel, out_shape=(jax.ShapeDtypeStruct(q.shape, jnp.b...  47.3 us
    pallas_call x2, Pallas kernels, move_heads(): pl.pallas_call(functools.partial(kernel, shards), out_shape=jax.ShapeDtyp...  44.5 us
    pallas_call x1, Pallas kernels, attention(): pl.pallas_call(fwd_kernel, out_shape=(jax.ShapeDtypeStruct(packed, jnp.bf...  37.5 us
    unnamed x191, local copies, waits for them, and re-layouts  16.8 us
    ppermute x3, starting transfers between devices, extended(): before = lax.ppermute(last, axis, up)  11.9 us
  transfers between devices with their start and end apart: 6, of which 0 were waited for; matrix products, arithmetic and copies ran while one was open for 11% of the time, Pallas kernels for 21%

profile of v1, /device:TPU:0, one launch (start us, length us, event | category | flops | bytes accessed | tf_op | source)
XLA Modules:
  0.0 576.8 jit_solution(311825872225951452)
XLA Ops:
  4.5 3.0 collective-permute-start
  8.9 5.1 collective-permute-start.2
  15.3 2.3 copy.211
  32.3 2.5 slice_bitcast_fusion.16
  39.9 4.3 multiply_reduce_fusion.2
  44.2 3.0 copy.212
  47.3 4.8 slice.330
  52.1 4.8 slice.331
  68.2 2.5 convolution_convert_fusion.7
  72.6 2.5 convolution_convert_fusion.8
  82.4 57.2 %gather_keys.1 = (bf16[2,2,384,128]{3,2,1,0:T(8,128)(2,1)}, bf16[2,4096,384]{2,1,0:T(8,128)(2,1)}, s32[2,2,2,2,2,8,128]{6,5,4,3,2,1,0:T(8,128)}) custom-call(bf16[4,384,128]{2,1,0:T(8,128)(2,1)} %maximum_maximum_fusion.q_ref, bf16[4,256,384]{2,1,0:T(8,128)(2,1)} %bitcast.332, s32[8,128]{1,0:T(8,128)} %pad.23.label_ref), custom_call_target="tpu_custom_call" | custom-call | tf_op jit(solution)/shard_map/gather_keys/pallas_call | solution.py:306
  144.4 37.5 %attention.1 = (bf16[2,2,384,128]{3,2,1,0:T(8,128)(2,1)}, f32[2,2,384,128]{3,2,1,0:T(8,128)}, f32[2,2,3,1,256]{4,3,2,1,0:T(1,128)}, bf16[3,4,512,256]{3,2,1,0:T(8,128)(2,1)}) custom-call(s32[2,2,6]{2,1,0:T(2,128)} %stack.71.bounds, f32[3,32]{1,0:T(4,128)} %convert_bitcast_fusion.table, bf16[2,2,384,128]{3,2,1,0:T(8,128)(2,1)} %get-tuple-element.30.q_ref, ...), custom_call_target="tpu_custom_call" | custom-call | tf_op jit(solution)/shard_map/attention/pallas_call | solution.py:682
  181.9 17.6 %move_heads_4.1 = bf16[4,384,128]{2,1,0:T(8,128)(2,1)} custom-call(bf16[2,2,384,128]{3,2,1,0:T(8,128)(2,1)} %get-tuple-element.32.o_ref), custom_call_target="tpu_custom_call" | custom-call | tf_op jit(solution)/shard_map/move_heads_4/pallas_call | solution.py:204
  207.3 2.3 fusion.21
  211.8 2.4 multiply_convert_fusion
  220.5 26.9 %move_heads_5.1.do_ref = bf16[2,2,384,128]{3,2,1,0:T(8,128)(2,1)} custom-call(bf16[4,384,128]{2,1,0:T(8,128)(2,1)} %maximum_maximum_fusion.1.q_ref), custom_call_target="tpu_custom_call" | custom-call | tf_op jit(solution)/shard_map/move_heads_5/pallas_call | solution.py:204
  247.4 47.3 %attention_back.1 = (bf16[2,2,384,128]{3,2,1,0:T(8,128)(2,1)}, bf16[2,4096,384]{2,1,0:T(8,128)(2,1)}, f32[3,32,256]{2,1,0:T(8,128)}) custom-call(s32[2,2,6]{2,1,0:T(2,128)} %stack.71.bounds, f32[3,32]{1,0:T(4,128)} %convert_bitcast_fusion.table, bf16[2,2,384,128]{3,2,1,0:T(8,128)(2,1)} %get-tuple-element.30.q_ref, ...), custom_call_target="tpu_custom_call" | custom-call | tf_op jit(solution)/shard_map/attention_back/pallas_call | solution.py:842
  294.7 56.2 %reduce_keys.1 = (bf16[4,384,128]{2,1,0:T(8,128)(2,1)}, bf16[4,256,384]{2,1,0:T(8,128)(2,1)}) custom-call(bf16[2,2,384,128]{3,2,1,0:T(8,128)(2,1)} %get-tuple-element.36.q_ref, bf16[2,4,2,2,256,384]{5,4,3,2,1,0:T(8,128)(2,1)} %bitcast.318), custom_call_target="tpu_custom_call" | custom-call | tf_op jit(solution)/shard_map/reduce_keys/pallas_call | solution.py:421
  356.5 2.6 convolution_convert_fusion
  359.2 2.7 convolution_convert_fusion.1
  364.5 2.7 fusion.156
  367.2 2.4 copy.235
  376.1 3.3 copy.236
  379.4 2.9 multiply_reduce_fusion.1
  383.1 2.3 multiply_reduce_fusion
  393.6 3.8 collective-permute-start.4
  414.5 6.7 %pad_maximum_fusion.1 = bf16[32,48,2048]{2,1,0:T(8,128)(2,1)} fusion(bf16[32,24,2048]{2,1,0:T(8,128)(2,1)} %convolution_convert_fusion, bf16[32,24,2048]{2,1,0:T(8,128)(2,1)} %convolution_convert_fusion.1), kind=kLoop, calls=%fused_computation.5 | loop fusion | flops 12582912 | bytes 12582912 | tf_op jit(solution)/shard_map/concatenate | solution.py:1061
  427.4 2.6 convert_dynamic-update-slice_fusion
  430.1 119.0 %reduce_weights.1 = (f32[48,2048]{1,0:T(8,128)}, f32[160,768]{1,0:T(8,128)}, f32[24,128]{1,0:T(8,128)}) custom-call(bf16[2,2,2,2,2,48,2048]{6,5,4,3,2,1,0:T(8,128)(2,1)} %bitcast.314, bf16[2,2,2,2,2,160,768]{6,5,4,3,2,1,0:T(8,128)(2,1)} %bitcast.93.refs_1_, f32[24,128]{1,0:T(8,128)} %pad_bitcast_fusion.refs_2_), custom_call_target="tpu_custom_call" | custom-call | tf_op jit(solution)/shard_map/reduce_weights/pallas_call | solution.py:516
  561.5 4.8 fusion.5
  567.1 7.0 %fusion.33 = bf16[1,512,768]{1,2,0:T(8,128)(2,1)} fusion(f32[1,518,4,768]{1,3,2,0:T(8,128)S(1)} %convert.3, f32[512]{0:T(512)S(1)} %bitcast.365, f32[512]{0:T(512)S(1)} %bitcast.363, f32[512]{0:T(512)S(1)} %bitcast.361, f32[512]{0:T(512)S(1)} %bitcast.359, f32[512]{0:T(512)S(1)} %bitcast.355, f32[512]{0:T(512)S(1)} %bitcast.357, f32[512]{0:T(512)S(1)} %bitcast.377, ...), kind=kLoop, calls=%fused_computation.55 | loop fusion | flops 11010048 | bytes 25976832 | tf_op jit(solution)/shard_map/convert_element_type | solution.py:1081
  574.1 2.3 copy.265
  (330 shorter events, 127.1 us)
Async XLA Ops:
  0.6 206.6 %copy-start = (bf16[768,2048]{1,0:T(8,128)(2,1)S(1)}, bf16[768,2048]{1,0:T(8,128)(2,1)}, u32[]{:S(2)}) copy-start(bf16[768,2048]{1,0:T(8,128)(2,1)} %param.25) | copy-start | bytes 9437188
  0.7 18.4 %copy-start.90 = (bf16[768]{0:T(1024)(128)(2,1)S(1)}, bf16[768]{0:T(1024)(128)(2,1)}, u32[]{:S(2)}) copy-start(bf16[768]{0:T(1024)(128)(2,1)} %param.16) | copy-start | bytes 4612
  2.4 28.3 %collective-permute-start.1 = (bf16[1,2,768]{1,2,0:T(8,128)(2,1)}, bf16[1,2,768]{1,2,0:T(8,128)(2,1)S(1)}, u32[]{:S(2)}, u32[]{:S(2)}) collective-permute-start(bf16[1,2,768]{1,2,0:T(8,128)(2,1)} %copy.210), channel_id=1, source_target_pairs={{1,0},{2,1},{3,2},{4,3},{5,4},{6,5},{7,6},{8,7},{9,8},{10,9},{11,1... | collective-permute-start | bytes 9224 | tf_op jit(solution)/shard_map/ppermute | solution.py:24
  4.5 26.2 %collective-permute-start = (bf16[1,2,768]{1,2,0:T(8,128)(2,1)}, bf16[1,2,768]{1,2,0:T(8,128)(2,1)S(1)}, u32[]{:S(2)}, u32[]{:S(2)}) collective-permute-start(bf16[1,2,768]{1,2,0:T(8,128)(2,1)} %copy.209), channel_id=1, source_target_pairs={{0,1},{1,2},{2,3},{3,4},{4,5},{5,6},{6,7},{7,8},{8,9},{9,10},{10,1... | collective-permute-start | bytes 9224 | tf_op jit(solution)/shard_map/ppermute | solution.py:23
  8.9 18.4 %collective-permute-start.2 = (s32[1,2]{1,0:T(1,128)}, s32[1,2]{1,0:T(1,128)}, u32[]{:S(2)}, u32[]{:S(2)}) collective-permute-start(s32[1,2]{1,0:T(1,128)} %get-tuple-element.206), channel_id=1, source_target_pairs={{0,1},{1,2},{2,3},{3,4},{4,5},{5,6},{6,7},{7,8},{8,9},{9,10},{10,1... | collective-permute-start | bytes 32 | tf_op jit(solution)/shard_map/ppermute | solution.py:23
  14.0 13.4 %collective-permute-start.3 = (s32[1,2]{1,0:T(1,128)}, s32[1,2]{1,0:T(1,128)}, u32[]{:S(2)}, u32[]{:S(2)}) collective-permute-start(s32[1,2]{1,0:T(1,128)} %get-tuple-element.205), channel_id=1, source_target_pairs={{1,0},{2,1},{3,2},{4,3},{5,4},{6,5},{7,6},{8,7},{9,8},{10,9},{11,1... | collective-permute-start | bytes 32 | tf_op jit(solution)/shard_map/ppermute | solution.py:24
  28.9 6.0 %copy-start.54 = (f32[1,512]{1,0:T(1,128)}, f32[1,512]{1,0:T(1,128)S(1)}, u32[]{:S(2)}) copy-start(f32[1,512]{1,0:T(1,128)S(1)} %get-tuple-element.126) | copy-start | bytes 6148
  28.9 6.0 %copy-start.70 = (f32[1,512]{1,0:T(1,128)}, f32[1,512]{1,0:T(1,128)S(1)}, u32[]{:S(2)}) copy-start(f32[1,512]{1,0:T(1,128)S(1)} %get-tuple-element.127) | copy-start | bytes 6148
  28.9 6.0 %copy-start.72 = (f32[1,512]{1,0:T(1,128)}, f32[1,512]{1,0:T(1,128)S(1)}, u32[]{:S(2)}) copy-start(f32[1,512]{1,0:T(1,128)S(1)} %get-tuple-element.128) | copy-start | bytes 6148
  29.7 5.1 copy-start.52
  29.7 5.1 copy-start.58
  29.8 5.1 copy-start.60
  29.8 5.1 copy-start.62
  29.8 5.1 copy-start.64
  29.8 5.1 copy-start.66
  29.8 5.1 copy-start.68
  30.6 4.3 copy-start.56
  30.6 4.3 copy-start.74
  30.7 4.3 copy-start.76
  39.2 5.0 copy-start.43
  39.2 5.0 copy-start.45
  206.0 11.4 %copy-start.12 = (f32[1,256,768]{2,1,0:T(8,128)}, f32[1,256,768]{2,1,0:T(8,128)S(1)}, u32[]{:S(2)}) copy-start(f32[1,256,768]{2,1,0:T(8,128)S(1)} %get-tuple-element.210) | copy-start | bytes 2359300
  206.0 11.4 %copy-start.50 = (f32[256]{0:T(256)}, f32[256]{0:T(256)S(1)}, u32[]{:S(2)}) copy-start(f32[256]{0:T(256)S(1)} %fusion.135) | copy-start | bytes 3076
  218.6 154.4 %copy-start.15 = (f32[1,256,768]{2,1,0:T(8,128)}, f32[1,256,768]{2,1,0:T(8,128)S(1)}, u32[]{:S(2)}) copy-start(f32[1,256,768]{2,1,0:T(8,128)S(1)} %fusion.70) | copy-start | bytes 2359300
  294.7 59.7 %copy-start.13 = (f32[1,256,768]{2,1,0:T(8,128)S(1)}, f32[1,256,768]{2,1,0:T(8,128)}, u32[]{:S(2)}) copy-start(f32[1,256,768]{2,1,0:T(8,128)} %copy-done.12) | copy-start | bytes 2359300
  294.7 59.7 %copy-start.51 = (f32[256]{0:T(256)S(1)}, f32[256]{0:T(256)}, u32[]{:S(2)}) copy-start(f32[256]{0:T(256)} %copy-done.50) | copy-start | bytes 3076
  350.9 5.6 copy-start.21
  390.3 167.3 %collective-permute-start.5 = (bf16[1,2,3072]{2,1,0:T(2,128)(2,1)}, bf16[1,2,3072]{2,1,0:T(2,128)(2,1)}, u32[]{:S(2)}, u32[]{:S(2)}) collective-permute-start(bf16[1,2,3072]{2,1,0:T(2,128)(2,1)} %copy.238), channel_id=1, source_target_pairs={{1,0},{2,1},{3,2},{4,3},{5,4},{6,5},{7,6},{8,7},{9,8},{10,9},{11,1... | collective-permute-start | bytes 36872 | tf_op jit(solution)/shard_map/ppermute | solution.py:24
  393.6 165.9 %collective-permute-start.4 = (bf16[1,2,3072]{2,1,0:T(2,128)(2,1)}, bf16[1,2,3072]{2,1,0:T(2,128)(2,1)}, u32[]{:S(2)}, u32[]{:S(2)}) collective-permute-start(bf16[1,2,3072]{2,1,0:T(2,128)(2,1)} %copy.237), channel_id=1, source_target_pairs={{0,1},{1,2},{2,3},{3,4},{4,5},{5,6},{6,7},{7,8},{8,9},{9,10},{10,1... | collective-permute-start | bytes 36872 | tf_op jit(solution)/shard_map/ppermute | solution.py:23
  414.5 6.7 %copy-start.26 = (bf16[768,256]{1,0:T(8,128)(2,1)S(1)}, bf16[768,256]{1,0:T(8,128)(2,1)}, u32[]{:S(2)}) copy-start(bf16[768,256]{1,0:T(8,128)(2,1)} %copy.259) | copy-start | bytes 1179652
  414.5 6.7 %copy-start.30 = (bf16[256,4,192]{0,2,1:T(8,128)(2,1)S(1)}, bf16[256,4,192]{0,2,1:T(8,128)(2,1)}, u32[]{:S(2)}) copy-start(bf16[256,4,192]{0,2,1:T(8,128)(2,1)} %copy-done.29) | copy-start | bytes 1179652
  567.1 9.3 %copy-start.1 = (bf16[768,2048]{1,0:T(8,128)(2,1)S(1)}, bf16[768,2048]{1,0:T(8,128)(2,1)}, u32[]{:S(2)}) copy-start(bf16[768,2048]{1,0:T(8,128)(2,1)} %param.25) | copy-start | bytes 9437188
  (66 other events, 140.0 us)

commit v2 on v1

--- a/solution.py
+++ b/solution.py
@@ -11,19 +11,6 @@
 BUCKETS = 32
 MAX_BLOCK = 4
 VMEM_BYTES = 60 * 2**20
-
-
-def extended(shard, sides, width):
-    for axis, dim in sides:
-        peers, length = (lax.axis_size(axis), shard.shape[dim])
-        up = [(i, (i + 1) % peers) for i in range(peers - 1)]
-        down = [(j, i) for i, j in up]
-        last = lax.slice_in_dim(shard, length - width, length, axis=dim)
-        leading = lax.slice_in_dim(shard, 0, width, axis=dim)
-        before = lax.ppermute(last, axis, up)
-        after = lax.ppermute(leading, axis, down)
-        shard = jnp.concatenate([before, shard, after], axis=dim)
-    return shard
 
 
 def buckets_of(relative):
@@ -33,32 +20,6 @@
         beyond = beyond + (distance >= border).astype(jnp.int32)
     nearer = jnp.where(distance < 8, distance, 8 + beyond)
     return nearer + BUCKETS // 2 * (relative > 0).astype(jnp.int32)
-
-
-def rms_norm(values, gain):
-    return values * lax.rsqrt(jnp.mean(values * values, axis=-1, keepdims=True) + 1e-06) * gain
-
-
-def geglu(gate_proj, up_proj):
-    return jax.nn.gelu(gate_proj, approximate=True) * up_proj
-
-
-def pool_masks(labels, base, length):
-    positions = jnp.arange(length + 6, dtype=jnp.int32) + base - 3
-    centre = labels[:, 3 : 3 + length]
-    centre_pos = positions[3 : 3 + length]
-    result = []
-    for block_width in range(1, MAX_BLOCK + 1):
-        pool_terms = []
-        for offset in range(1 - block_width, block_width):
-            near_labels = labels[:, 3 + offset : 3 + offset + length]
-            near_pos = positions[3 + offset : 3 + offset + length]
-            same_block = near_pos // block_width == centre_pos // block_width
-            keep_mask = jnp.logical_and(near_labels == centre, same_block[None, :])
-            pool_terms.append((offset, keep_mask.astype(jnp.float32)))
-        counts = sum((entry[1] for entry in pool_terms))
-        result.append((pool_terms, counts))
-    return result
 
 
 MESH_ID = pl.DeviceIdType.MESH
@@ -197,6 +158,10 @@
     greet(line_and_row(place))
     return_heads(place, o_ref, out_ref, send_sem, recv_sem)
     return_heads_wait(place, o_ref, out_ref, send_sem, recv_sem)
+
+
+SMEM_SPEC = pl.BlockSpec(memory_space=pltpu.SMEM)
+VMEM_SPEC = pl.BlockSpec(memory_space=pltpu.VMEM)
 
 
 def move_heads(kernel, lead, shards, ident, packed):
@@ -345,12 +310,194 @@
     lax.fori_loop(0, total, one, 0)
 
 
-def reduce_kernel(shards, q_ref, kv_ref, qo_ref, kvo_ref, q_send, q_recv, send_sem, recv_sem, z_send, z_recv, *bufs):
+class Stream:
+    def __init__(self, axes, at, kept, order, src, bufs, out, send_sem, recv_sem):
+        self.axes, self.at, self.kept, self.order = axes, at, kept, order
+        self.src, self.bufs, self.out = src, bufs, out
+        self.send_sem, self.recv_sem = send_sem, recv_sem
+
+    def own(self, p):
+        axis, mask = self.axes[p]
+        return bit(self.at[axis], mask)
+
+    def target(self, p):
+        axis, mask = self.axes[p]
+        moved = dict(self.at)
+        moved[axis] = flipped(self.at[axis], mask)
+        return (moved["dp"], moved["blk"])
+
+    def stage(self, k):
+        kept = [p for p in self.kept if p not in self.order[:k]]
+        return kept, self.src if k == 0 else self.bufs[k - 1], self.order[k]
+
+    def copy(self, k):
+        kept, src, now = self.stage(k)
+        index = tuple(1 - self.own(p) if p == now else slice(None) for p in kept)
+        return remote(src.at[index], self.bufs[k], self.send_sem.at[k], self.recv_sem.at[k], self.target(now))
+
+    def absorb(self, k):
+        kept, src, now = self.stage(k)
+        buf = self.bufs[k]
+        if k == len(self.order) - 1:
+            mine = src[self.own(now)].astype(jnp.float32)
+            self.out[...] = buf[...].astype(jnp.float32) + mine
+        else:
+            add_blocks(buf, src, tuple(self.own(p) if p == now else None for p in kept), buf.shape)
+
+
+class Whole:
+    def __init__(self, axes, at, order, src, bufs, out, send_sem, recv_sem):
+        self.stream = Stream(axes, at, order, order, src, bufs, out, send_sem, recv_sem)
+        self.order, self.src, self.bufs, self.out = order, src, bufs, out
+
+    def held(self, k):
+        return self.src if k == 0 else self.bufs.at[1, k - 1]
+
+    def copy(self, k):
+        s = self.stream
+        return remote(self.held(k), self.bufs.at[0, k], s.send_sem.at[k], s.recv_sem.at[k], s.target(self.order[k]))
+
+    def absorb(self, k):
+        total = self.held(k)[...] + self.bufs[0, k]
+        if k == len(self.order) - 1:
+            self.out[...] = total
+        else:
+            self.bufs[1, k] = total
+
+
+def run_streams(streams, first=0):
+    for stage in range(max(len(s.order) for s in streams)):
+        for s in streams:
+            if stage < len(s.order):
+                s.copy(stage).wait()
+                s.absorb(stage)
+                if stage < len(s.order) - 1:
+                    s.copy(stage + 1).start()
+
+
+def bit_axes(shape):
+    return [("dp", m) for m in bits_of(shape["dp"])] + [("blk", m) for m in bits_of(shape["blk"])]
+
+
+def stream_scratch(lead, order, rows, cols):
+    return [pltpu.VMEM((2,) * (lead - 1 - k) + (rows, cols), jnp.bfloat16) for k in range(len(order))]
+
+
+def weights_kernel(shards, da_ref, n2_ref, att_ref, act_ref, dg_ref, du_ref, ct_ref, db_ref,
+                   do_ref, keep_a, send_a, keep_b, send_b, keep_c, send_c,
+                   q_send, q_recv, core_send, core_recv, gate, up, down, out, wide_out, slim_out, wide_in, slim_in):
+    place = Place(shards)
+    core_target = place.other_rest(1)
+    greet(line_and_row(place) + [core_target])
+    spread_heads(place, da_ref, do_ref, q_send, q_recv)
+    per = gate.shape[0] // 32
+    per_ff = down.shape[0] // 32
+    half = wide_out.shape[2] // 2
+    core = place.rest % 2
+
+    n2_t = n2_ref[...].T
+    step = 512
+    for j in range(gate.shape[1] // step):
+        cols = slice(j * step, j * step + step)
+        gate[:, cols] = mxu(n2_t, dg_ref[:, cols])
+        up[:, cols] = mxu(n2_t, du_ref[:, cols])
+
+    def wide_rows(block):
+        rows = pl.ds(pl.multiple_of(block * per, 8), per)
+        return jnp.concatenate([gate[rows, :], up[rows, :]], axis=0)
+
+    def slim_rows(block):
+        rows, more = pl.ds(pl.multiple_of(block * per, 8), per), pl.ds(pl.multiple_of(block * per_ff, 8), per_ff)
+        empty = jnp.zeros((32 - per, out.shape[1]), jnp.float32)
+        return jnp.concatenate([out[rows, :], empty, down[more, :]], axis=0)
+
+    def send_wide(m, _):
+        wide_out[m] = wide_rows(2 * m + 1 - core).astype(jnp.bfloat16)
+        return 0
+
+    lax.fori_loop(0, 16, send_wide, 0)
+    wide_copy = remote(wide_out, wide_in, core_send.at[0], core_recv.at[0], core_target)
+    wide_copy.start()
+    out[...] = mxu(att_ref[...].T, db_ref[...])
+    for j in range(down.shape[0] // step):
+        rows = slice(j * step, j * step + step)
+        down[rows, :] = mxu(act_ref[:, rows].T, ct_ref[...])
+
+    def send_slim(m, _):
+        slim_out[m] = slim_rows(2 * m + 1 - core).astype(jnp.bfloat16)
+        return 0
+
+    lax.fori_loop(0, 16, send_slim, 0)
+    slim_copy = remote(slim_out, slim_in, core_send.at[1], core_recv.at[1], core_target)
+    slim_copy.start()
+
+    def number(j, bit_at, value):
+        return j // bit_at * (2 * bit_at) + value * bit_at + j % bit_at
+
+    wide_copy.wait()
+    for (keep, send), bit_at, mine, cols in (
+        ((keep_a, send_a), 8, place.row, slice(0, half)),
+        ((keep_b, send_b), 1, bit(place.rest, 2), slice(half, 2 * half)),
+    ):
+        for ref, value in ((send, 1 - mine), (keep, mine)):
+            def one(j, _):
+                m = number(j, bit_at, value)
+                ref[j] = (wide_rows(2 * m + core)[:, cols] + wide_in[m, :, cols].astype(jnp.float32)).astype(jnp.bfloat16)
+                return 0
+            lax.fori_loop(0, 8, one, 0)
+    slim_copy.wait()
+    mine = bit(place.group, 1)
+    for ref, value in ((send_c, 1 - mine), (keep_c, mine)):
+        def one(j, _):
+            m = number(j, 2, value)
+            ref[j] = (slim_rows(2 * m + core) + slim_in[m].astype(jnp.float32)).astype(jnp.bfloat16)
+            return 0
+        lax.fori_loop(0, 8, one, 0)
+    spread_heads_wait(place, da_ref, do_ref, q_send, q_recv)
+
+
+def spread_and_weights(shards, da, n2, att, act, dg, du, ct, db):
+    width, ff = n2.shape[1], act.shape[1]
+    per, per_ff = width // 32, ff // 32
+    sem, low = pltpu.SemaphoreType.DMA, jnp.bfloat16
+    wide, slim = (2 * per, ff), (32 + per_ff, width)
+    halves = [jax.ShapeDtypeStruct((8, 2 * per, ff // 2), low)] * 4 + [jax.ShapeDtypeStruct((8,) + slim, low)] * 2
+    return pl.pallas_call(
+        functools.partial(weights_kernel, shards),
+        out_shape=(jax.ShapeDtypeStruct((2, 2) + da.shape[1:], da.dtype),) + tuple(halves),
+        in_specs=[VMEM_SPEC] * 8,
+        out_specs=(VMEM_SPEC,) * 7,
+        scratch_shapes=[
+            sem((4,)), sem((4,)), sem((2,)), sem((2,)),
+            pltpu.VMEM((width, ff), jnp.float32), pltpu.VMEM((width, ff), jnp.float32),
+            pltpu.VMEM((ff, width), jnp.float32), pltpu.VMEM((width, width), jnp.float32),
+            pltpu.VMEM((16,) + wide, low), pltpu.VMEM((16,) + slim, low),
+            pltpu.VMEM((16,) + wide, low), pltpu.VMEM((16,) + slim, low),
+        ],
+        compiler_params=pltpu.CompilerParams(collective_id=5, has_side_effects=True, vmem_limit_bytes=VMEM_BYTES),
+        name="spread_and_weights",
+    )(da, n2, att, act, dg, du, ct, db)
+
+
+def reduce_kernel(shards, axes, orders, *refs):
+    count = len(orders)
+    q_ref, kv_ref = refs[:2]
+    pairs = refs[2 : 2 + 2 * count]
+    qo_ref, kvo_ref = refs[2 + 2 * count : 4 + 2 * count]
+    sums = refs[4 + 2 * count : 4 + 3 * count]
+    q_send, q_recv, send_sem, recv_sem, z_send, z_recv, w_send, w_recv = refs[4 + 3 * count : 12 + 3 * count]
+    bufs = refs[12 + 3 * count :]
     place = Place(shards)
     rest_bits = bits_of(place.rest_size)
     greet(line_and_row(place) + [place.other_rest(mask) for mask in rest_bits])
     return_heads(place, q_ref, qo_ref, q_send, q_recv)
     ndim = 1 + len(rest_bits)
+    at = {"dp": place.dp, "blk": place.blk}
+    streams, used = [], ndim
+    for s, (kept, order) in enumerate(orders):
+        src, more = bufs[used], bufs[used + 1 : used + 1 + len(order)]
+        used += 1 + len(order)
+        streams.append(Stream(axes, at, kept, order, src, more, sums[s], w_send.at[s], w_recv.at[s]))
     own = [place.row] + [bit(place.rest, m) for m in rest_bits]
     targets = [place.other_row()] + [place.other_rest(m) for m in rest_bits]
     state = {}
@@ -396,6 +543,9 @@
     steps = (2, 1, 3, 0)
     for step in steps:
         copy_of(step, 0).start()
+    for s, stream in enumerate(streams):
+        add_two(stream.src, pairs[2 * s], pairs[2 * s + 1])
+        stream.copy(0).start()
     for stage in range(ndim):
         for step in steps:
             copy_of(step, stage).wait()
@@ -406,123 +556,115 @@
                 remote(bufs[stage].at[step], kvo_ref.at[place.group], z_send.at[step], z_recv.at[(GROUPS - step) % GROUPS], place.other_group(step)).start()
             else:
                 kvo_ref[place.group] = bufs[stage][step]
+        for stream in streams:
+            if stage < len(stream.order):
+                stream.copy(stage).wait()
+                stream.absorb(stage)
+                if stage < len(stream.order) - 1:
+                    stream.copy(stage + 1).start()
     for step in (1, 3, 2):
         there = kvo_ref.at[(place.group + step) % GROUPS]
         remote(bufs[ndim - 1].at[step], there, z_send.at[step], z_recv.at[step], place.other_group(step)).wait()
     return_heads_wait(place, q_ref, qo_ref, q_send, q_recv)
 
 
-def reduce_all(shards, q_packed, kv_sums):
+def add_two(dst_ref, one_ref, two_ref):
+    lead = dst_ref.shape[:-2]
+
+    def one(step, _):
+        place, left = [], step
+        for size in reversed(lead):
+            place.append(left % size)
+            left = left // size
+        place = tuple(reversed(place))
+        dst_ref[place] = (one_ref[place].astype(jnp.float32) + two_ref[place].astype(jnp.float32)).astype(dst_ref.dtype)
+        return 0
+
+    lax.fori_loop(0, math.prod(lead), one, 0)
+
+
+def reduce_all(shape, q_packed, kv_sums, orders, pairs):
+    shards = shape["blk"]
     tokens_all, width = kv_sums.shape[1:]
     tokens = tokens_all // shards
     rest_bits = bits_of(shards // GROUPS)
     ndim = 1 + len(rest_bits)
     sem = pltpu.SemaphoreType.DMA
+    scratch = [pltpu.VMEM((GROUPS,) + (2,) * (ndim - 1 - s) + (tokens, width), kv_sums.dtype) for s in range(ndim)]
+    flat, sums = [], []
+    for (kept, order), pair in zip(orders, pairs):
+        rows, cols = pair[0].shape[-2:]
+        flat += [part.reshape((2,) * len(kept) + (rows, cols)) for part in pair]
+        sums.append(jax.ShapeDtypeStruct((rows, cols), jnp.float32))
+        scratch.append(pltpu.VMEM((2,) * len(kept) + (rows, cols), jnp.bfloat16))
+        scratch += stream_scratch(len(kept), order, rows, cols)
+    stages = max([len(order) for _, order in orders], default=1)
     return pl.pallas_call(
-        functools.partial(reduce_kernel, shards),
+        functools.partial(reduce_kernel, shards, bit_axes(shape), orders),
         out_shape=(
             jax.ShapeDtypeStruct((GROUPS,) + q_packed.shape[2:], q_packed.dtype),
             jax.ShapeDtypeStruct((GROUPS, tokens, width), kv_sums.dtype),
-        ),
-        in_specs=[pl.BlockSpec(memory_space=pltpu.VMEM)] * 2,
-        out_specs=(pl.BlockSpec(memory_space=pltpu.VMEM),) * 2,
-        scratch_shapes=[sem((4,)), sem((4,)), sem((ndim, GROUPS)), sem((ndim, GROUPS)), sem((GROUPS,)), sem((GROUPS,))]
-        + [pltpu.VMEM((GROUPS,) + (2,) * (ndim - 1 - s) + (tokens, width), kv_sums.dtype) for s in range(ndim)],
+        ) + tuple(sums),
+        in_specs=[VMEM_SPEC] * (2 + len(flat)),
+        out_specs=(VMEM_SPEC,) * (2 + len(sums)),
+        scratch_shapes=[sem((4,)), sem((4,)), sem((ndim, GROUPS)), sem((ndim, GROUPS)), sem((GROUPS,)), sem((GROUPS,)),
+                        sem((max(len(orders), 1), stages)), sem((max(len(orders), 1), stages))] + scratch,
         compiler_params=pltpu.CompilerParams(collective_id=2, has_side_effects=True, vmem_limit_bytes=VMEM_BYTES),
         name="reduce_keys",
-    )(q_packed, kv_sums.reshape((2, GROUPS) + (2,) * len(rest_bits) + (tokens, width)))
-
-
-def weights_kernel(orders, axes, *refs):
-    streams = len(orders) - 1
-    ins, small_ref = refs[:streams], refs[streams]
-    outs, small_out = refs[streams + 1 : 2 * streams + 1], refs[2 * streams + 1]
-    send_sem, recv_sem = refs[2 * streams + 2 : 2 * streams + 4]
-    bufs = refs[2 * streams + 4 :]
+    )(q_packed, kv_sums.reshape((2, GROUPS) + (2,) * len(rest_bits) + (tokens, width)), *flat)
+
+
+def sums_kernel(shards, axes, orders, *refs):
+    count = len(orders) - 1
+    ins, small_ref, spill_ref = refs[:count], refs[count], refs[count + 1]
+    outs, small_out, spill_out = refs[count + 2 : 2 * count + 2], refs[2 * count + 2], refs[2 * count + 3]
+    w_send, w_recv, s_send, s_recv = refs[2 * count + 4 : 2 * count + 8]
+    bufs = refs[2 * count + 8 :]
+    at = {"dp": lax.axis_index("dp"), "blk": lax.axis_index("blk")}
+    whole = Whole(axes, at, orders[-1], small_ref, bufs[-1], small_out, w_send.at[count], w_recv.at[count])
+    streams, used = [], 0
+    for s in range(count):
+        more = bufs[used : used + len(orders[s])]
+        used += len(orders[s])
+        streams.append(Stream(axes, at, sorted(orders[s]), orders[s], ins[s], more, outs[s], w_send.at[s], w_recv.at[s]))
+    left = (at["dp"], (at["blk"] + shards - 1) % shards)
+    right = (at["dp"], (at["blk"] + 1) % shards)
+    greet([whole.stream.target(p) for p in range(len(axes))] + [left, right])
+    spills = [
+        remote(spill_ref.at[0], spill_out.at[1], s_send.at[0], s_recv.at[1], left),
+        remote(spill_ref.at[1], spill_out.at[0], s_send.at[1], s_recv.at[0], right),
+    ]
+    streams.append(whole)
+    for stream in streams:
+        stream.copy(0).start()
+    for copy in spills:
+        copy.start()
+    run_streams(streams)
+    for copy in spills:
+        copy.wait()
+
+
+def last_sums(shape, blocks, orders, small, spill):
+    axes = bit_axes(shape)
     ndim = len(axes)
-    at = {"dp": lax.axis_index("dp"), "blk": lax.axis_index("blk")}
-    own = [bit(at[axis], mask) for axis, mask in axes]
-
-    def target(p):
-        axis, mask = axes[p]
-        moved = dict(at)
-        moved[axis] = flipped(at[axis], mask)
-        return (moved["dp"], moved["blk"])
-
-    greet([target(p) for p in range(ndim)])
-    small_bufs = bufs[streams * ndim]
-    small_out[...] = small_ref[...]
-
-    def parts(s, stage):
-        order = orders[s]
-        if s == streams:
-            src = small_ref if stage == 0 else small_bufs.at[1, stage - 1]
-            return src, small_bufs.at[0, stage], None
-        kept = [p for p in range(ndim) if p not in order[:stage]]
-        src = ins[s] if stage == 0 else bufs[s * ndim + stage - 1]
-        return src, bufs[s * ndim + stage], kept
-
-    def copy_of(s, stage):
-        src, buf, kept = parts(s, stage)
-        p_now = orders[s][stage]
-        if kept is not None:
-            src = src.at[tuple(1 - own[p] if p == p_now else slice(None) for p in kept)]
-        return remote(src, buf, send_sem.at[s, stage], recv_sem.at[s, stage], target(p_now))
-
-    def absorb(s, stage):
-        src, buf, kept = parts(s, stage)
-        if kept is None:
-            total = src[...] + buf[...]
-            if stage == ndim - 1:
-                small_out[...] = total
-            else:
-                small_bufs[1, stage] = total
-            return
-        p_now = orders[s][stage]
-        index = tuple(own[p] if p == p_now else None for p in kept)
-        if stage == ndim - 1:
-            outs[s][...] = buf[...].astype(jnp.float32) + src[index[0]].astype(jnp.float32)
-        else:
-            add_blocks(buf, src, index, buf.shape)
-
-    for s in range(streams + 1):
-        copy_of(s, 0).start()
-    for stage in range(ndim):
-        for s in range(streams + 1):
-            copy_of(s, stage).wait()
-            absorb(s, stage)
-            if stage < ndim - 1:
-                copy_of(s, stage + 1).start()
-
-
-def reduce_weights(shape, blocks, small):
-    axes = [("dp", m) for m in bits_of(shape["dp"])] + [("blk", m) for m in bits_of(shape["blk"])]
-    ndim = len(axes)
-    rest_bits = bits_of(shape["blk"] // GROUPS)
-    core = ndim - 1
-    across = list(range(len(bits_of(shape["dp"]))))
-    up = [ndim - len(rest_bits) + p for p in range(len(rest_bits) - 1)]
-    along = [ndim - len(rest_bits) - 1, ndim - len(rest_bits) - 2]
-    first = [core] + across + up + along
-    second = [core] + up + across + along
-    orders = [first if s % 2 == 0 else second for s in range(len(blocks))] + [first]
     sem = pltpu.SemaphoreType.DMA
-    scratch = []
-    for block in blocks:
+    scratch, sums = [], []
+    for block, order in zip(blocks, orders):
         rows, cols = block.shape[-2:]
-        scratch += [pltpu.VMEM((2,) * (ndim - 1 - s) + (rows, cols), block.dtype) for s in range(ndim)]
+        scratch += stream_scratch(ndim, order, rows, cols)
+        sums.append(jax.ShapeDtypeStruct((rows, cols), jnp.float32))
+    count = len(blocks)
     scratch.append(pltpu.VMEM((2, ndim) + small.shape, small.dtype))
-    wide = [block.reshape((2,) * ndim + block.shape[-2:]) for block in blocks]
     found = pl.pallas_call(
-        functools.partial(weights_kernel, orders, axes),
-        out_shape=tuple(jax.ShapeDtypeStruct(b.shape[-2:], jnp.float32) for b in blocks) + (jax.ShapeDtypeStruct(small.shape, small.dtype),),
-        in_specs=[pl.BlockSpec(memory_space=pltpu.VMEM)] * (len(blocks) + 1),
-        out_specs=(pl.BlockSpec(memory_space=pltpu.VMEM),) * (len(blocks) + 1),
-        scratch_shapes=[sem((len(blocks) + 1, ndim)), sem((len(blocks) + 1, ndim))] + scratch,
+        functools.partial(sums_kernel, shape["blk"], axes, orders),
+        out_shape=tuple(sums) + (jax.ShapeDtypeStruct(small.shape, small.dtype), jax.ShapeDtypeStruct(spill.shape, spill.dtype)),
+        in_specs=[VMEM_SPEC] * (count + 2),
+        out_specs=(VMEM_SPEC,) * (count + 2),
+        scratch_shapes=[sem((count + 1, ndim)), sem((count + 1, ndim)), sem((2,)), sem((2,))] + scratch,
         compiler_params=pltpu.CompilerParams(collective_id=3, has_side_effects=True, vmem_limit_bytes=VMEM_BYTES),
-        name="reduce_weights",
-    )(*wide, small)
-    return found[:-1], found[-1]
+        name="last_sums",
+    )(*[b.reshape((2,) * ndim + b.shape[-2:]) for b in blocks], small, spill)
+    return found[:count], found[count], found[count + 1]
 
 
 TQ = 256
@@ -670,10 +812,6 @@
         return 0
 
     lax.fori_loop(0, 2, row_body, 0)
-
-
-SMEM_SPEC = pl.BlockSpec(memory_space=pltpu.SMEM)
-VMEM_SPEC = pl.BlockSpec(memory_space=pltpu.VMEM)
 
 
 def attention(bounds, table, q, kv, se):
@@ -863,21 +1001,390 @@
     )(bounds, table, q, do, keep, kv, bias, se, lse)
 
 
-def pack_heads(array):
-    tokens, width = array.shape
-    parts = jnp.transpose(array.reshape(tokens, GROUPS, width // GROUPS), (1, 0, 2))
+TAPS = tuple(range(-3, 5))
+LEAD = 8
+
+
+def pool_scalars(y_rows, lab_rows, first):
+    tokens = y_rows[0].shape[1]
+    t = lax.broadcasted_iota(jnp.int32, (1, tokens), 1)
+    at = lambda rows, k: rows[k + 3]
+    found = []
+    for p in range(2):
+        inside = {1: 0 * t, 2: 0 * t + p, 3: (first + 2 * t + p) % 3, 4: 2 * (t % 2) + p}
+        weights, scores = {}, []
+        for b in range(1, MAX_BLOCK + 1):
+            keep = {}
+            for o in range(1 - b, b):
+                same = jnp.logical_and(inside[b] + o >= 0, inside[b] + o < b)
+                same = jnp.logical_and(same, at(lab_rows, p + o) == at(lab_rows, p))
+                keep[o] = same.astype(jnp.float32)
+            inverse = 1.0 / sum(keep.values())
+            for o in keep:
+                weights[b, o] = keep[o] * inverse
+            scores.append(sum(weights[b, o] * at(y_rows, p + o) for o in keep))
+        top = functools.reduce(jnp.maximum, scores)
+        grown = [jnp.exp(s - top) for s in scores]
+        total = sum(grown)
+        found.append(([g / total for g in grown], weights))
+    return found
+
+
+def tap_weights(found):
+    rows = []
+    for k in TAPS:
+        row = 0.0
+        for p, (probs, weights) in enumerate(found):
+            for b in range(1, MAX_BLOCK + 1):
+                if (b, k - p) in weights:
+                    row = row + probs[b - 1] * weights[b, k - p]
+        rows.append(0.5 * row)
+    return rows
+
+
+def as_columns(rows):
+    tokens = rows[0].shape[1]
+    return jnp.concatenate(list(rows) + [jnp.zeros((128 - len(rows), tokens), jnp.float32)], axis=0).T
+
+
+def load_bytes(x_ref, before_ref, after_ref, xs):
+    length, width = x_ref.shape
+    for j in range(width // 128):
+        cols = slice(j * 128, j * 128 + 128)
+        xs[j, 0:LEAD, :] = jnp.zeros((LEAD, 128), jnp.float32)
+        xs[j, LEAD + length :, :] = jnp.zeros((LEAD, 128), jnp.float32)
+        xs[j, LEAD - 2 : LEAD, :] = before_ref[0:2, cols].astype(jnp.float32)
+        xs[j, LEAD + length : LEAD + length + 2, :] = after_ref[0:2, cols].astype(jnp.float32)
+        xs[j, LEAD : LEAD + length, :] = x_ref[:, cols].astype(jnp.float32)
+
+
+def tap(xs, k, tokens):
+    return jnp.concatenate([xs[j, pl.ds(LEAD + k, tokens, stride=2), :] for j in range(xs.shape[0])], axis=1)
+
+
+def strips(buf, first, rows):
+    return jnp.concatenate([buf[j, first : first + rows, :] for j in range(buf.shape[0])], axis=1)
+
+
+def unit_rows(values):
+    return lax.rsqrt(jnp.mean(values * values, axis=-1, keepdims=True) + 1e-06)
+
+
+def pool_kernel(shards, scale, x_ref, before_ref, after_ref, lab_ref, score_ref, gain_ref, wq_ref, wk_ref, wv_ref,
+                hidden_ref, n1_ref, y_ref, share_ref, q_ref, kv_ref, xs):
+    tokens = hidden_ref.shape[0]
+    width = hidden_ref.shape[1]
+    load_bytes(x_ref, before_ref, after_ref, xs)
+    score = jnp.broadcast_to(score_ref[...], (8, width))
+    for k in TAPS:
+        y_ref[k + 3 : k + 4, :] = mxu(score, tap(xs, k, tokens).astype(jnp.bfloat16), NT)[0:1]
+    rows = [y_ref[j : j + 1, :] for j in range(8)]
+    labels = [lab_ref[j : j + 1, :] for j in range(8)]
+    first = (lax.axis_index("blk") * x_ref.shape[0]) % 3
+    found = pool_scalars(rows, labels, first)
+    lane = lax.broadcasted_iota(jnp.int32, (1, 128), 1)
+    share = jnp.zeros((1, 128), jnp.float32)
+    for b in range(MAX_BLOCK):
+        share = jnp.where(lane == b, jnp.sum(found[0][0][b] + found[1][0][b], axis=1, keepdims=True) * scale, share)
+    share_ref[...] = share
+    columns = as_columns(tap_weights(found))
+    hidden = sum(columns[:, k + 3 : k + 4] * tap(xs, k, tokens) for k in TAPS)
+    hidden_ref[...] = hidden
+    n1 = (hidden * unit_rows(hidden) * gain_ref[...].astype(jnp.float32)).astype(jnp.bfloat16)
+    n1_ref[...] = n1
+    keys = mxu(n1, wk_ref[...]).astype(jnp.bfloat16)
+    values = mxu(n1, wv_ref[...]).astype(jnp.bfloat16)
+    low = lane < 64
+    for j in range(width // 128):
+        k_pair, v_pair = keys[:, j * 128 : j * 128 + 128], values[:, j * 128 : j * 128 + 128]
+        one = jnp.where(low, k_pair, turned(v_pair))
+        two = jnp.where(low, turned(k_pair), v_pair)
+        for head, tile in ((2 * j, one), (2 * j + 1, two)):
+            kv_ref[head // 3, :, head % 3 * 128 : head % 3 * 128 + 128] = tile
+    queries = mxu(n1, wq_ref[...]).astype(jnp.bfloat16) * jnp.bfloat16(0.125)
+    put_packed(queries, q_ref)
+
+
+def put_packed(array, out_ref):
+    tokens = array.shape[0]
     half = tokens // 2
-    last = jnp.concatenate([parts[:, :half, 128:], parts[:, half:, 128:]], axis=2)
-    return jnp.concatenate([parts[:, :, :128], last], axis=1)
-
-
-def unpack_heads(packed):
-    rows = packed.shape[1]
-    tokens = rows * 2 // 3
-    last = packed[:, tokens:]
-    last = jnp.concatenate([last[:, :, :64], last[:, :, 64:]], axis=1)
-    parts = jnp.concatenate([packed[:, :tokens], last], axis=2)
-    return jnp.transpose(parts, (1, 0, 2)).reshape(tokens, -1)
+    for g in range(GROUPS):
+        part = array[:, g * 192 : g * 192 + 192]
+        out_ref[g, 0:tokens, :] = part[:, 0:128]
+        out_ref[g, tokens:, :] = jnp.concatenate([part[:half, 128:], part[half:, 128:]], axis=1)
+
+
+def get_packed(packed_ref):
+    tokens = packed_ref.shape[1] * 2 // 3
+    parts = []
+    for g in range(GROUPS):
+        last = packed_ref[g, tokens:, :]
+        parts += [packed_ref[g, 0:tokens, :], jnp.concatenate([last[:, :64], last[:, 64:]], axis=0)]
+    return jnp.concatenate(parts, axis=1)
+
+
+def pool_and_project(shards, scale, x, before, after, labels, score, gain, wq, wk, wv):
+    length, width = x.shape
+    tokens = length // 2
+    return pl.pallas_call(
+        functools.partial(pool_kernel, shards, scale),
+        out_shape=(
+            jax.ShapeDtypeStruct((tokens, width), jnp.float32),
+            jax.ShapeDtypeStruct((tokens, width), jnp.bfloat16),
+            jax.ShapeDtypeStruct((8, tokens), jnp.float32),
+            jax.ShapeDtypeStruct((1, 128), jnp.float32),
+            jax.ShapeDtypeStruct((GROUPS, tokens * 3 // 2, 128), jnp.bfloat16),
+            jax.ShapeDtypeStruct((GROUPS, tokens, width * 2 // GROUPS), jnp.bfloat16),
+        ),
+        in_specs=[VMEM_SPEC] * 9,
+        out_specs=(VMEM_SPEC,) * 6,
+        scratch_shapes=[pltpu.VMEM((width // 128, length + 2 * LEAD, 128), jnp.float32)],
+        compiler_params=pltpu.CompilerParams(vmem_limit_bytes=VMEM_BYTES),
+        name="pool_and_project",
+    )(x, before, after, labels, score, gain, wq, wk, wv)
+
+
+GELU_A = math.sqrt(2.0 / math.pi)
+GELU_B = 0.044715
+
+
+def norm_back(d_out, rows, gain):
+    unit = unit_rows(rows)
+    flat = rows * unit
+    scaled = d_out * gain
+    d_rows = unit * (scaled - flat * jnp.mean(scaled * flat, axis=-1, keepdims=True))
+    return d_rows, jnp.sum(d_out * flat, axis=0, keepdims=True)
+
+
+def feed_kernel(o_ref, hidden_ref, ct_ref, gain_ref, wo_ref, wg_ref, wu_ref, wd_ref,
+                out_ref, dres_ref, da_ref, dgain_ref, n2_ref, att_ref, act_ref, dg_ref, du_ref, db_ref, acc, dn2):
+    ff = wg_ref.shape[1]
+    step = 512
+    att = get_packed(o_ref)
+    att_ref[...] = att
+    residual = hidden_ref[...] + mxu(att, wo_ref[...])
+    gain = gain_ref[...].astype(jnp.float32)
+    n2_ref[...] = (residual * unit_rows(residual) * gain).astype(jnp.bfloat16)
+    acc[...] = residual
+    dn2[...] = jnp.zeros_like(dn2)
+
+    for j in range(ff // step):
+        cols = slice(j * step, j * step + step)
+        n2 = n2_ref[...]
+        gate = mxu(n2, wg_ref[:, cols])
+        up = mxu(n2, wu_ref[:, cols])
+        d_act = mxu(ct_ref[...], wd_ref[cols, :], NT)
+        square = gate * gate
+        curve = jnp.tanh(GELU_A * gate * (1.0 + GELU_B * square))
+        half = 0.5 * (1.0 + curve)
+        grown = gate * half
+        slope = half + 0.5 * gate * (1.0 - curve * curve) * (GELU_A * (1.0 + 3.0 * GELU_B * square))
+        act = (grown * up).astype(jnp.bfloat16)
+        d_gate = (d_act * up * slope).astype(jnp.bfloat16)
+        d_up = (d_act * grown).astype(jnp.bfloat16)
+        act_ref[:, cols] = act
+        dg_ref[:, cols] = d_gate
+        du_ref[:, cols] = d_up
+        acc[...] += mxu(act, wd_ref[cols, :])
+        dn2[...] += mxu(d_gate, wg_ref[:, cols], NT) + mxu(d_up, wu_ref[:, cols], NT)
+
+    out_ref[...] = acc[...].astype(jnp.bfloat16)
+    residual = hidden_ref[...] + mxu(att_ref[...], wo_ref[...])
+    d_rows, d_gain = norm_back(dn2[...], residual, gain)
+    dgain_ref[...] = d_gain
+    d_res = ct_ref[...].astype(jnp.float32) + d_rows
+    dres_ref[...] = d_res
+    d_branch = d_res.astype(jnp.bfloat16)
+    db_ref[...] = d_branch
+    put_packed(mxu(d_branch, wo_ref[...], NT).astype(jnp.bfloat16), da_ref)
+
+
+def feed_forward(o_home, hidden, ct, gain, wo, wg, wu, wd):
+    tokens, width = hidden.shape
+    ff = wg.shape[1]
+    low = lambda cols: jax.ShapeDtypeStruct((tokens, cols), jnp.bfloat16)
+    return pl.pallas_call(
+        feed_kernel,
+        out_shape=(
+            low(width),
+            jax.ShapeDtypeStruct((tokens, width), jnp.float32),
+            jax.ShapeDtypeStruct(o_home.shape, jnp.bfloat16),
+            jax.ShapeDtypeStruct((1, width), jnp.float32),
+            low(width), low(width), low(ff), low(ff), low(ff), low(width),
+        ),
+        in_specs=[VMEM_SPEC] * 8,
+        out_specs=(VMEM_SPEC,) * 10,
+        scratch_shapes=[pltpu.VMEM((tokens, width), jnp.float32)] * 2,
+        compiler_params=pltpu.CompilerParams(vmem_limit_bytes=VMEM_BYTES),
+        name="feed_forward",
+    )(o_home, hidden, ct, gain, wo, wg, wu, wd)
+
+
+def last_kernel(with_blocks, dq_ref, dkv_ref, hidden_ref, dres_ref, n1_ref, x_ref, before_ref, after_ref, lab_ref, y_ref, score_ref,
+                gain_ref, wq_ref, wk_ref, wv_ref, dgain2_ref, share_ref, tab_ref,
+                gb_ref, edge_ref, spill_ref, small_ref, w_ref, xs, gbuf, *grads):
+    tokens, width = hidden_ref.shape
+    length = x_ref.shape[0]
+    lane = lax.broadcasted_iota(jnp.int32, (1, 128), 1)
+    low = lane < 64
+    dq = get_packed(dq_ref)
+    dk_parts, dv_parts = [], []
+    for j in range(width // 128):
+        one, two = [dkv_ref[h // 3, :, h % 3 * 128 : h % 3 * 128 + 128] for h in (2 * j, 2 * j + 1)]
+        dk_parts.append(jnp.where(low, one, turned(two)))
+        dv_parts.append(jnp.where(low, turned(one), two))
+    dk, dv = jnp.concatenate(dk_parts, axis=1), jnp.concatenate(dv_parts, axis=1)
+    d_n1 = mxu(dq, wq_ref[...], NT) + mxu(dk, wk_ref[...], NT) + mxu(dv, wv_ref[...], NT)
+    d_rows, d_gain1 = norm_back(d_n1, hidden_ref[...], gain_ref[...].astype(jnp.float32))
+    d_hidden = dres_ref[...] + d_rows
+
+    load_bytes(x_ref, before_ref, after_ref, xs)
+    met = jnp.zeros((tokens, 128), jnp.float32)
+    for k in TAPS:
+        met = jnp.where(lane == k + 3, jnp.sum(d_hidden * tap(xs, k, tokens), axis=-1, keepdims=True), met)
+    met = met.T
+    first = (lax.axis_index("blk") * length) % 3
+    found = pool_scalars([y_ref[j : j + 1, :] for j in range(8)], [lab_ref[j : j + 1, :] for j in range(8)], first)
+    touch = [0.0] * 8
+    for p, (probs, weights) in enumerate(found):
+        d_block = []
+        for b in range(1, MAX_BLOCK + 1):
+            d_block.append(0.5 * sum(weights[b, o] * met[p + o + 3 : p + o + 4] for o in range(1 - b, b)))
+        mean = sum(q * d for q, d in zip(probs, d_block))
+        for b in range(1, MAX_BLOCK + 1):
+            d_score = probs[b - 1] * (d_block[b - 1] - mean)
+            for o in range(1 - b, b):
+                touch[p + o + 3] = touch[p + o + 3] + d_score * weights[b, o]
+    share_cols = as_columns(tap_weights(found) + touch)
+    score = score_ref[...].astype(jnp.float32)
+    gbuf[...] = jnp.zeros_like(gbuf)
+    d_score_vec = jnp.zeros((1, width), jnp.float32)
+    for k in TAPS:
+        own, via = share_cols[:, k + 3 : k + 4], share_cols[:, k + 11 : k + 12]
+        added = own * d_hidden + via * score
+        for j in range(gbuf.shape[0]):
+            gbuf[j, pl.ds(LEAD + k, tokens, stride=2), :] += added[:, j * 128 : j * 128 + 128]
+        d_score_vec = d_score_vec + jnp.sum(via * tap(xs, k, tokens), axis=0, keepdims=True)
+    gb_ref[...] = strips(gbuf, LEAD, length).astype(jnp.bfloat16)
+    edge_ref[0] = strips(gbuf, LEAD, 16)
+    edge_ref[1] = strips(gbuf, LEAD + length - 16, 16)
+    spill_ref[0] = strips(gbuf, 0, LEAD)
+    spill_ref[1] = strips(gbuf, LEAD + length, LEAD)
+
+    small_ref[...] = jnp.zeros_like(small_ref)
+    for row, vector in ((0, d_score_vec), (6, d_gain1), (12, dgain2_ref[...])):
+        for j in range(width // 128):
+            small_ref[row + j : row + j + 1, :] = vector[:, j * 128 : j * 128 + 128]
+    heads = tab_ref.shape[0]
+    group = lax.axis_index("blk") // (lax.axis_size("blk") // GROUPS)
+    for h in range(heads):
+        total = lax.dot_general(
+            jnp.ones((8, tab_ref.shape[2]), jnp.float32), tab_ref[h], NT,
+            precision=lax.Precision.HIGHEST, preferred_element_type=jnp.float32,
+        )
+        small_ref[pl.ds(18 + group * heads + h, 1), 0:BUCKETS] = total[0:1]
+    small_ref[30:31, :] = share_ref[...]
+
+    if with_blocks:
+        (whole,) = grads
+        n1_t = n1_ref[...].T
+        for j, part in enumerate((dq, dk, dv)):
+            whole[j] = mxu(n1_t, part)
+        per = width // w_ref.shape[0]
+
+        def block(d, _):
+            start = pl.multiple_of(d * per, 8)
+            parts = [whole[j, pl.ds(start, per), :] for j in range(3)]
+            parts.append(jnp.zeros((w_ref.shape[1] - 3 * per, width), jnp.float32))
+            w_ref[d] = jnp.concatenate(parts, axis=0).astype(jnp.bfloat16)
+            return 0
+
+        lax.fori_loop(0, w_ref.shape[0], block, 0)
+    else:
+        w_ref[0] = dq
+        w_ref[1] = dk
+        w_ref[2] = dv
+
+
+def last_part(devices, dq, dkv, hidden, dres, n1, x, before, after, labels, y, score, gain, wq, wk, wv, dgain2, share, tab):
+    tokens, width = hidden.shape
+    length = x.shape[0]
+    with_blocks = devices <= 32
+    full = jax.ShapeDtypeStruct
+    blocks = (devices, -(-3 * (width // devices) // 16) * 16, width) if with_blocks else (3, tokens, width)
+    scratch = [pltpu.VMEM((width // 128, length + 2 * LEAD, 128), jnp.float32)] * 2
+    if with_blocks:
+        scratch.append(pltpu.VMEM((3, width, width), jnp.float32))
+    return pl.pallas_call(
+        functools.partial(last_kernel, with_blocks),
+        out_shape=(
+            full((length, width), jnp.bfloat16),
+            full((2, 16, width), jnp.float32),
+            full((2, LEAD, width), jnp.float32),
+            full((32, 128), jnp.float32),
+            full(blocks, jnp.bfloat16),
+        ),
+        in_specs=[VMEM_SPEC] * 18,
+        out_specs=(VMEM_SPEC,) * 5,
+        scratch_shapes=scratch,
+        compiler_params=pltpu.CompilerParams(vmem_limit_bytes=VMEM_BYTES),
+        name="last_part",
+    )(dq, dkv, hidden, dres, n1, x, before, after, labels, y, score, gain, wq, wk, wv, dgain2, share, tab)
+
+
+def finish_kernel(shards, heads_all, gb_ref, edge_ref, spill_ref, small_ref, *refs):
+    position = lax.axis_index("blk")
+    streams, outs = refs[: len(refs) - (5 if len(refs) == 5 else 12)], refs[len(refs) - (5 if len(refs) == 5 else 12) :]
+    bytes_ref, score_ref, gain1_ref, gain2_ref, tab_ref = outs[:5]
+    length = gb_ref.shape[0]
+    bytes_ref[...] = gb_ref[...]
+    zero = jnp.zeros((16 - LEAD, gb_ref.shape[1]), jnp.float32)
+    left = jnp.where(position > 0, spill_ref[0], 0.0)
+    right = jnp.where(position < shards - 1, spill_ref[1], 0.0)
+    bytes_ref[0:16, :] = (edge_ref[0] + jnp.concatenate([left, zero], axis=0)).astype(jnp.bfloat16)
+    bytes_ref[length - 16 :, :] = (edge_ref[1] + jnp.concatenate([zero, right], axis=0)).astype(jnp.bfloat16)
+    for row, ref in ((0, score_ref), (6, gain1_ref), (12, gain2_ref)):
+        for j in range(6):
+            ref[:, j * 128 : j * 128 + 128] = small_ref[row + j : row + j + 1, :]
+    tab_ref[...] = small_ref[16:32, :]
+    if streams:
+        gq, gk, gv, go, gg, gu, gd = outs[5:]
+        per = gq.shape[0]
+        wide_a, wide_b, slim, *thirds = streams
+        for j, ref in enumerate((gq, gk, gv)):
+            for c, third in enumerate(thirds):
+                ref[:, c * 256 : c * 256 + 256] = third[j * per : j * per + per, :]
+        half = wide_a.shape[1]
+        for c, ref in ((0, wide_a), (1, wide_b)):
+            gg[:, c * half : c * half + half] = ref[0:per, :]
+            gu[:, c * half : c * half + half] = ref[per : 2 * per, :]
+        go[...] = slim[0:per, :]
+        gd[...] = slim[32:, :]
+
+
+def finish(shards, heads_all, per, ff, gb, edge, spill, small, streams):
+    width = gb.shape[1]
+    full = jax.ShapeDtypeStruct
+    line = full((1, width), jnp.float32)
+    outs = [full(gb.shape, jnp.bfloat16), line, line, line, full((16, 128), jnp.float32)]
+    if streams:
+        square, broad = full((per, width), jnp.float32), full((per, ff), jnp.float32)
+        outs += [square] * 4 + [broad] * 2 + [full((streams[2].shape[0] - 32, width), jnp.float32)]
+    return pl.pallas_call(
+        functools.partial(finish_kernel, shards, heads_all),
+        out_shape=tuple(outs),
+        in_specs=[VMEM_SPEC] * (4 + len(streams)),
+        out_specs=(VMEM_SPEC,) * len(outs),
+        compiler_params=pltpu.CompilerParams(vmem_limit_bytes=VMEM_BYTES),
+        name="finish",
+    )(gb, edge, spill, small, *streams)
+
+
+def neighbours(rows):
+    peers = lax.axis_size("blk")
+    up = [(i, i + 1) for i in range(peers - 1)]
+    last, leading = rows
+    return lax.ppermute(last, "blk", up), lax.ppermute(leading, "blk", [(j, i) for i, j in up])
 
 
 def body(
@@ -896,59 +1403,37 @@
     w_down,
     cotangent,
 ):
-    row_count, length, width_d = byte_embeds.shape
+    row_count, length, width = byte_embeds.shape
     tokens = length // 2
     shards = lax.axis_size("blk")
-    devices_all = shards * lax.axis_size("dp")
+    shape = {"dp": lax.axis_size("dp"), "blk": shards}
+    devices = shards * shape["dp"]
+    heads = rel_bias.shape[1] // GROUPS
     position = lax.axis_index("blk")
-    base = position * length
-    head_count = rel_bias.shape[1]
-    head_dim = width_d // head_count
-    score_scale = 1.0 / math.sqrt(head_dim)
-    bias_table = rel_bias.astype(jnp.float32)
-    score_vec = score_weight.astype(jnp.float32)
-    rim_bytes = extended(byte_embeds, (("blk", 1),), 2)
-    padded = jnp.pad(rim_bytes.astype(jnp.float32), ((0, 0), (1, 1), (0, 0)))
-    rim_labels = extended(segments + 1, (("blk", 1),), 2)
-    labels_pad = jnp.pad(rim_labels, ((0, 0), (1, 1)))
-    masks_all = pool_masks(labels_pad, base, length)
-    pools = []
-    for pool_terms, counts in masks_all:
-        summed = sum(
-            (
-                keep_mask[:, :, None] * padded[:, 3 + offset : 3 + offset + length]
-                for offset, keep_mask in pool_terms
-            )
-        )
-        pools.append(summed / counts[:, :, None])
-    stacked = jnp.stack(pools, axis=2)
-    block_scores = jnp.sum(stacked * score_vec, axis=-1)
-    block_probs = jax.nn.softmax(block_scores, axis=-1)
-    mixed = jnp.sum(block_probs[..., None] * stacked, axis=2)
-    hidden = 0.5 * (mixed[:, 0::2] + mixed[:, 1::2])
-    tok_labels = segments[:, 0::2]
-    gain_one = norm_gain1.astype(jnp.float32)
-    normed1, norm1_back = jax.vjp(rms_norm, hidden, gain_one)
-    n1_low = normed1.astype(jnp.bfloat16)
-    query_low = jnp.dot(n1_low, w_query, preferred_element_type=jnp.float32).astype(jnp.bfloat16)
-    key_low = jnp.dot(n1_low, w_key, preferred_element_type=jnp.float32).astype(jnp.bfloat16)
-    value_low = jnp.dot(n1_low, w_value, preferred_element_type=jnp.float32).astype(jnp.bfloat16)
-    shape = {"dp": lax.axis_size("dp"), "blk": shards}
-    group = position // (shards // GROUPS)
-    rest = position % (shards // GROUPS)
+    rest_size = shards // GROUPS
+    group, rest = position // rest_size, position % rest_size
     row = lax.axis_index("dp") % 2
-    group_heads = head_count // GROUPS
-    q_packed = pack_heads(query_low[0] * jnp.bfloat16(score_scale))
-    kv_parts = jnp.stack([key_low.reshape(tokens, head_count, head_dim), value_low.reshape(tokens, head_count, head_dim)], axis=2)
-    kv_parts = jnp.transpose(kv_parts.reshape(tokens, GROUPS, group_heads * 2 * head_dim), (1, 0, 2))
-    label_block = jnp.pad(tok_labels.reshape(tokens // 128, 128), ((0, 8 - tokens // 128), (0, 0)))
+    x, ids_here = byte_embeds[0], segments[0]
+
+    marks = (ids_here + 1).astype(jnp.bfloat16)
+    with_marks = lambda part, two: jnp.concatenate([part, jnp.pad(two, (0, width - 2))[None]], axis=0)
+    before, after = neighbours((with_marks(x[-2:], marks[-2:]), with_marks(x[:2], marks[:2])))
+    line = jnp.concatenate([before[2, :2], marks, after[2, :2]])
+    line = jnp.pad(line, (1, 1)).astype(jnp.int32).reshape(tokens + 3, 2).T
+    labels = jnp.stack([line[j % 2, j // 2 : j // 2 + tokens] for j in range(8)])
+
+    score_row, gain1, gain2 = score_weight[None], norm_gain1[None], norm_gain2[None]
+    hidden, n1, y, share, q_packed, kv_parts = pool_and_project(
+        shards, 1.0 / (row_count * length * devices), x, before, after, labels, score_row, gain1, w_query, w_key, w_value
+    )
+
+    label_block = jnp.pad(ids_here[0::2].reshape(tokens // 128, 128), ((0, 8 - tokens // 128), (0, 0)))
     q_all, kv_all, labels_all = gather_all(shards, q_packed, kv_parts, label_block)
     labels_all = labels_all.reshape(2, shards, 8, 128)[:, :, : tokens // 128].reshape(2, shards * tokens)
     ids = jnp.arange(8, dtype=jnp.int32)
     counts = jnp.sum((labels_all[:, None, :] == ids[None, :, None]).astype(jnp.int32), axis=2)
     ends = jnp.sum(jnp.where(ids[None, :] <= ids[:, None], counts[:, None, :], 0), axis=2)
     begins = ends - counts
-    rest_size = shards // GROUPS
     query_labels = jnp.stack(
         [lax.dynamic_slice_in_dim(labels_all, ((2 * row + i) * rest_size + rest) * tokens, tokens, 1) for i in range(2)],
         axis=1,
@@ -971,126 +1456,65 @@
         ],
         axis=-1,
     ).astype(jnp.int32)
-    table = lax.dynamic_slice_in_dim(bias_table.T, group * group_heads, group_heads, 0)
+    table = lax.dynamic_slice_in_dim(rel_bias.astype(jnp.float32).T, group * heads, heads, 0)
+
     o_packed, o_kept, log_total, bias_tiles = attention(bounds, table, q_all, kv_all, span)
     o_home = move_heads(return_kernel, (GROUPS,), shards, 4, o_packed)
-    attended_low = unpack_heads(o_home)[None]
-    residual = hidden + jnp.dot(attended_low, w_out, preferred_element_type=jnp.float32)
-    gain_two = norm_gain2.astype(jnp.float32)
-    normed2, norm2_back = jax.vjp(rms_norm, residual, gain_two)
-    n2_low = normed2.astype(jnp.bfloat16)
-    gate_proj = jnp.dot(n2_low, w_gate, preferred_element_type=jnp.float32)
-    up_proj = jnp.dot(n2_low, w_up, preferred_element_type=jnp.float32)
-    activated, geglu_back = jax.vjp(geglu, gate_proj, up_proj)
-    act_low = activated.astype(jnp.bfloat16)
-    block_out = (residual + jnp.dot(act_low, w_down, preferred_element_type=jnp.float32)).astype(
-        jnp.bfloat16
+    ct = cotangent[0]
+    block_out, d_res, da_packed, d_gain2, n2, att, act, d_gate, d_up, d_branch = feed_forward(
+        o_home, hidden, ct, gain2, w_out, w_gate, w_up, w_down
     )
-    grad_down = jnp.einsum("rtf,rtd->fd", act_low, cotangent, preferred_element_type=jnp.float32)
-    d_act = jnp.einsum("rtd,fd->rtf", cotangent, w_down, preferred_element_type=jnp.float32)
-    d_gate, d_up = geglu_back(d_act)
-    d_gate_low = d_gate.astype(jnp.bfloat16)
-    d_up_low = d_up.astype(jnp.bfloat16)
-    grad_gate = jnp.einsum("rtd,rtf->df", n2_low, d_gate_low, preferred_element_type=jnp.float32)
-    grad_up = jnp.einsum("rtd,rtf->df", n2_low, d_up_low, preferred_element_type=jnp.float32)
-    d_normed2 = jnp.einsum(
-        "rtf,df->rtd", d_gate_low, w_gate, preferred_element_type=jnp.float32
-    ) + jnp.einsum("rtf,df->rtd", d_up_low, w_up, preferred_element_type=jnp.float32)
-    d_res_part, d_gain_two = norm2_back(d_normed2)
-    d_residual = cotangent.astype(jnp.float32) + d_res_part
-    d_branch = d_residual.astype(jnp.bfloat16)
-    grad_out = jnp.einsum("rtd,rte->de", attended_low, d_branch, preferred_element_type=jnp.float32)
-    d_attended = jnp.einsum(
-        "rte,de->rtd", d_branch, w_out, preferred_element_type=jnp.float32
-    ).astype(jnp.bfloat16)
-    do_all = move_heads(spread_kernel, (2, 2), shards, 5, pack_heads(d_attended[0]))
+
+    orders, pairs = [], []
+    if devices == 32:
+        do_all, keep_a, send_a, keep_b, send_b, keep_c, send_c = spread_and_weights(
+            shards, da_packed, n2, att, act, d_gate, d_up, ct, d_branch
+        )
+        swap = lambda part, axis, mask: lax.ppermute(part, axis, [(i, i ^ mask) for i in range(lax.axis_size(axis))])
+        orders = [((1, 2, 3), (3, 2, 1)), ((0, 1, 2), (0, 2, 1)), ((0, 1, 3), (3, 0, 1))]
+        pairs = [(keep_a, swap(send_a, "dp", 1)), (keep_b, swap(send_b, "blk", 2)), (keep_c, swap(send_c, "blk", 4))]
+    else:
+        do_all = move_heads(spread_kernel, (2, 2), shards, 5, da_packed)
+
     dq_packed, dkv_all, d_table_lanes = attention_back(
         bounds, table, q_all, do_all, o_kept, kv_all, bias_tiles, span, log_total
     )
-    dq_home, dkv_home = reduce_all(shards, dq_packed, dkv_all)
-    d_query_low = unpack_heads(dq_home)[None]
-    dkv_home = jnp.transpose(dkv_home, (1, 0, 2)).reshape(1, tokens, head_count, 2, head_dim)
-    d_key_low = dkv_home[:, :, :, 0].reshape(1, tokens, width_d)
-    d_value_low = dkv_home[:, :, :, 1].reshape(1, tokens, width_d)
-    d_table = jnp.zeros((head_count, BUCKETS), jnp.float32)
-    d_table = lax.dynamic_update_slice_in_dim(d_table, jnp.sum(d_table_lanes, axis=-1), group * group_heads, 0).T
-    grad_query = jnp.einsum("rtd,rte->de", n1_low, d_query_low, preferred_element_type=jnp.float32)
-    grad_key = jnp.einsum("rtd,rte->de", n1_low, d_key_low, preferred_element_type=jnp.float32)
-    grad_value = jnp.einsum("rtd,rte->de", n1_low, d_value_low, preferred_element_type=jnp.float32)
-    d_normed1 = (
-        jnp.einsum("rte,de->rtd", d_query_low, w_query, preferred_element_type=jnp.float32)
-        + jnp.einsum("rte,de->rtd", d_key_low, w_key, preferred_element_type=jnp.float32)
-        + jnp.einsum("rte,de->rtd", d_value_low, w_value, preferred_element_type=jnp.float32)
+    dq_home, dkv_home, *sums = reduce_all(shape, dq_packed, dkv_all, orders, pairs)
+    grad_bytes, edge, spill, small, last_blocks = last_part(
+        devices, dq_home, dkv_home, hidden, d_res, n1, x, before, after, labels, y, score_row, gain1,
+        w_query, w_key, w_value, d_gain2, share, d_table_lanes,
     )
-    d_hid_part, d_gain_one = norm1_back(d_normed1)
-    d_hidden = d_residual + d_hid_part
-    d_mixed = 0.5 * jnp.repeat(d_hidden, 2, axis=1)
-    d_block = jnp.sum(d_mixed[:, :, None, :] * stacked, axis=-1)
-    d_block_scores = block_probs * (
-        d_block - jnp.sum(block_probs * d_block, axis=-1, keepdims=True)
+    across = len(bits_of(shape["dp"]))
+    ndim = across + len(bits_of(shards))
+    small_order = tuple(reversed(range(ndim)))
+    if devices == 32:
+        third = width // 3
+        blocks = [last_blocks[:, :, c * third : c * third + third] for c in range(3)]
+        thirds, small, spill = last_sums(
+            shape, blocks, [(4, 0, 3, 2, 1), (4, 3, 2, 1, 0), (4, 2, 0, 3, 1), small_order], small, spill
+        )
+        sums = list(sums) + list(thirds)
+    else:
+        _, small, spill = last_sums(shape, [], [small_order], small, spill)
+    per = width // devices
+    grad_bytes, g_score, g_gain1, g_gain2, rows, *grads = finish(
+        shards, rel_bias.shape[1], per, w_gate.shape[1], grad_bytes, edge, spill, small, sums
     )
-    grad_score_local = jnp.sum(d_block_scores[..., None] * stacked, axis=(0, 1, 2))
-    d_pools = (
-        block_probs[..., None] * d_mixed[:, :, None, :] + d_block_scores[..., None] * score_vec
-    )
-    spread = jnp.stack(
-        [
-            d_pools[:, :, width_index] / masks_all[width_index][1][:, :, None]
-            for width_index in range(MAX_BLOCK)
-        ],
-        axis=2,
-    ).reshape(row_count, length, MAX_BLOCK * width_d)
-    rim_spread = extended(spread.astype(jnp.bfloat16), (("blk", 1),), 2).astype(spread.dtype)
-    spread_pad = jnp.pad(rim_spread, ((0, 0), (1, 1), (0, 0))).reshape(
-        row_count, length + 6, MAX_BLOCK, width_d
-    )
-    d_bytes = jnp.zeros((row_count, length, width_d), jnp.float32)
-    for width_index in range(MAX_BLOCK):
-        for offset, keep_mask in masks_all[width_index][0]:
-            d_bytes = (
-                d_bytes
-                + keep_mask[:, :, None]
-                * spread_pad[:, 3 + offset : 3 + offset + length, width_index]
-            )
-    share_local = jnp.sum(block_probs, axis=(0, 1)) / (row_count * length * devices_all)
-    small = (grad_score_local, d_gain_one, d_gain_two, d_table, share_local)
-    if devices_all <= 32:
-        def blocks(grad):
-            return grad.reshape(devices_all, grad.shape[0] // devices_all, grad.shape[1]).astype(jnp.bfloat16)
-
-        wide = jnp.concatenate([blocks(grad_gate), blocks(grad_up)], axis=1)
-        slim = jnp.concatenate([blocks(g) for g in (grad_query, grad_key, grad_value, grad_out, grad_down)], axis=1)
-        flat = jnp.concatenate([part.reshape(-1) for part in small])
-        flat = jnp.pad(flat, (0, -flat.shape[0] % 1024)).reshape(-1, 128)
-        (wide, slim), flat = reduce_weights(shape, (wide, slim), flat)
-        per = width_d // devices_all
-        summed_weights = [slim[p * per : (p + 1) * per] for p in range(4)]
-        summed_weights += [wide[:per], wide[per:], slim[4 * per :]]
-        flat, summed_small = flat.reshape(-1), []
-        for part in small:
-            summed_small.append(flat[: part.size].reshape(part.shape))
-            flat = flat[part.size :]
-    else:
-        summed_weights = [
-            lax.psum_scatter(grad, ("dp", "blk"), scatter_dimension=0, tiled=True)
-            for grad in (grad_query, grad_key, grad_value, grad_out, grad_gate, grad_up, grad_down)
-        ]
-        summed_small = lax.psum(small, ("dp", "blk"))
+    if devices != 32:
+        product = lambda left, right: jnp.einsum("td,te->de", left, right, preferred_element_type=jnp.float32)
+        grads = [product(n1, last_blocks[j]) for j in range(3)]
+        grads += [product(att, d_branch), product(n2, d_gate), product(n2, d_up), product(act, ct)]
+        grads = [lax.psum_scatter(grad, ("dp", "blk"), scatter_dimension=0, tiled=True) for grad in grads]
     return (
-        block_out,
-        d_bytes.astype(jnp.bfloat16),
-        summed_small[0],
-        summed_small[1],
-        summed_weights[0],
-        summed_weights[1],
-        summed_weights[2],
-        summed_weights[3],
-        summed_small[3],
-        summed_small[2],
-        summed_weights[4],
-        summed_weights[5],
-        summed_weights[6],
-        summed_small[4],
+        block_out[None],
+        grad_bytes[None],
+        g_score[0],
+        g_gain1[0],
+        *grads[:4],
+        rows[2 : 2 + rel_bias.shape[1], :BUCKETS].T,
+        g_gain2[0],
+        *grads[4:],
+        rows[14, :MAX_BLOCK],
     )
 
 

time: 587 us -> 369 us (0.63); the launches traced: 577 us -> 367 us
  local copies, waits for them, and re-layouts: 95.2 us -> 16.7 us
  other arithmetic: 63.6 us -> 7.97 us
  matrix products: 38.3 us -> 0 us
  Pallas kernels: 362 us -> 336 us
  starting transfers between devices: 15.7 us -> 5.92 us
    dot_general x21 -> x0, matrix products: 38.3 us -> none  [the longest x1 2.69 us: body(): jnp.einsum('rtd,rtf->df', n2_low, d_gate_low, preferred_element_type=jnp....]
    slice x25 -> x5, local copies, waits for them, and re-layouts: 37.4 us -> 5.86 us  [the longest x1 4.08 us: body(): blocks = [last_blocks[:, :, c * third:c * third + third] for c in range(3)]]
    pallas_call x2 -> x1, Pallas kernels: 44.5 us -> 18.1 us  [move_heads(): pl.pallas_call(functools.partial(kernel, shards), out_shape=jax.ShapeDtyp...]
    concatenate x6 -> x2, other arithmetic: 16.2 us -> 0.02 us  [body(): jnp.concatenate([part, jnp.pad(two, (0, width - 2))[None]], axis=0)]
    unnamed x191 -> x10, local copies, waits for them, and re-layouts: 16.8 us -> 1.56 us
    reduce_sum x9 -> x0, other arithmetic: 14.3 us -> none  [the longest x1 4.34 us: body(): mixed = jnp.sum(block_probs[..., None] * stacked, axis=2)]
    convert_element_type x7 -> x1, other arithmetic: 11.1 us -> 0.69 us  [body(): marks = (ids_here + 1).astype(jnp.bfloat16)]
    ppermute x6 -> x5, starting transfers between devices: 15.7 us -> 5.92 us  [the longest x1 2.36 us: neighbours(): lax.ppermute(last, 'blk', up)]
  transfers between devices with their start and end apart: 6 -> 5, of which waited for: 0 -> 0; matrix products, arithmetic and copies ran while one was open for 11% -> 2% of each run, Pallas kernels for 21% -> 13%
where the time goes in v2:
time: 369 us; the launch traced here: 367 us
  Pallas kernels  336 us (91%)
  local copies, waits for them, and re-layouts  16.7 us (5%)
  other arithmetic  7.97 us (2%)
  starting transfers between devices  5.92 us (2%)
    pallas_call x1, Pallas kernels, reduce_all(): pl.pallas_call(functools.partial(reduce_kernel, shards, bit_axes(shape),...  78.6 us
    pallas_call x1, Pallas kernels, gather_all(): pl.pallas_call(functools.partial(gather_kernel, shards), out_shape=(jax.S...  59.4 us
    pallas_call x1, Pallas kernels, attention_back(): pl.pallas_call(bwd_kernel, out_shape=(jax.ShapeDtypeStruct(q.shape, jnp.b...  47.3 us
    pallas_call x1, Pallas kernels, attention(): pl.pallas_call(fwd_kernel, out_shape=(jax.ShapeDtypeStruct(packed, jnp.bf...  37.5 us
    pallas_call x1, Pallas kernels, last_sums(): pl.pallas_call(functools.partial(sums_kernel, shape['blk'], axes, orders)...  35.7 us
    pallas_call x1, Pallas kernels, spread_and_weights(): pl.pallas_call(functools.partial(weights_kernel, shards), out_shape=(jax....  26.5 us
    pallas_call x1, Pallas kernels, move_heads(): pl.pallas_call(functools.partial(kernel, shards), out_shape=jax.ShapeDtyp...  18.1 us
    pallas_call x1, Pallas kernels, feed_forward(): pl.pallas_call(feed_kernel, out_shape=(low(width), jax.ShapeDtypeStruct((...  13.1 us
  transfers between devices with their start and end apart: 5, of which 0 were waited for; matrix products, arithmetic and copies ran while one was open for 2% of the time, Pallas kernels for 13%

profile of v2, /device:TPU:0, one launch (start us, length us, event | category | flops | bytes accessed | tf_op | source)
XLA Modules:
  0.0 367.3 jit_solution(14188053026980914989)
XLA Ops:
  0.6 0.7 add_convert_fusion
  1.4 0.7 slice_bitcast_fusion.1
  2.2 2.4 collective-permute-start
  4.6 1.3 collective-permute-start.1
  6.0 1.3 convert_bitcast_fusion.table
  7.3 0.9 slice.77
  8.2 1.3 broadcast_in_dim.66.score_ref
  9.5 1.3 broadcast_in_dim.67.gain_ref
  11.4 1.3 broadcast_in_dim.74.gain_ref
  13.0 0.6 pad_add_fusion.lab_ref
  13.7 6.1 %pool_and_project.1 = (f32[256,768]{1,0:T(8,128)}, bf16[256,768]{1,0:T(8,128)(2,1)}, f32[8,256]{1,0:T(8,128)}, f32[1,128]{1,0:T(1,128)}, bf16[4,384,128]{2,1,0:T(8,128)(2,1)}, /*index=5*/bf16[4,256,384]{2,1,0:T(8,128)(2,1)}) custom-call(bf16[512,768]{1,0:T(8,128)(2,1)} %bitcast.42, bf16[3,768]{1,0:T(4,128)(2,1)} %copy-done.3, bf16[3,768]{1,0:T(4,128)(2,1)} %copy-done.4, ...), custom_call_target="tpu_custom_call" | custom-call | tf_op jit(solution)/shard_map/pool_and_project/pallas_call | solution.py:1129
  19.8 59.4 %gather_keys.1 = (bf16[2,2,384,128]{3,2,1,0:T(8,128)(2,1)}, bf16[2,4096,384]{2,1,0:T(8,128)(2,1)}, s32[2,2,2,2,2,8,128]{6,5,4,3,2,1,0:T(8,128)}) custom-call(bf16[4,384,128]{2,1,0:T(8,128)(2,1)} %get-tuple-element.74.q_ref, bf16[4,256,384]{2,1,0:T(8,128)(2,1)} %get-tuple-element.75.kv_ref, s32[8,128]{1,0:T(8,128)} %pad.18.label_ref), custom_call_target="tpu_custom_call" | custom-call | tf_op jit(solution)/shard_map/gather_keys/pallas_call | solution.py:271
  79.2 0.9 slice.90
  82.0 0.7 stack.44.bounds
  82.7 37.5 %attention.1 = (bf16[2,2,384,128]{3,2,1,0:T(8,128)(2,1)}, f32[2,2,384,128]{3,2,1,0:T(8,128)}, f32[2,2,3,1,256]{4,3,2,1,0:T(1,128)}, bf16[3,4,512,256]{3,2,1,0:T(8,128)(2,1)}) custom-call(s32[2,2,6]{2,1,0:T(2,128)} %stack.44.bounds, f32[3,32]{1,0:T(4,128)} %convert_bitcast_fusion.table, bf16[2,2,384,128]{3,2,1,0:T(8,128)(2,1)} %get-tuple-element.77.q_ref, ...), custom_call_target="tpu_custom_call" | custom-call | tf_op jit(solution)/shard_map/attention/pallas_call | solution.py:820
  120.2 18.1 %move_heads_4.1.o_ref = bf16[4,384,128]{2,1,0:T(8,128)(2,1)} custom-call(bf16[2,2,384,128]{3,2,1,0:T(8,128)(2,1)} %get-tuple-element.79.o_ref), custom_call_target="tpu_custom_call" | custom-call | tf_op jit(solution)/shard_map/move_heads_4/pallas_call | solution.py:169
  138.3 13.1 %feed_forward.1 = (bf16[256,768]{1,0:T(8,128)(2,1)}, f32[256,768]{1,0:T(8,128)}, bf16[4,384,128]{2,1,0:T(8,128)(2,1)}, f32[1,768]{1,0:T(1,128)}, bf16[256,768]{1...) custom-call(bf16[4,384,128]{2,1,0:T(8,128)(2,1)} %move_heads_4.1.o_r, ...), custom_call_target="tpu_custom_call" | custom-call | tf_op jit(solution)/shard_map/feed_forward/pallas_call | solution.py:1206
  151.4 26.5 %spread_and_weights.1 = (bf16[2,2,384,128]{3,2,1,0:T(8,128)(2,1)}, bf16[8,48,1024]{2,1,0:T(8,128)(2,1)}, bf16[8,48,1024]{2,1,0:T(8,128)(2,1)}, bf16[8,48,1024]{2...) custom-call(bf16[4,384,128]{2,1,0:T(8,128)(2,1)} %get-tuple-element.82.da, ...), custom_call_target="tpu_custom_call" | custom-call | tf_op jit(solution)/shard_map/spread_and_weights/pallas_call | solution.py:465
  177.9 0.6 collective-permute-start.4
  178.8 1.4 collective-permute-start.3
  180.2 47.3 %attention_back.1 = (bf16[2,2,384,128]{3,2,1,0:T(8,128)(2,1)}, bf16[2,4096,384]{2,1,0:T(8,128)(2,1)}, f32[3,32,256]{2,1,0:T(8,128)}) custom-call(s32[2,2,6]{2,1,0:T(2,128)} %stack.44.bounds, f32[3,32]{1,0:T(4,128)} %convert_bitcast_fusion.table, bf16[2,2,384,128]{3,2,1,0:T(8,128)(2,1)} %get-tuple-element.77.q_ref, ...), custom_call_target="tpu_custom_call" | custom-call | tf_op jit(solution)/shard_map/attention_back/pallas_call | solution.py:980
  227.5 0.9 copy-done.1
  229.1 78.6 %reduce_keys.1 = (bf16[4,384,128]{2,1,0:T(8,128)(2,1)}, bf16[4,256,384]{2,1,0:T(8,128)(2,1)}, f32[48,1024]{1,0:T(8,128)}, f32[48,1024]{1,0:T(8,128)}, f32[96,768]{1,0:T(8,128)}) custom-call(bf16[2,2,384,128]{3,2,1,0:T(8,128)(2,1)} %get-tuple-element.93.refs_0_, bf16[2,4,2,2,256,384]{5,4,3,2,1,0:T(8,128)(2,1)} %bitcast.38, ...), custom_call_target="tpu_custom_call" | custom-call | tf_op jit(solution)/shard_map/reduce_keys/pallas_call | solution.py:602
  307.7 10.7 %last_part.1 = (bf16[512,768]{1,0:T(8,128)(2,1)}, f32[2,16,768]{2,1,0:T(8,128)}, f32[2,8,768]{2,1,0:T(8,128)}, f32[32,128]{1,0:T(8,128)}, bf16[32,80,768]{2,1,0:T(8,128)(2,1)}) custom-call(bf16[4,384,128]{2,1,0:T(8,128)(2,1)} %get-tuple-element.101.dq_ref, bf16[4,256,384]{2,1,0:T(8,128)(2,1)} %get-tuple-element.102.dkv_ref, ...), custom_call_target="tpu_custom_call" | custom-call | tf_op jit(solution)/shard_map/last_part/pallas_call | solution.py:1318
  318.4 4.1 %fusion.11 = (bf16[32,80,256]{2,1,0:T(8,128)(2,1)}, bf16[32,80,256]{2,1,0:T(8,128)(2,1)}, bf16[32,80,256]{2,1,0:T(8,128)(2,1)}) fusion(bf16[32,80,768]{2,1,0:T(8,128)(2,1)} %get-tuple-element.111), kind=kLoop, calls=%fused_computation.61 | loop fusion | bytes 7864320 | tf_op jit(solution)/shard_map/slice | solution.py:1492
  322.5 35.7 %last_sums.1 = (f32[80,256]{1,0:T(8,128)}, f32[80,256]{1,0:T(8,128)}, f32[80,256]{1,0:T(8,128)}, f32[32,128]{1,0:T(8,128)}, f32[2,8,768]{2,1,0:T(8,128)}) custom-call(bf16[2,2,2,2,2,80,256]{6,5,4,3,2,1,0:T(8,128)(2,1)} %bitcast.41, bf16[2,2,2,2,2,80,256]{6,5,4,3,2,1,0:T(8,128)(2,1)} %bitcast.40, bf16[2,2,2,2,2,80,256]{6,5,4,3,2,1,0:T(8,128)(2,1)} %bitcast.39, ...), custom_call_target="tpu_custom_call" | custom-call | tf_op jit(solution)/shard_map/last_sums/pallas_call | solution.py:658
  358.2 2.7 finish.1
  360.9 1.2 slice_bitcast_fusion.5
  362.1 1.3 slice_bitcast_fusion
  363.4 1.3 reduce
  364.7 1.3 reduce.1
  366.0 1.3 reduce.2
  (54 shorter events, 4.0 us)
Async XLA Ops:
  2.2 10.4 %collective-permute-start = (bf16[3,768]{1,0:T(4,128)(2,1)S(1)}, bf16[3,768]{1,0:T(4,128)(2,1)S(1)}, u32[]{:S(2)}, u32[]{:S(2)}) collective-permute-start(bf16[3,768]{1,0:T(4,128)(2,1)S(1)} %pad_maximum_fusion), channel_id=1, source_target_pairs={{0,1},{1,2},{2,3},{3,4},{4,5},{5,6},{6,7},{7,8},{8,9},{9,10},{10,1... | collective-permute-start | bytes 13832 | tf_op jit(solution)/shard_map/ppermute | solution.py:1387
  4.6 8.0 %collective-permute-start.1 = (bf16[3,768]{1,0:T(4,128)(2,1)S(1)}, bf16[3,768]{1,0:T(4,128)(2,1)S(1)}, u32[]{:S(2)}, u32[]{:S(2)}) collective-permute-start(bf16[3,768]{1,0:T(4,128)(2,1)S(1)} %pad_maximum_fusion.1), channel_id=1, source_target_pairs={{1,0},{2,1},{3,2},{4,3},{5,4},{6,5},{7,6},{8,7},{9,8},{10,9},{11,1... | collective-permute-start | bytes 13832 | tf_op jit(solution)/shard_map/ppermute | solution.py:1387
  12.6 1.1 copy-start.3
  12.6 1.1 copy-start.4
  177.9 49.6 %collective-permute-start.4 = (bf16[8,96,768]{2,1,0:T(8,128)(2,1)}, bf16[8,96,768]{2,1,0:T(8,128)(2,1)S(1)}, u32[]{:S(2)}, u32[]{:S(2)}) collective-permute-start(bf16[8,96,768]{2,1,0:T(8,128)(2,1)} %get-tuple-element.100), channel_id=1, source_target_pairs={{0,4},{1,5},{2,6},{3,7},{4,0},{5,1},{6,2},{7,3},{8,12},{9,13},{10,... | collective-permute-start | bytes 3538952 | tf_op jit(solution)/shard_map/ppermute | solution.py:1473
  178.6 48.9 %collective-permute-start.2 = (bf16[8,48,1024]{2,1,0:T(8,128)(2,1)}, bf16[8,48,1024]{2,1,0:T(8,128)(2,1)S(1)}, u32[]{:S(2)}, u32[]{:S(2)}) collective-permute-start(bf16[8,48,1024]{2,1,0:T(8,128)(2,1)} %get-tuple-element.96), channel_id=1, source_target_pairs={{0,16},{16,0},{1,17},{17,1},{2,18},{18,2},{3,19},{19,3},{4,20},{20... | collective-permute-start | bytes 2359304 | tf_op jit(solution)/shard_map/ppermute | solution.py:1473
  178.8 48.7 %collective-permute-start.3 = (bf16[8,48,1024]{2,1,0:T(8,128)(2,1)}, bf16[8,48,1024]{2,1,0:T(8,128)(2,1)S(1)}, u32[]{:S(2)}, u32[]{:S(2)}) collective-permute-start(bf16[8,48,1024]{2,1,0:T(8,128)(2,1)} %get-tuple-element.98), channel_id=1, source_target_pairs={{0,2},{1,3},{2,0},{3,1},{4,6},{5,7},{6,4},{7,5},{8,10},{9,11},{10,... | collective-permute-start | bytes 2359304 | tf_op jit(solution)/shard_map/ppermute | solution.py:1473
  227.5 0.9 copy-start.1
  227.5 1.1 copy-start.2
  227.5 1.6 copy-start

commit v3 on v2

--- a/solution.py
+++ b/solution.py
@@ -64,11 +64,19 @@
         return self.at(self.row, (self.group + step) % GROUPS, self.rest)
 
 
-def greet(targets):
+def hail(targets):
     barrier = pltpu.get_barrier_semaphore()
     for target in targets:
         pl.semaphore_signal(barrier, inc=1, device_id=target, device_id_type=MESH_ID)
-    pl.semaphore_wait(barrier, len(targets))
+    return len(targets)
+
+
+def await_all(count):
+    pl.semaphore_wait(pltpu.get_barrier_semaphore(), count)
+
+
+def greet(targets):
+    await_all(hail(targets))
 
 
 def remote(src, dst, send_sem, recv_sem, target):
@@ -225,12 +233,13 @@
         copy = remote(kv_ref.at[(place.group + step) % GROUPS], held(0, 0, 0), z_send.at[step], sem_of((GROUPS - step) % GROUPS, 0, 0), place.other_group(step))
         copy.start()
         waits.append(copy)
-    spread_heads(place, q_ref, qo_ref, q_send, q_recv)
 
     used = 0
     events = sorted(((dz, off) for dz in range(GROUPS) for off in range(count)), key=lambda e: (bin(e[1]).count("1"), (0, 1, 3, 2).index(e[0])))
     core_target = place.other_rest(core)
-    for dz, off in events:
+    for step, (dz, off) in enumerate(events):
+        if step == GROUPS:
+            spread_heads(place, q_ref, qo_ref, q_send, q_recv)
         here = held(dz, off, 0)
         if dz == 0 and off == 0:
             src = kv_ref.at[place.group]
@@ -338,7 +347,7 @@
     def absorb(self, k):
         kept, src, now = self.stage(k)
         buf = self.bufs[k]
-        if k == len(self.order) - 1:
+        if k == len(self.order) - 1 and self.out is not None:
             mine = src[self.own(now)].astype(jnp.float32)
             self.out[...] = buf[...].astype(jnp.float32) + mine
         else:
@@ -365,14 +374,12 @@
             self.bufs[1, k] = total
 
 
-def run_streams(streams, first=0):
-    for stage in range(max(len(s.order) for s in streams)):
-        for s in streams:
-            if stage < len(s.order):
-                s.copy(stage).wait()
-                s.absorb(stage)
-                if stage < len(s.order) - 1:
-                    s.copy(stage + 1).start()
+def advance(stream, stage):
+    if stage < len(stream.order):
+        stream.copy(stage).wait()
+        stream.absorb(stage)
+        if stage < len(stream.order) - 1:
+            stream.copy(stage + 1).start()
 
 
 def bit_axes(shape):
@@ -383,9 +390,9 @@
     return [pltpu.VMEM((2,) * (lead - 1 - k) + (rows, cols), jnp.bfloat16) for k in range(len(order))]
 
 
-def weights_kernel(shards, da_ref, n2_ref, att_ref, act_ref, dg_ref, du_ref, ct_ref, db_ref,
-                   do_ref, keep_a, send_a, keep_b, send_b, keep_c, send_c,
-                   q_send, q_recv, core_send, core_recv, gate, up, down, out, wide_out, slim_out, wide_in, slim_in):
+def weights_kernel(shards, da_ref, n2_ref, act_ref, dg_ref, du_ref, ct_ref,
+                   do_ref, left_ref, right_ref, slim_ref,
+                   q_send, q_recv, core_send, core_recv, gate, up, down, wide_out, slim_out, wide_in, slim_in):
     place = Place(shards)
     core_target = place.other_rest(1)
     greet(line_and_row(place) + [core_target])
@@ -407,9 +414,7 @@
         return jnp.concatenate([gate[rows, :], up[rows, :]], axis=0)
 
     def slim_rows(block):
-        rows, more = pl.ds(pl.multiple_of(block * per, 8), per), pl.ds(pl.multiple_of(block * per_ff, 8), per_ff)
-        empty = jnp.zeros((32 - per, out.shape[1]), jnp.float32)
-        return jnp.concatenate([out[rows, :], empty, down[more, :]], axis=0)
+        return down[pl.ds(pl.multiple_of(block * per_ff, 8), per_ff), :]
 
     def send_wide(m, _):
         wide_out[m] = wide_rows(2 * m + 1 - core).astype(jnp.bfloat16)
@@ -418,7 +423,6 @@
     lax.fori_loop(0, 16, send_wide, 0)
     wide_copy = remote(wide_out, wide_in, core_send.at[0], core_recv.at[0], core_target)
     wide_copy.start()
-    out[...] = mxu(att_ref[...].T, db_ref[...])
     for j in range(down.shape[0] // step):
         rows = slice(j * step, j * step + step)
         down[rows, :] = mxu(act_ref[:, rows].T, ct_ref[...])
@@ -431,52 +435,46 @@
     slim_copy = remote(slim_out, slim_in, core_send.at[1], core_recv.at[1], core_target)
     slim_copy.start()
 
-    def number(j, bit_at, value):
-        return j // bit_at * (2 * bit_at) + value * bit_at + j % bit_at
-
     wide_copy.wait()
-    for (keep, send), bit_at, mine, cols in (
-        ((keep_a, send_a), 8, place.row, slice(0, half)),
-        ((keep_b, send_b), 1, bit(place.rest, 2), slice(half, 2 * half)),
-    ):
-        for ref, value in ((send, 1 - mine), (keep, mine)):
-            def one(j, _):
-                m = number(j, bit_at, value)
-                ref[j] = (wide_rows(2 * m + core)[:, cols] + wide_in[m, :, cols].astype(jnp.float32)).astype(jnp.bfloat16)
-                return 0
-            lax.fori_loop(0, 8, one, 0)
+
+    def sum_wide(m, _):
+        total = wide_rows(2 * m + core) + wide_in[m].astype(jnp.float32)
+        left_ref[m] = total[:, :half].astype(jnp.bfloat16)
+        right_ref[m] = total[:, half:].astype(jnp.bfloat16)
+        return 0
+
+    lax.fori_loop(0, 16, sum_wide, 0)
     slim_copy.wait()
-    mine = bit(place.group, 1)
-    for ref, value in ((send_c, 1 - mine), (keep_c, mine)):
-        def one(j, _):
-            m = number(j, 2, value)
-            ref[j] = (slim_rows(2 * m + core) + slim_in[m].astype(jnp.float32)).astype(jnp.bfloat16)
-            return 0
-        lax.fori_loop(0, 8, one, 0)
+
+    def sum_slim(m, _):
+        slim_ref[m] = (slim_rows(2 * m + core) + slim_in[m].astype(jnp.float32)).astype(jnp.bfloat16)
+        return 0
+
+    lax.fori_loop(0, 16, sum_slim, 0)
     spread_heads_wait(place, da_ref, do_ref, q_send, q_recv)
 
 
-def spread_and_weights(shards, da, n2, att, act, dg, du, ct, db):
+def spread_and_weights(shards, da, n2, act, dg, du, ct):
     width, ff = n2.shape[1], act.shape[1]
     per, per_ff = width // 32, ff // 32
     sem, low = pltpu.SemaphoreType.DMA, jnp.bfloat16
-    wide, slim = (2 * per, ff), (32 + per_ff, width)
-    halves = [jax.ShapeDtypeStruct((8, 2 * per, ff // 2), low)] * 4 + [jax.ShapeDtypeStruct((8,) + slim, low)] * 2
+    wide, slim = (2 * per, ff), (per_ff, width)
+    sums = [jax.ShapeDtypeStruct((16, 2 * per, ff // 2), low)] * 2 + [jax.ShapeDtypeStruct((16,) + slim, low)]
     return pl.pallas_call(
         functools.partial(weights_kernel, shards),
-        out_shape=(jax.ShapeDtypeStruct((2, 2) + da.shape[1:], da.dtype),) + tuple(halves),
-        in_specs=[VMEM_SPEC] * 8,
-        out_specs=(VMEM_SPEC,) * 7,
+        out_shape=(jax.ShapeDtypeStruct((2, 2) + da.shape[1:], da.dtype),) + tuple(sums),
+        in_specs=[VMEM_SPEC] * 6,
+        out_specs=(VMEM_SPEC,) * 4,
         scratch_shapes=[
             sem((4,)), sem((4,)), sem((2,)), sem((2,)),
             pltpu.VMEM((width, ff), jnp.float32), pltpu.VMEM((width, ff), jnp.float32),
-            pltpu.VMEM((ff, width), jnp.float32), pltpu.VMEM((width, width), jnp.float32),
+            pltpu.VMEM((ff, width), jnp.float32),
             pltpu.VMEM((16,) + wide, low), pltpu.VMEM((16,) + slim, low),
             pltpu.VMEM((16,) + wide, low), pltpu.VMEM((16,) + slim, low),
         ],
         compiler_params=pltpu.CompilerParams(collective_id=5, has_side_effects=True, vmem_limit_bytes=VMEM_BYTES),
         name="spread_and_weights",
-    )(da, n2, att, act, dg, du, ct, db)
+    )(da, n2, act, dg, du, ct)
 
 
 def reduce_kernel(shards, axes, orders, *refs):
@@ -614,59 +612,6 @@
     )(q_packed, kv_sums.reshape((2, GROUPS) + (2,) * len(rest_bits) + (tokens, width)), *flat)
 
 
-def sums_kernel(shards, axes, orders, *refs):
-    count = len(orders) - 1
-    ins, small_ref, spill_ref = refs[:count], refs[count], refs[count + 1]
-    outs, small_out, spill_out = refs[count + 2 : 2 * count + 2], refs[2 * count + 2], refs[2 * count + 3]
-    w_send, w_recv, s_send, s_recv = refs[2 * count + 4 : 2 * count + 8]
-    bufs = refs[2 * count + 8 :]
-    at = {"dp": lax.axis_index("dp"), "blk": lax.axis_index("blk")}
-    whole = Whole(axes, at, orders[-1], small_ref, bufs[-1], small_out, w_send.at[count], w_recv.at[count])
-    streams, used = [], 0
-    for s in range(count):
-        more = bufs[used : used + len(orders[s])]
-        used += len(orders[s])
-        streams.append(Stream(axes, at, sorted(orders[s]), orders[s], ins[s], more, outs[s], w_send.at[s], w_recv.at[s]))
-    left = (at["dp"], (at["blk"] + shards - 1) % shards)
-    right = (at["dp"], (at["blk"] + 1) % shards)
-    greet([whole.stream.target(p) for p in range(len(axes))] + [left, right])
-    spills = [
-        remote(spill_ref.at[0], spill_out.at[1], s_send.at[0], s_recv.at[1], left),
-        remote(spill_ref.at[1], spill_out.at[0], s_send.at[1], s_recv.at[0], right),
-    ]
-    streams.append(whole)
-    for stream in streams:
-        stream.copy(0).start()
-    for copy in spills:
-        copy.start()
-    run_streams(streams)
-    for copy in spills:
-        copy.wait()
-
-
-def last_sums(shape, blocks, orders, small, spill):
-    axes = bit_axes(shape)
-    ndim = len(axes)
-    sem = pltpu.SemaphoreType.DMA
-    scratch, sums = [], []
-    for block, order in zip(blocks, orders):
-        rows, cols = block.shape[-2:]
-        scratch += stream_scratch(ndim, order, rows, cols)
-        sums.append(jax.ShapeDtypeStruct((rows, cols), jnp.float32))
-    count = len(blocks)
-    scratch.append(pltpu.VMEM((2, ndim) + small.shape, small.dtype))
-    found = pl.pallas_call(
-        functools.partial(sums_kernel, shape["blk"], axes, orders),
-        out_shape=tuple(sums) + (jax.ShapeDtypeStruct(small.shape, small.dtype), jax.ShapeDtypeStruct(spill.shape, spill.dtype)),
-        in_specs=[VMEM_SPEC] * (count + 2),
-        out_specs=(VMEM_SPEC,) * (count + 2),
-        scratch_shapes=[sem((count + 1, ndim)), sem((count + 1, ndim)), sem((2,)), sem((2,))] + scratch,
-        compiler_params=pltpu.CompilerParams(collective_id=3, has_side_effects=True, vmem_limit_bytes=VMEM_BYTES),
-        name="last_sums",
-    )(*[b.reshape((2,) * ndim + b.shape[-2:]) for b in blocks], small, spill)
-    return found[:count], found[count], found[count + 1]
-
-
 TQ = 256
 TK = 512
 NEAR_ROWS = 448
@@ -838,27 +783,68 @@
     )(bounds, table, q, kv, se)
 
 
-def bwd_kernel(bounds, table, q_ref, do_ref, keep_ref, kv_ref, bias_ref, se_ref, lse_ref,
-               dq_ref, dkv_ref, tab_ref, kt, dqt, dkv, grid, side, qp, dp_ref, delta):
+def prepare(q, do, keep, q_out, do_out, delta):
+    for h, tile in enumerate(spread_lanes(q, False)):
+        q_out[h] = tile
+    for h, tile in enumerate(spread_lanes(do, True)):
+        do_out[h] = tile
+    prod = (do.astype(jnp.float32) * keep).T
+    top, low = prod[:, 0:TQ], prod[:, TQ:]
+    delta[0] = jnp.sum(top[0:64], axis=0, keepdims=True)
+    delta[1] = jnp.sum(top[64:128], axis=0, keepdims=True)
+    delta[2] = jnp.concatenate(
+        [jnp.sum(low[0:64], axis=0, keepdims=True), jnp.sum(low[64:128], axis=0, keepdims=True)], axis=1
+    )
+
+
+def near_start(parity):
+    return 416 - TQ * parity
+
+
+def far_sums(grid, h, first, end):
+    def one(step, total):
+        rows = grid[h, pl.ds(pl.multiple_of(step * 32, 32), 32)]
+        return total + jnp.sum(rows.reshape(4, 8, TQ), axis=0)
+    total = lax.fori_loop(first // 32, end // 32, one, jnp.zeros((8, TQ), jnp.float32))
+    return jnp.sum(total, axis=0, keepdims=True)
+
+
+def bucket_sums(parity, near, side, tab_ref, tab8):
+    heads = near.shape[0]
+    tab8[...] = jnp.zeros_like(tab8)
+
+    def inner(step, _):
+        start = pl.multiple_of(step * 32, 32)
+        which = near_buckets(near_start(parity) + start, 32, parity)
+        for b in range(BUCKETS):
+            here = which == b
+            for h in range(heads):
+                rows = jnp.where(here, near[h, pl.ds(start, 32)], 0.0)
+                tab8[h, b] += jnp.sum(rows.reshape(4, 8, TQ), axis=0)
+        return 0
+
+    lax.fori_loop(0, NEAR_ROWS // 32, inner, 0)
+    for h in range(heads):
+        tab_ref[h] = jnp.sum(tab8[h], axis=1)
+        tab_ref[h, 15:16] += side[h, 0:1]
+        tab_ref[h, 31:32] += side[h, 1:2]
+
+
+def bwd_kernel(alone, bounds, table, q_ref, do_ref, keep_ref, kv_ref, bias_ref, se_ref, lse_ref,
+               dq_ref, dkv_ref, near_ref, side, *rest):
+    tab_ref, tab8, rest = (None, None, rest) if alone else (rest[0], rest[-1], rest[1:-1])
+    kt, dqt, dkv, grid, qp, dp_ref, delta = rest
     heads = lse_ref.shape[2]
     n = kv_ref.shape[1]
     grid[...] = jnp.zeros_like(grid)
     side[...] = jnp.zeros_like(side)
-    for r in range(2):
+    base = 1 - bounds[0, 0, 6] if alone else 0
+    for at in range(1 if alone else 2):
         for i in range(2):
-            for h, tile in enumerate(spread_lanes(q_ref[r, i], False)):
-                qp[r, i, h] = tile
-            for h, tile in enumerate(spread_lanes(do_ref[r, i], True)):
-                dp_ref[r, i, h] = tile
-            prod = (do_ref[r, i].astype(jnp.float32) * keep_ref[r, i]).T
-            top, low = prod[:, 0:TQ], prod[:, TQ:]
-            delta[r, i, 0] = jnp.sum(top[0:64], axis=0, keepdims=True)
-            delta[r, i, 1] = jnp.sum(top[64:128], axis=0, keepdims=True)
-            delta[r, i, 2] = jnp.concatenate(
-                [jnp.sum(low[0:64], axis=0, keepdims=True), jnp.sum(low[64:128], axis=0, keepdims=True)], axis=1
-            )
-
-    def row_body(r, _):
+            prepare(q_ref[base + at, i], do_ref[base + at, i], keep_ref[base + at, i], qp.at[at, i], dp_ref.at[at, i], delta.at[at, i])
+
+    def row_body(at, _):
+        r = base + at
         lo_all = jnp.minimum(bounds[r, 0, 0], bounds[r, 1, 0])
         hi_all = jnp.maximum(bounds[r, 0, 1], bounds[r, 1, 1])
 
@@ -890,20 +876,20 @@
                 def finish(h, p, ds, where):
                     ds_low = ds.astype(jnp.bfloat16)
                     two = jnp.concatenate([ds_low, p.astype(jnp.bfloat16)], axis=1)
-                    both = jnp.concatenate([qp[r, i, h], dp_ref[r, i, h]], axis=0)
+                    both = jnp.concatenate([qp[at, i, h], dp_ref[at, i, h]], axis=0)
                     dkv[h, pl.ds(k0, TK), :] += mxu(two, both)
                     dqt[h, where] += mxu(kt[h, :, pl.ds(k0, TK)], ds_low)
 
                 def products(h):
                     tile = kv_ref[r, pl.ds(k0, TK), h * 128 : h * 128 + 128]
-                    return mxu(tile, qp[r, i, h], NT), mxu(tile, dp_ref[r, i, h], NT)
+                    return mxu(tile, qp[at, i, h], NT), mxu(tile, dp_ref[at, i, h], NT)
 
                 @pl.when(plain)
                 def _():
                     for h in range(heads):
                         s, d_probs = products(h)
                         p = jnp.exp(s - (lse_ref[r, i, h] - jnp.where(slot == 0, table[h, 15], table[h, 31])))
-                        finish(h, p, p * (d_probs - delta[r, i, h]), jnp.where(slot == 0, 0, 2))
+                        finish(h, p, p * (d_probs - delta[at, i, h]), jnp.where(slot == 0, 0, 2))
 
                 @pl.when(jnp.logical_not(plain))
                 def _():
@@ -912,8 +898,8 @@
                         s, d_probs = products(h)
                         s = s + bias_ref[h, slot].astype(jnp.float32)
                         p = jnp.where(ok, jnp.exp(jnp.where(ok, s, NEG) - lse_ref[r, i, h]), 0.0)
-                        ds = p * (d_probs - delta[r, i, h])
-                        grid[h, slot] += ds
+                        ds = p * (d_probs - delta[at, i, h])
+                        grid[h, pl.ds(pl.multiple_of(slot * TK, TK), TK)] += ds
                         finish(h, p, ds, 1)
 
                 return 0
@@ -924,7 +910,7 @@
                 parts.append((dqt[h, 0, 0:64] + dqt[h, 1, 0:64] + dqt[h, 2, 0:64]).T * 0.125)
                 side[h, 0:1] += dqt[h, 0, 64:65]
                 side[h, 1:2] += dqt[h, 2, 64:65]
-            dq_ref[r, i] = join_heads(parts).astype(jnp.bfloat16)
+            dq_ref[at, i] = join_heads(parts).astype(jnp.bfloat16)
             return 0
 
         lax.fori_loop(0, 2, q_body, 0)
@@ -932,73 +918,326 @@
         def put(t, _):
             k0 = pl.multiple_of(t * TK, TK)
             for h in range(heads):
-                dkv_ref[r, pl.ds(k0, TK), h * 128 : h * 128 + 128] = dkv[h, pl.ds(k0, TK), :].astype(jnp.bfloat16)
+                dkv_ref[at, pl.ds(k0, TK), h * 128 : h * 128 + 128] = dkv[h, pl.ds(k0, TK), :].astype(jnp.bfloat16)
             return 0
 
         lax.fori_loop(0, n // TK, put, 0)
         return 0
 
-    lax.fori_loop(0, 2, row_body, 0)
+    lax.fori_loop(0, 1 if alone else 2, row_body, 0)
 
     parity = bounds[0, 0, 5]
-    tab_ref[...] = jnp.zeros_like(tab_ref)
+    first = TK + near_start(parity)
     for h in range(heads):
-        tab_ref[h, 15:16] = side[h, 0:1] + jnp.sum(grid[h, 0], axis=0, keepdims=True)
-        tab_ref[h, 31:32] = side[h, 1:2] + jnp.sum(grid[h, 3], axis=0, keepdims=True)
-
-    first = 13 - 8 * parity
-    count = NEAR_ROWS // 32
-
-    def block(h, step):
-        tile = step // (TK // 32)
-        start = pl.multiple_of((step % (TK // 32)) * 32, 32)
-        return grid[h, tile + 1, pl.ds(start, 32)]
-
-    def outer(bucket):
-        def one(step, _):
-            for h in range(heads):
-                tab_ref[h, bucket : bucket + 1] += jnp.sum(block(h, step), axis=0, keepdims=True)
-            return 0
-        return one
-
-    lax.fori_loop(0, first, outer(15), 0)
-    lax.fori_loop(first + count, 2 * TK // 32, outer(31), 0)
-
-    def inner(step, _):
-        which = near_buckets(step * 32, 32, parity)
-        for b in range(BUCKETS):
-            here = which == b
-            for h in range(heads):
-                tab_ref[h, b : b + 1] += jnp.sum(jnp.where(here, block(h, step), 0.0), axis=0, keepdims=True)
-        return 0
-
-    lax.fori_loop(first, first + count, inner, 0)
-
-
-def attention_back(bounds, table, q, do, keep, kv, bias, se, lse):
+        near_ref[h] = grid[h, pl.ds(pl.multiple_of(first, 32), NEAR_ROWS)]
+        side[h, 0:1] += far_sums(grid, h, 0, first)
+        side[h, 1:2] += far_sums(grid, h, first + NEAR_ROWS, 4 * TK)
+    if not alone:
+        bucket_sums(parity, near_ref, side, tab_ref, tab8)
+
+
+def attention_back(alone, bounds, table, q, do, keep, kv, bias, se, lse):
     heads, n = kv.shape[2] // 128, kv.shape[1]
+    count = 1 if alone else 2
+    table_out = [] if alone else [jax.ShapeDtypeStruct((heads, BUCKETS, TQ), jnp.float32)]
     return pl.pallas_call(
-        bwd_kernel,
+        functools.partial(bwd_kernel, alone),
         out_shape=(
-            jax.ShapeDtypeStruct(q.shape, jnp.bfloat16),
-            jax.ShapeDtypeStruct(kv.shape, jnp.bfloat16),
-            jax.ShapeDtypeStruct((heads, BUCKETS, TQ), jnp.float32),
-        ),
+            jax.ShapeDtypeStruct((count,) + q.shape[1:], jnp.bfloat16),
+            jax.ShapeDtypeStruct((count,) + kv.shape[1:], jnp.bfloat16),
+            jax.ShapeDtypeStruct((heads, NEAR_ROWS, TQ), jnp.float32),
+            jax.ShapeDtypeStruct((heads, 2, TQ), jnp.float32),
+        ) + tuple(table_out),
         in_specs=[SMEM_SPEC] * 2 + [VMEM_SPEC] * 7,
-        out_specs=(VMEM_SPEC,) * 3,
+        out_specs=(VMEM_SPEC,) * (4 + len(table_out)),
         scratch_shapes=[
             pltpu.VMEM((heads, 80, n), jnp.bfloat16),
             pltpu.VMEM((heads, 3, 80, TQ), jnp.float32),
             pltpu.VMEM((heads, n, 128), jnp.float32),
-            pltpu.VMEM((heads, 4, TK, TQ), jnp.float32),
-            pltpu.VMEM((heads, 2, TQ), jnp.float32),
-            pltpu.VMEM((2, 2, heads, TQ, 128), jnp.bfloat16),
-            pltpu.VMEM((2, 2, heads, TQ, 128), jnp.bfloat16),
-            pltpu.VMEM((2, 2, heads, 1, TQ), jnp.float32),
-        ],
+            pltpu.VMEM((heads, 4 * TK, TQ), jnp.float32),
+            pltpu.VMEM((count, 2, heads, TQ, 128), jnp.bfloat16),
+            pltpu.VMEM((count, 2, heads, TQ, 128), jnp.bfloat16),
+            pltpu.VMEM((count, 2, heads, 1, TQ), jnp.float32),
+        ] + [pltpu.VMEM((heads, BUCKETS, 8, TQ), jnp.float32) for _ in table_out],
         compiler_params=pltpu.CompilerParams(vmem_limit_bytes=VMEM_BYTES),
         name="attention_back",
     )(bounds, table, q, do, keep, kv, bias, se, lse)
+
+
+def dense_kernel(shards, axes, orders, bounds, table, q_ref, do_ref, keep_ref, kv_ref, bias_ref, lse_ref, dqs_ref, dkvs_ref, nears_ref, sides_ref, *refs):
+    count = len(orders)
+    weights, refs = refs[:count], refs[count:]
+    dq_out, kvo_ref, tab_ref, refs = refs[0], refs[1], refs[2], refs[3:]
+    more, refs = refs[:count], refs[count:]
+    (kt, dqt, acc, grid, side, tab8, qp, dp_ref, delta, held, core_in, s_in, s_sum, x_out, x_in, y_out, y_in, kept, z_out, dq_rows,
+     core_send, core_recv, x_send, x_recv, y_send, y_recv, z_send, z_recv, s_send, s_recv, q_send, q_recv, w_send, w_recv) = refs
+    place = Place(shards)
+    heads = lse_ref.shape[2]
+    tokens = TQ
+    across, core_to, row_to = place.other_rest(2), place.other_rest(1), place.other_row()
+    y, core = bit(place.rest, 2), place.rest % 2
+    met = hail(line_and_row(place) + [across, core_to])
+    at = {"dp": place.dp, "blk": place.blk}
+    streams = [
+        Stream(axes, at, kept_bits, order, weights[s], [more[s]], None, w_send.at[s], w_recv.at[s])
+        for s, (kept_bits, order) in enumerate(orders)
+    ]
+    s_core = remote(dkvs_ref.at[:, :, 1 - core], s_in, s_send, s_recv, core_to)
+
+    dense = bounds[0, 0, 6]
+    mine_dense = dense == place.row
+    parity = core
+    for i in range(2):
+        prepare(q_ref[dense, i], do_ref[dense, i], keep_ref[dense, i], qp.at[i], dp_ref.at[i], delta.at[i])
+    dqt[...] = jnp.zeros_like(dqt)
+    grid[...] = jnp.zeros_like(grid)
+    await_all(met)
+    s_core.start()
+    for stream in streams:
+        stream.copy(0).start()
+
+    wide = lambda value: value.astype(jnp.float32)
+    slim = lambda value: value.astype(jnp.bfloat16)
+
+    def group_of(n):
+        return (place.group + 1 + n) % GROUPS
+
+    def core_copy(n, j):
+        return remote(held.at[n, j, 1 - core], core_in.at[n, j], core_send.at[n, j], core_recv.at[n, j], core_to)
+
+    def x_copy(n, j):
+        return remote(x_out.at[n, j], x_in.at[n, j], x_send.at[n, j], x_recv.at[n, j], row_to)
+
+    def y_copy(n, j):
+        return remote(y_out.at[n, j], y_in.at[n, j], y_send.at[n, j], y_recv.at[n, j], across)
+
+    def z_copy(n):
+        return remote(z_out.at[n], kvo_ref.at[place.group], z_send.at[n], z_recv.at[n], place.at(place.row, group_of(n), place.rest))
+
+    def over_cores(n, j):
+        core_copy(n, j).wait()
+        return wide(held[n, j, core]) + wide(core_in[n, j])
+
+    def send_x(n, j, one, two):
+        x_out[n, j] = slim(jnp.where(mine_dense, two, one))
+        x_copy(n, j).start()
+        return jnp.where(mine_dense, one, two)
+
+    def deliver(n, total):
+        if isinstance(n, int):
+            if n == GROUPS - 1:
+                kvo_ref[place.group] = slim(total)
+            else:
+                z_out[n] = slim(total)
+                z_copy(n).start()
+            return
+
+        z_out[n] = slim(total)
+
+        @pl.when(n < GROUPS - 1)
+        def _():
+            z_copy(n).start()
+
+        @pl.when(n == GROUPS - 1)
+        def _():
+            kvo_ref[place.group] = z_out[n]
+
+    def y_first_1(n):
+        y_out[n, 0] = slim(over_cores(n, 0))
+        y_out[n, 1] = s_sum[n, 0]
+        y_copy(n, 0).start()
+        y_copy(n, 1).start()
+
+    def y_first_3(n):
+        y_copy(n, 0).wait()
+        y_copy(n, 1).wait()
+        kept[n, 0] = send_x(n, 0, over_cores(n, 1) + wide(y_in[n, 0]), wide(s_sum[n, 1]) + wide(y_in[n, 1]))
+
+    def y_first_5(n):
+        x_copy(n, 0).wait()
+        deliver(n, kept[n, 0] + wide(x_in[n, 0]))
+
+    def x_first_1(n):
+        kept[n, 0] = send_x(n, 0, over_cores(n, 0), wide(s_sum[n, 0]))
+
+    def x_first_2(n):
+        kept[n, 1] = send_x(n, 1, over_cores(n, 1), wide(s_sum[n, 1]))
+
+    def x_first_3(n):
+        x_copy(n, 0).wait()
+        y_out[n, 0] = slim(kept[n, 0] + wide(x_in[n, 0]))
+        y_copy(n, 0).start()
+
+    def x_first_5(n):
+        x_copy(n, 1).wait()
+        y_copy(n, 0).wait()
+        deliver(n, kept[n, 1] + wide(x_in[n, 1]) + wide(y_in[n, 0]))
+
+    actions = ((1, 0, y_first_1), (1, 1, x_first_1), (2, 1, x_first_2), (6, 0, y_first_3), (5, 1, x_first_3))
+
+    def tile_body(m, _):
+        n, j = m // 2, m % 2
+        place_y = jnp.where(j == 0, 1 - y, y)
+        t = group_of(n) * 2 + place_y
+        k0 = pl.multiple_of(t * TK, TK)
+        acc[...] = jnp.zeros_like(acc)
+        for h in range(heads):
+            kt[h, 0:64] = kv_ref[dense, pl.ds(k0, TK), h * 128 : h * 128 + 128].T[0:64]
+            kt[h, 64:80] = jnp.ones((16, TK), jnp.bfloat16)
+
+        def part(i, _):
+            first = ((2 * place.row + i) * place.rest_size + place.rest) * tokens
+            slot = jnp.clip(t - (first // TK - 1 + parity) + 1, 0, 3)
+            away = jnp.logical_or(slot == 0, slot == 3)
+
+            def finish(h, p, ds, where):
+                ds_low = ds.astype(jnp.bfloat16)
+                two = jnp.concatenate([ds_low, p.astype(jnp.bfloat16)], axis=1)
+                both = jnp.concatenate([qp[i, h], dp_ref[i, h]], axis=0)
+                acc[:, h * 128 : h * 128 + 128] += mxu(two, both)
+                dqt[i, h, where] += mxu(kt[h], ds_low)
+
+            def products(h):
+                tile = kv_ref[dense, pl.ds(k0, TK), h * 128 : h * 128 + 128]
+                return mxu(tile, qp[i, h], NT), mxu(tile, dp_ref[i, h], NT)
+
+            @pl.when(away)
+            def _():
+                for h in range(heads):
+                    s, d_probs = products(h)
+                    p = jnp.exp(s - (lse_ref[dense, i, h] - jnp.where(slot == 0, table[h, 15], table[h, 31])))
+                    finish(h, p, p * (d_probs - delta[i, h]), jnp.where(slot == 0, 0, 2))
+
+            @pl.when(jnp.logical_not(away))
+            def _():
+                for h in range(heads):
+                    s, d_probs = products(h)
+                    p = jnp.exp(s + bias_ref[h, slot].astype(jnp.float32) - lse_ref[dense, i, h])
+                    ds = p * (d_probs - delta[i, h])
+                    grid[h, pl.ds(pl.multiple_of((slot - 1) * TK, TK), TK)] += ds
+                    finish(h, p, ds, 1)
+
+            return 0
+
+        lax.fori_loop(0, 2, part, 0)
+        for half in range(2):
+            held[n, j, half] = acc[half * tokens : half * tokens + tokens].astype(jnp.bfloat16)
+        core_copy(n, j).start()
+
+        @pl.when(m == 0)
+        def _():
+            s_core.wait()
+
+            def one(step, _):
+                n_s, far = step // 2, step % 2
+                row = jnp.where(far == 0, 1 - y, y)
+                group = group_of(n_s)
+                s_sum[n_s, far] = slim(wide(dkvs_ref[group, row, core]) + wide(s_in[group, row]))
+                return 0
+
+            lax.fori_loop(0, 2 * GROUPS, one, 0)
+
+        for delay, odd, action in actions:
+            back = m - delay + 2 * GROUPS
+            n_then = back // 2 - GROUPS
+
+            @pl.when(jnp.logical_and(back % 2 == 0, jnp.logical_and(n_then >= 0, n_then % 2 == odd)))
+            def _():
+                action(n_then)
+
+        return 0
+
+    lax.fori_loop(0, 2 * GROUPS, tile_body, 0)
+    x_first_2(GROUPS - 1)
+
+    for i in range(2):
+        parts = []
+        for h in range(heads):
+            parts.append((dqt[i, h, 0, 0:64] + dqt[i, h, 1, 0:64] + dqt[i, h, 2, 0:64]).T * 0.125)
+        mine = join_heads(parts)
+        other = dqs_ref[0, i].astype(jnp.float32)
+        for r in range(2):
+            dq_rows[r, i] = jnp.where(dense == r, mine, other).astype(jnp.bfloat16)
+    return_heads(place, dq_rows, dq_out, q_send, q_recv)
+    y_first_5(0)
+    x_first_3(3)
+    y_first_3(2)
+    first = near_start(parity)
+    for h in range(heads):
+        side[h, 0:1] = dqt[0, h, 0, 64:65] + dqt[1, h, 0, 64:65] + sides_ref[h, 0:1] + far_sums(grid, h, 0, first)
+        side[h, 1:2] = dqt[0, h, 2, 64:65] + dqt[1, h, 2, 64:65] + sides_ref[h, 1:2] + far_sums(grid, h, first + NEAR_ROWS, 2 * TK)
+        rows = pl.ds(pl.multiple_of(first, 32), NEAR_ROWS)
+        grid[h, rows] += nears_ref[h]
+    bucket_sums(parity, NearRows(grid, first), side, tab_ref, tab8)
+    x_first_5(1)
+    for stream in streams:
+        stream.copy(0).wait()
+        stream.absorb(0)
+    y_first_5(2)
+    x_first_5(3)
+    for n in range(GROUPS - 1):
+        remote(z_out.at[n], kvo_ref.at[(place.group - 1 - n + GROUPS) % GROUPS], z_send.at[n], z_recv.at[n], row_to).wait()
+    return_heads_wait(place, dq_rows, dq_out, q_send, q_recv)
+
+
+class NearRows:
+    def __init__(self, grid, first):
+        self.grid, self.first, self.shape = grid, first, grid.shape
+
+    def __getitem__(self, index):
+        h, rows = index
+        return self.grid[h, pl.ds(pl.multiple_of(self.first + rows.start, 32), rows.size)]
+
+
+def dense_back(shape, bounds, table, q, do, keep, kv, bias, lse, dq_other, dkv_other, near_other, side_other, orders, blocks):
+    shards = shape["blk"]
+    heads, n, width = kv.shape[2] // 128, kv.shape[1], kv.shape[2]
+    tokens = n // shards
+    sem, low = pltpu.SemaphoreType.DMA, jnp.bfloat16
+    chunk = (tokens, width)
+    flat, outs = [], []
+    for (kept, _), block in zip(orders, blocks):
+        rows, cols = block.shape[-2:]
+        flat.append(block.reshape((2,) * len(kept) + (rows, cols)))
+        outs.append(jax.ShapeDtypeStruct((2,) * (len(kept) - 1) + (rows, cols), low))
+    count = len(orders)
+    pairs = lambda: sem((GROUPS, 2))
+    return pl.pallas_call(
+        functools.partial(dense_kernel, shards, bit_axes(shape), orders),
+        out_shape=(
+            jax.ShapeDtypeStruct((GROUPS,) + q.shape[2:], low),
+            jax.ShapeDtypeStruct((GROUPS,) + chunk, low),
+            jax.ShapeDtypeStruct((heads, BUCKETS, TQ), jnp.float32),
+        ) + tuple(outs),
+        in_specs=[SMEM_SPEC] * 2 + [VMEM_SPEC] * (10 + count),
+        out_specs=(VMEM_SPEC,) * (3 + count),
+        scratch_shapes=[
+            pltpu.VMEM((heads, 80, TK), low),
+            pltpu.VMEM((2, heads, 3, 80, TQ), jnp.float32),
+            pltpu.VMEM((TK, width), jnp.float32),
+            pltpu.VMEM((heads, 2 * TK, TQ), jnp.float32),
+            pltpu.VMEM((heads, 2, TQ), jnp.float32),
+            pltpu.VMEM((heads, BUCKETS, 8, TQ), jnp.float32),
+            pltpu.VMEM((2, heads, TQ, 128), low),
+            pltpu.VMEM((2, heads, TQ, 128), low),
+            pltpu.VMEM((2, heads, 1, TQ), jnp.float32),
+            pltpu.VMEM((GROUPS, 2, 2) + chunk, low),
+            pltpu.VMEM((GROUPS, 2) + chunk, low),
+            pltpu.VMEM((GROUPS, 2) + chunk, low),
+            pltpu.VMEM((GROUPS, 2) + chunk, low),
+            pltpu.VMEM((GROUPS, 2) + chunk, low),
+            pltpu.VMEM((GROUPS, 2) + chunk, low),
+            pltpu.VMEM((GROUPS, 2) + chunk, low),
+            pltpu.VMEM((GROUPS, 2) + chunk, low),
+            pltpu.VMEM((GROUPS, 2) + chunk, jnp.float32),
+            pltpu.VMEM((GROUPS,) + chunk, low),
+            pltpu.VMEM((2, 2) + q.shape[2:], low),
+            pairs(), pairs(), pairs(), pairs(), pairs(), pairs(), sem((GROUPS,)), sem((GROUPS,)),
+            sem, sem, sem((4,)), sem((4,)), sem((count, 1)), sem((count, 1)),
+        ],
+        compiler_params=pltpu.CompilerParams(collective_id=2, has_side_effects=True, vmem_limit_bytes=VMEM_BYTES),
+        name="dense_back",
+    )(bounds, table, q, do, keep, kv, bias, lse, dq_other, dkv_other.reshape((GROUPS, 2, 2) + chunk), near_other, side_other, *flat)
 
 
 TAPS = tuple(range(-3, 5))
@@ -1220,25 +1459,21 @@
     )(o_home, hidden, ct, gain, wo, wg, wu, wd)
 
 
-def last_kernel(with_blocks, dq_ref, dkv_ref, hidden_ref, dres_ref, n1_ref, x_ref, before_ref, after_ref, lab_ref, y_ref, score_ref,
-                gain_ref, wq_ref, wk_ref, wv_ref, dgain2_ref, share_ref, tab_ref,
-                gb_ref, edge_ref, spill_ref, small_ref, w_ref, xs, gbuf, *grads):
-    tokens, width = hidden_ref.shape
-    length = x_ref.shape[0]
-    lane = lax.broadcasted_iota(jnp.int32, (1, 128), 1)
-    low = lane < 64
-    dq = get_packed(dq_ref)
+def unpack_pairs(dkv_ref, width):
+    low = lax.broadcasted_iota(jnp.int32, (1, 128), 1) < 64
     dk_parts, dv_parts = [], []
     for j in range(width // 128):
         one, two = [dkv_ref[h // 3, :, h % 3 * 128 : h % 3 * 128 + 128] for h in (2 * j, 2 * j + 1)]
         dk_parts.append(jnp.where(low, one, turned(two)))
         dv_parts.append(jnp.where(low, turned(one), two))
-    dk, dv = jnp.concatenate(dk_parts, axis=1), jnp.concatenate(dv_parts, axis=1)
-    d_n1 = mxu(dq, wq_ref[...], NT) + mxu(dk, wk_ref[...], NT) + mxu(dv, wv_ref[...], NT)
-    d_rows, d_gain1 = norm_back(d_n1, hidden_ref[...], gain_ref[...].astype(jnp.float32))
-    d_hidden = dres_ref[...] + d_rows
-
-    load_bytes(x_ref, before_ref, after_ref, xs)
+    return jnp.concatenate(dk_parts, axis=1), jnp.concatenate(dv_parts, axis=1)
+
+
+def pool_back(d_hidden, x_refs, lab_ref, y_ref, score_ref, gb_ref, edge_ref, spill_ref, xs, gbuf):
+    x_ref = x_refs[0]
+    tokens, width = d_hidden.shape
+    length = x_ref.shape[0]
+    lane = lax.broadcasted_iota(jnp.int32, (1, 128), 1)
     met = jnp.zeros((tokens, 128), jnp.float32)
     for k in TAPS:
         met = jnp.where(lane == k + 3, jnp.sum(d_hidden * tap(xs, k, tokens), axis=-1, keepdims=True), met)
@@ -1270,10 +1505,13 @@
     edge_ref[1] = strips(gbuf, LEAD + length - 16, 16)
     spill_ref[0] = strips(gbuf, 0, LEAD)
     spill_ref[1] = strips(gbuf, LEAD + length, LEAD)
-
+    return d_score_vec
+
+
+def put_small(small_ref, vectors, tab_ref, share_ref):
     small_ref[...] = jnp.zeros_like(small_ref)
-    for row, vector in ((0, d_score_vec), (6, d_gain1), (12, dgain2_ref[...])):
-        for j in range(width // 128):
+    for row, vector in zip((0, 6, 12), vectors):
+        for j in range(6):
             small_ref[row + j : row + j + 1, :] = vector[:, j * 128 : j * 128 + 128]
     heads = tab_ref.shape[0]
     group = lax.axis_index("blk") // (lax.axis_size("blk") // GROUPS)
@@ -1285,51 +1523,126 @@
         small_ref[pl.ds(18 + group * heads + h, 1), 0:BUCKETS] = total[0:1]
     small_ref[30:31, :] = share_ref[...]
 
-    if with_blocks:
-        (whole,) = grads
+
+def last_kernel(shards, axes, kepts, orders, *refs):
+    with_weights = len(orders) > 1
+    (dq_ref, dkv_ref, hidden_ref, dres_ref, n1_ref, att_ref, db_ref, x_ref, before_ref, after_ref, lab_ref, y_ref, score_ref,
+     gain_ref, wq_ref, wk_ref, wv_ref, dgain2_ref, share_ref, tab_ref), refs = refs[:20], refs[20:]
+    firsts = len(orders) - 3 if with_weights else 0
+    halves, refs = refs[:firsts], refs[firsts:]
+    (gb_ref, edge_ref, spill_out, small_out, parts_ref), refs = refs[:5], refs[5:]
+    count = len(orders) - 1
+    outs, refs = refs[:count], refs[count:]
+    (w_send, w_recv, s_send, s_recv, xs, gbuf, spill_ref, small_ref, small_bufs), refs = refs[:9], refs[9:]
+    at = {"dp": lax.axis_index("dp"), "blk": lax.axis_index("blk")}
+    tokens, width = hidden_ref.shape
+    whole = Whole(axes, at, orders[-1], small_ref, small_bufs, small_out, w_send.at[count], w_recv.at[count])
+    left = (at["dp"], (at["blk"] + shards - 1) % shards)
+    right = (at["dp"], (at["blk"] + 1) % shards)
+    met = hail([whole.stream.target(p) for p in range(len(axes))] + [left, right])
+    streams, used = [], 0
+    if with_weights:
+        total, blocks, refs = refs[0], refs[1:3], refs[3:]
+        sources = list(halves) + list(blocks)
+        for s in range(count):
+            more = refs[used : used + len(orders[s])]
+            used += len(orders[s])
+            streams.append(Stream(axes, at, kepts[s], orders[s], sources[s], more, outs[s], w_send.at[s], w_recv.at[s]))
+    load_bytes(x_ref, before_ref, after_ref, xs)
+    dq = get_packed(dq_ref)
+    dk, dv = unpack_pairs(dkv_ref, width)
+    await_all(met)
+    for stream in streams[:firsts]:
+        stream.copy(0).start()
+    if with_weights:
         n1_t = n1_ref[...].T
         for j, part in enumerate((dq, dk, dv)):
-            whole[j] = mxu(n1_t, part)
-        per = width // w_ref.shape[0]
+            total[j] = mxu(n1_t, part)
+        total[3] = mxu(att_ref[...].T, db_ref[...])
+        devices = 1 << len(axes)
+        per = width // devices
+        half = width // 2
 
         def block(d, _):
             start = pl.multiple_of(d * per, 8)
-            parts = [whole[j, pl.ds(start, per), :] for j in range(3)]
-            parts.append(jnp.zeros((w_ref.shape[1] - 3 * per, width), jnp.float32))
-            w_ref[d] = jnp.concatenate(parts, axis=0).astype(jnp.bfloat16)
+            rows = jnp.concatenate([total[j, pl.ds(start, per), :] for j in range(4)], axis=0).astype(jnp.bfloat16)
+            place, rest = [], d
+            for _ in axes:
+                place.append(rest % 2)
+                rest = rest // 2
+            place = tuple(reversed(place))
+            blocks[0][place] = rows[:, :half]
+            blocks[1][place] = rows[:, half:]
             return 0
 
-        lax.fori_loop(0, w_ref.shape[0], block, 0)
+        lax.fori_loop(0, devices, block, 0)
+        for stream in streams[firsts:]:
+            stream.copy(0).start()
     else:
-        w_ref[0] = dq
-        w_ref[1] = dk
-        w_ref[2] = dv
-
-
-def last_part(devices, dq, dkv, hidden, dres, n1, x, before, after, labels, y, score, gain, wq, wk, wv, dgain2, share, tab):
+        parts_ref[0], parts_ref[1], parts_ref[2] = dq, dk, dv
+    d_n1 = mxu(dq, wq_ref[...], NT) + mxu(dk, wk_ref[...], NT) + mxu(dv, wv_ref[...], NT)
+    d_rows, d_gain1 = norm_back(d_n1, hidden_ref[...], gain_ref[...].astype(jnp.float32))
+    d_hidden = dres_ref[...] + d_rows
+    for stream in streams[firsts:] + streams[:firsts]:
+        advance(stream, 0)
+    d_score = pool_back(d_hidden, (x_ref, before_ref, after_ref), lab_ref, y_ref, score_ref, gb_ref, edge_ref, spill_ref, xs, gbuf)
+    put_small(small_ref, (d_score, d_gain1, dgain2_ref[...]), tab_ref, share_ref)
+    whole.copy(0).start()
+    spills = [
+        remote(spill_ref.at[0], spill_out.at[1], s_send.at[0], s_recv.at[1], left),
+        remote(spill_ref.at[1], spill_out.at[0], s_send.at[1], s_recv.at[0], right),
+    ]
+    for copy in spills:
+        copy.start()
+    for stage in range(1, len(axes)):
+        for stream in streams[firsts:]:
+            advance(stream, stage)
+        advance(whole, stage - 1)
+        for stream in streams[:firsts]:
+            advance(stream, stage)
+    advance(whole, len(axes) - 1)
+    for copy in spills:
+        copy.wait()
+    if with_weights:
+        parts_ref[...] = jnp.zeros_like(parts_ref)
+
+
+def last_part(shape, halves, kepts, orders, dq, dkv, hidden, dres, n1, att, db, x, before, after, labels, y, score, gain, wq, wk, wv, dgain2, share, tab):
     tokens, width = hidden.shape
     length = x.shape[0]
-    with_blocks = devices <= 32
-    full = jax.ShapeDtypeStruct
-    blocks = (devices, -(-3 * (width // devices) // 16) * 16, width) if with_blocks else (3, tokens, width)
-    scratch = [pltpu.VMEM((width // 128, length + 2 * LEAD, 128), jnp.float32)] * 2
-    if with_blocks:
-        scratch.append(pltpu.VMEM((3, width, width), jnp.float32))
+    axes = bit_axes(shape)
+    ndim = len(axes)
+    devices = 1 << ndim
+    full, sem, low = jax.ShapeDtypeStruct, pltpu.SemaphoreType.DMA, jnp.bfloat16
+    count = len(orders) - 1
+    strip = pltpu.VMEM((width // 128, length + 2 * LEAD, 128), jnp.float32)
+    scratch = [
+        sem((count + 1, ndim)), sem((count + 1, ndim)), sem((2,)), sem((2,)), strip, strip,
+        pltpu.VMEM((2, LEAD, width), jnp.float32), pltpu.VMEM((32, 128), jnp.float32), pltpu.VMEM((2, ndim, 32, 128), jnp.float32),
+    ]
+    sums = []
+    if count:
+        per = width // devices
+        own = (4 * per, width // 2)
+        scratch += [pltpu.VMEM((4, width, width), jnp.float32)] + [pltpu.VMEM((2,) * ndim + own, low)] * 2
+        for rows, cols, order in [h.shape[-2:] + (o,) for h, o in zip(halves, orders)] + [own + (o,) for o in orders[-3:-1]]:
+            scratch += stream_scratch(len(order), order, rows, cols)
+            sums.append(full((rows, cols), jnp.float32))
     return pl.pallas_call(
-        functools.partial(last_kernel, with_blocks),
+        functools.partial(last_kernel, shape["blk"], axes, kepts, orders),
         out_shape=(
-            full((length, width), jnp.bfloat16),
+            full((length, width), low),
             full((2, 16, width), jnp.float32),
             full((2, LEAD, width), jnp.float32),
             full((32, 128), jnp.float32),
-            full(blocks, jnp.bfloat16),
-        ),
-        in_specs=[VMEM_SPEC] * 18,
-        out_specs=(VMEM_SPEC,) * 5,
+            full((16, 128) if count else (3, tokens, width), low),
+        ) + tuple(sums),
+        in_specs=[VMEM_SPEC] * (20 + len(halves)),
+        out_specs=(VMEM_SPEC,) * (5 + count),
         scratch_shapes=scratch,
-        compiler_params=pltpu.CompilerParams(vmem_limit_bytes=VMEM_BYTES),
+        compiler_params=pltpu.CompilerParams(collective_id=3, has_side_effects=True, vmem_limit_bytes=VMEM_BYTES),
         name="last_part",
-    )(dq, dkv, hidden, dres, n1, x, before, after, labels, y, score, gain, wq, wk, wv, dgain2, share, tab)
+    )(dq, dkv, hidden, dres, n1, att, db, x, before, after, labels, y, score, gain, wq, wk, wv, dgain2, share, tab, *halves)
 
 
 def finish_kernel(shards, heads_all, gb_ref, edge_ref, spill_ref, small_ref, *refs):
@@ -1345,31 +1658,31 @@
     bytes_ref[length - 16 :, :] = (edge_ref[1] + jnp.concatenate([zero, right], axis=0)).astype(jnp.bfloat16)
     for row, ref in ((0, score_ref), (6, gain1_ref), (12, gain2_ref)):
         for j in range(6):
-            ref[:, j * 128 : j * 128 + 128] = small_ref[row + j : row + j + 1, :]
+            ref[j * 128 : j * 128 + 128] = small_ref[row + j, :]
     tab_ref[...] = small_ref[16:32, :]
     if streams:
         gq, gk, gv, go, gg, gu, gd = outs[5:]
         per = gq.shape[0]
         wide_a, wide_b, slim, *thirds = streams
-        for j, ref in enumerate((gq, gk, gv)):
+        third_width = thirds[0].shape[1]
+        for j, ref in enumerate((gq, gk, gv, go)):
             for c, third in enumerate(thirds):
-                ref[:, c * 256 : c * 256 + 256] = third[j * per : j * per + per, :]
+                ref[:, c * third_width : (c + 1) * third_width] = third[j * per : j * per + per, :]
         half = wide_a.shape[1]
         for c, ref in ((0, wide_a), (1, wide_b)):
             gg[:, c * half : c * half + half] = ref[0:per, :]
             gu[:, c * half : c * half + half] = ref[per : 2 * per, :]
-        go[...] = slim[0:per, :]
-        gd[...] = slim[32:, :]
+        gd[...] = slim[...]
 
 
 def finish(shards, heads_all, per, ff, gb, edge, spill, small, streams):
     width = gb.shape[1]
     full = jax.ShapeDtypeStruct
-    line = full((1, width), jnp.float32)
+    line = full((width,), jnp.float32)
     outs = [full(gb.shape, jnp.bfloat16), line, line, line, full((16, 128), jnp.float32)]
     if streams:
         square, broad = full((per, width), jnp.float32), full((per, ff), jnp.float32)
-        outs += [square] * 4 + [broad] * 2 + [full((streams[2].shape[0] - 32, width), jnp.float32)]
+        outs += [square] * 4 + [broad] * 2 + [full((streams[2].shape[0], width), jnp.float32)]
     return pl.pallas_call(
         functools.partial(finish_kernel, shards, heads_all),
         out_shape=tuple(outs),
@@ -1453,6 +1766,7 @@
             -(-jnp.max(span[:, :, 0], axis=-1) // TK),
             jnp.min(span[:, :, 1], axis=-1) // TK,
             jnp.broadcast_to(parity, (2, 2)),
+            jnp.broadcast_to((labels_all[0, -1] > 0).astype(jnp.int32), (2, 2)),
         ],
         axis=-1,
     ).astype(jnp.int32)
@@ -1465,54 +1779,51 @@
         o_home, hidden, ct, gain2, w_out, w_gate, w_up, w_down
     )
 
-    orders, pairs = [], []
     if devices == 32:
-        do_all, keep_a, send_a, keep_b, send_b, keep_c, send_c = spread_and_weights(
-            shards, da_packed, n2, att, act, d_gate, d_up, ct, d_branch
+        do_all, *blocks = spread_and_weights(shards, da_packed, n2, act, d_gate, d_up, ct)
+        dq_other, dkv_other, near_other, side_other = attention_back(
+            True, bounds, table, q_all, do_all, o_kept, kv_all, bias_tiles, span, log_total
         )
-        swap = lambda part, axis, mask: lax.ppermute(part, axis, [(i, i ^ mask) for i in range(lax.axis_size(axis))])
-        orders = [((1, 2, 3), (3, 2, 1)), ((0, 1, 2), (0, 2, 1)), ((0, 1, 3), (3, 0, 1))]
-        pairs = [(keep_a, swap(send_a, "dp", 1)), (keep_b, swap(send_b, "blk", 2)), (keep_c, swap(send_c, "blk", 4))]
+        orders = [((0, 1, 2, 3), (0,)), ((0, 1, 2, 3), (3,)), ((0, 1, 2, 3), (2,))]
+        dq_home, dkv_home, d_table_lanes, *sums = dense_back(
+            shape, bounds, table, q_all, do_all, o_kept, kv_all, bias_tiles, log_total, dq_other, dkv_other, near_other, side_other,
+            orders, blocks,
+        )
     else:
         do_all = move_heads(spread_kernel, (2, 2), shards, 5, da_packed)
-
-    dq_packed, dkv_all, d_table_lanes = attention_back(
-        bounds, table, q_all, do_all, o_kept, kv_all, bias_tiles, span, log_total
-    )
-    dq_home, dkv_home, *sums = reduce_all(shape, dq_packed, dkv_all, orders, pairs)
-    grad_bytes, edge, spill, small, last_blocks = last_part(
-        devices, dq_home, dkv_home, hidden, d_res, n1, x, before, after, labels, y, score_row, gain1,
-        w_query, w_key, w_value, d_gain2, share, d_table_lanes,
-    )
+        dq_packed, dkv_all, _, _, d_table_lanes = attention_back(
+            False, bounds, table, q_all, do_all, o_kept, kv_all, bias_tiles, span, log_total
+        )
+        dq_home, dkv_home = reduce_all(shape, dq_packed, dkv_all, [], [])
+        sums = []
     across = len(bits_of(shape["dp"]))
     ndim = across + len(bits_of(shards))
-    small_order = tuple(reversed(range(ndim)))
+    orders, kepts = [tuple(reversed(range(ndim)))], []
     if devices == 32:
-        third = width // 3
-        blocks = [last_blocks[:, :, c * third : c * third + third] for c in range(3)]
-        thirds, small, spill = last_sums(
-            shape, blocks, [(4, 0, 3, 2, 1), (4, 3, 2, 1, 0), (4, 2, 0, 3, 1), small_order], small, spill
-        )
-        sums = list(sums) + list(thirds)
-    else:
-        _, small, spill = last_sums(shape, [], [small_order], small, spill)
+        every = (0, 1, 2, 3, 4)
+        kepts = [(1, 2, 3), (0, 1, 2), (0, 1, 3), every, every]
+        orders = [(3, 2, 1), (0, 2, 1), (3, 0, 1), (4, 0, 3, 2, 1), (4, 3, 0, 2, 1)] + orders
+    grad_bytes, edge, spill, small, last_parts, *sums = last_part(
+        shape, sums, kepts, orders, dq_home, dkv_home, hidden, d_res, n1, att, d_branch, x, before, after, labels, y,
+        score_row, gain1, w_query, w_key, w_value, d_gain2, share, d_table_lanes,
+    )
     per = width // devices
     grad_bytes, g_score, g_gain1, g_gain2, rows, *grads = finish(
         shards, rel_bias.shape[1], per, w_gate.shape[1], grad_bytes, edge, spill, small, sums
     )
     if devices != 32:
         product = lambda left, right: jnp.einsum("td,te->de", left, right, preferred_element_type=jnp.float32)
-        grads = [product(n1, last_blocks[j]) for j in range(3)]
+        grads = [product(n1, last_parts[j]) for j in range(3)]
         grads += [product(att, d_branch), product(n2, d_gate), product(n2, d_up), product(act, ct)]
         grads = [lax.psum_scatter(grad, ("dp", "blk"), scatter_dimension=0, tiled=True) for grad in grads]
     return (
         block_out[None],
         grad_bytes[None],
-        g_score[0],
-        g_gain1[0],
+        g_score,
+        g_gain1,
         *grads[:4],
         rows[2 : 2 + rel_bias.shape[1], :BUCKETS].T,
-        g_gain2[0],
+        g_gain2,
         *grads[4:],
         rows[14, :MAX_BLOCK],
     )

time: 369 us -> 343 us (0.930)
  Pallas kernels: 336 us -> 320 us
  local copies, waits for them, and re-layouts: 16.7 us -> 11.6 us
  other arithmetic: 7.97 us -> 4.14 us
    pallas_call x4 -> x3, Pallas kernels: 172 us -> 167 us  [the longest x1 79.6 us: dense_back(): pl.pallas_call(functools.partial(dense_kernel, shards, bit_axes(shape), o...]
    pallas_call x1, Pallas kernels: 59.4 us -> 54.2 us  [gather_all(): pl.pallas_call(functools.partial(gather_kernel, shards), out_shape=(jax.S...]
    pallas_call x3 -> x0, other arithmetic: 3.85 us -> none  [finish(): pl.pallas_call(functools.partial(finish_kernel, shards, heads_all), out_s...]
  transfers between devices with their start and end apart: 5 -> 2, of which waited for: 0 -> 0; matrix products, arithmetic and copies ran while one was open for 2% -> 2% of each run, Pallas kernels for 13% -> 0%
where the time goes in v3:
time: 343 us; the launch traced here: 341 us
  Pallas kernels  320 us (93%)
  local copies, waits for them, and re-layouts  11.6 us (3%)
  other arithmetic  4.14 us (1%)
  starting transfers between devices  3.65 us (1%)
    pallas_call x1, Pallas kernels, dense_back(): pl.pallas_call(functools.partial(dense_kernel, shards, bit_axes(shape), o...  79.6 us
    pallas_call x1, Pallas kernels, last_part(): pl.pallas_call(functools.partial(last_kernel, shape['blk'], axes, kepts,...  70.5 us
    pallas_call x1, Pallas kernels, gather_all(): pl.pallas_call(functools.partial(gather_kernel, shards), out_shape=(jax.S...  54.2 us
    pallas_call x1, Pallas kernels, attention(): pl.pallas_call(fwd_kernel, out_shape=(jax.ShapeDtypeStruct(packed, jnp.bf...  36 us
    pallas_call x1, Pallas kernels, spread_and_weights(): pl.pallas_call(functools.partial(weights_kernel, shards), out_shape=(jax....  23.1 us
    pallas_call x1, Pallas kernels, move_heads(): pl.pallas_call(functools.partial(kernel, shards), out_shape=jax.ShapeDtyp...  18 us
    pallas_call x1, Pallas kernels, attention_back(): pl.pallas_call(functools.partial(bwd_kernel, alone), out_shape=(jax.Shape...  16.6 us
    pallas_call x1, Pallas kernels, feed_forward(): pl.pallas_call(feed_kernel, out_shape=(low(width), jax.ShapeDtypeStruct((...  13.2 us
  transfers between devices with their start and end apart: 2, of which 0 were waited for; matrix products, arithmetic and copies ran while one was open for 2% of the time, Pallas kernels for 0%

profile of v3, /device:TPU:0, one launch (start us, length us, event | category | flops | bytes accessed | tf_op | source)
XLA Modules:
  0.0 340.9 jit_solution(5142606787039684795)
XLA Ops:
  0.6 0.7 add_convert_fusion
  1.4 0.7 slice_bitcast_fusion.1
  2.2 2.4 collective-permute-start
  4.6 1.3 collective-permute-start.1
  6.0 1.3 convert_bitcast_fusion.table
  7.3 0.9 slice.71
  8.2 1.3 broadcast_in_dim.66.score_ref.refs_12_
  9.5 1.3 broadcast_in_dim.67.gain_ref.refs_13_
  10.8 0.6 pad.18.label_ref
  11.4 1.3 broadcast_in_dim.74.gain_ref
  12.8 0.1 reshape.279
  13.1 0.6 pad_add_fusion.lab_ref.refs_10_
  13.7 6.1 %pool_and_project.1 = (f32[256,768]{1,0:T(8,128)}, bf16[256,768]{1,0:T(8,128)(2,1)}, f32[8,256]{1,0:T(8,128)}, f32[1,128]{1,0:T(1,128)}, bf16[4,384,128]{2,1,0:T(8,128)(2,1)}, /*index=5*/bf16[4,256,384]{2,1,0:T(8,128)(2,1)}) custom-call(bf16[512,768]{1,0:T(8,128)(2,1)} %bitcast.33, bf16[3,768]{1,0:T(4,128)(2,1)} %copy-done, bf16[3,768]{1,0:T(4,128)(2,1)} %copy-done.1, ...), custom_call_target="tpu_custom_call" | custom-call | tf_op jit(solution)/shard_map/pool_and_project/pallas_call | solution.py:1368
  19.8 54.2 %gather_keys.1 = (bf16[2,2,384,128]{3,2,1,0:T(8,128)(2,1)}, bf16[2,4096,384]{2,1,0:T(8,128)(2,1)}, s32[2,2,2,2,2,8,128]{6,5,4,3,2,1,0:T(8,128)}) custom-call(bf16[4,384,128]{2,1,0:T(8,128)(2,1)} %get-tuple-element.72.q_ref, bf16[4,256,384]{2,1,0:T(8,128)(2,1)} %get-tuple-element.73.kv_ref, s32[8,128]{1,0:T(8,128)} %pad.18.label_ref), custom_call_target="tpu_custom_call" | custom-call | tf_op jit(solution)/shard_map/gather_keys/pallas_call | solution.py:280
  74.0 0.9 slice.82
  74.9 0.6 slice.83
  75.5 0.2 convert_reduce_fusion
  75.7 0.2 select_reduce_fusion.2
  75.9 0.1 select_reduce_fusion
  76.0 0.2 fusion.9
  77.4 0.6 pad_add_fusion.1.se_ref
  78.0 0.7 stack.44.bounds
  78.7 36.0 %attention.1 = (bf16[2,2,384,128]{3,2,1,0:T(8,128)(2,1)}, f32[2,2,384,128]{3,2,1,0:T(8,128)}, f32[2,2,3,1,256]{4,3,2,1,0:T(1,128)}, bf16[3,4,512,256]{3,2,1,0:T(8,128)(2,1)}) custom-call(s32[2,2,7]{2,1,0:T(2,128)} %stack.44.bounds, f32[3,32]{1,0:T(4,128)} %convert_bitcast_fusion.table, bf16[2,2,384,128]{3,2,1,0:T(8,128)(2,1)} %get-tuple-element.75.q_ref, ...), custom_call_target="tpu_custom_call" | custom-call | tf_op jit(solution)/shard_map/attention/pallas_call | solution.py:765
  114.7 18.0 %move_heads_4.1.o_ref = bf16[4,384,128]{2,1,0:T(8,128)(2,1)} custom-call(bf16[2,2,384,128]{3,2,1,0:T(8,128)(2,1)} %get-tuple-element.77.o_ref), custom_call_target="tpu_custom_call" | custom-call | tf_op jit(solution)/shard_map/move_heads_4/pallas_call | solution.py:177
  132.8 13.2 %feed_forward.1 = (bf16[256,768]{1,0:T(8,128)(2,1)}, f32[256,768]{1,0:T(8,128)}, bf16[4,384,128]{2,1,0:T(8,128)(2,1)}, f32[1,768]{1,0:T(1,128)}, bf16[256,768]{1...) custom-call(bf16[4,384,128]{2,1,0:T(8,128)(2,1)} %move_heads_4.1.o_r, ...), custom_call_target="tpu_custom_call" | custom-call | tf_op jit(solution)/shard_map/feed_forward/pallas_call | solution.py:1445
  145.9 23.1 %spread_and_weights.1 = (bf16[2,2,384,128]{3,2,1,0:T(8,128)(2,1)}, bf16[16,48,1024]{2,1,0:T(8,128)(2,1)}, bf16[16,48,1024]{2,1,0:T(8,128)(2,1)}, bf16[16,64,768]{2,1,0:T(8,128)(2,1)}) custom-call(bf16[4,384,128]{2,1,0:T(8,128)(2,1)} %get-tuple-element.80.da_ref, bf16[256,768]{1,0:T(8,128)(2,1)} %get-tuple-element.81.n2_ref, ...), custom_call_target="tpu_custom_call" | custom-call | tf_op jit(solution)/shard_map/spread_and_weights/pallas_call | solution.py:463
  169.1 16.6 %attention_back.1 = (bf16[1,2,384,128]{3,2,1,0:T(8,128)(2,1)}, bf16[1,4096,384]{2,1,0:T(8,128)(2,1)}, f32[3,448,256]{2,1,0:T(8,128)}, f32[3,2,256]{2,1,0:T(2,128)}) custom-call(s32[2,2,7]{2,1,0:T(2,128)} %stack.44.bounds, f32[3,32]{1,0:T(4,128)} %convert_bitcast_fusion.table, bf16[2,2,384,128]{3,2,1,0:T(8,128)(2,1)} %get-tuple-element.75.q_ref, ...), custom_call_target="tpu_custom_call" | custom-call | tf_op jit(solution)/shard_map/attention_back/pallas_call | solution.py:943
  185.7 79.6 %dense_back.1 = (bf16[4,384,128]{2,1,0:T(8,128)(2,1)}, bf16[4,256,384]{2,1,0:T(8,128)(2,1)}, f32[3,32,256]{2,1,0:T(8,128)}, bf16[2,2,2,48,1024]{4,3,2,1,0:T(8,12...) custom-call(s32[2,2,7]{2,1,0:T(2,128)} %stack.44.bounds, ...), custom_call_target="tpu_custom_call" | custom-call | tf_op jit(solution)/shard_map/dense_back/pallas_call | solution.py:1205
  265.2 70.5 %last_part.1 = (bf16[512,768]{1,0:T(8,128)(2,1)}, f32[2,16,768]{2,1,0:T(8,128)}, f32[2,8,768]{2,1,0:T(8,128)}, f32[32,128]{1,0:T(8,128)}, bf16[16,128]{1,0:T(8,1...) custom-call(bf16[4,384,128]{2,1,0:T(8,128)(2,1)} %get-tuple-element., ...), custom_call_target="tpu_custom_call" | custom-call | tf_op jit(solution)/shard_map/last_part/pallas_call | solution.py:1631
  335.7 2.7 finish.1
  338.4 1.2 slice_bitcast_fusion.5
  339.6 1.3 slice_bitcast_fusion
  (39 shorter events, 1.1 us)
Async XLA Ops:
  2.2 10.5 %collective-permute-start = (bf16[3,768]{1,0:T(4,128)(2,1)S(1)}, bf16[3,768]{1,0:T(4,128)(2,1)S(1)}, u32[]{:S(2)}, u32[]{:S(2)}) collective-permute-start(bf16[3,768]{1,0:T(4,128)(2,1)S(1)} %pad_maximum_fusion), channel_id=1, source_target_pairs={{0,1},{1,2},{2,3},{3,4},{4,5},{5,6},{6,7},{7,8},{8,9},{9,10},{10,1... | collective-permute-start | bytes 13832 | tf_op jit(solution)/shard_map/ppermute | solution.py:1700
  4.6 8.1 %collective-permute-start.1 = (bf16[3,768]{1,0:T(4,128)(2,1)S(1)}, bf16[3,768]{1,0:T(4,128)(2,1)S(1)}, u32[]{:S(2)}, u32[]{:S(2)}) collective-permute-start(bf16[3,768]{1,0:T(4,128)(2,1)S(1)} %pad_maximum_fusion.1), channel_id=1, source_target_pairs={{1,0},{2,1},{3,2},{4,3},{5,4},{6,5},{7,6},{8,7},{9,8},{10,9},{11,1... | collective-permute-start | bytes 13832 | tf_op jit(solution)/shard_map/ppermute | solution.py:1700
  12.6 1.1 copy-start
  12.7 1.1 copy-start.1

commit v4 on v2

--- a/solution.py
+++ b/solution.py
@@ -10,7 +10,7 @@
 
 BUCKETS = 32
 MAX_BLOCK = 4
-VMEM_BYTES = 60 * 2**20
+VMEM_BYTES = 61 * 2**20
 
 
 def buckets_of(relative):
@@ -64,11 +64,19 @@
         return self.at(self.row, (self.group + step) % GROUPS, self.rest)
 
 
-def greet(targets):
+def hail(targets):
     barrier = pltpu.get_barrier_semaphore()
     for target in targets:
         pl.semaphore_signal(barrier, inc=1, device_id=target, device_id_type=MESH_ID)
-    pl.semaphore_wait(barrier, len(targets))
+    return len(targets)
+
+
+def await_all(count):
+    pl.semaphore_wait(pltpu.get_barrier_semaphore(), count)
+
+
+def greet(targets):
+    await_all(hail(targets))
 
 
 def remote(src, dst, send_sem, recv_sem, target):
@@ -225,12 +233,13 @@
         copy = remote(kv_ref.at[(place.group + step) % GROUPS], held(0, 0, 0), z_send.at[step], sem_of((GROUPS - step) % GROUPS, 0, 0), place.other_group(step))
         copy.start()
         waits.append(copy)
-    spread_heads(place, q_ref, qo_ref, q_send, q_recv)
 
     used = 0
     events = sorted(((dz, off) for dz in range(GROUPS) for off in range(count)), key=lambda e: (bin(e[1]).count("1"), (0, 1, 3, 2).index(e[0])))
     core_target = place.other_rest(core)
-    for dz, off in events:
+    for step, (dz, off) in enumerate(events):
+        if step == GROUPS:
+            spread_heads(place, q_ref, qo_ref, q_send, q_recv)
         here = held(dz, off, 0)
         if dz == 0 and off == 0:
             src = kv_ref.at[place.group]
@@ -338,7 +347,7 @@
     def absorb(self, k):
         kept, src, now = self.stage(k)
         buf = self.bufs[k]
-        if k == len(self.order) - 1:
+        if k == len(self.order) - 1 and self.out is not None:
             mine = src[self.own(now)].astype(jnp.float32)
             self.out[...] = buf[...].astype(jnp.float32) + mine
         else:
@@ -365,14 +374,12 @@
             self.bufs[1, k] = total
 
 
-def run_streams(streams, first=0):
-    for stage in range(max(len(s.order) for s in streams)):
-        for s in streams:
-            if stage < len(s.order):
-                s.copy(stage).wait()
-                s.absorb(stage)
-                if stage < len(s.order) - 1:
-                    s.copy(stage + 1).start()
+def advance(stream, stage):
+    if stage < len(stream.order):
+        stream.copy(stage).wait()
+        stream.absorb(stage)
+        if stage < len(stream.order) - 1:
+            stream.copy(stage + 1).start()
 
 
 def bit_axes(shape):
@@ -392,7 +399,8 @@
     spread_heads(place, da_ref, do_ref, q_send, q_recv)
     per = gate.shape[0] // 32
     per_ff = down.shape[0] // 32
-    half = wide_out.shape[2] // 2
+    first = keep_a.shape[2]
+    half = out.shape[1] // 2
     core = place.rest % 2
 
     n2_t = n2_ref[...].T
@@ -401,15 +409,15 @@
         cols = slice(j * step, j * step + step)
         gate[:, cols] = mxu(n2_t, dg_ref[:, cols])
         up[:, cols] = mxu(n2_t, du_ref[:, cols])
+    out[...] = mxu(att_ref[...].T, db_ref[...])
 
     def wide_rows(block):
         rows = pl.ds(pl.multiple_of(block * per, 8), per)
-        return jnp.concatenate([gate[rows, :], up[rows, :]], axis=0)
+        last = jnp.concatenate([out[rows, :half], out[rows, half:]], axis=0)
+        return jnp.concatenate([jnp.concatenate([gate[rows, :], up[rows, :]], axis=0), last], axis=1)
 
     def slim_rows(block):
-        rows, more = pl.ds(pl.multiple_of(block * per, 8), per), pl.ds(pl.multiple_of(block * per_ff, 8), per_ff)
-        empty = jnp.zeros((32 - per, out.shape[1]), jnp.float32)
-        return jnp.concatenate([out[rows, :], empty, down[more, :]], axis=0)
+        return down[pl.ds(pl.multiple_of(block * per_ff, 8), per_ff), :]
 
     def send_wide(m, _):
         wide_out[m] = wide_rows(2 * m + 1 - core).astype(jnp.bfloat16)
@@ -418,7 +426,6 @@
     lax.fori_loop(0, 16, send_wide, 0)
     wide_copy = remote(wide_out, wide_in, core_send.at[0], core_recv.at[0], core_target)
     wide_copy.start()
-    out[...] = mxu(att_ref[...].T, db_ref[...])
     for j in range(down.shape[0] // step):
         rows = slice(j * step, j * step + step)
         down[rows, :] = mxu(act_ref[:, rows].T, ct_ref[...])
@@ -436,8 +443,8 @@
 
     wide_copy.wait()
     for (keep, send), bit_at, mine, cols in (
-        ((keep_a, send_a), 8, place.row, slice(0, half)),
-        ((keep_b, send_b), 1, bit(place.rest, 2), slice(half, 2 * half)),
+        ((keep_a, send_a), 8, place.row, slice(0, first)),
+        ((keep_b, send_b), 1, bit(place.rest, 2), slice(first, wide_out.shape[2])),
     ):
         for ref, value in ((send, 1 - mine), (keep, mine)):
             def one(j, _):
@@ -460,11 +467,13 @@
     width, ff = n2.shape[1], act.shape[1]
     per, per_ff = width // 32, ff // 32
     sem, low = pltpu.SemaphoreType.DMA, jnp.bfloat16
-    wide, slim = (2 * per, ff), (32 + per_ff, width)
-    halves = [jax.ShapeDtypeStruct((8, 2 * per, ff // 2), low)] * 4 + [jax.ShapeDtypeStruct((8,) + slim, low)] * 2
+    wide, slim = (2 * per, ff + width // 2), (per_ff, width)
+    first = (wide[1] // 256 + 1) * 128
+    sums = [jax.ShapeDtypeStruct((8, 2 * per, cols), low) for cols in (first, first, wide[1] - first, wide[1] - first)]
+    sums += [jax.ShapeDtypeStruct((8,) + slim, low)] * 2
     return pl.pallas_call(
         functools.partial(weights_kernel, shards),
-        out_shape=(jax.ShapeDtypeStruct((2, 2) + da.shape[1:], da.dtype),) + tuple(halves),
+        out_shape=(jax.ShapeDtypeStruct((2, 2) + da.shape[1:], da.dtype),) + tuple(sums),
         in_specs=[VMEM_SPEC] * 8,
         out_specs=(VMEM_SPEC,) * 7,
         scratch_shapes=[
@@ -614,59 +623,6 @@
     )(q_packed, kv_sums.reshape((2, GROUPS) + (2,) * len(rest_bits) + (tokens, width)), *flat)
 
 
-def sums_kernel(shards, axes, orders, *refs):
-    count = len(orders) - 1
-    ins, small_ref, spill_ref = refs[:count], refs[count], refs[count + 1]
-    outs, small_out, spill_out = refs[count + 2 : 2 * count + 2], refs[2 * count + 2], refs[2 * count + 3]
-    w_send, w_recv, s_send, s_recv = refs[2 * count + 4 : 2 * count + 8]
-    bufs = refs[2 * count + 8 :]
-    at = {"dp": lax.axis_index("dp"), "blk": lax.axis_index("blk")}
-    whole = Whole(axes, at, orders[-1], small_ref, bufs[-1], small_out, w_send.at[count], w_recv.at[count])
-    streams, used = [], 0
-    for s in range(count):
-        more = bufs[used : used + len(orders[s])]
-        used += len(orders[s])
-        streams.append(Stream(axes, at, sorted(orders[s]), orders[s], ins[s], more, outs[s], w_send.at[s], w_recv.at[s]))
-    left = (at["dp"], (at["blk"] + shards - 1) % shards)
-    right = (at["dp"], (at["blk"] + 1) % shards)
-    greet([whole.stream.target(p) for p in range(len(axes))] + [left, right])
-    spills = [
-        remote(spill_ref.at[0], spill_out.at[1], s_send.at[0], s_recv.at[1], left),
-        remote(spill_ref.at[1], spill_out.at[0], s_send.at[1], s_recv.at[0], right),
-    ]
-    streams.append(whole)
-    for stream in streams:
-        stream.copy(0).start()
-    for copy in spills:
-        copy.start()
-    run_streams(streams)
-    for copy in spills:
-        copy.wait()
-
-
-def last_sums(shape, blocks, orders, small, spill):
-    axes = bit_axes(shape)
-    ndim = len(axes)
-    sem = pltpu.SemaphoreType.DMA
-    scratch, sums = [], []
-    for block, order in zip(blocks, orders):
-        rows, cols = block.shape[-2:]
-        scratch += stream_scratch(ndim, order, rows, cols)
-        sums.append(jax.ShapeDtypeStruct((rows, cols), jnp.float32))
-    count = len(blocks)
-    scratch.append(pltpu.VMEM((2, ndim) + small.shape, small.dtype))
-    found = pl.pallas_call(
-        functools.partial(sums_kernel, shape["blk"], axes, orders),
-        out_shape=tuple(sums) + (jax.ShapeDtypeStruct(small.shape, small.dtype), jax.ShapeDtypeStruct(spill.shape, spill.dtype)),
-        in_specs=[VMEM_SPEC] * (count + 2),
-        out_specs=(VMEM_SPEC,) * (count + 2),
-        scratch_shapes=[sem((count + 1, ndim)), sem((count + 1, ndim)), sem((2,)), sem((2,))] + scratch,
-        compiler_params=pltpu.CompilerParams(collective_id=3, has_side_effects=True, vmem_limit_bytes=VMEM_BYTES),
-        name="last_sums",
-    )(*[b.reshape((2,) * ndim + b.shape[-2:]) for b in blocks], small, spill)
-    return found[:count], found[count], found[count + 1]
-
-
 TQ = 256
 TK = 512
 NEAR_ROWS = 448
@@ -717,7 +673,7 @@
     return buckets_of(relative)
 
 
-def make_bias(table, parity, bias_ref):
+def make_bias(table, parity, bias_ref, near_ref):
     heads = bias_ref.shape[0]
     for h in range(heads):
         bias_ref[h, 0] = jnp.full((TK, TQ), table[h, 15], jnp.float32).astype(jnp.bfloat16)
@@ -731,6 +687,7 @@
                 for b in range(BUCKETS):
                     value = jnp.where(which == b, table[h, b], value)
                 bias_ref[h, tile + 1, pl.ds(start, 32)] = value.astype(jnp.bfloat16)
+                near_ref[h, tile, pl.ds(start, 32)] = value.astype(jnp.bfloat16)
             return 0
         lax.fori_loop(0, TK // 32, rows, 0)
 
@@ -742,9 +699,9 @@
     return slot, jnp.logical_and(away, inside)
 
 
-def fwd_kernel(bounds, table, q_ref, kv_ref, se_ref, o_ref, keep_ref, lse_ref, bias_ref, vt, acc, mx, qp):
+def fwd_kernel(bounds, table, q_ref, kv_ref, se_ref, o_ref, keep_ref, lse_ref, bias_ref, near_ref, vt, acc, mx, qp):
     heads = lse_ref.shape[2]
-    make_bias(table, bounds[0, 0, 5], bias_ref)
+    make_bias(table, bounds[0, 0, 5], bias_ref, near_ref)
     for r in range(2):
         for i in range(2):
             for h, tile in enumerate(spread_lanes(q_ref[r, i], False)):
@@ -824,9 +781,10 @@
             jax.ShapeDtypeStruct(packed, jnp.float32),
             jax.ShapeDtypeStruct((2, 2, heads, 1, TQ), jnp.float32),
             jax.ShapeDtypeStruct((heads, 4, TK, TQ), jnp.bfloat16),
+            jax.ShapeDtypeStruct((heads, 2, TK, TQ), jnp.bfloat16),
         ),
         in_specs=[SMEM_SPEC] * 2 + [VMEM_SPEC] * 3,
-        out_specs=(VMEM_SPEC,) * 4,
+        out_specs=(VMEM_SPEC,) * 5,
         scratch_shapes=[
             pltpu.VMEM((heads, 80, n), jnp.bfloat16),
             pltpu.VMEM((heads, 80, TQ), jnp.float32),
@@ -838,27 +796,74 @@
     )(bounds, table, q, kv, se)
 
 
-def bwd_kernel(bounds, table, q_ref, do_ref, keep_ref, kv_ref, bias_ref, se_ref, lse_ref,
-               dq_ref, dkv_ref, tab_ref, kt, dqt, dkv, grid, side, qp, dp_ref, delta):
+def prepare(q, do, q_out, do_out):
+    for h, tile in enumerate(spread_lanes(q, False)):
+        q_out[h] = tile
+    for h, tile in enumerate(spread_lanes(do, True)):
+        do_out[h] = tile
+
+
+def row_deltas(do, keep, delta):
+    prod = (do.astype(jnp.float32) * keep).T
+    top, low = prod[:, 0:TQ], prod[:, TQ:]
+    delta[0] = jnp.sum(top[0:64], axis=0, keepdims=True)
+    delta[1] = jnp.sum(top[64:128], axis=0, keepdims=True)
+    delta[2] = jnp.concatenate(
+        [jnp.sum(low[0:64], axis=0, keepdims=True), jnp.sum(low[64:128], axis=0, keepdims=True)], axis=1
+    )
+
+
+def near_start(parity):
+    return 416 - TQ * parity
+
+
+def far_sums(grid, h, first, end):
+    def one(step, total):
+        rows = grid[h, pl.ds(pl.multiple_of(step * 32, 32), 32)]
+        return total + jnp.sum(rows.reshape(4, 8, TQ), axis=0)
+    total = lax.fori_loop(first // 32, end // 32, one, jnp.zeros((8, TQ), jnp.float32))
+    return jnp.sum(total, axis=0, keepdims=True)
+
+
+def bucket_sums(parity, near, side, tab_ref, tab8):
+    heads = near.shape[0]
+    tab8[...] = jnp.zeros_like(tab8)
+
+    def inner(step, _):
+        start = pl.multiple_of(step * 32, 32)
+        which = near_buckets(near_start(parity) + start, 32, parity)
+        for b in range(BUCKETS):
+            here = which == b
+            for h in range(heads):
+                rows = jnp.where(here, near[h, pl.ds(start, 32)], 0.0)
+                tab8[h, b] += jnp.sum(rows.reshape(4, 8, TQ), axis=0)
+        return 0
+
+    lax.fori_loop(0, NEAR_ROWS // 32, inner, 0)
+    for h in range(heads):
+        tab_ref[h] = jnp.sum(tab8[h], axis=1)
+        tab_ref[h, 15:16] += side[h, 0:1]
+        tab_ref[h, 31:32] += side[h, 1:2]
+
+
+def bwd_kernel(alone, bounds, table, q_ref, do_ref, keep_ref, kv_ref, bias_ref, se_ref, lse_ref,
+               dq_ref, dkv_ref, near_ref, side, delta, *rest):
+    tab_ref, tab8, rest = (None, None, rest) if alone else (rest[0], rest[-1], rest[1:-1])
+    kt, dqt, dkv, grid, qp, dp_ref = rest
     heads = lse_ref.shape[2]
     n = kv_ref.shape[1]
     grid[...] = jnp.zeros_like(grid)
     side[...] = jnp.zeros_like(side)
+    base = 1 - bounds[0, 0, 6] if alone else 0
+    for at in range(1 if alone else 2):
+        for i in range(2):
+            prepare(q_ref[base + at, i], do_ref[base + at, i], qp.at[at, i], dp_ref.at[at, i])
     for r in range(2):
         for i in range(2):
-            for h, tile in enumerate(spread_lanes(q_ref[r, i], False)):
-                qp[r, i, h] = tile
-            for h, tile in enumerate(spread_lanes(do_ref[r, i], True)):
-                dp_ref[r, i, h] = tile
-            prod = (do_ref[r, i].astype(jnp.float32) * keep_ref[r, i]).T
-            top, low = prod[:, 0:TQ], prod[:, TQ:]
-            delta[r, i, 0] = jnp.sum(top[0:64], axis=0, keepdims=True)
-            delta[r, i, 1] = jnp.sum(top[64:128], axis=0, keepdims=True)
-            delta[r, i, 2] = jnp.concatenate(
-                [jnp.sum(low[0:64], axis=0, keepdims=True), jnp.sum(low[64:128], axis=0, keepdims=True)], axis=1
-            )
-
-    def row_body(r, _):
+            row_deltas(do_ref[r, i], keep_ref[r, i], delta.at[r, i])
+
+    def row_body(at, _):
+        r = base + at
         lo_all = jnp.minimum(bounds[r, 0, 0], bounds[r, 1, 0])
         hi_all = jnp.maximum(bounds[r, 0, 1], bounds[r, 1, 1])
 
@@ -890,13 +895,13 @@
                 def finish(h, p, ds, where):
                     ds_low = ds.astype(jnp.bfloat16)
                     two = jnp.concatenate([ds_low, p.astype(jnp.bfloat16)], axis=1)
-                    both = jnp.concatenate([qp[r, i, h], dp_ref[r, i, h]], axis=0)
+                    both = jnp.concatenate([qp[at, i, h], dp_ref[at, i, h]], axis=0)
                     dkv[h, pl.ds(k0, TK), :] += mxu(two, both)
                     dqt[h, where] += mxu(kt[h, :, pl.ds(k0, TK)], ds_low)
 
                 def products(h):
                     tile = kv_ref[r, pl.ds(k0, TK), h * 128 : h * 128 + 128]
-                    return mxu(tile, qp[r, i, h], NT), mxu(tile, dp_ref[r, i, h], NT)
+                    return mxu(tile, qp[at, i, h], NT), mxu(tile, dp_ref[at, i, h], NT)
 
                 @pl.when(plain)
                 def _():
@@ -913,7 +918,7 @@
                         s = s + bias_ref[h, slot].astype(jnp.float32)
                         p = jnp.where(ok, jnp.exp(jnp.where(ok, s, NEG) - lse_ref[r, i, h]), 0.0)
                         ds = p * (d_probs - delta[r, i, h])
-                        grid[h, slot] += ds
+                        grid[h, pl.ds(pl.multiple_of(slot * TK, TK), TK)] += ds
                         finish(h, p, ds, 1)
 
                 return 0
@@ -924,7 +929,7 @@
                 parts.append((dqt[h, 0, 0:64] + dqt[h, 1, 0:64] + dqt[h, 2, 0:64]).T * 0.125)
                 side[h, 0:1] += dqt[h, 0, 64:65]
                 side[h, 1:2] += dqt[h, 2, 64:65]
-            dq_ref[r, i] = join_heads(parts).astype(jnp.bfloat16)
+            dq_ref[at, i] = join_heads(parts).astype(jnp.bfloat16)
             return 0
 
         lax.fori_loop(0, 2, q_body, 0)
@@ -932,70 +937,47 @@
         def put(t, _):
             k0 = pl.multiple_of(t * TK, TK)
             for h in range(heads):
-                dkv_ref[r, pl.ds(k0, TK), h * 128 : h * 128 + 128] = dkv[h, pl.ds(k0, TK), :].astype(jnp.bfloat16)
+                dkv_ref[at, pl.ds(k0, TK), h * 128 : h * 128 + 128] = dkv[h, pl.ds(k0, TK), :].astype(jnp.bfloat16)
             return 0
 
         lax.fori_loop(0, n // TK, put, 0)
         return 0
 
-    lax.fori_loop(0, 2, row_body, 0)
+    lax.fori_loop(0, 1 if alone else 2, row_body, 0)
 
     parity = bounds[0, 0, 5]
-    tab_ref[...] = jnp.zeros_like(tab_ref)
+    first = TK + near_start(parity)
     for h in range(heads):
-        tab_ref[h, 15:16] = side[h, 0:1] + jnp.sum(grid[h, 0], axis=0, keepdims=True)
-        tab_ref[h, 31:32] = side[h, 1:2] + jnp.sum(grid[h, 3], axis=0, keepdims=True)
-
-    first = 13 - 8 * parity
-    count = NEAR_ROWS // 32
-
-    def block(h, step):
-        tile = step // (TK // 32)
-        start = pl.multiple_of((step % (TK // 32)) * 32, 32)
-        return grid[h, tile + 1, pl.ds(start, 32)]
-
-    def outer(bucket):
-        def one(step, _):
-            for h in range(heads):
-                tab_ref[h, bucket : bucket + 1] += jnp.sum(block(h, step), axis=0, keepdims=True)
-            return 0
-        return one
-
-    lax.fori_loop(0, first, outer(15), 0)
-    lax.fori_loop(first + count, 2 * TK // 32, outer(31), 0)
-
-    def inner(step, _):
-        which = near_buckets(step * 32, 32, parity)
-        for b in range(BUCKETS):
-            here = which == b
-            for h in range(heads):
-                tab_ref[h, b : b + 1] += jnp.sum(jnp.where(here, block(h, step), 0.0), axis=0, keepdims=True)
-        return 0
-
-    lax.fori_loop(first, first + count, inner, 0)
-
-
-def attention_back(bounds, table, q, do, keep, kv, bias, se, lse):
+        near_ref[h] = grid[h, pl.ds(pl.multiple_of(first, 32), NEAR_ROWS)]
+        side[h, 0:1] += far_sums(grid, h, 0, first)
+        side[h, 1:2] += far_sums(grid, h, first + NEAR_ROWS, 4 * TK)
+    if not alone:
+        bucket_sums(parity, near_ref, side, tab_ref, tab8)
+
+
+def attention_back(alone, bounds, table, q, do, keep, kv, bias, se, lse):
     heads, n = kv.shape[2] // 128, kv.shape[1]
+    count = 1 if alone else 2
+    table_out = [] if alone else [jax.ShapeDtypeStruct((heads, BUCKETS, TQ), jnp.float32)]
     return pl.pallas_call(
-        bwd_kernel,
+        functools.partial(bwd_kernel, alone),
         out_shape=(
-            jax.ShapeDtypeStruct(q.shape, jnp.bfloat16),
-            jax.ShapeDtypeStruct(kv.shape, jnp.bfloat16),
-            jax.ShapeDtypeStruct((heads, BUCKETS, TQ), jnp.float32),
-        ),
+            jax.ShapeDtypeStruct((count,) + q.shape[1:], jnp.bfloat16),
+            jax.ShapeDtypeStruct((count,) + kv.shape[1:], jnp.bfloat16),
+            jax.ShapeDtypeStruct((heads, NEAR_ROWS, TQ), jnp.float32),
+            jax.ShapeDtypeStruct((heads, 2, TQ), jnp.float32),
+            jax.ShapeDtypeStruct((2, 2, heads, 1, TQ), jnp.float32),
+        ) + tuple(table_out),
         in_specs=[SMEM_SPEC] * 2 + [VMEM_SPEC] * 7,
-        out_specs=(VMEM_SPEC,) * 3,
+        out_specs=(VMEM_SPEC,) * (5 + len(table_out)),
         scratch_shapes=[
             pltpu.VMEM((heads, 80, n), jnp.bfloat16),
             pltpu.VMEM((heads, 3, 80, TQ), jnp.float32),
             pltpu.VMEM((heads, n, 128), jnp.float32),
-            pltpu.VMEM((heads, 4, TK, TQ), jnp.float32),
-            pltpu.VMEM((heads, 2, TQ), jnp.float32),
-            pltpu.VMEM((2, 2, heads, TQ, 128), jnp.bfloat16),
-            pltpu.VMEM((2, 2, heads, TQ, 128), jnp.bfloat16),
-            pltpu.VMEM((2, 2, heads, 1, TQ), jnp.float32),
-        ],
+            pltpu.VMEM((heads, 4 * TK, TQ), jnp.float32),
+            pltpu.VMEM((count, 2, heads, TQ, 128), jnp.bfloat16),
+            pltpu.VMEM((count, 2, heads, TQ, 128), jnp.bfloat16),
+        ] + [pltpu.VMEM((heads, BUCKETS, 8, TQ), jnp.float32) for _ in table_out],
         compiler_params=pltpu.CompilerParams(vmem_limit_bytes=VMEM_BYTES),
         name="attention_back",
     )(bounds, table, q, do, keep, kv, bias, se, lse)
@@ -1220,25 +1202,21 @@
     )(o_home, hidden, ct, gain, wo, wg, wu, wd)
 
 
-def last_kernel(with_blocks, dq_ref, dkv_ref, hidden_ref, dres_ref, n1_ref, x_ref, before_ref, after_ref, lab_ref, y_ref, score_ref,
-                gain_ref, wq_ref, wk_ref, wv_ref, dgain2_ref, share_ref, tab_ref,
-                gb_ref, edge_ref, spill_ref, small_ref, w_ref, xs, gbuf, *grads):
-    tokens, width = hidden_ref.shape
-    length = x_ref.shape[0]
-    lane = lax.broadcasted_iota(jnp.int32, (1, 128), 1)
-    low = lane < 64
-    dq = get_packed(dq_ref)
+def unpack_pairs(dkv_ref, width):
+    low = lax.broadcasted_iota(jnp.int32, (1, 128), 1) < 64
     dk_parts, dv_parts = [], []
     for j in range(width // 128):
         one, two = [dkv_ref[h // 3, :, h % 3 * 128 : h % 3 * 128 + 128] for h in (2 * j, 2 * j + 1)]
         dk_parts.append(jnp.where(low, one, turned(two)))
         dv_parts.append(jnp.where(low, turned(one), two))
-    dk, dv = jnp.concatenate(dk_parts, axis=1), jnp.concatenate(dv_parts, axis=1)
-    d_n1 = mxu(dq, wq_ref[...], NT) + mxu(dk, wk_ref[...], NT) + mxu(dv, wv_ref[...], NT)
-    d_rows, d_gain1 = norm_back(d_n1, hidden_ref[...], gain_ref[...].astype(jnp.float32))
-    d_hidden = dres_ref[...] + d_rows
-
-    load_bytes(x_ref, before_ref, after_ref, xs)
+    return jnp.concatenate(dk_parts, axis=1), jnp.concatenate(dv_parts, axis=1)
+
+
+def pool_back(d_hidden, x_refs, lab_ref, y_ref, score_ref, gb_ref, edge_ref, spill_ref, xs, gbuf):
+    x_ref = x_refs[0]
+    tokens, width = d_hidden.shape
+    length = x_ref.shape[0]
+    lane = lax.broadcasted_iota(jnp.int32, (1, 128), 1)
     met = jnp.zeros((tokens, 128), jnp.float32)
     for k in TAPS:
         met = jnp.where(lane == k + 3, jnp.sum(d_hidden * tap(xs, k, tokens), axis=-1, keepdims=True), met)
@@ -1270,10 +1248,13 @@
     edge_ref[1] = strips(gbuf, LEAD + length - 16, 16)
     spill_ref[0] = strips(gbuf, 0, LEAD)
     spill_ref[1] = strips(gbuf, LEAD + length, LEAD)
-
+    return d_score_vec
+
+
+def put_small(small_ref, vectors, tab_ref, share_ref):
     small_ref[...] = jnp.zeros_like(small_ref)
-    for row, vector in ((0, d_score_vec), (6, d_gain1), (12, dgain2_ref[...])):
-        for j in range(width // 128):
+    for row, vector in zip((0, 6, 12), vectors):
+        for j in range(6):
             small_ref[row + j : row + j + 1, :] = vector[:, j * 128 : j * 128 + 128]
     heads = tab_ref.shape[0]
     group = lax.axis_index("blk") // (lax.axis_size("blk") // GROUPS)
@@ -1285,51 +1266,63 @@
         small_ref[pl.ds(18 + group * heads + h, 1), 0:BUCKETS] = total[0:1]
     small_ref[30:31, :] = share_ref[...]
 
-    if with_blocks:
-        (whole,) = grads
-        n1_t = n1_ref[...].T
-        for j, part in enumerate((dq, dk, dv)):
-            whole[j] = mxu(n1_t, part)
-        per = width // w_ref.shape[0]
-
-        def block(d, _):
-            start = pl.multiple_of(d * per, 8)
-            parts = [whole[j, pl.ds(start, per), :] for j in range(3)]
-            parts.append(jnp.zeros((w_ref.shape[1] - 3 * per, width), jnp.float32))
-            w_ref[d] = jnp.concatenate(parts, axis=0).astype(jnp.bfloat16)
-            return 0
-
-        lax.fori_loop(0, w_ref.shape[0], block, 0)
-    else:
-        w_ref[0] = dq
-        w_ref[1] = dk
-        w_ref[2] = dv
-
-
-def last_part(devices, dq, dkv, hidden, dres, n1, x, before, after, labels, y, score, gain, wq, wk, wv, dgain2, share, tab):
+
+def last_kernel(shards, axes, order, dq_ref, dkv_ref, hidden_ref, dres_ref, x_ref, before_ref, after_ref, lab_ref, y_ref, score_ref,
+                gain_ref, wq_ref, wk_ref, wv_ref, dgain2_ref, share_ref, tab_ref, gb_ref, edge_ref, spill_out, small_out, parts_ref,
+                w_send, w_recv, s_send, s_recv, xs, gbuf, spill_ref, small_ref, small_bufs):
+    at = {"dp": lax.axis_index("dp"), "blk": lax.axis_index("blk")}
+    width = hidden_ref.shape[1]
+    whole = Whole(axes, at, order, small_ref, small_bufs, small_out, w_send, w_recv)
+    left = (at["dp"], (at["blk"] + shards - 1) % shards)
+    right = (at["dp"], (at["blk"] + 1) % shards)
+    greet([whole.stream.target(p) for p in range(len(axes))] + [left, right])
+    load_bytes(x_ref, before_ref, after_ref, xs)
+    dq = get_packed(dq_ref)
+    dk, dv = unpack_pairs(dkv_ref, width)
+    parts_ref[0], parts_ref[1], parts_ref[2] = dq, dk, dv
+    d_n1 = mxu(dq, wq_ref[...], NT) + mxu(dk, wk_ref[...], NT) + mxu(dv, wv_ref[...], NT)
+    d_rows, d_gain1 = norm_back(d_n1, hidden_ref[...], gain_ref[...].astype(jnp.float32))
+    d_hidden = dres_ref[...] + d_rows
+    d_score = pool_back(d_hidden, (x_ref, before_ref, after_ref), lab_ref, y_ref, score_ref, gb_ref, edge_ref, spill_ref, xs, gbuf)
+    put_small(small_ref, (d_score, d_gain1, dgain2_ref[...]), tab_ref, share_ref)
+    spills = [
+        remote(spill_ref.at[0], spill_out.at[1], s_send.at[0], s_recv.at[1], left),
+        remote(spill_ref.at[1], spill_out.at[0], s_send.at[1], s_recv.at[0], right),
+    ]
+    whole.copy(0).start()
+    for copy in spills:
+        copy.start()
+    for stage in range(len(axes)):
+        advance(whole, stage)
+    for copy in spills:
+        copy.wait()
+
+
+def last_part(shape, dq, dkv, hidden, dres, x, before, after, labels, y, score, gain, wq, wk, wv, dgain2, share, tab):
     tokens, width = hidden.shape
     length = x.shape[0]
-    with_blocks = devices <= 32
-    full = jax.ShapeDtypeStruct
-    blocks = (devices, -(-3 * (width // devices) // 16) * 16, width) if with_blocks else (3, tokens, width)
-    scratch = [pltpu.VMEM((width // 128, length + 2 * LEAD, 128), jnp.float32)] * 2
-    if with_blocks:
-        scratch.append(pltpu.VMEM((3, width, width), jnp.float32))
+    axes = bit_axes(shape)
+    ndim = len(axes)
+    full, sem, low = jax.ShapeDtypeStruct, pltpu.SemaphoreType.DMA, jnp.bfloat16
+    strip = pltpu.VMEM((width // 128, length + 2 * LEAD, 128), jnp.float32)
     return pl.pallas_call(
-        functools.partial(last_kernel, with_blocks),
+        functools.partial(last_kernel, shape["blk"], axes, tuple(reversed(range(ndim)))),
         out_shape=(
-            full((length, width), jnp.bfloat16),
+            full((length, width), low),
             full((2, 16, width), jnp.float32),
             full((2, LEAD, width), jnp.float32),
             full((32, 128), jnp.float32),
-            full(blocks, jnp.bfloat16),
+            full((3, tokens, width), low),
         ),
-        in_specs=[VMEM_SPEC] * 18,
+        in_specs=[VMEM_SPEC] * 17,
         out_specs=(VMEM_SPEC,) * 5,
-        scratch_shapes=scratch,
-        compiler_params=pltpu.CompilerParams(vmem_limit_bytes=VMEM_BYTES),
+        scratch_shapes=[
+            sem((ndim,)), sem((ndim,)), sem((2,)), sem((2,)), strip, strip,
+            pltpu.VMEM((2, LEAD, width), jnp.float32), pltpu.VMEM((32, 128), jnp.float32), pltpu.VMEM((2, ndim, 32, 128), jnp.float32),
+        ],
+        compiler_params=pltpu.CompilerParams(collective_id=3, has_side_effects=True, vmem_limit_bytes=VMEM_BYTES),
         name="last_part",
-    )(dq, dkv, hidden, dres, n1, x, before, after, labels, y, score, gain, wq, wk, wv, dgain2, share, tab)
+    )(dq, dkv, hidden, dres, x, before, after, labels, y, score, gain, wq, wk, wv, dgain2, share, tab)
 
 
 def finish_kernel(shards, heads_all, gb_ref, edge_ref, spill_ref, small_ref, *refs):
@@ -1345,31 +1338,33 @@
     bytes_ref[length - 16 :, :] = (edge_ref[1] + jnp.concatenate([zero, right], axis=0)).astype(jnp.bfloat16)
     for row, ref in ((0, score_ref), (6, gain1_ref), (12, gain2_ref)):
         for j in range(6):
-            ref[:, j * 128 : j * 128 + 128] = small_ref[row + j : row + j + 1, :]
+            ref[j * 128 : j * 128 + 128] = small_ref[row + j, :]
     tab_ref[...] = small_ref[16:32, :]
     if streams:
         gq, gk, gv, go, gg, gu, gd = outs[5:]
-        per = gq.shape[0]
-        wide_a, wide_b, slim, *thirds = streams
-        for j, ref in enumerate((gq, gk, gv)):
-            for c, third in enumerate(thirds):
-                ref[:, c * 256 : c * 256 + 256] = third[j * per : j * per + per, :]
-        half = wide_a.shape[1]
-        for c, ref in ((0, wide_a), (1, wide_b)):
-            gg[:, c * half : c * half + half] = ref[0:per, :]
-            gu[:, c * half : c * half + half] = ref[per : 2 * per, :]
-        go[...] = slim[0:per, :]
-        gd[...] = slim[32:, :]
+        per, width = gq.shape
+        half, ff = width // 2, gg.shape[1]
+        one, two, down, *thirds = streams
+        for ref, third in zip((gq, gk, gv), thirds):
+            ref[:, :half] = third[:per, :]
+            ref[:, half:] = third[per:, :]
+        first = one.shape[1]
+        for ref, rows in ((gg, slice(0, per)), (gu, slice(per, 2 * per))):
+            ref[:, :first] = one[rows, :]
+            ref[:, first:] = two[rows, : ff - first]
+        go[:, :half] = two[:per, ff - first :]
+        go[:, half:] = two[per:, ff - first :]
+        gd[...] = down[...]
 
 
 def finish(shards, heads_all, per, ff, gb, edge, spill, small, streams):
     width = gb.shape[1]
     full = jax.ShapeDtypeStruct
-    line = full((1, width), jnp.float32)
+    line = full((width,), jnp.float32)
     outs = [full(gb.shape, jnp.bfloat16), line, line, line, full((16, 128), jnp.float32)]
     if streams:
         square, broad = full((per, width), jnp.float32), full((per, ff), jnp.float32)
-        outs += [square] * 4 + [broad] * 2 + [full((streams[2].shape[0] - 32, width), jnp.float32)]
+        outs += [square] * 4 + [broad] * 2 + [full((streams[2].shape[0], width), jnp.float32)]
     return pl.pallas_call(
         functools.partial(finish_kernel, shards, heads_all),
         out_shape=tuple(outs),
@@ -1378,6 +1373,441 @@
         compiler_params=pltpu.CompilerParams(vmem_limit_bytes=VMEM_BYTES),
         name="finish",
     )(gb, edge, spill, small, *streams)
+
+
+class NearRows:
+    def __init__(self, grid, first):
+        self.grid, self.first, self.shape = grid, first, grid.shape
+
+    def __getitem__(self, index):
+        h, rows = index
+        return self.grid[h, pl.ds(pl.multiple_of(self.first + rows.start, 32), rows.size)]
+
+
+class Refs:
+    def __init__(self, names, refs):
+        for name, ref in zip(names, refs, strict=True):
+            setattr(self, name, ref)
+
+
+wide = lambda value: value.astype(jnp.float32)
+slim = lambda value: value.astype(jnp.bfloat16)
+
+
+class DenseBack:
+    def __init__(self, place, r):
+        self.place, self.r = place, r
+        self.heads = r.lse.shape[2]
+        self.tokens = TQ
+        self.across, self.core_to, self.row_to = place.other_rest(2), place.other_rest(1), place.other_row()
+        self.y, self.core = bit(place.rest, 2), place.rest % 2
+        self.s_core = remote(r.dkvs_hbm.at[:, :, 1 - self.core], r.s_in, r.s_send, r.s_recv, self.core_to)
+        self.own_rows = pltpu.make_async_copy(r.dkvs_hbm.at[:, :, self.core], r.dkvs, r.own_sem)
+        self.near_rows = pltpu.make_async_copy(r.nears_hbm, r.nears, r.near_sem)
+
+    def group_of(self, n):
+        return (self.place.group + 1 + n) % GROUPS
+
+    def tile_start(self, m):
+        place_y = jnp.where(m % 2 == 0, 1 - self.y, self.y)
+        return pl.multiple_of((self.group_of(m // 2) * 2 + place_y) * TK, TK)
+
+    def fetch(self, m):
+        r = self.r
+        return pltpu.make_async_copy(r.kv_hbm.at[:, pl.ds(self.tile_start(m), TK)], r.kv.at[m % 4], r.kv_sem.at[m % 4])
+
+    def prepare(self):
+        r = self.r
+        for m in range(4):
+            self.fetch(m).start()
+        self.own_rows.start()
+        self.near_rows.start()
+        self.dense = r.bounds[0, 0, 6]
+        self.mine_dense = self.dense == self.place.row
+        for i in range(2):
+            for h, tile in enumerate(spread_lanes(r.q[self.dense, i], False)):
+                r.qp[i, h] = tile
+            for h, tile in enumerate(spread_lanes(r.do[self.dense, i], True)):
+                r.dp[i, h] = tile
+        r.dqt[...] = jnp.zeros_like(r.dqt)
+        r.grid[...] = jnp.zeros_like(r.grid)
+
+    def core_copy(self, n, j):
+        r = self.r
+        return remote(r.held.at[n, j, 1 - self.core], r.core_in.at[n, j], r.core_send.at[n, j], r.core_recv.at[n, j], self.core_to)
+
+    def x_copy(self, n, j):
+        r = self.r
+        return remote(r.x_out.at[n, j], r.x_in.at[n, j], r.x_send.at[n, j], r.x_recv.at[n, j], self.row_to)
+
+    def y_copy(self, n, j):
+        r = self.r
+        return remote(r.y_out.at[n, j], r.y_in.at[n, j], r.y_send.at[n, j], r.y_recv.at[n, j], self.across)
+
+    def z_copy(self, n):
+        r, place = self.r, self.place
+        return remote(r.z_out.at[n], r.dkv_home.at[place.group], r.z_send.at[n], r.z_recv.at[n], place.at(place.row, self.group_of(n), place.rest))
+
+    def by_rows(self, one):
+        def step(k, _):
+            one(pl.ds(pl.multiple_of(k * 32, 32), 32))
+            return 0
+        lax.fori_loop(0, self.tokens // 32, step, 0)
+
+    def own_sum(self, n, j, rows):
+        return wide(self.r.held[n, j, self.core, rows]) + wide(self.r.core_in[n, j, rows])
+
+    def split_rows(self, one, two):
+        return slim(jnp.where(self.mine_dense, two, one)), slim(jnp.where(self.mine_dense, one, two))
+
+    def other_sums(self):
+        r = self.r
+        self.s_core.wait()
+        self.own_rows.wait()
+
+        def one(step, _):
+            n, far = step // 2, step % 2
+            row = jnp.where(far == 0, 1 - self.y, self.y)
+            group = self.group_of(n)
+
+            def some(rows):
+                r.s_in[group, row, rows] = slim(wide(r.dkvs[group, row, rows]) + wide(r.s_in[group, row, rows]))
+
+            self.by_rows(some)
+            pl.when(jnp.logical_and(far == 0, n % 2 == 0))(self.y_other(n).start)
+            return 0
+
+        lax.fori_loop(0, 2 * GROUPS, one, 0)
+
+    def other(self, n, j):
+        return self.r.s_in.at[self.group_of(n), 1 - self.y if j == 0 else self.y]
+
+    def y_other(self, n):
+        r = self.r
+        return remote(self.other(n, 0), r.y_in.at[n, 1], r.y_send.at[n, 1], r.y_recv.at[n, 1], self.across)
+
+    def y_first_1(self, n):
+        r = self.r
+        self.core_copy(n, 0).wait()
+
+        def one(rows):
+            r.y_out[n, 0, rows] = slim(self.own_sum(n, 0, rows))
+
+        self.by_rows(one)
+        self.y_copy(n, 0).start()
+
+    def y_first_3(self, n):
+        r = self.r
+        self.core_copy(n, 1).wait()
+        self.y_other(n).wait()
+        self.y_copy(n, 0).wait()
+
+        def one(rows):
+            first = self.own_sum(n, 1, rows) + wide(r.y_in[n, 0, rows])
+            second = wide(self.other(n, 1)[rows]) + wide(r.y_in[n, 1, rows])
+            r.x_out[n, 0, rows], r.kept[n, 0, rows] = self.split_rows(first, second)
+
+        self.by_rows(one)
+        self.x_copy(n, 0).start()
+
+    def y_first_5(self, n):
+        r = self.r
+        self.x_copy(n, 0).wait()
+
+        def one(rows):
+            r.z_out[n, rows] = slim(wide(r.kept[n, 0, rows]) + wide(r.x_in[n, 0, rows]))
+
+        self.by_rows(one)
+        self.z_copy(n).start()
+
+    def x_first_1(self, n, j=0):
+        r = self.r
+        self.core_copy(n, j).wait()
+
+        def one(rows):
+            r.x_out[n, j, rows], r.kept[n, j, rows] = self.split_rows(self.own_sum(n, j, rows), wide(self.other(n, j)[rows]))
+
+        self.by_rows(one)
+        self.x_copy(n, j).start()
+
+    def x_first_2(self, n):
+        self.x_first_1(n, 1)
+
+    def x_first_3(self, n):
+        r = self.r
+        self.x_copy(n, 0).wait()
+
+        def one(rows):
+            r.y_out[n, 0, rows] = slim(wide(r.kept[n, 0, rows]) + wide(r.x_in[n, 0, rows]))
+
+        self.by_rows(one)
+        self.y_copy(n, 0).start()
+
+    def x_first_5(self, n):
+        r = self.r
+        self.x_copy(n, 1).wait()
+        self.y_copy(n, 0).wait()
+
+        def one(rows):
+            total = slim(wide(r.kept[n, 1, rows]) + wide(r.x_in[n, 1, rows]) + wide(r.y_in[n, 0, rows]))
+            if n == GROUPS - 1:
+                r.dkv_home[self.place.group, rows] = total
+            else:
+                r.z_out[n, rows] = total
+
+        self.by_rows(one)
+        if n < GROUPS - 1:
+            self.z_copy(n).start()
+
+    def tile(self, m):
+        r, place, heads = self.r, self.place, self.heads
+        n, j = m // 2, m % 2
+        t = self.tile_start(m) // TK
+        self.fetch(m).wait()
+        r.acc[...] = jnp.zeros_like(r.acc)
+        r.keys[...] = jnp.where(self.dense == 0, r.kv[m % 4, 0], r.kv[m % 4, 1])
+        keys = lambda h: r.keys[:, h * 128 : h * 128 + 128]
+        for h in range(heads):
+            r.kt[h, 0:64] = keys(h).T[0:64]
+            r.kt[h, 64:80] = jnp.ones((16, TK), jnp.bfloat16)
+
+        def part(i, _):
+            first = ((2 * place.row + i) * place.rest_size + place.rest) * self.tokens
+            slot = jnp.clip(t - (first // TK - 1 + self.core) + 1, 0, 3)
+            away = jnp.logical_or(slot == 0, slot == 3)
+
+            def finish(h, p, ds, where):
+                ds_low = ds.astype(jnp.bfloat16)
+                two = jnp.concatenate([ds_low, p.astype(jnp.bfloat16)], axis=1)
+                both = jnp.concatenate([r.qp[i, h], r.dp[i, h]], axis=0)
+                r.acc[:, h * 128 : h * 128 + 128] += mxu(two, both)
+                r.dqt[i, h, where] += mxu(r.kt[h], ds_low)
+
+            def products(h):
+                return mxu(keys(h), r.qp[i, h], NT), mxu(keys(h), r.dp[i, h], NT)
+
+            @pl.when(away)
+            def _():
+                for h in range(heads):
+                    s, d_probs = products(h)
+                    p = jnp.exp(s - (r.lse[self.dense, i, h] - jnp.where(slot == 0, r.table[h, 15], r.table[h, 31])))
+                    finish(h, p, p * (d_probs - r.delta[self.dense, i, h]), jnp.where(slot == 0, 0, 2))
+
+            @pl.when(jnp.logical_not(away))
+            def _():
+                for h in range(heads):
+                    s, d_probs = products(h)
+                    p = jnp.exp(s + r.bias[h, slot - 1].astype(jnp.float32) - r.lse[self.dense, i, h])
+                    ds = p * (d_probs - r.delta[self.dense, i, h])
+                    r.grid[h, pl.ds(pl.multiple_of((slot - 1) * TK, TK), TK)] += ds
+                    finish(h, p, ds, 1)
+
+            return 0
+
+        lax.fori_loop(0, 2, part, 0)
+        for half in range(2):
+            r.held[n, j, half] = r.acc[half * self.tokens : half * self.tokens + self.tokens].astype(jnp.bfloat16)
+        self.core_copy(n, j).start()
+        pl.when(m < 4)(lambda: self.fetch(m + 4).start())
+
+    def queries(self):
+        r = self.r
+        for i in range(2):
+            parts = []
+            for h in range(self.heads):
+                parts.append((r.dqt[i, h, 0, 0:64] + r.dqt[i, h, 1, 0:64] + r.dqt[i, h, 2, 0:64]).T * 0.125)
+            mine = join_heads(parts)
+            other = r.dqs[0, i].astype(jnp.float32)
+            for row in range(2):
+                r.dq_rows[row, i] = jnp.where(self.dense == row, mine, other).astype(jnp.bfloat16)
+
+    def buckets(self):
+        r = self.r
+        self.near_rows.wait()
+        first = near_start(self.core)
+        for h in range(self.heads):
+            r.side[h, 0:1] = r.dqt[0, h, 0, 64:65] + r.dqt[1, h, 0, 64:65] + r.sides[h, 0:1] + far_sums(r.grid, h, 0, first)
+            r.side[h, 1:2] = r.dqt[0, h, 2, 64:65] + r.dqt[1, h, 2, 64:65] + r.sides[h, 1:2] + far_sums(r.grid, h, first + NEAR_ROWS, 2 * TK)
+            rows = pl.ds(pl.multiple_of(first, 32), NEAR_ROWS)
+            r.grid[h, rows] += r.nears[h]
+        bucket_sums(self.core, NearRows(r.grid, first), r.side, r.tab, r.tab8)
+
+    def wait_home(self):
+        r, place = self.r, self.place
+        for n in range(GROUPS - 1):
+            there = r.dkv_home.at[(place.group - 1 - n + GROUPS) % GROUPS]
+            remote(r.z_out.at[n], there, r.z_send.at[n], r.z_recv.at[n], self.row_to).wait()
+
+
+def back_kernel(shards, axes, names, plans, *refs):
+    r = Refs(names, refs)
+    place = Place(shards)
+    at = {"dp": place.dp, "blk": place.blk}
+    tokens, width = r.hidden.shape
+    back = DenseBack(place, r)
+    streams = []
+    for s, (kept, order) in enumerate(plans):
+        bufs = [getattr(r, "buf%d_%d" % (s, k)) for k in range(len(order))]
+        streams.append(Stream(axes, at, kept, order, getattr(r, "src%d" % s), bufs, getattr(r, "sum%d" % s), r.w_send.at[s], r.w_recv.at[s]))
+    early, late = streams[:3], streams[3:]
+    whole = Whole(axes, at, (4, 0, 3, 2, 1), r.small, r.small_bufs, r.small_out, r.w_send.at[len(plans)], r.w_recv.at[len(plans)])
+    left, right = (place.dp, (place.blk + shards - 1) % shards), (place.dp, (place.blk + 1) % shards)
+
+    met = hail(line_and_row(place) + [back.across, back.core_to, left, right])
+    fetches = [pltpu.make_async_copy(getattr(r, "came%d_hbm" % s), early[s].src, r.came_sem.at[s]) for s in range(3)]
+    for copy in fetches:
+        copy.start()
+    back.prepare()
+    for s in range(3):
+        fetches[s].wait()
+        add_two(early[s].src, early[s].src, getattr(r, "keep%d" % s))
+    await_all(met)
+    back.s_core.start()
+    for stream in early:
+        stream.copy(0).start()
+
+    def step(m, _):
+        back.tile(m)
+        pl.when(m == 0)(back.other_sums)
+        for when, n, action in (
+            (1, 0, back.y_first_1), (3, 1, back.x_first_1), (4, 1, back.x_first_2), (5, 2, back.y_first_1),
+            (6, 0, back.y_first_3), (6, 1, back.x_first_3), (7, 3, back.x_first_1),
+        ):
+            pl.when(m == when)(functools.partial(action, n))
+        return 0
+
+    lax.fori_loop(0, 2 * GROUPS, step, 0)
+    back.x_first_2(3)
+    back.queries()
+    return_heads(place, r.dq_rows, r.dq_home, r.q_send, r.q_recv)
+    for stream in early:
+        advance(stream, 0)
+    back.y_first_5(0)
+    back.x_first_3(3)
+    back.x_first_5(1)
+    back.y_first_3(2)
+    back.buckets()
+    for stream in early:
+        advance(stream, 1)
+    back.y_first_5(2)
+    back.x_first_5(3)
+    load_bytes(r.x, r.before, r.after, r.xs)
+    n1_t = r.n1[...].T
+    return_heads_wait(place, r.dq_rows, r.dq_home, r.q_send, r.q_recv)
+    dq = get_packed(r.dq_home)
+    devices = 1 << len(axes)
+    per = width // devices
+    half = width // 2
+
+    def weights(stream, part):
+        r.total[...] = mxu(n1_t, part)
+
+        def block(d, _):
+            rows = pl.ds(pl.multiple_of(d * per, 8), per)
+            index, rest = [], d
+            for _ in axes:
+                index.append(rest % 2)
+                rest = rest // 2
+            part = r.total[rows, :]
+            stream.src[tuple(reversed(index))] = jnp.concatenate([part[:, :half], part[:, half:]], axis=0).astype(jnp.bfloat16)
+            return 0
+
+        lax.fori_loop(0, devices, block, 0)
+        stream.copy(0).start()
+
+    weights(late[0], dq)
+    back.wait_home()
+    dk, dv = unpack_pairs(r.dkv_home, width)
+    weights(late[1], dk)
+    weights(late[2], dv)
+    d_n1 = mxu(dq, r.wq[...], NT) + mxu(dk, r.wk[...], NT) + mxu(dv, r.wv[...], NT)
+    d_rows, d_gain1 = norm_back(d_n1, r.hidden[...], r.gain[...].astype(jnp.float32))
+    d_hidden = r.dres[...] + d_rows
+    for stream in late:
+        advance(stream, 0)
+    for stream in early:
+        advance(stream, 2)
+    d_score = pool_back(d_hidden, (r.x, r.before, r.after), r.labels, r.y, r.score, r.gb, r.edge, r.spill, r.xs, r.gbuf)
+    put_small(r.small, (d_score, d_gain1, r.dgain2[...]), r.tab, r.share)
+    whole.copy(0).start()
+    spills = [
+        remote(r.spill.at[0], r.spill_out.at[1], r.s2_send.at[0], r.s2_recv.at[1], left),
+        remote(r.spill.at[1], r.spill_out.at[0], r.s2_send.at[1], r.s2_recv.at[0], right),
+    ]
+    for copy in spills:
+        copy.start()
+    for stage in range(1, len(axes)):
+        for stream in late:
+            advance(stream, stage)
+        advance(whole, stage - 1)
+    advance(whole, len(axes) - 1)
+    for copy in spills:
+        copy.wait()
+
+
+def back_and_last(shape, halves, inputs):
+    shards = shape["blk"]
+    axes = bit_axes(shape)
+    ndim = len(axes)
+    named = dict(inputs)
+    kv, q, hidden = named["kv_hbm"], named["q"], named["hidden"]
+    heads, n, width = kv.shape[2] // 128, kv.shape[1], kv.shape[2]
+    tokens, features = hidden.shape
+    length = named["x"].shape[0]
+    f32, low, sem = jnp.float32, jnp.bfloat16, pltpu.SemaphoreType.DMA
+    chunk = (tokens, width)
+    every = (0, 1, 2, 3, 4)
+    plans = [
+        ((1, 2, 3), (3, 2, 1)), ((0, 1, 2), (2, 0, 1)), ((0, 1, 3), (0, 3, 1)),
+        (every, (4, 0, 3, 2, 1)), (every, (4, 3, 2, 0, 1)), (every, (4, 2, 0, 3, 1)),
+    ]
+    own = (2 * (features // (1 << ndim)), features // 2)
+    blocks = [h.shape[-2:] for h in halves[::2]] + [own] * 3
+    ins = list(inputs)
+    for s in range(3):
+        for k, kind in enumerate(("keep%d", "came%d_hbm")):
+            part = halves[2 * s + k]
+            ins.append((kind % s, part.reshape((2, 2, 2) + part.shape[-2:])))
+    spec_of = lambda name: pl.BlockSpec(memory_space=pl.ANY) if name.endswith("_hbm") else SMEM_SPEC if name in ("bounds", "table") else VMEM_SPEC
+    outs = [
+        ("gb", (length, features), low), ("edge", (2, 16, features), f32), ("spill_out", (2, LEAD, features), f32),
+        ("small_out", (32, 128), f32),
+    ] + [("sum%d" % s, block, f32) for s, block in enumerate(blocks)]
+    mem = lambda shape, dtype=low: pltpu.VMEM(shape, dtype)
+    pairs, fours = sem((GROUPS, 2)), sem((GROUPS,))
+    strip = mem((features // 128, length + 2 * LEAD, 128), f32)
+    scratch = [
+        ("kt", mem((heads, 80, TK))), ("dqt", mem((2, heads, 3, 80, TQ), f32)), ("acc", mem((TK, width), f32)),
+        ("grid", mem((heads, 2 * TK, TQ), f32)), ("side", mem((heads, 2, TQ), f32)), ("tab8", mem((heads, BUCKETS, 8, TQ), f32)),
+        ("tab", mem((heads, BUCKETS, TQ), f32)),
+        ("qp", mem((2, heads, TQ, 128))), ("dp", mem((2, heads, TQ, 128))),
+        ("kv", mem((4, 2, TK, width))), ("keys", mem((TK, width))), ("dkvs", mem((GROUPS, 2) + chunk)), ("nears", mem((heads, NEAR_ROWS, TQ), f32)),
+        ("held", mem((GROUPS, 2, 2) + chunk)), ("core_in", mem((GROUPS, 2) + chunk)), ("s_in", mem((GROUPS, 2) + chunk)),
+        ("x_out", mem((GROUPS, 2) + chunk)), ("x_in", mem((GROUPS, 2) + chunk)),
+        ("y_out", mem((GROUPS, 1) + chunk)), ("y_in", mem((GROUPS, 2) + chunk)), ("kept", mem((GROUPS, 2) + chunk)),
+        ("z_out", mem((GROUPS,) + chunk)), ("dkv_home", mem((GROUPS,) + chunk)),
+        ("dq_rows", mem((2, 2) + q.shape[2:])), ("dq_home", mem((GROUPS,) + q.shape[2:])),
+        ("core_send", pairs), ("core_recv", pairs), ("x_send", pairs), ("x_recv", pairs), ("y_send", pairs), ("y_recv", pairs),
+        ("z_send", fours), ("z_recv", fours), ("s_send", sem), ("s_recv", sem), ("q_send", fours), ("q_recv", fours),
+        ("kv_sem", fours), ("came_sem", sem((3,))), ("own_sem", sem), ("near_sem", sem),
+        ("w_send", sem((len(plans) + 1, ndim))), ("w_recv", sem((len(plans) + 1, ndim))), ("s2_send", sem((2,))), ("s2_recv", sem((2,))),
+        ("xs", strip), ("gbuf", strip), ("spill", mem((2, LEAD, features), f32)), ("small", mem((32, 128), f32)),
+        ("small_bufs", mem((2, ndim, 32, 128), f32)), ("total", mem((features, features), f32)),
+    ]
+    for s, ((kept, order), block) in enumerate(zip(plans, blocks)):
+        scratch.append(("src%d" % s, mem((2,) * len(kept) + block)))
+        for k, buf in enumerate(stream_scratch(len(kept), order, *block)):
+            scratch.append(("buf%d_%d" % (s, k), buf))
+    names = [name for name, _ in ins] + [name for name, _, _ in outs] + [name for name, _ in scratch]
+    return pl.pallas_call(
+        functools.partial(back_kernel, shards, axes, names, plans),
+        out_shape=tuple(jax.ShapeDtypeStruct(shape, dtype) for _, shape, dtype in outs),
+        in_specs=[spec_of(name) for name, _ in ins],
+        out_specs=(VMEM_SPEC,) * len(outs),
+        scratch_shapes=[kind for _, kind in scratch],
+        compiler_params=pltpu.CompilerParams(collective_id=6, has_side_effects=True, vmem_limit_bytes=VMEM_BYTES),
+        name="back_and_last",
+    )(*[array for _, array in ins])
 
 
 def neighbours(rows):
@@ -1453,66 +1883,68 @@
             -(-jnp.max(span[:, :, 0], axis=-1) // TK),
             jnp.min(span[:, :, 1], axis=-1) // TK,
             jnp.broadcast_to(parity, (2, 2)),
+            jnp.broadcast_to((labels_all[0, -1] > 0).astype(jnp.int32), (2, 2)),
         ],
         axis=-1,
     ).astype(jnp.int32)
     table = lax.dynamic_slice_in_dim(rel_bias.astype(jnp.float32).T, group * heads, heads, 0)
 
-    o_packed, o_kept, log_total, bias_tiles = attention(bounds, table, q_all, kv_all, span)
+    o_packed, o_kept, log_total, bias_tiles, near_bias = attention(bounds, table, q_all, kv_all, span)
     o_home = move_heads(return_kernel, (GROUPS,), shards, 4, o_packed)
     ct = cotangent[0]
     block_out, d_res, da_packed, d_gain2, n2, att, act, d_gate, d_up, d_branch = feed_forward(
         o_home, hidden, ct, gain2, w_out, w_gate, w_up, w_down
     )
 
-    orders, pairs = [], []
     if devices == 32:
         do_all, keep_a, send_a, keep_b, send_b, keep_c, send_c = spread_and_weights(
             shards, da_packed, n2, att, act, d_gate, d_up, ct, d_branch
         )
         swap = lambda part, axis, mask: lax.ppermute(part, axis, [(i, i ^ mask) for i in range(lax.axis_size(axis))])
-        orders = [((1, 2, 3), (3, 2, 1)), ((0, 1, 2), (0, 2, 1)), ((0, 1, 3), (3, 0, 1))]
-        pairs = [(keep_a, swap(send_a, "dp", 1)), (keep_b, swap(send_b, "blk", 2)), (keep_c, swap(send_c, "blk", 4))]
+        halves = [keep_a, swap(send_a, "dp", 1), keep_b, swap(send_b, "blk", 2), keep_c, swap(send_c, "blk", 4)]
+        dq_other, dkv_other, near_other, side_other, deltas = attention_back(
+            True, bounds, table, q_all, do_all, o_kept, kv_all, bias_tiles, span, log_total
+        )
+        grad_bytes, edge, spill, small, *sums = back_and_last(
+            shape,
+            halves,
+            (
+                ("bounds", bounds), ("table", table), ("q", q_all), ("do", do_all), ("delta", deltas), ("kv_hbm", kv_all),
+                ("bias", near_bias), ("lse", log_total), ("dqs", dq_other),
+                ("dkvs_hbm", dkv_other.reshape((GROUPS, 2, 2) + kv_parts.shape[1:])), ("nears_hbm", near_other), ("sides", side_other),
+                ("hidden", hidden), ("dres", d_res), ("n1", n1), ("x", x), ("before", before), ("after", after),
+                ("labels", labels), ("y", y), ("score", score_row), ("gain", gain1), ("wq", w_query), ("wk", w_key),
+                ("wv", w_value), ("dgain2", d_gain2), ("share", share),
+            ),
+        )
     else:
         do_all = move_heads(spread_kernel, (2, 2), shards, 5, da_packed)
-
-    dq_packed, dkv_all, d_table_lanes = attention_back(
-        bounds, table, q_all, do_all, o_kept, kv_all, bias_tiles, span, log_total
-    )
-    dq_home, dkv_home, *sums = reduce_all(shape, dq_packed, dkv_all, orders, pairs)
-    grad_bytes, edge, spill, small, last_blocks = last_part(
-        devices, dq_home, dkv_home, hidden, d_res, n1, x, before, after, labels, y, score_row, gain1,
-        w_query, w_key, w_value, d_gain2, share, d_table_lanes,
-    )
-    across = len(bits_of(shape["dp"]))
-    ndim = across + len(bits_of(shards))
-    small_order = tuple(reversed(range(ndim)))
-    if devices == 32:
-        third = width // 3
-        blocks = [last_blocks[:, :, c * third : c * third + third] for c in range(3)]
-        thirds, small, spill = last_sums(
-            shape, blocks, [(4, 0, 3, 2, 1), (4, 3, 2, 1, 0), (4, 2, 0, 3, 1), small_order], small, spill
+        dq_packed, dkv_all, _, _, _, d_table_lanes = attention_back(
+            False, bounds, table, q_all, do_all, o_kept, kv_all, bias_tiles, span, log_total
         )
-        sums = list(sums) + list(thirds)
-    else:
-        _, small, spill = last_sums(shape, [], [small_order], small, spill)
+        dq_home, dkv_home = reduce_all(shape, dq_packed, dkv_all, [], [])
+        grad_bytes, edge, spill, small, last_parts = last_part(
+            shape, dq_home, dkv_home, hidden, d_res, x, before, after, labels, y,
+            score_row, gain1, w_query, w_key, w_value, d_gain2, share, d_table_lanes,
+        )
+        sums = []
     per = width // devices
     grad_bytes, g_score, g_gain1, g_gain2, rows, *grads = finish(
         shards, rel_bias.shape[1], per, w_gate.shape[1], grad_bytes, edge, spill, small, sums
     )
     if devices != 32:
         product = lambda left, right: jnp.einsum("td,te->de", left, right, preferred_element_type=jnp.float32)
-        grads = [product(n1, last_blocks[j]) for j in range(3)]
+        grads = [product(n1, last_parts[j]) for j in range(3)]
         grads += [product(att, d_branch), product(n2, d_gate), product(n2, d_up), product(act, ct)]
         grads = [lax.psum_scatter(grad, ("dp", "blk"), scatter_dimension=0, tiled=True) for grad in grads]
     return (
         block_out[None],
         grad_bytes[None],
-        g_score[0],
-        g_gain1[0],
+        g_score,
+        g_gain1,
         *grads[:4],
         rows[2 : 2 + rel_bias.shape[1], :BUCKETS].T,
-        g_gain2[0],
+        g_gain2,
         *grads[4:],
         rows[14, :MAX_BLOCK],
     )

time: 369 us -> 324 us (0.88)
  Pallas kernels: 336 us -> 294 us
  waiting for transfers between devices: 0.01 us -> 6.63 us
  local copies, waits for them, and re-layouts: 16.7 us -> 12.6 us
  other arithmetic: 7.97 us -> 4.14 us
    pallas_call x4 -> x2, Pallas kernels: 172 us -> 137 us  [the longest x1 120 us: back_and_last(): pl.pallas_call(functools.partial(back_kernel, shards, axes, names, plans)...]
    ppermute x3, waiting for transfers between devices: 0.01 us -> 6.62 us  [body(): lax.ppermute(part, axis, [(i, i ^ mask) for i in range(lax.axis_size(axis...]
    pallas_call x1, Pallas kernels: 59.4 us -> 54.2 us  [gather_all(): pl.pallas_call(functools.partial(gather_kernel, shards), out_shape=(jax.S...]
    pallas_call x3 -> x0, other arithmetic: 3.85 us -> none  [finish(): pl.pallas_call(functools.partial(finish_kernel, shards, heads_all), out_s...]
  transfers between devices with their start and end apart: 5 -> 5, of which waited for: 0 -> 3; matrix products, arithmetic and copies ran while one was open for 2% -> 2% of each run, Pallas kernels for 13% -> 5%
where the time goes in v4:
time: 324 us
  Pallas kernels  294 us (91%)
  local copies, waits for them, and re-layouts  12.6 us (4%)
  waiting for transfers between devices  6.63 us (2%)
  starting transfers between devices  4.75 us (1%)
  other arithmetic  4.14 us (1%)
    pallas_call x1, Pallas kernels, back_and_last(): pl.pallas_call(functools.partial(back_kernel, shards, axes, names, plans)...  120 us
    pallas_call x1, Pallas kernels, gather_all(): pl.pallas_call(functools.partial(gather_kernel, shards), out_shape=(jax.S...  54.2 us
    pallas_call x1, Pallas kernels, attention(): pl.pallas_call(fwd_kernel, out_shape=(jax.ShapeDtypeStruct(packed, jnp.bf...  36.5 us
    pallas_call x1, Pallas kernels, spread_and_weights(): pl.pallas_call(functools.partial(weights_kernel, shards), out_shape=(jax....  24 us
    pallas_call x1, Pallas kernels, move_heads(): pl.pallas_call(functools.partial(kernel, shards), out_shape=jax.ShapeDtyp...  20.4 us
    pallas_call x1, Pallas kernels, attention_back(): pl.pallas_call(functools.partial(bwd_kernel, alone), out_shape=(jax.Shape...  16.6 us
    pallas_call x1, Pallas kernels, feed_forward(): pl.pallas_call(feed_kernel, out_shape=(low(width), jax.ShapeDtypeStruct((...  13.1 us
    ppermute x3, waiting for transfers between devices, body(): lax.ppermute(part, axis, [(i, i ^ mask) for i in range(lax.axis_size(axis...  6.62 us
  transfers between devices with their start and end apart: 5, of which 3 were waited for; matrix products, arithmetic and copies ran while one was open for 2% of the time, Pallas kernels for 5%

profile of v4, /device:TPU:0, one launch (start us, length us, event | category | flops | bytes accessed | tf_op | source)
XLA Modules:
  0.0 323.5 jit_solution(7949514216304840577)
XLA Ops:
  0.6 0.7 add_convert_fusion
  1.4 0.7 slice_bitcast_fusion.1
  2.2 2.4 collective-permute-start
  4.6 1.3 collective-permute-start.1
  6.0 1.3 convert_bitcast_fusion.table.refs_1_
  7.3 0.9 slice.71
  8.2 1.3 broadcast_in_dim.66.score_ref.refs_20_
  9.5 1.3 broadcast_in_dim.67.gain_ref.refs_21_
  10.8 0.6 pad.18.label_ref
  11.4 1.3 broadcast_in_dim.74.gain_ref
  13.1 0.6 pad_add_fusion.lab_ref.refs_18_
  13.7 6.1 %pool_and_project.1 = (f32[256,768]{1,0:T(8,128)}, bf16[256,768]{1,0:T(8,128)(2,1)}, f32[8,256]{1,0:T(8,128)}, f32[1,128]{1,0:T(1,128)}, bf16[4,384,128]{2,1,0:T(8,128)(2,1)}, /*index=5*/bf16[4,256,384]{2,1,0:T(8,128)(2,1)}) custom-call(bf16[512,768]{1,0:T(8,128)(2,1)} %bitcast.36, bf16[3,768]{1,0:T(4,128)(2,1)} %copy-done.3, bf16[3,768]{1,0:T(4,128)(2,1)} %copy-done.4, ...), custom_call_target="tpu_custom_call" | custom-call | tf_op jit(solution)/shard_map/pool_and_project/pallas_call | solution.py:1111
  19.8 54.2 %gather_keys.1 = (bf16[2,2,384,128]{3,2,1,0:T(8,128)(2,1)}, bf16[2,4096,384]{2,1,0:T(8,128)(2,1)}, s32[2,2,2,2,2,8,128]{6,5,4,3,2,1,0:T(8,128)}) custom-call(bf16[4,384,128]{2,1,0:T(8,128)(2,1)} %get-tuple-element.72.q_ref, bf16[4,256,384]{2,1,0:T(8,128)(2,1)} %get-tuple-element.73.kv_ref, s32[8,128]{1,0:T(8,128)} %pad.18.label_ref), custom_call_target="tpu_custom_call" | custom-call | tf_op jit(solution)/shard_map/gather_keys/pallas_call | solution.py:280
  74.0 0.9 slice.82
  74.9 0.6 slice.83
  77.4 0.6 pad_add_fusion.1.se_ref
  78.0 0.7 stack.44.bounds.refs_0_
  78.7 36.5 %attention.1 = (bf16[2,2,384,128]{3,2,1,0:T(8,128)(2,1)}, f32[2,2,384,128]{3,2,1,0:T(8,128)}, f32[2,2,3,1,256]{4,3,2,1,0:T(1,128)}, bf16[3,4,512,256]{3,2,1,0:T(8,128)(2,1)}, bf16[3,2,512,256]{3,2,1,0:T(8,128)(2,1)}) custom-call(s32[2,2,7]{2,1,0:T(2,128)} %stack.44.bounds.refs_0_, f32[3,32]{1,0:T(4,128)} %convert_bitcast_fusion.table.refs_1_, ...), custom_call_target="tpu_custom_call" | custom-call | tf_op jit(solution)/shard_map/attention/pallas_call | solution.py:777
  115.3 20.4 %move_heads_4.1.o_ref = bf16[4,384,128]{2,1,0:T(8,128)(2,1)} custom-call(bf16[2,2,384,128]{3,2,1,0:T(8,128)(2,1)} %get-tuple-element.77.o_ref), custom_call_target="tpu_custom_call" | custom-call | tf_op jit(solution)/shard_map/move_heads_4/pallas_call | solution.py:177
  135.7 13.1 %feed_forward.1 = (bf16[256,768]{1,0:T(8,128)(2,1)}, f32[256,768]{1,0:T(8,128)}, bf16[4,384,128]{2,1,0:T(8,128)(2,1)}, f32[1,768]{1,0:T(1,128)}, bf16[256,768]{1...) custom-call(bf16[4,384,128]{2,1,0:T(8,128)(2,1)} %move_heads_4.1.o_r, ...), custom_call_target="tpu_custom_call" | custom-call | tf_op jit(solution)/shard_map/feed_forward/pallas_call | solution.py:1188
  148.8 24.0 %spread_and_weights.1 = (bf16[2,2,384,128]{3,2,1,0:T(8,128)(2,1)}, bf16[8,48,1280]{2,1,0:T(8,128)(2,1)}, bf16[8,48,1280]{2,1,0:T(8,128)(2,1)}, bf16[8,48,1152]{2...) custom-call(bf16[4,384,128]{2,1,0:T(8,128)(2,1)} %get-tuple-element.80.da, ...), custom_call_target="tpu_custom_call" | custom-call | tf_op jit(solution)/shard_map/spread_and_weights/pallas_call | solution.py:474
  172.9 0.5 collective-permute-start.2
  173.4 0.6 collective-permute-start.4
  174.0 16.6 %attention_back.1 = (bf16[1,2,384,128]{3,2,1,0:T(8,128)(2,1)}, bf16[1,4096,384]{2,1,0:T(8,128)(2,1)}, f32[3,448,256]{2,1,0:T(8,128)}, f32[3,2,256]{2,1,0:T(2,128)}, f32[2,2,3,1,256]{4,3,2,1,0:T(1,128)}) custom-call(s32[2,2,7]{2,1,0:T(2,128)} %stack.44.bounds.refs_0_, f32[3,32]{1,0:T(4,128)} %convert_bitcast_fusion.table.refs_1_, ...), custom_call_target="tpu_custom_call" | custom-call | tf_op jit(solution)/shard_map/attention_back/pallas_call | solution.py:962
  190.6 2.6 collective-permute-done.4
  193.2 2.1 collective-permute-done.3
  195.3 1.9 collective-permute-done.2
  197.2 0.9 copy-done
  198.1 120.2 %back_and_last.1 = (bf16[512,768]{1,0:T(8,128)(2,1)}, f32[2,16,768]{2,1,0:T(8,128)}, f32[2,8,768]{2,1,0:T(8,128)}, f32[32,128]{1,0:T(8,128)}, f32[48,1280]{1,0:T...) custom-call(s32[2,2,7]{2,1,0:T(2,128)} %stack.44.bounds.refs_0_, ...), custom_call_target="tpu_custom_call" | custom-call | tf_op jit(solution)/shard_map/back_and_last/pallas_call | solution.py:1802
  318.3 2.7 finish.1
  321.0 1.2 slice_bitcast_fusion.5
  322.2 1.3 slice_bitcast_fusion
  (50 shorter events, 1.9 us)
Async XLA Ops:
  2.2 10.5 %collective-permute-start = (bf16[3,768]{1,0:T(4,128)(2,1)S(1)}, bf16[3,768]{1,0:T(4,128)(2,1)S(1)}, u32[]{:S(2)}, u32[]{:S(2)}) collective-permute-start(bf16[3,768]{1,0:T(4,128)(2,1)S(1)} %pad_maximum_fusion), channel_id=1, source_target_pairs={{0,1},{1,2},{2,3},{3,4},{4,5},{5,6},{6,7},{7,8},{8,9},{9,10},{10,1... | collective-permute-start | bytes 13832 | tf_op jit(solution)/shard_map/ppermute | solution.py:1817
  4.6 8.1 %collective-permute-start.1 = (bf16[3,768]{1,0:T(4,128)(2,1)S(1)}, bf16[3,768]{1,0:T(4,128)(2,1)S(1)}, u32[]{:S(2)}, u32[]{:S(2)}) collective-permute-start(bf16[3,768]{1,0:T(4,128)(2,1)S(1)} %pad_maximum_fusion.1), channel_id=1, source_target_pairs={{1,0},{2,1},{3,2},{4,3},{5,4},{6,5},{7,6},{8,7},{9,8},{10,9},{11,1... | collective-permute-start | bytes 13832 | tf_op jit(solution)/shard_map/ppermute | solution.py:1817
  12.6 1.1 copy-start.3
  12.7 1.1 copy-start.4
  172.9 24.3 %collective-permute-start.2 = (bf16[8,48,1280]{2,1,0:T(8,128)(2,1)}, bf16[8,48,1280]{2,1,0:T(8,128)(2,1)S(1)}, u32[]{:S(2)}, u32[]{:S(2)}) collective-permute-start(bf16[8,48,1280]{2,1,0:T(8,128)(2,1)} %get-tuple-element.103), channel_id=1, source_target_pairs={{0,16},{16,0},{1,17},{17,1},{2,18},{18,2},{3,19},{19,3},{4,20},{20... | collective-permute-start | bytes 2949128 | tf_op jit(solution)/shard_map/ppermute | solution.py:1903
  173.4 21.8 %collective-permute-start.3 = (bf16[8,48,1152]{2,1,0:T(8,128)(2,1)}, bf16[8,48,1152]{2,1,0:T(8,128)(2,1)S(1)}, u32[]{:S(2)}, u32[]{:S(2)}) collective-permute-start(bf16[8,48,1152]{2,1,0:T(8,128)(2,1)} %get-tuple-element.105), channel_id=1, source_target_pairs={{0,2},{1,3},{2,0},{3,1},{4,6},{5,7},{6,4},{7,5},{8,10},{9,11},{10,... | collective-permute-start | bytes 2654216 | tf_op jit(solution)/shard_map/ppermute | solution.py:1903
  173.4 19.7 %collective-permute-start.4 = (bf16[8,64,768]{2,1,0:T(8,128)(2,1)}, bf16[8,64,768]{2,1,0:T(8,128)(2,1)S(1)}, u32[]{:S(2)}, u32[]{:S(2)}) collective-permute-start(bf16[8,64,768]{2,1,0:T(8,128)(2,1)} %get-tuple-element.107), channel_id=1, source_target_pairs={{0,4},{1,5},{2,6},{3,7},{4,0},{5,1},{6,2},{7,3},{8,12},{9,13},{10,... | collective-permute-start | bytes 2359304 | tf_op jit(solution)/shard_map/ppermute | solution.py:1903
  193.1 4.0 %copy-start.2 = (bf16[8,64,768]{2,1,0:T(8,128)(2,1)}, bf16[8,64,768]{2,1,0:T(8,128)(2,1)S(1)}, u32[]{:S(2)}) copy-start(bf16[8,64,768]{2,1,0:T(8,128)(2,1)S(1)} %collective-permute-done.4) | copy-start | bytes 2359300
  195.3 1.9 copy-start.1
  197.2 0.9 copy-start

commit v5 on v4

--- a/solution.py
+++ b/solution.py
@@ -117,17 +117,25 @@
             pl.when(at_home)(pltpu.make_async_copy(src, dst, mine).start)
 
 
-def spread_heads_wait(place, q_ref, out_ref, send_sem, recv_sem):
-    at_home = place.group // 2 == place.row
+def spread_heads_come(q_ref, out_ref, recv_sem):
     for row in range(2):
         for slot in range(2):
             pltpu.make_async_copy(q_ref.at[0], out_ref.at[row, slot], recv_sem.at[row * 2 + slot]).wait()
+
+
+def spread_heads_gone(place, q_ref, out_ref, send_sem, recv_sem):
+    at_home = place.group // 2 == place.row
     for step in range(GROUPS):
         copy = remote(q_ref.at[0], out_ref.at[0, 0], send_sem.at[step], recv_sem.at[0], place.other_row())
         if step:
             copy.wait_send()
         else:
             pl.when(jnp.logical_not(at_home))(copy.wait_send)
+
+
+def spread_heads_wait(place, q_ref, out_ref, send_sem, recv_sem):
+    spread_heads_come(q_ref, out_ref, recv_sem)
+    spread_heads_gone(place, q_ref, out_ref, send_sem, recv_sem)
 
 
 def return_heads(place, o_ref, out_ref, send_sem, recv_sem):
@@ -170,6 +178,7 @@
 
 SMEM_SPEC = pl.BlockSpec(memory_space=pltpu.SMEM)
 VMEM_SPEC = pl.BlockSpec(memory_space=pltpu.VMEM)
+ANY_SPEC = pl.BlockSpec(memory_space=pl.ANY)
 
 
 def move_heads(kernel, lead, shards, ident, packed):
@@ -390,13 +399,10 @@
     return [pltpu.VMEM((2,) * (lead - 1 - k) + (rows, cols), jnp.bfloat16) for k in range(len(order))]
 
 
-def weights_kernel(shards, da_ref, n2_ref, att_ref, act_ref, dg_ref, du_ref, ct_ref, db_ref,
-                   do_ref, keep_a, send_a, keep_b, send_b, keep_c, send_c,
-                   q_send, q_recv, core_send, core_recv, gate, up, down, out, wide_out, slim_out, wide_in, slim_in):
-    place = Place(shards)
+def feed_weights(place, n2_ref, att_ref, act_ref, dg_ref, du_ref, ct_ref, db_ref,
+                 keep_a, send_a, keep_b, send_b, keep_c, send_c,
+                 core_send, core_recv, gate, up, down, out, wide_out, slim_out, wide_in, slim_in):
     core_target = place.other_rest(1)
-    greet(line_and_row(place) + [core_target])
-    spread_heads(place, da_ref, do_ref, q_send, q_recv)
     per = gate.shape[0] // 32
     per_ff = down.shape[0] // 32
     first = keep_a.shape[2]
@@ -460,32 +466,6 @@
             ref[j] = (slim_rows(2 * m + core) + slim_in[m].astype(jnp.float32)).astype(jnp.bfloat16)
             return 0
         lax.fori_loop(0, 8, one, 0)
-    spread_heads_wait(place, da_ref, do_ref, q_send, q_recv)
-
-
-def spread_and_weights(shards, da, n2, att, act, dg, du, ct, db):
-    width, ff = n2.shape[1], act.shape[1]
-    per, per_ff = width // 32, ff // 32
-    sem, low = pltpu.SemaphoreType.DMA, jnp.bfloat16
-    wide, slim = (2 * per, ff + width // 2), (per_ff, width)
-    first = (wide[1] // 256 + 1) * 128
-    sums = [jax.ShapeDtypeStruct((8, 2 * per, cols), low) for cols in (first, first, wide[1] - first, wide[1] - first)]
-    sums += [jax.ShapeDtypeStruct((8,) + slim, low)] * 2
-    return pl.pallas_call(
-        functools.partial(weights_kernel, shards),
-        out_shape=(jax.ShapeDtypeStruct((2, 2) + da.shape[1:], da.dtype),) + tuple(sums),
-        in_specs=[VMEM_SPEC] * 8,
-        out_specs=(VMEM_SPEC,) * 7,
-        scratch_shapes=[
-            sem((4,)), sem((4,)), sem((2,)), sem((2,)),
-            pltpu.VMEM((width, ff), jnp.float32), pltpu.VMEM((width, ff), jnp.float32),
-            pltpu.VMEM((ff, width), jnp.float32), pltpu.VMEM((width, width), jnp.float32),
-            pltpu.VMEM((16,) + wide, low), pltpu.VMEM((16,) + slim, low),
-            pltpu.VMEM((16,) + wide, low), pltpu.VMEM((16,) + slim, low),
-        ],
-        compiler_params=pltpu.CompilerParams(collective_id=5, has_side_effects=True, vmem_limit_bytes=VMEM_BYTES),
-        name="spread_and_weights",
-    )(da, n2, att, act, dg, du, ct, db)
 
 
 def reduce_kernel(shards, axes, orders, *refs):
@@ -673,21 +653,30 @@
     return buckets_of(relative)
 
 
-def make_bias(table, parity, bias_ref, near_ref):
-    heads = bias_ref.shape[0]
-    for h in range(heads):
-        bias_ref[h, 0] = jnp.full((TK, TQ), table[h, 15], jnp.float32).astype(jnp.bfloat16)
-        bias_ref[h, 3] = jnp.full((TK, TQ), table[h, 31], jnp.float32).astype(jnp.bfloat16)
-    for tile in range(2):
+def make_bias(table, parity, near_ref, tiles=(0, 1)):
+    heads = near_ref.shape[0]
+    for tile in tiles:
         def rows(step, _):
             start = pl.multiple_of(step * 32, 32)
-            which = near_buckets(tile * TK + start, 32, parity)
-            for h in range(heads):
-                value = jnp.zeros((32, TQ), jnp.float32)
-                for b in range(BUCKETS):
-                    value = jnp.where(which == b, table[h, b], value)
-                bias_ref[h, tile + 1, pl.ds(start, 32)] = value.astype(jnp.bfloat16)
-                near_ref[h, tile, pl.ds(start, 32)] = value.astype(jnp.bfloat16)
+            place = tile * TK + start
+            after = place - near_start(parity)
+            inside = jnp.logical_and(after >= 0, after < NEAR_ROWS)
+
+            @pl.when(inside)
+            def _():
+                which = near_buckets(place, 32, parity)
+                for h in range(heads):
+                    value = jnp.zeros((32, TQ), jnp.float32)
+                    for b in range(BUCKETS):
+                        value = jnp.where(which == b, table[h, b], value)
+                    near_ref[h, tile, pl.ds(start, 32)] = value.astype(jnp.bfloat16)
+
+            @pl.when(jnp.logical_not(inside))
+            def _():
+                for h in range(heads):
+                    value = jnp.where(after < 0, table[h, 15], table[h, 31])
+                    near_ref[h, tile, pl.ds(start, 32)] = jnp.full((32, TQ), value, jnp.float32).astype(jnp.bfloat16)
+
             return 0
         lax.fori_loop(0, TK // 32, rows, 0)
 
@@ -699,22 +688,38 @@
     return slot, jnp.logical_and(away, inside)
 
 
-def fwd_kernel(bounds, table, q_ref, kv_ref, se_ref, o_ref, keep_ref, lse_ref, bias_ref, near_ref, vt, acc, mx, qp):
+def fwd_kernel(alone, bounds, table, q_ref, kv_hbm, se_ref, *refs):
+    if alone:
+        near_ref, o_in, keep_in, lse_in, o_ref, keep_ref, lse_ref, vt, acc, mx, qp, kv_ref, kv_sem = refs
+    else:
+        o_ref, keep_ref, lse_ref, near_ref, vt, acc, mx, qp, kv_ref, kv_sem = refs
+        make_bias(table, bounds[0, 0, 5], near_ref)
     heads = lse_ref.shape[2]
-    make_bias(table, bounds[0, 0, 5], bias_ref, near_ref)
-    for r in range(2):
+    base = 1 - bounds[0, 0, 6] if alone else 0
+
+    def row_body(at, _):
+        r = base + at
+        lo_all = jnp.minimum(bounds[r, 0, 0], bounds[r, 1, 0])
+        hi_all = jnp.maximum(bounds[r, 0, 1], bounds[r, 1, 1])
+
+        def fetch(t):
+            rows = pl.ds(pl.multiple_of(t * TK, TK), TK)
+            return pltpu.make_async_copy(kv_hbm.at[r, rows], kv_ref.at[rows], kv_sem.at[t])
+
+        def begin(t, _):
+            fetch(t).start()
+            return 0
+
+        lax.fori_loop(lo_all, hi_all, begin, 0)
         for i in range(2):
             for h, tile in enumerate(spread_lanes(q_ref[r, i], False)):
-                qp[r, i, h] = tile
-
-    def row_body(r, _):
-        lo_all = jnp.minimum(bounds[r, 0, 0], bounds[r, 1, 0])
-        hi_all = jnp.maximum(bounds[r, 0, 1], bounds[r, 1, 1])
+                qp[i, h] = tile
 
         def turn(t, _):
+            fetch(t).wait()
             k0 = pl.multiple_of(t * TK, TK)
             for h in range(heads):
-                tile = kv_ref[r, pl.ds(k0, TK), h * 128 : h * 128 + 128]
+                tile = kv_ref[pl.ds(k0, TK), h * 128 : h * 128 + 128]
                 vt[h, 0:64, pl.ds(k0, TK)] = tile.T[64:128, :]
                 vt[h, 64:80, pl.ds(k0, TK)] = jnp.ones((16, TK), jnp.bfloat16)
             return 0
@@ -728,9 +733,10 @@
             def tile_body(t, _):
                 k0 = pl.multiple_of(t * TK, TK)
                 slot, plain = tile_kind(bounds, r, i, t)
+                near = jnp.logical_and(slot > 0, slot < 3)
 
                 def scores(h):
-                    return mxu(kv_ref[r, pl.ds(k0, TK), h * 128 : h * 128 + 128], qp[r, i, h], NT)
+                    return mxu(kv_ref[pl.ds(k0, TK), h * 128 : h * 128 + 128], qp[i, h], NT)
 
                 def finish(h, s, b):
                     m_old = mx[h]
@@ -745,11 +751,18 @@
                     for h in range(heads):
                         finish(h, found[h], jnp.where(slot == 0, table[h, 15], table[h, 31]))
 
-                @pl.when(jnp.logical_not(plain))
+                @pl.when(near)
                 def _():
                     ok = valid_mask(se_ref, r, i, k0)
                     for h in range(heads):
-                        s = scores(h) + bias_ref[h, slot].astype(jnp.float32)
+                        s = scores(h) + near_ref[h, slot - 1].astype(jnp.float32)
+                        finish(h, jnp.where(ok, s, NEG), 0.0)
+
+                @pl.when(jnp.logical_not(jnp.logical_or(plain, near)))
+                def _():
+                    ok = valid_mask(se_ref, r, i, k0)
+                    for h in range(heads):
+                        s = scores(h) + jnp.where(slot == 0, table[h, 15], table[h, 31])
                         finish(h, jnp.where(ok, s, NEG), 0.0)
 
                 return 0
@@ -768,32 +781,39 @@
         lax.fori_loop(0, 2, q_body, 0)
         return 0
 
-    lax.fori_loop(0, 2, row_body, 0)
-
-
-def attention(bounds, table, q, kv, se):
+    lax.fori_loop(0, 1 if alone else 2, row_body, 0)
+    if alone:
+        o_ref[1 - base] = o_in[...]
+        keep_ref[1 - base] = keep_in[...]
+        lse_ref[1 - base] = lse_in[...]
+
+
+def attention(bounds, table, q, kv, se, ready=()):
     heads, n = kv.shape[2] // 128, kv.shape[1]
     packed = q.shape
+    outs = [
+        jax.ShapeDtypeStruct(packed, jnp.bfloat16),
+        jax.ShapeDtypeStruct(packed, jnp.float32),
+        jax.ShapeDtypeStruct((2, 2, heads, 1, TQ), jnp.float32),
+    ]
+    if not ready:
+        outs.append(jax.ShapeDtypeStruct((heads, 2, TK, TQ), jnp.bfloat16))
     return pl.pallas_call(
-        fwd_kernel,
-        out_shape=(
-            jax.ShapeDtypeStruct(packed, jnp.bfloat16),
-            jax.ShapeDtypeStruct(packed, jnp.float32),
-            jax.ShapeDtypeStruct((2, 2, heads, 1, TQ), jnp.float32),
-            jax.ShapeDtypeStruct((heads, 4, TK, TQ), jnp.bfloat16),
-            jax.ShapeDtypeStruct((heads, 2, TK, TQ), jnp.bfloat16),
-        ),
-        in_specs=[SMEM_SPEC] * 2 + [VMEM_SPEC] * 3,
-        out_specs=(VMEM_SPEC,) * 5,
+        functools.partial(fwd_kernel, bool(ready)),
+        out_shape=tuple(outs),
+        in_specs=[SMEM_SPEC] * 2 + [VMEM_SPEC, ANY_SPEC, VMEM_SPEC] + [VMEM_SPEC] * len(ready),
+        out_specs=(VMEM_SPEC,) * len(outs),
         scratch_shapes=[
             pltpu.VMEM((heads, 80, n), jnp.bfloat16),
             pltpu.VMEM((heads, 80, TQ), jnp.float32),
             pltpu.VMEM((heads, 1, TQ), jnp.float32),
-            pltpu.VMEM((2, 2, heads, TQ, 128), jnp.bfloat16),
+            pltpu.VMEM((2, heads, TQ, 128), jnp.bfloat16),
+            pltpu.VMEM(kv.shape[1:], jnp.bfloat16),
+            pltpu.SemaphoreType.DMA((n // TK,)),
         ],
         compiler_params=pltpu.CompilerParams(vmem_limit_bytes=VMEM_BYTES),
         name="attention",
-    )(bounds, table, q, kv, se)
+    )(bounds, table, q, kv, se, *ready)
 
 
 def prepare(q, do, q_out, do_out):
@@ -846,12 +866,12 @@
         tab_ref[h, 31:32] += side[h, 1:2]
 
 
-def bwd_kernel(alone, bounds, table, q_ref, do_ref, keep_ref, kv_ref, bias_ref, se_ref, lse_ref,
+def bwd_kernel(alone, bounds, table, q_ref, do_ref, keep_ref, kv_hbm, bias_ref, se_ref, lse_ref,
                dq_ref, dkv_ref, near_ref, side, delta, *rest):
     tab_ref, tab8, rest = (None, None, rest) if alone else (rest[0], rest[-1], rest[1:-1])
-    kt, dqt, dkv, grid, qp, dp_ref = rest
+    kt, dqt, dkv, grid, qp, dp_ref, kv_ref, kv_sem = rest
     heads = lse_ref.shape[2]
-    n = kv_ref.shape[1]
+    n = kv_hbm.shape[1]
     grid[...] = jnp.zeros_like(grid)
     side[...] = jnp.zeros_like(side)
     base = 1 - bounds[0, 0, 6] if alone else 0
@@ -867,6 +887,16 @@
         lo_all = jnp.minimum(bounds[r, 0, 0], bounds[r, 1, 0])
         hi_all = jnp.maximum(bounds[r, 0, 1], bounds[r, 1, 1])
 
+        def fetch(t):
+            rows = pl.ds(pl.multiple_of(t * TK, TK), TK)
+            return pltpu.make_async_copy(kv_hbm.at[r, rows], kv_ref.at[rows], kv_sem.at[t])
+
+        def begin(t, _):
+            fetch(t).start()
+            return 0
+
+        lax.fori_loop(lo_all, hi_all, begin, 0)
+
         def clear(t, _):
             k0 = pl.multiple_of(t * TK, TK)
             for h in range(heads):
@@ -876,9 +906,10 @@
         lax.fori_loop(0, n // TK, clear, 0)
 
         def turn(t, _):
+            fetch(t).wait()
             k0 = pl.multiple_of(t * TK, TK)
             for h in range(heads):
-                tile = kv_ref[r, pl.ds(k0, TK), h * 128 : h * 128 + 128]
+                tile = kv_ref[pl.ds(k0, TK), h * 128 : h * 128 + 128]
                 kt[h, 0:64, pl.ds(k0, TK)] = tile.T[0:64, :]
                 kt[h, 64:80, pl.ds(k0, TK)] = jnp.ones((16, TK), jnp.bfloat16)
             return 0
@@ -900,7 +931,7 @@
                     dqt[h, where] += mxu(kt[h, :, pl.ds(k0, TK)], ds_low)
 
                 def products(h):
-                    tile = kv_ref[r, pl.ds(k0, TK), h * 128 : h * 128 + 128]
+                    tile = kv_ref[pl.ds(k0, TK), h * 128 : h * 128 + 128]
                     return mxu(tile, qp[at, i, h], NT), mxu(tile, dp_ref[at, i, h], NT)
 
                 @pl.when(plain)
@@ -910,17 +941,20 @@
                         p = jnp.exp(s - (lse_ref[r, i, h] - jnp.where(slot == 0, table[h, 15], table[h, 31])))
                         finish(h, p, p * (d_probs - delta[r, i, h]), jnp.where(slot == 0, 0, 2))
 
-                @pl.when(jnp.logical_not(plain))
-                def _():
+                def general(bias):
                     ok = valid_mask(se_ref, r, i, k0)
                     for h in range(heads):
                         s, d_probs = products(h)
-                        s = s + bias_ref[h, slot].astype(jnp.float32)
+                        s = s + bias(h)
                         p = jnp.where(ok, jnp.exp(jnp.where(ok, s, NEG) - lse_ref[r, i, h]), 0.0)
                         ds = p * (d_probs - delta[r, i, h])
                         grid[h, pl.ds(pl.multiple_of(slot * TK, TK), TK)] += ds
                         finish(h, p, ds, 1)
 
+                near = jnp.logical_and(slot > 0, slot < 3)
+                pl.when(near)(lambda: general(lambda h: bias_ref[h, slot - 1].astype(jnp.float32)))
+                away = jnp.logical_not(jnp.logical_or(plain, near))
+                pl.when(away)(lambda: general(lambda h: jnp.where(slot == 0, table[h, 15], table[h, 31])))
                 return 0
 
             lax.fori_loop(bounds[r, i, 0], bounds[r, i, 1], tile_body, 0)
@@ -968,7 +1002,7 @@
             jax.ShapeDtypeStruct((heads, 2, TQ), jnp.float32),
             jax.ShapeDtypeStruct((2, 2, heads, 1, TQ), jnp.float32),
         ) + tuple(table_out),
-        in_specs=[SMEM_SPEC] * 2 + [VMEM_SPEC] * 7,
+        in_specs=[SMEM_SPEC] * 2 + [VMEM_SPEC] * 3 + [ANY_SPEC] + [VMEM_SPEC] * 3,
         out_specs=(VMEM_SPEC,) * (5 + len(table_out)),
         scratch_shapes=[
             pltpu.VMEM((heads, 80, n), jnp.bfloat16),
@@ -977,6 +1011,8 @@
             pltpu.VMEM((heads, 4 * TK, TQ), jnp.float32),
             pltpu.VMEM((count, 2, heads, TQ, 128), jnp.bfloat16),
             pltpu.VMEM((count, 2, heads, TQ, 128), jnp.bfloat16),
+            pltpu.VMEM(kv.shape[1:], jnp.bfloat16),
+            pltpu.SemaphoreType.DMA((n // TK,)),
         ] + [pltpu.VMEM((heads, BUCKETS, 8, TQ), jnp.float32) for _ in table_out],
         compiler_params=pltpu.CompilerParams(vmem_limit_bytes=VMEM_BYTES),
         name="attention_back",
@@ -1385,9 +1421,39 @@
 
 
 class Refs:
-    def __init__(self, names, refs):
-        for name, ref in zip(names, refs, strict=True):
-            setattr(self, name, ref)
+    def __init__(self, **refs):
+        self.__dict__.update(refs)
+
+
+class Held:
+    def __init__(self, array, space):
+        self.array, self.space = array, space
+
+
+def call(kernel, ident, ins, outs, scratch):
+    leaf = lambda entry: isinstance(entry, Held) or isinstance(entry, tuple) or not isinstance(entry, (dict, list))
+    parts = [jax.tree.flatten(part, is_leaf=leaf) for part in (ins, outs, scratch)]
+    counts = [len(part[0]) for part in parts]
+    given, wanted, kept = [part[0] for part in parts]
+
+    def run(*refs):
+        named, start = {}, 0
+        for count, (_, tree) in zip(counts, parts):
+            named.update(jax.tree.unflatten(tree, refs[start : start + count]))
+            start += count
+        kernel(Refs(**named))
+
+    space = lambda entry, at: entry.space if isinstance(entry, Held) else entry[2] if isinstance(entry, tuple) and len(entry) > 2 else at
+    found = pl.pallas_call(
+        run,
+        out_shape=tuple(jax.ShapeDtypeStruct(entry[0], entry[1]) for entry in wanted),
+        in_specs=[pl.BlockSpec(memory_space=space(entry, pltpu.VMEM)) for entry in given],
+        out_specs=tuple(pl.BlockSpec(memory_space=space(entry, pltpu.VMEM)) for entry in wanted),
+        scratch_shapes=kept,
+        compiler_params=pltpu.CompilerParams(collective_id=ident, has_side_effects=True, vmem_limit_bytes=VMEM_BYTES),
+        name=kernel.func.__name__,
+    )(*[entry.array if isinstance(entry, Held) else entry for entry in given])
+    return Refs(**jax.tree.unflatten(parts[1][1], found))
 
 
 wide = lambda value: value.astype(jnp.float32)
@@ -1639,28 +1705,26 @@
             remote(r.z_out.at[n], there, r.z_send.at[n], r.z_recv.at[n], self.row_to).wait()
 
 
-def back_kernel(shards, axes, names, plans, *refs):
-    r = Refs(names, refs)
+def back_kernel(shards, axes, plans, r):
     place = Place(shards)
     at = {"dp": place.dp, "blk": place.blk}
     tokens, width = r.hidden.shape
     back = DenseBack(place, r)
     streams = []
     for s, (kept, order) in enumerate(plans):
-        bufs = [getattr(r, "buf%d_%d" % (s, k)) for k in range(len(order))]
-        streams.append(Stream(axes, at, kept, order, getattr(r, "src%d" % s), bufs, getattr(r, "sum%d" % s), r.w_send.at[s], r.w_recv.at[s]))
+        streams.append(Stream(axes, at, kept, order, r.src[s], r.bufs[s], r.sums[s], r.w_send.at[s], r.w_recv.at[s]))
     early, late = streams[:3], streams[3:]
     whole = Whole(axes, at, (4, 0, 3, 2, 1), r.small, r.small_bufs, r.small_out, r.w_send.at[len(plans)], r.w_recv.at[len(plans)])
     left, right = (place.dp, (place.blk + shards - 1) % shards), (place.dp, (place.blk + 1) % shards)
 
     met = hail(line_and_row(place) + [back.across, back.core_to, left, right])
-    fetches = [pltpu.make_async_copy(getattr(r, "came%d_hbm" % s), early[s].src, r.came_sem.at[s]) for s in range(3)]
+    fetches = [pltpu.make_async_copy(r.came_hbm[s], early[s].src, r.came_sem.at[s]) for s in range(3)]
     for copy in fetches:
         copy.start()
     back.prepare()
     for s in range(3):
         fetches[s].wait()
-        add_two(early[s].src, early[s].src, getattr(r, "keep%d" % s))
+        add_two(early[s].src, early[s].src, r.keeps[s])
     await_all(met)
     back.s_core.start()
     for stream in early:
@@ -1745,15 +1809,14 @@
         copy.wait()
 
 
-def back_and_last(shape, halves, inputs):
+def back_and_last(shape, keeps, came, inputs):
     shards = shape["blk"]
     axes = bit_axes(shape)
     ndim = len(axes)
-    named = dict(inputs)
-    kv, q, hidden = named["kv_hbm"], named["q"], named["hidden"]
+    kv, q, hidden = inputs["kv_hbm"].array, inputs["q"], inputs["hidden"]
     heads, n, width = kv.shape[2] // 128, kv.shape[1], kv.shape[2]
     tokens, features = hidden.shape
-    length = named["x"].shape[0]
+    length = inputs["x"].shape[0]
     f32, low, sem = jnp.float32, jnp.bfloat16, pltpu.SemaphoreType.DMA
     chunk = (tokens, width)
     every = (0, 1, 2, 3, 4)
@@ -1762,52 +1825,323 @@
         (every, (4, 0, 3, 2, 1)), (every, (4, 3, 2, 0, 1)), (every, (4, 2, 0, 3, 1)),
     ]
     own = (2 * (features // (1 << ndim)), features // 2)
-    blocks = [h.shape[-2:] for h in halves[::2]] + [own] * 3
-    ins = list(inputs)
-    for s in range(3):
-        for k, kind in enumerate(("keep%d", "came%d_hbm")):
-            part = halves[2 * s + k]
-            ins.append((kind % s, part.reshape((2, 2, 2) + part.shape[-2:])))
-    spec_of = lambda name: pl.BlockSpec(memory_space=pl.ANY) if name.endswith("_hbm") else SMEM_SPEC if name in ("bounds", "table") else VMEM_SPEC
-    outs = [
-        ("gb", (length, features), low), ("edge", (2, 16, features), f32), ("spill_out", (2, LEAD, features), f32),
-        ("small_out", (32, 128), f32),
-    ] + [("sum%d" % s, block, f32) for s, block in enumerate(blocks)]
+    blocks = [part.shape[-2:] for part in keeps] + [own] * 3
+    bits = lambda part: part.reshape((2, 2, 2) + part.shape[-2:])
+    ins = dict(inputs, keeps=[bits(part) for part in keeps], came_hbm=[Held(bits(part), pl.ANY) for part in came])
+    outs = dict(
+        gb=((length, features), low), edge=((2, 16, features), f32), spill_out=((2, LEAD, features), f32),
+        small_out=((32, 128), f32), sums=[(block, f32) for block in blocks],
+    )
     mem = lambda shape, dtype=low: pltpu.VMEM(shape, dtype)
     pairs, fours = sem((GROUPS, 2)), sem((GROUPS,))
     strip = mem((features // 128, length + 2 * LEAD, 128), f32)
-    scratch = [
-        ("kt", mem((heads, 80, TK))), ("dqt", mem((2, heads, 3, 80, TQ), f32)), ("acc", mem((TK, width), f32)),
-        ("grid", mem((heads, 2 * TK, TQ), f32)), ("side", mem((heads, 2, TQ), f32)), ("tab8", mem((heads, BUCKETS, 8, TQ), f32)),
-        ("tab", mem((heads, BUCKETS, TQ), f32)),
-        ("qp", mem((2, heads, TQ, 128))), ("dp", mem((2, heads, TQ, 128))),
-        ("kv", mem((4, 2, TK, width))), ("keys", mem((TK, width))), ("dkvs", mem((GROUPS, 2) + chunk)), ("nears", mem((heads, NEAR_ROWS, TQ), f32)),
-        ("held", mem((GROUPS, 2, 2) + chunk)), ("core_in", mem((GROUPS, 2) + chunk)), ("s_in", mem((GROUPS, 2) + chunk)),
-        ("x_out", mem((GROUPS, 2) + chunk)), ("x_in", mem((GROUPS, 2) + chunk)),
-        ("y_out", mem((GROUPS, 1) + chunk)), ("y_in", mem((GROUPS, 2) + chunk)), ("kept", mem((GROUPS, 2) + chunk)),
-        ("z_out", mem((GROUPS,) + chunk)), ("dkv_home", mem((GROUPS,) + chunk)),
-        ("dq_rows", mem((2, 2) + q.shape[2:])), ("dq_home", mem((GROUPS,) + q.shape[2:])),
-        ("core_send", pairs), ("core_recv", pairs), ("x_send", pairs), ("x_recv", pairs), ("y_send", pairs), ("y_recv", pairs),
-        ("z_send", fours), ("z_recv", fours), ("s_send", sem), ("s_recv", sem), ("q_send", fours), ("q_recv", fours),
-        ("kv_sem", fours), ("came_sem", sem((3,))), ("own_sem", sem), ("near_sem", sem),
-        ("w_send", sem((len(plans) + 1, ndim))), ("w_recv", sem((len(plans) + 1, ndim))), ("s2_send", sem((2,))), ("s2_recv", sem((2,))),
-        ("xs", strip), ("gbuf", strip), ("spill", mem((2, LEAD, features), f32)), ("small", mem((32, 128), f32)),
-        ("small_bufs", mem((2, ndim, 32, 128), f32)), ("total", mem((features, features), f32)),
-    ]
-    for s, ((kept, order), block) in enumerate(zip(plans, blocks)):
-        scratch.append(("src%d" % s, mem((2,) * len(kept) + block)))
-        for k, buf in enumerate(stream_scratch(len(kept), order, *block)):
-            scratch.append(("buf%d_%d" % (s, k), buf))
-    names = [name for name, _ in ins] + [name for name, _, _ in outs] + [name for name, _ in scratch]
-    return pl.pallas_call(
-        functools.partial(back_kernel, shards, axes, names, plans),
-        out_shape=tuple(jax.ShapeDtypeStruct(shape, dtype) for _, shape, dtype in outs),
-        in_specs=[spec_of(name) for name, _ in ins],
-        out_specs=(VMEM_SPEC,) * len(outs),
-        scratch_shapes=[kind for _, kind in scratch],
-        compiler_params=pltpu.CompilerParams(collective_id=6, has_side_effects=True, vmem_limit_bytes=VMEM_BYTES),
-        name="back_and_last",
-    )(*[array for _, array in ins])
+    scratch = dict(
+        kt=mem((heads, 80, TK)), dqt=mem((2, heads, 3, 80, TQ), f32), acc=mem((TK, width), f32),
+        grid=mem((heads, 2 * TK, TQ), f32), side=mem((heads, 2, TQ), f32), tab8=mem((heads, BUCKETS, 8, TQ), f32),
+        tab=mem((heads, BUCKETS, TQ), f32),
+        qp=mem((2, heads, TQ, 128)), dp=mem((2, heads, TQ, 128)),
+        kv=mem((4, 2, TK, width)), keys=mem((TK, width)), dkvs=mem((GROUPS, 2) + chunk), nears=mem((heads, NEAR_ROWS, TQ), f32),
+        held=mem((GROUPS, 2, 2) + chunk), core_in=mem((GROUPS, 2) + chunk), s_in=mem((GROUPS, 2) + chunk),
+        x_out=mem((GROUPS, 2) + chunk), x_in=mem((GROUPS, 2) + chunk),
+        y_out=mem((GROUPS, 1) + chunk), y_in=mem((GROUPS, 2) + chunk), kept=mem((GROUPS, 2) + chunk),
+        z_out=mem((GROUPS,) + chunk), dkv_home=mem((GROUPS,) + chunk),
+        dq_rows=mem((2, 2) + q.shape[2:]), dq_home=mem((GROUPS,) + q.shape[2:]),
+        core_send=pairs, core_recv=pairs, x_send=pairs, x_recv=pairs, y_send=pairs, y_recv=pairs,
+        z_send=fours, z_recv=fours, s_send=sem, s_recv=sem, q_send=fours, q_recv=fours,
+        kv_sem=fours, came_sem=sem((3,)), own_sem=sem, near_sem=sem,
+        w_send=sem((len(plans) + 1, ndim)), w_recv=sem((len(plans) + 1, ndim)), s2_send=sem((2,)), s2_recv=sem((2,)),
+        xs=strip, gbuf=strip, spill=mem((2, LEAD, features), f32), small=mem((32, 128), f32),
+        small_bufs=mem((2, ndim, 32, 128), f32), total=mem((features, features), f32),
+    )
+    scratch["src"] = [mem((2,) * len(kept) + block) for (kept, _), block in zip(plans, blocks)]
+    scratch["bufs"] = [stream_scratch(len(kept), order, *block) for (kept, order), block in zip(plans, blocks)]
+    return call(functools.partial(back_kernel, shards, axes, plans), 6, ins, outs, scratch)
+
+
+class DenseForward:
+    def __init__(self, place, r):
+        self.place, self.r, self.heads = place, r, r.lse.shape[1]
+
+    def prepare(self, dense):
+        r = self.r
+        self.dense = dense
+        for i in range(2):
+            for h, tile in enumerate(spread_lanes(jnp.where(dense == 0, r.q_all[0, i], r.q_all[1, i]), False)):
+                r.qp[i, h] = tile
+        r.acc[...] = jnp.zeros_like(r.acc)
+        r.mx[...] = jnp.full_like(r.mx, FIRST_MAX)
+
+    def tile(self, group, place_y):
+        r, place = self.r, self.place
+        t = group * 2 + place_y
+        rows = pl.ds(pl.multiple_of(t * TK, TK), TK)
+        r.keys[...] = jnp.where(self.dense == 0, r.kv_all[0, rows], r.kv_all[1, rows])
+        for h in range(self.heads):
+            r.vt[h, 0:64] = r.keys[:, h * 128 : h * 128 + 128].T[64:128]
+            r.vt[h, 64:80] = jnp.ones((16, TK), jnp.bfloat16)
+
+        def part(i, _):
+            first = ((2 * place.row + i) * place.rest_size + place.rest) * TQ
+            slot = jnp.clip(t - (first // TK - 1 + place.rest % 2) + 1, 0, 3)
+            away = jnp.logical_or(slot == 0, slot == 3)
+
+            def scores(h):
+                return mxu(r.keys[:, h * 128 : h * 128 + 128], r.qp[i, h], NT)
+
+            def finish(h, s, b):
+                m_old = r.mx[i, h]
+                m_new = jnp.maximum(m_old, jnp.max(s, axis=0, keepdims=True) + b)
+                p = jnp.exp(s - (m_new - b)).astype(jnp.bfloat16)
+                r.mx[i, h] = m_new
+                r.acc[i, h] = r.acc[i, h] * jnp.exp(m_old - m_new) + mxu(r.vt[h], p)
+
+            @pl.when(away)
+            def _():
+                found = [scores(h) for h in range(self.heads)]
+                for h in range(self.heads):
+                    finish(h, found[h], jnp.where(slot == 0, r.table[h, 15], r.table[h, 31]))
+
+            @pl.when(jnp.logical_not(away))
+            def _():
+                for h in range(self.heads):
+                    finish(h, scores(h) + r.near[h, slot - 1].astype(jnp.float32), 0.0)
+
+            return 0
+
+        lax.fori_loop(0, 2, part, 0)
+
+    def end(self):
+        r = self.r
+        for i in range(2):
+            parts = []
+            for h in range(self.heads):
+                total = r.acc[i, h, 64:65, :]
+                parts.append((r.acc[i, h, 0:64, :] / total).T)
+                r.lse[i, h] = r.mx[i, h] + jnp.log(total)
+            joined = join_heads(parts)
+            r.o[i] = joined.astype(jnp.bfloat16)
+            r.keep[i] = joined
+
+
+def label_spans(place, r):
+    ids = range(8)
+    shards = place.shards
+    blocks = r.labels_all[...].reshape(2, shards, 8, 128)
+    ends = []
+    for row in range(2):
+        here = blocks[row]
+        ends.append([jnp.sum(jnp.logical_and(here >= 0, here <= k).astype(jnp.int32)) for k in ids])
+    dense = (ends[0][0] < shards * TQ).astype(jnp.int32)
+    for row in range(2):
+        for i in range(2):
+            group = 2 * place.row + i
+            chunk = r.labels_all[tuple([row] + [bit(group * place.rest_size + place.rest, m) for m in bits_of(shards)])]
+            line = jnp.concatenate([chunk[0:1], chunk[1:2]], axis=1)
+            begin, end = jnp.zeros((1, TQ), jnp.int32), jnp.zeros((1, TQ), jnp.int32)
+            for k in ids:
+                begin = jnp.where(line == k, ends[row][k - 1] if k else 0, begin)
+                end = jnp.where(line == k, ends[row][k], end)
+            r.span[row, i, 0:1] = begin
+            r.span[row, i, 1:2] = end
+            first = (group * place.rest_size + place.rest) * TQ
+            r.bounds[row, i, 0] = jnp.min(begin) // TK
+            r.bounds[row, i, 1] = (jnp.max(end) + TK - 1) // TK
+            r.bounds[row, i, 2] = first // TK - 1 + place.rest % 2
+            r.bounds[row, i, 3] = (jnp.max(begin) + TK - 1) // TK
+            r.bounds[row, i, 4] = jnp.min(end) // TK
+            r.bounds[row, i, 5] = place.rest % 2
+            r.bounds[row, i, 6] = dense
+    return dense
+
+
+def front_kernel(shards, r):
+    place = Place(shards)
+    tokens = r.kv.shape[1]
+    y, core = bit(place.rest, 2), place.rest % 2
+    core_to, across, row_to = place.other_rest(1), place.other_rest(2), place.other_row()
+    met = hail(line_and_row(place) + [core_to, across])
+    dims = [("row", 1)] + [("blk", m) for m in bits_of(shards)]
+    lab_index = [place.row] + [bit(place.blk, m) for _, m in dims[1:]]
+
+    def lab_copy(stage):
+        index = tuple(slice(None) if p < stage else lab_index[p] for p in range(len(dims)))
+        axis, mask = dims[stage]
+        target = row_to if axis == "row" else (place.dp, flipped(place.blk, mask))
+        there = r.labels_all.at[index]
+        return remote(there, there, r.lab_send.at[stage], r.lab_recv.at[stage], target)
+
+    def held(dz, off, core_off):
+        row = 1 - place.row if off & 1 else place.row
+        rest = flipped(place.rest, 2) if off & 2 else place.rest
+        rest = flipped(rest, 1) if core_off else rest
+        start = pl.multiple_of(place.chunk((place.group + dz) % GROUPS, rest) * tokens, tokens)
+        return r.kv_all.at[row, pl.ds(start, tokens)]
+
+    def sem_of(dz, off, core_off):
+        return r.kv_recv.at[(core_off * 4 + off) * GROUPS + dz]
+
+    waits = []
+
+    def send(src, dz, off, core_off, target):
+        copy = remote(src, held(dz, off & 3, 0), r.kv_send.at[len(waits)], sem_of(*core_off), target)
+        copy.start()
+        waits.append(copy)
+
+    def arrived(dz, off, core_off=0):
+        here = held(dz, off, core_off)
+        remote(here, here, r.kv_send.at[0], sem_of(dz, off, core_off), core_to).wait_recv()
+
+    def pass_on(dz, off):
+        src = r.kv.at[place.group] if dz == 0 and off == 0 else held(dz, off, 0)
+        if not (dz == 0 and off == 0):
+            arrived(dz, off)
+        order = (0, 1) if dz % 2 == 0 else (1, 0)
+        last = max([order.index(p) for p in range(2) if off >> p & 1], default=-1)
+        for p in order[last + 1 :]:
+            send(src, dz, off, (dz, off | 1 << p, 0), across if p else row_to)
+        send(src, dz, off, (dz, off, 1), core_to)
+
+    r.labels_all[tuple(lab_index)] = r.label[...]
+    await_all(met)
+    lab_copy(0).start()
+    own = pltpu.make_async_copy(r.kv.at[place.group], held(0, 0, 0), r.own_sem)
+    own.start()
+
+    def along(step):
+        copy = remote(r.kv.at[(place.group + step) % GROUPS], held(0, 0, 0), r.z_send.at[step], sem_of((GROUPS - step) % GROUPS, 0, 0), place.other_group(step))
+        copy.start()
+        return copy
+
+    def label_stage(stage):
+        lab_copy(stage).wait()
+        if stage + 1 < len(dims):
+            lab_copy(stage + 1).start()
+
+    work = DenseForward(place, r)
+
+    def tile(dz, off_y):
+        for off in (2 * off_y, 2 * off_y + 1):
+            arrived(dz, off, 1)
+        work.tile((place.group + dz) % GROUPS, 1 - y if off_y else y)
+
+    first = [along(1), along(3)]
+    pass_on(0, 0)
+    make_bias(r.table, core, r.near, (0,))
+    label_stage(0)
+    pass_on(0, 1)
+    pass_on(0, 2)
+    make_bias(r.table, core, r.near, (1,))
+    label_stage(1)
+    for copy in first:
+        copy.wait_send()
+    spread_heads(place, r.q, r.q_all, r.q_send, r.q_recv)
+    pass_on(1, 0)
+    label_stage(2)
+    pass_on(3, 0)
+    label_stage(3)
+    pass_on(0, 3)
+    spread_heads_gone(place, r.q, r.q_all, r.q_send, r.q_recv)
+    last = along(2)
+    label_stage(4)
+    dense = label_spans(place, r)
+    pass_on(1, 1)
+    pass_on(1, 2)
+    spread_heads_come(r.q, r.q_all, r.q_recv)
+    own.wait()
+    work.prepare(dense)
+    pass_on(3, 1)
+    pass_on(3, 2)
+    tile(0, 0)
+    pass_on(1, 3)
+    tile(0, 1)
+    pass_on(3, 3)
+    tile(1, 0)
+    pass_on(2, 0)
+    tile(1, 1)
+    pass_on(2, 1)
+    pass_on(2, 2)
+    tile(3, 0)
+    pass_on(2, 3)
+    tile(3, 1)
+    tile(2, 0)
+    tile(2, 1)
+    last.wait_send()
+    work.end()
+    for copy in waits:
+        copy.wait_send()
+
+
+def front(shards, table, q_packed, kv_parts, label):
+    tokens, width = kv_parts.shape[1:]
+    heads = width // 128
+    nbits = 1 + len(bits_of(shards))
+    sem, f32, low = pltpu.SemaphoreType.DMA, jnp.float32, jnp.bfloat16
+    half = q_packed.shape[1:]
+    ins = dict(table=Held(table, pltpu.SMEM), q=q_packed, kv=kv_parts, label=label)
+    outs = dict(
+        q_all=((2, 2) + half, low), kv_all=((2, shards * tokens, width), low), bounds=((2, 2, 7), jnp.int32, pltpu.SMEM),
+        span=((2, 2, 2, TQ), jnp.int32), near=((heads, 2, TK, TQ), low),
+        o=((2,) + half, low), keep=((2,) + half, f32), lse=((2, heads, 1, TQ), f32),
+    )
+    scratch = dict(
+        labels_all=pltpu.VMEM((2,) * nbits + label.shape, label.dtype),
+        qp=pltpu.VMEM((2, heads, TQ, 128), low), acc=pltpu.VMEM((2, heads, 80, TQ), f32),
+        mx=pltpu.VMEM((2, heads, 1, TQ), f32), keys=pltpu.VMEM((TK, width), low), vt=pltpu.VMEM((heads, 80, TK), low),
+        q_send=sem((4,)), q_recv=sem((4,)), kv_send=sem((28,)), z_send=sem((GROUPS,)), kv_recv=sem((32,)), own_sem=sem,
+        lab_send=sem((nbits,)), lab_recv=sem((nbits,)),
+    )
+    return call(functools.partial(front_kernel, shards), 7, ins, outs, scratch)
+
+
+def middle_kernel(shards, r):
+    place = Place(shards)
+    met = hail(line_and_row(place) + [place.other_rest(1)])
+    pairs = ((r.wo_hbm, r.wo), (r.wg_hbm, r.wg), (r.wu_hbm, r.wu), (r.wd_hbm, r.wd))
+    fetches = [pltpu.make_async_copy(src, dst, r.w_sem.at[k]) for k, (src, dst) in enumerate(pairs)]
+    for copy in fetches:
+        copy.start()
+    await_all(met)
+    return_heads(place, r.o, r.o_home, r.o_send, r.o_recv)
+    for copy in fetches:
+        copy.wait()
+    return_heads_wait(place, r.o, r.o_home, r.o_send, r.o_recv)
+    feed_kernel(r.o_home, r.hidden, r.ct, r.gain, r.wo, r.wg, r.wu, r.wd, r.block_out, r.dres, r.da, r.dgain,
+                r.n2, r.att, r.act, r.dg, r.du, r.db, r.acc, r.dn2)
+    spread_heads(place, r.da, r.do, r.q_send, r.q_recv)
+    feed_weights(place, r.n2, r.att, r.act, r.dg, r.du, r.ct, r.db, r.keep_a, r.send_a, r.keep_b, r.send_b, r.keep_c, r.send_c,
+                 r.core_send, r.core_recv, r.gate, r.up, r.down, r.out, r.wide_out, r.slim_out, r.wide_in, r.slim_in)
+    spread_heads_wait(place, r.da, r.do, r.q_send, r.q_recv)
+
+
+def middle(shards, o_packed, hidden, ct, gain, wo, wg, wu, wd):
+    tokens, width = hidden.shape
+    ff = wg.shape[1]
+    per, per_ff = width // 32, ff // 32
+    sem, low, f32 = pltpu.SemaphoreType.DMA, jnp.bfloat16, jnp.float32
+    half = o_packed.shape[2:]
+    wide_cols = ff + width // 2
+    first = (wide_cols // 256 + 1) * 128
+    ins = dict(o=o_packed, hidden=hidden, ct=ct, gain=gain, wo_hbm=Held(wo, pl.ANY), wg_hbm=Held(wg, pl.ANY), wu_hbm=Held(wu, pl.ANY), wd_hbm=Held(wd, pl.ANY))
+    outs = dict(
+        block_out=((tokens, width), low), dres=((tokens, width), f32), dgain=((1, width), f32), do=((2, 2) + half, low),
+        keep_a=((8, 2 * per, first), low), send_a=((8, 2 * per, first), low),
+        keep_b=((8, 2 * per, wide_cols - first), low), send_b=((8, 2 * per, wide_cols - first), low),
+        keep_c=((8, per_ff, width), low), send_c=((8, per_ff, width), low),
+    )
+    mem = lambda shape, dtype=low: pltpu.VMEM(shape, dtype)
+    scratch = dict(
+        o_home=mem((GROUPS,) + half), da=mem((GROUPS,) + half),
+        n2=mem((tokens, width)), att=mem((tokens, width)), db=mem((tokens, width)),
+        act=mem((tokens, ff)), dg=mem((tokens, ff)), du=mem((tokens, ff)),
+        acc=mem((tokens, width), f32), dn2=mem((tokens, width), f32),
+        wo=mem(wo.shape), wg=mem(wg.shape), wu=mem(wu.shape), wd=mem(wd.shape),
+        gate=mem((width, ff), f32), up=mem((width, ff), f32), down=mem((ff, width), f32), out=mem((width, width), f32),
+        wide_out=mem((16, 2 * per, wide_cols)), slim_out=mem((16, per_ff, width)),
+        wide_in=mem((16, 2 * per, wide_cols)), slim_in=mem((16, per_ff, width)),
+        w_sem=sem((4,)), o_send=sem((4,)), o_recv=sem((4,)), q_send=sem((4,)), q_recv=sem((4,)),
+        core_send=sem((2,)), core_recv=sem((2,)),
+    )
+    return call(functools.partial(middle_kernel, shards), 8, ins, outs, scratch)
 
 
 def neighbours(rows):
@@ -1857,70 +2191,75 @@
         shards, 1.0 / (row_count * length * devices), x, before, after, labels, score_row, gain1, w_query, w_key, w_value
     )
 
-    label_block = jnp.pad(ids_here[0::2].reshape(tokens // 128, 128), ((0, 8 - tokens // 128), (0, 0)))
-    q_all, kv_all, labels_all = gather_all(shards, q_packed, kv_parts, label_block)
-    labels_all = labels_all.reshape(2, shards, 8, 128)[:, :, : tokens // 128].reshape(2, shards * tokens)
-    ids = jnp.arange(8, dtype=jnp.int32)
-    counts = jnp.sum((labels_all[:, None, :] == ids[None, :, None]).astype(jnp.int32), axis=2)
-    ends = jnp.sum(jnp.where(ids[None, :] <= ids[:, None], counts[:, None, :], 0), axis=2)
-    begins = ends - counts
-    query_labels = jnp.stack(
-        [lax.dynamic_slice_in_dim(labels_all, ((2 * row + i) * rest_size + rest) * tokens, tokens, 1) for i in range(2)],
-        axis=1,
-    )
-    chosen = query_labels[:, :, None, :] == ids[None, None, :, None]
-    span = jnp.stack(
-        [jnp.sum(jnp.where(chosen, edge[:, None, :, None], 0), axis=2) for edge in (begins, ends)], axis=2
-    )
-    parity = rest % 2
-    firsts = jnp.stack([((2 * row + i) * rest_size + rest) * tokens for i in range(2)])
-    near = jnp.broadcast_to((firsts // TK - 1 + parity)[None], (2, 2))
-    bounds = jnp.stack(
-        [
-            jnp.min(span[:, :, 0], axis=-1) // TK,
-            -(-jnp.max(span[:, :, 1], axis=-1) // TK),
-            near,
-            -(-jnp.max(span[:, :, 0], axis=-1) // TK),
-            jnp.min(span[:, :, 1], axis=-1) // TK,
-            jnp.broadcast_to(parity, (2, 2)),
-            jnp.broadcast_to((labels_all[0, -1] > 0).astype(jnp.int32), (2, 2)),
-        ],
-        axis=-1,
-    ).astype(jnp.int32)
+    label_block = jnp.pad(ids_here[0::2].reshape(tokens // 128, 128), ((0, 8 - tokens // 128), (0, 0)), constant_values=-1)
     table = lax.dynamic_slice_in_dim(rel_bias.astype(jnp.float32).T, group * heads, heads, 0)
-
-    o_packed, o_kept, log_total, bias_tiles, near_bias = attention(bounds, table, q_all, kv_all, span)
-    o_home = move_heads(return_kernel, (GROUPS,), shards, 4, o_packed)
+    if devices == 32:
+        got = front(shards, table, q_packed, kv_parts, label_block)
+        bounds, span, q_all, kv_all, near_bias = got.bounds, got.span, got.q_all, got.kv_all, got.near
+        o_packed, o_kept, log_total = attention(
+            bounds, table, q_all, kv_all, span, (near_bias, got.o, got.keep, got.lse)
+        )
+    else:
+        q_all, kv_all, labels_all = gather_all(shards, q_packed, kv_parts, label_block)
+        labels_all = labels_all.reshape(2, shards, 8, 128)[:, :, : tokens // 128].reshape(2, shards * tokens)
+        ids = jnp.arange(8, dtype=jnp.int32)
+        counts = jnp.sum((labels_all[:, None, :] == ids[None, :, None]).astype(jnp.int32), axis=2)
+        ends = jnp.sum(jnp.where(ids[None, :] <= ids[:, None], counts[:, None, :], 0), axis=2)
+        begins = ends - counts
+        query_labels = jnp.stack(
+            [lax.dynamic_slice_in_dim(labels_all, ((2 * row + i) * rest_size + rest) * tokens, tokens, 1) for i in range(2)],
+            axis=1,
+        )
+        chosen = query_labels[:, :, None, :] == ids[None, None, :, None]
+        span = jnp.stack(
+            [jnp.sum(jnp.where(chosen, edge[:, None, :, None], 0), axis=2) for edge in (begins, ends)], axis=2
+        )
+        parity = rest % 2
+        firsts = jnp.stack([((2 * row + i) * rest_size + rest) * tokens for i in range(2)])
+        near = jnp.broadcast_to((firsts // TK - 1 + parity)[None], (2, 2))
+        bounds = jnp.stack(
+            [
+                jnp.min(span[:, :, 0], axis=-1) // TK,
+                -(-jnp.max(span[:, :, 1], axis=-1) // TK),
+                near,
+                -(-jnp.max(span[:, :, 0], axis=-1) // TK),
+                jnp.min(span[:, :, 1], axis=-1) // TK,
+                jnp.broadcast_to(parity, (2, 2)),
+                jnp.broadcast_to((labels_all[0, -1] > 0).astype(jnp.int32), (2, 2)),
+            ],
+            axis=-1,
+        ).astype(jnp.int32)
+        o_packed, o_kept, log_total, near_bias = attention(bounds, table, q_all, kv_all, span)
     ct = cotangent[0]
-    block_out, d_res, da_packed, d_gain2, n2, att, act, d_gate, d_up, d_branch = feed_forward(
-        o_home, hidden, ct, gain2, w_out, w_gate, w_up, w_down
-    )
-
     if devices == 32:
-        do_all, keep_a, send_a, keep_b, send_b, keep_c, send_c = spread_and_weights(
-            shards, da_packed, n2, att, act, d_gate, d_up, ct, d_branch
+        mid = middle(shards, o_packed, hidden, ct, gain2, w_out, w_gate, w_up, w_down)
+        block_out, d_res, d_gain2, do_all = mid.block_out, mid.dres, mid.dgain, mid.do
+        swap = lambda part, axis, mask: lax.ppermute(part, axis, [(i, i ^ mask) for i in range(lax.axis_size(axis))])
+        came = [swap(mid.send_a, "dp", 1), swap(mid.send_b, "blk", 2), swap(mid.send_c, "blk", 4)]
+        dq_other, dkv_other, near_other, side_other, deltas = attention_back(
+            True, bounds, table, q_all, do_all, o_kept, kv_all, near_bias, span, log_total
         )
-        swap = lambda part, axis, mask: lax.ppermute(part, axis, [(i, i ^ mask) for i in range(lax.axis_size(axis))])
-        halves = [keep_a, swap(send_a, "dp", 1), keep_b, swap(send_b, "blk", 2), keep_c, swap(send_c, "blk", 4)]
-        dq_other, dkv_other, near_other, side_other, deltas = attention_back(
-            True, bounds, table, q_all, do_all, o_kept, kv_all, bias_tiles, span, log_total
-        )
-        grad_bytes, edge, spill, small, *sums = back_and_last(
+        last = back_and_last(
             shape,
-            halves,
-            (
-                ("bounds", bounds), ("table", table), ("q", q_all), ("do", do_all), ("delta", deltas), ("kv_hbm", kv_all),
-                ("bias", near_bias), ("lse", log_total), ("dqs", dq_other),
-                ("dkvs_hbm", dkv_other.reshape((GROUPS, 2, 2) + kv_parts.shape[1:])), ("nears_hbm", near_other), ("sides", side_other),
-                ("hidden", hidden), ("dres", d_res), ("n1", n1), ("x", x), ("before", before), ("after", after),
-                ("labels", labels), ("y", y), ("score", score_row), ("gain", gain1), ("wq", w_query), ("wk", w_key),
-                ("wv", w_value), ("dgain2", d_gain2), ("share", share),
+            [mid.keep_a, mid.keep_b, mid.keep_c],
+            came,
+            dict(
+                bounds=Held(bounds, pltpu.SMEM), table=Held(table, pltpu.SMEM), q=q_all, do=do_all, delta=deltas, kv_hbm=Held(kv_all, pl.ANY),
+                bias=near_bias, lse=log_total, dqs=dq_other,
+                dkvs_hbm=Held(dkv_other.reshape((GROUPS, 2, 2) + kv_parts.shape[1:]), pl.ANY), nears_hbm=Held(near_other, pl.ANY),
+                sides=side_other, hidden=hidden, dres=d_res, n1=n1, x=x, before=before, after=after,
+                labels=labels, y=y, score=score_row, gain=gain1, wq=w_query, wk=w_key, wv=w_value, dgain2=d_gain2, share=share,
             ),
         )
+        grad_bytes, edge, spill, small, sums = last.gb, last.edge, last.spill_out, last.small_out, last.sums
     else:
+        o_home = move_heads(return_kernel, (GROUPS,), shards, 4, o_packed)
+        block_out, d_res, da_packed, d_gain2, n2, att, act, d_gate, d_up, d_branch = feed_forward(
+            o_home, hidden, ct, gain2, w_out, w_gate, w_up, w_down
+        )
         do_all = move_heads(spread_kernel, (2, 2), shards, 5, da_packed)
         dq_packed, dkv_all, _, _, _, d_table_lanes = attention_back(
-            False, bounds, table, q_all, do_all, o_kept, kv_all, bias_tiles, span, log_total
+            False, bounds, table, q_all, do_all, o_kept, kv_all, near_bias, span, log_total
         )
         dq_home, dkv_home = reduce_all(shape, dq_packed, dkv_all, [], [])
         grad_bytes, edge, spill, small, last_parts = last_part(

time: 324 us -> 298 us (0.920); the launches traced: 324 us -> 294 us
  Pallas kernels: 294 us -> 266 us
  starting transfers between devices: 4.75 us -> 12.2 us
  waiting for transfers between devices: 6.63 us -> 1.28 us
    pallas_call x6 -> x4, Pallas kernels: 268 us -> 241 us  [the longest x3 229 us: call(): pl.pallas_call(run, out_shape=tuple((jax.ShapeDtypeStruct(entry[0], entry...]
    ppermute x3, starting transfers between devices: 1.1 us -> 8.52 us  [body(): lax.ppermute(part, axis, [(i, i ^ mask) for i in range(lax.axis_size(axis...]
    ppermute x3, waiting for transfers between devices: 6.62 us -> 1.27 us  [body(): lax.ppermute(part, axis, [(i, i ^ mask) for i in range(lax.axis_size(axis...]
  transfers between devices with their start and end apart: 5 -> 5, of which waited for: 3 -> 2; matrix products, arithmetic and copies ran while one was open for 2% -> 2% of each run, Pallas kernels for 5% -> 6%
where the time goes in v5:
time: 298 us; the launch traced here: 294 us
  Pallas kernels  266 us (89%)
  starting transfers between devices  12.2 us (4%)
  local copies, waits for them, and re-layouts  11 us (4%)
    pallas_call x3, Pallas kernels, call(): pl.pallas_call(run, out_shape=tuple((jax.ShapeDtypeStruct(entry[0], entry...  229 us
    pallas_call x1, Pallas kernels, attention_back(): pl.pallas_call(functools.partial(bwd_kernel, alone), out_shape=(jax.Shape...  16.5 us
    pallas_call x1, Pallas kernels, attention(): pl.pallas_call(functools.partial(fwd_kernel, bool(ready)), out_shape=tupl...  12 us
    ppermute x3, starting transfers between devices, body(): lax.ppermute(part, axis, [(i, i ^ mask) for i in range(lax.axis_size(axis...  8.52 us
    pallas_call x1, Pallas kernels, pool_and_project(): pl.pallas_call(functools.partial(pool_kernel, shards, scale), out_shape=(...  6.07 us
  transfers between devices with their start and end apart: 5, of which 2 were waited for; matrix products, arithmetic and copies ran while one was open for 2% of the time, Pallas kernels for 6%

profile of v5, /device:TPU:0, one launch (start us, length us, event | category | flops | bytes accessed | tf_op | source)
XLA Modules:
  0.0 294.0 jit_solution(16648846922912320781)
XLA Ops:
  0.6 0.7 add_convert_fusion
  1.4 0.7 slice_bitcast_fusion.1
  2.2 2.4 collective-permute-start
  4.6 1.3 collective-permute-start.1
  5.9 1.3 convert_bitcast_fusion.refs_3_.table.refs_27_
  7.2 0.9 slice.65
  8.1 1.3 broadcast_in_dim.24.score_ref.refs_24_
  9.3 1.3 broadcast_in_dim.25.gain_ref.refs_13_
  10.6 0.6 pad.18.refs_1_
  11.2 1.3 broadcast_in_dim.21.refs_1_
  12.5 0.1 fusion.6
  12.6 0.1 reshape.67
  12.7 0.1 copy.28
  12.9 0.6 pad_add_fusion.lab_ref.refs_19_
  13.5 6.1 %pool_and_project.1 = (f32[256,768]{1,0:T(8,128)}, bf16[256,768]{1,0:T(8,128)(2,1)}, f32[8,256]{1,0:T(8,128)}, f32[1,128]{1,0:T(1,128)}, bf16[4,384,128]{2,1,0:T(8,128)(2,1)}, /*index=5*/bf16[4,256,384]{2,1,0:T(8,128)(2,1)}) custom-call(bf16[512,768]{1,0:T(8,128)(2,1)} %bitcast.28, bf16[3,768]{1,0:T(4,128)(2,1)} %copy-done.4, bf16[3,768]{1,0:T(4,128)(2,1)} %copy-done.5, ...), custom_call_target="tpu_custom_call" | custom-call | tf_op jit(solution)/shard_map/pool_and_project/pallas_call | solution.py:1147
  19.6 62.5 %front_kernel.1 = (s32[2,2,7]{2,1,0:T(2,128)}, f32[2,384,128]{2,1,0:T(8,128)}, bf16[2,4096,384]{2,1,0:T(8,128)(2,1)}, f32[2,3,1,256]{3,2,1,0:T(1,128)}, bf16[3,2...) custom-call(bf16[4,256,384]{2,1,0:T(8,128)(2,1)} %get-tuple-element., ...), custom_call_target="tpu_custom_call" | custom-call | tf_op jit(solution)/shard_map/front_kernel/pallas_call | solution.py:1447
  82.1 12.0 %attention.1 = (bf16[2,2,384,128]{3,2,1,0:T(8,128)(2,1)}, f32[2,2,384,128]{3,2,1,0:T(8,128)}, f32[2,2,3,1,256]{4,3,2,1,0:T(1,128)}) custom-call(s32[2,2,7]{2,1,0:T(2,128)} %get-tuple-element.71.bounds.refs_3_, f32[3,32]{1,0:T(4,128)} %convert_bitcast_fusion.refs_3_.table.refs_27_, bf16[2,2,384,128]{3,2,1,0:T(8,128)(2,1)} %get-tuple-element.72.q_ref.refs_23_, ...), custom_call_target="tpu_custom_call" | custom-call | tf_op jit(solution)/shard_map/attention/pallas_call | solution.py:801
  94.1 40.7 %middle_kernel.1 = (bf16[256,768]{1,0:T(8,128)(2,1)}, f32[1,768]{1,0:T(1,128)}, bf16[2,2,384,128]{3,2,1,0:T(8,128)(2,1)}, f32[256,768]{1,0:T(8,128)}, bf16[8,48,...) custom-call(bf16[256,768]{1,0:T(8,128)(2,1)} %bitcast.38, ...), custom_call_target="tpu_custom_call" | custom-call | tf_op jit(solution)/shard_map/middle_kernel/pallas_call | solution.py:1447
  134.8 3.8 %collective-permute-start.2 = (bf16[8,48,1280]{2,1,0:T(8,128)(2,1)}, bf16[8,48,1280]{2,1,0:T(8,128)(2,1)S(1)}, u32[]{:S(2)}, u32[]{:S(2)}) collective-permute-start(bf16[8,48,1280]{2,1,0:T(8,128)(2,1)} %get-tuple-element.81), channel_id=1, source_target_pairs={{0,16},{16,0},{1,17},{17,1},{2,18},{18,2},{3,19},{19,3},{4,20},{20... | collective-permute-start | bytes 2949128 | tf_op jit(solution)/shard_map/ppermute | solution.py:2237
  138.6 2.0 collective-permute-start.3
  140.6 2.8 collective-permute-start.4
  143.4 16.5 %attention_back.1 = (bf16[1,2,384,128]{3,2,1,0:T(8,128)(2,1)}, bf16[1,4096,384]{2,1,0:T(8,128)(2,1)}, f32[3,448,256]{2,1,0:T(8,128)}, f32[3,2,256]{2,1,0:T(2,128)}, f32[2,2,3,1,256]{4,3,2,1,0:T(1,128)}) custom-call(s32[2,2,7]{2,1,0:T(2,128)} %get-tuple-element.71.bounds.refs_3_, f32[3,32]{1,0:T(4,128)} %convert_bitcast_fusion.refs_3_.table.refs_27_, ...), custom_call_target="tpu_custom_call" | custom-call | tf_op jit(solution)/shard_map/attention_back/pallas_call | solution.py:996
  159.8 1.0 collective-permute-done.4
  160.9 0.2 collective-permute-done.2
  161.1 0.7 copy-done.2
  161.8 0.3 copy-done.1
  162.1 0.3 copy-done
  162.4 125.4 %back_kernel.1 = (f32[2,16,768]{2,1,0:T(8,128)}, bf16[512,768]{1,0:T(8,128)(2,1)}, f32[32,128]{1,0:T(8,128)}, f32[2,8,768]{2,1,0:T(8,128)}, f32[48,1280]{1,0:T(8...) custom-call(bf16[3,768]{1,0:T(4,128)(2,1)} %copy-done.5, ...), custom_call_target="tpu_custom_call" | custom-call | tf_op jit(solution)/shard_map/back_kernel/pallas_call | solution.py:1447
  287.8 2.8 finish.1
  290.6 1.2 slice_bitcast_fusion.5
  291.8 1.3 slice_bitcast_fusion
  293.1 0.7 copy.30
  (22 shorter events, 0.2 us)
Async XLA Ops:
  2.2 10.3 %collective-permute-start = (bf16[3,768]{1,0:T(4,128)(2,1)S(1)}, bf16[3,768]{1,0:T(4,128)(2,1)S(1)}, u32[]{:S(2)}, u32[]{:S(2)}) collective-permute-start(bf16[3,768]{1,0:T(4,128)(2,1)S(1)} %pad_maximum_fusion), channel_id=1, source_target_pairs={{0,1},{1,2},{2,3},{3,4},{4,5},{5,6},{6,7},{7,8},{8,9},{9,10},{10,1... | collective-permute-start | bytes 13832 | tf_op jit(solution)/shard_map/ppermute | solution.py:2151
  4.6 7.9 %collective-permute-start.1 = (bf16[3,768]{1,0:T(4,128)(2,1)S(1)}, bf16[3,768]{1,0:T(4,128)(2,1)S(1)}, u32[]{:S(2)}, u32[]{:S(2)}) collective-permute-start(bf16[3,768]{1,0:T(4,128)(2,1)S(1)} %pad_maximum_fusion.1), channel_id=1, source_target_pairs={{1,0},{2,1},{3,2},{4,3},{5,4},{6,5},{7,6},{8,7},{9,8},{10,9},{11,1... | collective-permute-start | bytes 13832 | tf_op jit(solution)/shard_map/ppermute | solution.py:2151
  12.5 1.1 copy-start.4
  12.5 1.1 copy-start.5
  134.8 26.3 %collective-permute-start.2 = (bf16[8,48,1280]{2,1,0:T(8,128)(2,1)}, bf16[8,48,1280]{2,1,0:T(8,128)(2,1)S(1)}, u32[]{:S(2)}, u32[]{:S(2)}) collective-permute-start(bf16[8,48,1280]{2,1,0:T(8,128)(2,1)} %get-tuple-element.81), channel_id=1, source_target_pairs={{0,16},{16,0},{1,17},{17,1},{2,18},{18,2},{3,19},{19,3},{4,20},{20... | collective-permute-start | bytes 2949128 | tf_op jit(solution)/shard_map/ppermute | solution.py:2237
  138.6 22.3 %collective-permute-start.3 = (bf16[8,48,1152]{2,1,0:T(8,128)(2,1)}, bf16[8,48,1152]{2,1,0:T(8,128)(2,1)S(1)}, u32[]{:S(2)}, u32[]{:S(2)}) collective-permute-start(bf16[8,48,1152]{2,1,0:T(8,128)(2,1)} %get-tuple-element.82), channel_id=1, source_target_pairs={{0,2},{1,3},{2,0},{3,1},{4,6},{5,7},{6,4},{7,5},{8,10},{9,11},{10,... | collective-permute-start | bytes 2654216 | tf_op jit(solution)/shard_map/ppermute | solution.py:2237
  140.6 20.3 %collective-permute-start.4 = (bf16[8,64,768]{2,1,0:T(8,128)(2,1)}, bf16[8,64,768]{2,1,0:T(8,128)(2,1)S(1)}, u32[]{:S(2)}, u32[]{:S(2)}) collective-permute-start(bf16[8,64,768]{2,1,0:T(8,128)(2,1)} %get-tuple-element.83), channel_id=1, source_target_pairs={{0,4},{1,5},{2,6},{3,7},{4,0},{5,1},{6,2},{7,3},{8,12},{9,13},{10,... | collective-permute-start | bytes 2359304 | tf_op jit(solution)/shard_map/ppermute | solution.py:2237
  160.9 0.9 copy-start.2
  160.9 1.2 copy-start.1
  161.1 1.3 copy-start
  287.8 5.3 %copy-start.3 = (bf16[256,768]{1,0:T(8,128)(2,1)S(1)}, bf16[256,768]{1,0:T(8,128)(2,1)}, u32[]{:S(2)}) copy-start(bf16[256,768]{1,0:T(8,128)(2,1)} %get-tuple-element.80) | copy-start | bytes 1179652

commit v6 on v5

--- a/solution.py
+++ b/solution.py
@@ -399,13 +399,12 @@
     return [pltpu.VMEM((2,) * (lead - 1 - k) + (rows, cols), jnp.bfloat16) for k in range(len(order))]
 
 
-def feed_weights(place, n2_ref, att_ref, act_ref, dg_ref, du_ref, ct_ref, db_ref,
-                 keep_a, send_a, keep_b, send_b, keep_c, send_c,
+def feed_weights(place, n2_ref, att_ref, act_ref, dg_ref, du_ref, ct_ref, db_ref, sums,
                  core_send, core_recv, gate, up, down, out, wide_out, slim_out, wide_in, slim_in):
     core_target = place.other_rest(1)
     per = gate.shape[0] // 32
     per_ff = down.shape[0] // 32
-    first = keep_a.shape[2]
+    first = sums[0].shape[2]
     half = out.shape[1] // 2
     core = place.rest % 2
 
@@ -444,28 +443,22 @@
     slim_copy = remote(slim_out, slim_in, core_send.at[1], core_recv.at[1], core_target)
     slim_copy.start()
 
-    def number(j, bit_at, value):
-        return j // bit_at * (2 * bit_at) + value * bit_at + j % bit_at
-
     wide_copy.wait()
-    for (keep, send), bit_at, mine, cols in (
-        ((keep_a, send_a), 8, place.row, slice(0, first)),
-        ((keep_b, send_b), 1, bit(place.rest, 2), slice(first, wide_out.shape[2])),
-    ):
-        for ref, value in ((send, 1 - mine), (keep, mine)):
-            def one(j, _):
-                m = number(j, bit_at, value)
-                ref[j] = (wide_rows(2 * m + core)[:, cols] + wide_in[m, :, cols].astype(jnp.float32)).astype(jnp.bfloat16)
-                return 0
-            lax.fori_loop(0, 8, one, 0)
+
+    def sum_wide(m, _):
+        total = wide_rows(2 * m + core) + wide_in[m].astype(jnp.float32)
+        sums[0][m] = total[:, :first].astype(jnp.bfloat16)
+        sums[1][m] = total[:, first:].astype(jnp.bfloat16)
+        return 0
+
+    lax.fori_loop(0, 16, sum_wide, 0)
     slim_copy.wait()
-    mine = bit(place.group, 1)
-    for ref, value in ((send_c, 1 - mine), (keep_c, mine)):
-        def one(j, _):
-            m = number(j, 2, value)
-            ref[j] = (slim_rows(2 * m + core) + slim_in[m].astype(jnp.float32)).astype(jnp.bfloat16)
-            return 0
-        lax.fori_loop(0, 8, one, 0)
+
+    def sum_slim(m, _):
+        sums[2][m] = (slim_rows(2 * m + core) + slim_in[m].astype(jnp.float32)).astype(jnp.bfloat16)
+        return 0
+
+    lax.fori_loop(0, 16, sum_slim, 0)
 
 
 def reduce_kernel(shards, axes, orders, *refs):
@@ -1460,16 +1453,13 @@
 slim = lambda value: value.astype(jnp.bfloat16)
 
 
-class DenseBack:
+class RowBack:
     def __init__(self, place, r):
         self.place, self.r = place, r
-        self.heads = r.lse.shape[2]
+        self.heads = r.lse.shape[1]
         self.tokens = TQ
-        self.across, self.core_to, self.row_to = place.other_rest(2), place.other_rest(1), place.other_row()
+        self.across, self.core_to = place.other_rest(2), place.other_rest(1)
         self.y, self.core = bit(place.rest, 2), place.rest % 2
-        self.s_core = remote(r.dkvs_hbm.at[:, :, 1 - self.core], r.s_in, r.s_send, r.s_recv, self.core_to)
-        self.own_rows = pltpu.make_async_copy(r.dkvs_hbm.at[:, :, self.core], r.dkvs, r.own_sem)
-        self.near_rows = pltpu.make_async_copy(r.nears_hbm, r.nears, r.near_sem)
 
     def group_of(self, n):
         return (self.place.group + 1 + n) % GROUPS
@@ -1480,21 +1470,27 @@
 
     def fetch(self, m):
         r = self.r
-        return pltpu.make_async_copy(r.kv_hbm.at[:, pl.ds(self.tile_start(m), TK)], r.kv.at[m % 4], r.kv_sem.at[m % 4])
+        rows = pl.ds(self.tile_start(m), TK)
+        return (
+            pltpu.make_async_copy(r.kv_hbm.at[rows], r.kv.at[m], r.kv_sem.at[m]),
+            pltpu.make_async_copy(r.kl_hbm.at[rows], r.kl.at[m], r.kl_sem.at[m]),
+        )
 
     def prepare(self):
         r = self.r
-        for m in range(4):
-            self.fetch(m).start()
-        self.own_rows.start()
-        self.near_rows.start()
-        self.dense = r.bounds[0, 0, 6]
-        self.mine_dense = self.dense == self.place.row
-        for i in range(2):
-            for h, tile in enumerate(spread_lanes(r.q[self.dense, i], False)):
+        for m in range(2 * GROUPS):
+            for copy in self.fetch(m):
+                copy.start()
+
+        def one(i, _):
+            for h, tile in enumerate(spread_lanes(r.q[i], False)):
                 r.qp[i, h] = tile
-            for h, tile in enumerate(spread_lanes(r.do[self.dense, i], True)):
+            for h, tile in enumerate(spread_lanes(r.do[i], True)):
                 r.dp[i, h] = tile
+            row_deltas(r.do[i], r.keep[i], r.delta.at[i])
+            return 0
+
+        lax.fori_loop(0, GROUPS, one, 0)
         r.dqt[...] = jnp.zeros_like(r.dqt)
         r.grid[...] = jnp.zeros_like(r.grid)
 
@@ -1502,13 +1498,9 @@
         r = self.r
         return remote(r.held.at[n, j, 1 - self.core], r.core_in.at[n, j], r.core_send.at[n, j], r.core_recv.at[n, j], self.core_to)
 
-    def x_copy(self, n, j):
+    def y_copy(self, n):
         r = self.r
-        return remote(r.x_out.at[n, j], r.x_in.at[n, j], r.x_send.at[n, j], r.x_recv.at[n, j], self.row_to)
-
-    def y_copy(self, n, j):
-        r = self.r
-        return remote(r.y_out.at[n, j], r.y_in.at[n, j], r.y_send.at[n, j], r.y_recv.at[n, j], self.across)
+        return remote(r.y_out.at[n], r.y_in.at[n], r.y_send.at[n], r.y_recv.at[n], self.across)
 
     def z_copy(self, n):
         r, place = self.r, self.place
@@ -1523,123 +1515,47 @@
     def own_sum(self, n, j, rows):
         return wide(self.r.held[n, j, self.core, rows]) + wide(self.r.core_in[n, j, rows])
 
-    def split_rows(self, one, two):
-        return slim(jnp.where(self.mine_dense, two, one)), slim(jnp.where(self.mine_dense, one, two))
-
-    def other_sums(self):
-        r = self.r
-        self.s_core.wait()
-        self.own_rows.wait()
-
-        def one(step, _):
-            n, far = step // 2, step % 2
-            row = jnp.where(far == 0, 1 - self.y, self.y)
-            group = self.group_of(n)
-
-            def some(rows):
-                r.s_in[group, row, rows] = slim(wide(r.dkvs[group, row, rows]) + wide(r.s_in[group, row, rows]))
-
-            self.by_rows(some)
-            pl.when(jnp.logical_and(far == 0, n % 2 == 0))(self.y_other(n).start)
-            return 0
-
-        lax.fori_loop(0, 2 * GROUPS, one, 0)
-
-    def other(self, n, j):
-        return self.r.s_in.at[self.group_of(n), 1 - self.y if j == 0 else self.y]
-
-    def y_other(self, n):
-        r = self.r
-        return remote(self.other(n, 0), r.y_in.at[n, 1], r.y_send.at[n, 1], r.y_recv.at[n, 1], self.across)
-
-    def y_first_1(self, n):
+    def send_y(self, n):
         r = self.r
         self.core_copy(n, 0).wait()
 
         def one(rows):
-            r.y_out[n, 0, rows] = slim(self.own_sum(n, 0, rows))
+            r.y_out[n, rows] = slim(self.own_sum(n, 0, rows))
 
         self.by_rows(one)
-        self.y_copy(n, 0).start()
-
-    def y_first_3(self, n):
+        self.y_copy(n).start()
+
+    def send_home(self, n):
         r = self.r
         self.core_copy(n, 1).wait()
-        self.y_other(n).wait()
-        self.y_copy(n, 0).wait()
+        self.y_copy(n).wait()
+        here = isinstance(n, int) and n == GROUPS - 1
 
         def one(rows):
-            first = self.own_sum(n, 1, rows) + wide(r.y_in[n, 0, rows])
-            second = wide(self.other(n, 1)[rows]) + wide(r.y_in[n, 1, rows])
-            r.x_out[n, 0, rows], r.kept[n, 0, rows] = self.split_rows(first, second)
-
-        self.by_rows(one)
-        self.x_copy(n, 0).start()
-
-    def y_first_5(self, n):
-        r = self.r
-        self.x_copy(n, 0).wait()
-
-        def one(rows):
-            r.z_out[n, rows] = slim(wide(r.kept[n, 0, rows]) + wide(r.x_in[n, 0, rows]))
-
-        self.by_rows(one)
-        self.z_copy(n).start()
-
-    def x_first_1(self, n, j=0):
-        r = self.r
-        self.core_copy(n, j).wait()
-
-        def one(rows):
-            r.x_out[n, j, rows], r.kept[n, j, rows] = self.split_rows(self.own_sum(n, j, rows), wide(self.other(n, j)[rows]))
-
-        self.by_rows(one)
-        self.x_copy(n, j).start()
-
-    def x_first_2(self, n):
-        self.x_first_1(n, 1)
-
-    def x_first_3(self, n):
-        r = self.r
-        self.x_copy(n, 0).wait()
-
-        def one(rows):
-            r.y_out[n, 0, rows] = slim(wide(r.kept[n, 0, rows]) + wide(r.x_in[n, 0, rows]))
-
-        self.by_rows(one)
-        self.y_copy(n, 0).start()
-
-    def x_first_5(self, n):
-        r = self.r
-        self.x_copy(n, 1).wait()
-        self.y_copy(n, 0).wait()
-
-        def one(rows):
-            total = slim(wide(r.kept[n, 1, rows]) + wide(r.x_in[n, 1, rows]) + wide(r.y_in[n, 0, rows]))
-            if n == GROUPS - 1:
+            total = slim(self.own_sum(n, 1, rows) + wide(r.y_in[n, rows]))
+            if here:
                 r.dkv_home[self.place.group, rows] = total
             else:
                 r.z_out[n, rows] = total
 
         self.by_rows(one)
-        if n < GROUPS - 1:
+        if not here:
             self.z_copy(n).start()
 
     def tile(self, m):
         r, place, heads = self.r, self.place, self.heads
         n, j = m // 2, m % 2
         t = self.tile_start(m) // TK
-        self.fetch(m).wait()
+        for copy in self.fetch(m):
+            copy.wait()
         r.acc[...] = jnp.zeros_like(r.acc)
-        r.keys[...] = jnp.where(self.dense == 0, r.kv[m % 4, 0], r.kv[m % 4, 1])
-        keys = lambda h: r.keys[:, h * 128 : h * 128 + 128]
+        keys = lambda h: r.kv[m, :, h * 128 : h * 128 + 128]
         for h in range(heads):
             r.kt[h, 0:64] = keys(h).T[0:64]
             r.kt[h, 64:80] = jnp.ones((16, TK), jnp.bfloat16)
 
         def part(i, _):
-            first = ((2 * place.row + i) * place.rest_size + place.rest) * self.tokens
-            slot = jnp.clip(t - (first // TK - 1 + self.core) + 1, 0, 3)
+            slot = near_slot(place, i, t)
             away = jnp.logical_or(slot == 0, slot == 3)
 
             def finish(h, p, ds, where):
@@ -1650,114 +1566,107 @@
                 r.dqt[i, h, where] += mxu(r.kt[h], ds_low)
 
             def products(h):
-                return mxu(keys(h), r.qp[i, h], NT), mxu(keys(h), r.dp[i, h], NT)
+                s = mxu(jnp.concatenate([keys(h), r.kl[m]], axis=1), jnp.concatenate([r.qp[i, h], r.ql[i]], axis=1), NT)
+                return s, mxu(keys(h), r.dp[i, h], NT)
 
             @pl.when(away)
             def _():
                 for h in range(heads):
                     s, d_probs = products(h)
-                    p = jnp.exp(s - (r.lse[self.dense, i, h] - jnp.where(slot == 0, r.table[h, 15], r.table[h, 31])))
-                    finish(h, p, p * (d_probs - r.delta[self.dense, i, h]), jnp.where(slot == 0, 0, 2))
+                    p = jnp.exp(s - (r.lse[i, h] - jnp.where(slot == 0, r.table[h, 15], r.table[h, 31])))
+                    finish(h, p, p * (d_probs - r.delta[i, h]), jnp.where(slot == 0, 0, 2))
 
             @pl.when(jnp.logical_not(away))
             def _():
                 for h in range(heads):
                     s, d_probs = products(h)
-                    p = jnp.exp(s + r.bias[h, slot - 1].astype(jnp.float32) - r.lse[self.dense, i, h])
-                    ds = p * (d_probs - r.delta[self.dense, i, h])
+                    p = jnp.exp(s + r.bias[h, slot - 1].astype(jnp.float32) - r.lse[i, h])
+                    ds = p * (d_probs - r.delta[i, h])
                     r.grid[h, pl.ds(pl.multiple_of((slot - 1) * TK, TK), TK)] += ds
                     finish(h, p, ds, 1)
 
             return 0
 
-        lax.fori_loop(0, 2, part, 0)
+        lax.fori_loop(0, GROUPS, part, 0)
         for half in range(2):
             r.held[n, j, half] = r.acc[half * self.tokens : half * self.tokens + self.tokens].astype(jnp.bfloat16)
         self.core_copy(n, j).start()
-        pl.when(m < 4)(lambda: self.fetch(m + 4).start())
 
     def queries(self):
         r = self.r
-        for i in range(2):
+
+        def one(i, _):
             parts = []
             for h in range(self.heads):
                 parts.append((r.dqt[i, h, 0, 0:64] + r.dqt[i, h, 1, 0:64] + r.dqt[i, h, 2, 0:64]).T * 0.125)
-            mine = join_heads(parts)
-            other = r.dqs[0, i].astype(jnp.float32)
-            for row in range(2):
-                r.dq_rows[row, i] = jnp.where(self.dense == row, mine, other).astype(jnp.bfloat16)
+            r.dq[i] = slim(join_heads(parts))
+            return 0
+
+        lax.fori_loop(0, GROUPS, one, 0)
 
     def buckets(self):
         r = self.r
-        self.near_rows.wait()
         first = near_start(self.core)
         for h in range(self.heads):
-            r.side[h, 0:1] = r.dqt[0, h, 0, 64:65] + r.dqt[1, h, 0, 64:65] + r.sides[h, 0:1] + far_sums(r.grid, h, 0, first)
-            r.side[h, 1:2] = r.dqt[0, h, 2, 64:65] + r.dqt[1, h, 2, 64:65] + r.sides[h, 1:2] + far_sums(r.grid, h, first + NEAR_ROWS, 2 * TK)
-            rows = pl.ds(pl.multiple_of(first, 32), NEAR_ROWS)
-            r.grid[h, rows] += r.nears[h]
+            r.side[h, 0:1] = sum(r.dqt[i, h, 0, 64:65] for i in range(GROUPS)) + far_sums(r.grid, h, 0, first)
+            r.side[h, 1:2] = sum(r.dqt[i, h, 2, 64:65] for i in range(GROUPS)) + far_sums(r.grid, h, first + NEAR_ROWS, 2 * TK)
         bucket_sums(self.core, NearRows(r.grid, first), r.side, r.tab, r.tab8)
 
     def wait_home(self):
         r, place = self.r, self.place
         for n in range(GROUPS - 1):
             there = r.dkv_home.at[(place.group - 1 - n + GROUPS) % GROUPS]
-            remote(r.z_out.at[n], there, r.z_send.at[n], r.z_recv.at[n], self.row_to).wait()
+            remote(r.z_out.at[n], there, r.z_send.at[n], r.z_recv.at[n], self.core_to).wait()
 
 
 def back_kernel(shards, axes, plans, r):
     place = Place(shards)
     at = {"dp": place.dp, "blk": place.blk}
     tokens, width = r.hidden.shape
-    back = DenseBack(place, r)
+    back = RowBack(place, r)
     streams = []
     for s, (kept, order) in enumerate(plans):
-        streams.append(Stream(axes, at, kept, order, r.src[s], r.bufs[s], r.sums[s], r.w_send.at[s], r.w_recv.at[s]))
+        src = r.early[s] if s < 3 else r.late[s - 3]
+        streams.append(Stream(axes, at, kept, order, src, r.bufs[s], r.sums[s], r.w_send.at[s], r.w_recv.at[s]))
     early, late = streams[:3], streams[3:]
     whole = Whole(axes, at, (4, 0, 3, 2, 1), r.small, r.small_bufs, r.small_out, r.w_send.at[len(plans)], r.w_recv.at[len(plans)])
     left, right = (place.dp, (place.blk + shards - 1) % shards), (place.dp, (place.blk + 1) % shards)
 
-    met = hail(line_and_row(place) + [back.across, back.core_to, left, right])
-    fetches = [pltpu.make_async_copy(r.came_hbm[s], early[s].src, r.came_sem.at[s]) for s in range(3)]
-    for copy in fetches:
-        copy.start()
+    met = hail([place.other_group(step) for step in (1, 2, 3)] + [back.across, back.core_to, place.other_row(), left, right])
     back.prepare()
-    for s in range(3):
-        fetches[s].wait()
-        add_two(early[s].src, early[s].src, r.keeps[s])
     await_all(met)
-    back.s_core.start()
     for stream in early:
         stream.copy(0).start()
 
     def step(m, _):
         back.tile(m)
-        pl.when(m == 0)(back.other_sums)
-        for when, n, action in (
-            (1, 0, back.y_first_1), (3, 1, back.x_first_1), (4, 1, back.x_first_2), (5, 2, back.y_first_1),
-            (6, 0, back.y_first_3), (6, 1, back.x_first_3), (7, 3, back.x_first_1),
-        ):
-            pl.when(m == when)(functools.partial(action, n))
+        for delay, action in ((1, back.send_y), (3, back.send_home)):
+            then = m - delay + 2 * GROUPS
+            n = then // 2 - GROUPS
+
+            @pl.when(jnp.logical_and(then % 2 == 0, n >= 0))
+            def _():
+                action(n)
+
+        @pl.when(m == 5)
+        def _():
+            for stream in early:
+                advance(stream, 0)
+
         return 0
 
     lax.fori_loop(0, 2 * GROUPS, step, 0)
-    back.x_first_2(3)
     back.queries()
-    return_heads(place, r.dq_rows, r.dq_home, r.q_send, r.q_recv)
-    for stream in early:
-        advance(stream, 0)
-    back.y_first_5(0)
-    back.x_first_3(3)
-    back.x_first_5(1)
-    back.y_first_3(2)
-    back.buckets()
+    home = Line(place, r.dq, r.dq_home, r.q_send, r.q_recv)
+    home.keep().start()
+    home.start()
+    back.send_home(3)
     for stream in early:
         advance(stream, 1)
-    back.y_first_5(2)
-    back.x_first_5(3)
+    back.buckets()
     load_bytes(r.x, r.before, r.after, r.xs)
     n1_t = r.n1[...].T
-    return_heads_wait(place, r.dq_rows, r.dq_home, r.q_send, r.q_recv)
+    home.wait_all()
     dq = get_packed(r.dq_home)
     devices = 1 << len(axes)
     per = width // devices
@@ -1804,30 +1713,33 @@
         for stream in late:
             advance(stream, stage)
         advance(whole, stage - 1)
+        if stage == 1:
+            for stream in early:
+                advance(stream, 3)
     advance(whole, len(axes) - 1)
     for copy in spills:
         copy.wait()
 
 
-def back_and_last(shape, keeps, came, inputs):
+def back_and_last(shape, early, inputs):
     shards = shape["blk"]
     axes = bit_axes(shape)
     ndim = len(axes)
     kv, q, hidden = inputs["kv_hbm"].array, inputs["q"], inputs["hidden"]
-    heads, n, width = kv.shape[2] // 128, kv.shape[1], kv.shape[2]
+    heads, width = kv.shape[1] // 128, kv.shape[1]
     tokens, features = hidden.shape
     length = inputs["x"].shape[0]
     f32, low, sem = jnp.float32, jnp.bfloat16, pltpu.SemaphoreType.DMA
     chunk = (tokens, width)
     every = (0, 1, 2, 3, 4)
+    four = (0, 1, 2, 3)
     plans = [
-        ((1, 2, 3), (3, 2, 1)), ((0, 1, 2), (2, 0, 1)), ((0, 1, 3), (0, 3, 1)),
+        (four, (0, 3, 2, 1)), (four, (0, 3, 2, 1)), (four, (3, 0, 2, 1)),
         (every, (4, 0, 3, 2, 1)), (every, (4, 3, 2, 0, 1)), (every, (4, 2, 0, 3, 1)),
     ]
     own = (2 * (features // (1 << ndim)), features // 2)
-    blocks = [part.shape[-2:] for part in keeps] + [own] * 3
-    bits = lambda part: part.reshape((2, 2, 2) + part.shape[-2:])
-    ins = dict(inputs, keeps=[bits(part) for part in keeps], came_hbm=[Held(bits(part), pl.ANY) for part in came])
+    blocks = [part.shape[-2:] for part in early] + [own] * 3
+    ins = dict(inputs, early=[part.reshape((2, 2, 2, 2) + part.shape[-2:]) for part in early])
     outs = dict(
         gb=((length, features), low), edge=((2, 16, features), f32), spill_out=((2, LEAD, features), f32),
         small_out=((32, 128), f32), sums=[(block, f32) for block in blocks],
@@ -1835,58 +1747,93 @@
     mem = lambda shape, dtype=low: pltpu.VMEM(shape, dtype)
     pairs, fours = sem((GROUPS, 2)), sem((GROUPS,))
     strip = mem((features // 128, length + 2 * LEAD, 128), f32)
+    eights = sem((2 * GROUPS,))
     scratch = dict(
-        kt=mem((heads, 80, TK)), dqt=mem((2, heads, 3, 80, TQ), f32), acc=mem((TK, width), f32),
+        kt=mem((heads, 80, TK)), dqt=mem((GROUPS, heads, 3, 80, TQ), f32), acc=mem((TK, width), f32),
         grid=mem((heads, 2 * TK, TQ), f32), side=mem((heads, 2, TQ), f32), tab8=mem((heads, BUCKETS, 8, TQ), f32),
-        tab=mem((heads, BUCKETS, TQ), f32),
-        qp=mem((2, heads, TQ, 128)), dp=mem((2, heads, TQ, 128)),
-        kv=mem((4, 2, TK, width)), keys=mem((TK, width)), dkvs=mem((GROUPS, 2) + chunk), nears=mem((heads, NEAR_ROWS, TQ), f32),
-        held=mem((GROUPS, 2, 2) + chunk), core_in=mem((GROUPS, 2) + chunk), s_in=mem((GROUPS, 2) + chunk),
-        x_out=mem((GROUPS, 2) + chunk), x_in=mem((GROUPS, 2) + chunk),
-        y_out=mem((GROUPS, 1) + chunk), y_in=mem((GROUPS, 2) + chunk), kept=mem((GROUPS, 2) + chunk),
-        z_out=mem((GROUPS,) + chunk), dkv_home=mem((GROUPS,) + chunk),
-        dq_rows=mem((2, 2) + q.shape[2:]), dq_home=mem((GROUPS,) + q.shape[2:]),
-        core_send=pairs, core_recv=pairs, x_send=pairs, x_recv=pairs, y_send=pairs, y_recv=pairs,
-        z_send=fours, z_recv=fours, s_send=sem, s_recv=sem, q_send=fours, q_recv=fours,
-        kv_sem=fours, came_sem=sem((3,)), own_sem=sem, near_sem=sem,
+        tab=mem((heads, BUCKETS, TQ), f32), delta=mem((GROUPS, heads, 1, TQ), f32),
+        qp=mem((GROUPS, heads, TQ, 128)), dp=mem((GROUPS, heads, TQ, 128)),
+        kv=mem((2 * GROUPS, TK, width)), kl=mem((2 * GROUPS, TK, 128)),
+        held=mem((GROUPS, 2, 2) + chunk), core_in=mem((GROUPS, 2) + chunk),
+        y_out=mem((GROUPS,) + chunk), y_in=mem((GROUPS,) + chunk), z_out=mem((GROUPS,) + chunk), dkv_home=mem((GROUPS,) + chunk),
+        dq=mem(q.shape), dq_home=mem(q.shape),
+        core_send=pairs, core_recv=pairs, y_send=fours, y_recv=fours, z_send=fours, z_recv=fours, q_send=fours, q_recv=fours,
+        kv_sem=eights, kl_sem=eights,
         w_send=sem((len(plans) + 1, ndim)), w_recv=sem((len(plans) + 1, ndim)), s2_send=sem((2,)), s2_recv=sem((2,)),
         xs=strip, gbuf=strip, spill=mem((2, LEAD, features), f32), small=mem((32, 128), f32),
         small_bufs=mem((2, ndim, 32, 128), f32), total=mem((features, features), f32),
     )
-    scratch["src"] = [mem((2,) * len(kept) + block) for (kept, _), block in zip(plans, blocks)]
+    scratch["late"] = [mem((2,) * ndim + own)] * 3
     scratch["bufs"] = [stream_scratch(len(kept), order, *block) for (kept, order), block in zip(plans, blocks)]
     return call(functools.partial(back_kernel, shards, axes, plans), 6, ins, outs, scratch)
 
 
-class DenseForward:
+def label_features(line, unlike):
+    rows = [(line != k if unlike else line == k).astype(jnp.float32) for k in range(8)]
+    return slim(jnp.concatenate(rows + [jnp.zeros((120, line.shape[1]), jnp.float32)], axis=0).T)
+
+
+class Line:
+    def __init__(self, place, src, dst, send_sem, recv_sem):
+        self.place, self.src, self.dst, self.send_sem, self.recv_sem = place, src, dst, send_sem, recv_sem
+
+    def copy(self, step, slot):
+        group = self.place.group
+        return remote(
+            self.src.at[(group + step) % GROUPS], self.dst.at[slot], self.send_sem.at[step], self.recv_sem.at[step],
+            self.place.other_group(step),
+        )
+
+    def keep(self):
+        group = self.place.group
+        return pltpu.make_async_copy(self.src.at[group], self.dst.at[group], self.send_sem.at[0])
+
+    def start(self, steps=(1, 3, 2)):
+        for step in steps:
+            self.copy(step, self.place.group).start()
+
+    def wait(self, step):
+        self.copy(step, (self.place.group - step + GROUPS) % GROUPS).wait()
+
+    def wait_all(self):
+        for step in (1, 3, 2):
+            self.wait(step)
+        self.keep().wait()
+
+
+def near_slot(place, chunk, t):
+    first = (chunk * place.rest_size + place.rest) * TQ
+    return jnp.clip(t - (first // TK - 1 + place.rest % 2) + 1, 0, 3)
+
+
+class RowForward:
     def __init__(self, place, r):
         self.place, self.r, self.heads = place, r, r.lse.shape[1]
 
-    def prepare(self, dense):
+    def clear(self):
+        self.r.acc[...] = jnp.zeros_like(self.r.acc)
+        self.r.mx[...] = jnp.full_like(self.r.mx, FIRST_MAX)
+
+    def queries(self, chunk):
         r = self.r
-        self.dense = dense
-        for i in range(2):
-            for h, tile in enumerate(spread_lanes(jnp.where(dense == 0, r.q_all[0, i], r.q_all[1, i]), False)):
-                r.qp[i, h] = tile
-        r.acc[...] = jnp.zeros_like(r.acc)
-        r.mx[...] = jnp.full_like(r.mx, FIRST_MAX)
-
-    def tile(self, group, place_y):
-        r, place = self.r, self.place
-        t = group * 2 + place_y
+        for h, tile in enumerate(spread_lanes(r.q_all[chunk], False)):
+            r.qp[chunk, h] = jnp.concatenate([tile, r.ql[chunk]], axis=1)
+
+    def tile(self, t, chunks, turn=True):
+        r = self.r
         rows = pl.ds(pl.multiple_of(t * TK, TK), TK)
-        r.keys[...] = jnp.where(self.dense == 0, r.kv_all[0, rows], r.kv_all[1, rows])
-        for h in range(self.heads):
-            r.vt[h, 0:64] = r.keys[:, h * 128 : h * 128 + 128].T[64:128]
-            r.vt[h, 64:80] = jnp.ones((16, TK), jnp.bfloat16)
+        keys = lambda h: r.kv_all[rows, h * 128 : h * 128 + 128]
+        if turn:
+            for h in range(self.heads):
+                r.vt[h, 0:64] = keys(h).T[64:128]
+                r.vt[h, 64:80] = jnp.ones((16, TK), jnp.bfloat16)
 
         def part(i, _):
-            first = ((2 * place.row + i) * place.rest_size + place.rest) * TQ
-            slot = jnp.clip(t - (first // TK - 1 + place.rest % 2) + 1, 0, 3)
+            slot = near_slot(self.place, i, t)
             away = jnp.logical_or(slot == 0, slot == 3)
 
             def scores(h):
-                return mxu(r.keys[:, h * 128 : h * 128 + 128], r.qp[i, h], NT)
+                return mxu(jnp.concatenate([keys(h), r.kl[rows, :]], axis=1), r.qp[i, h], NT)
 
             def finish(h, s, b):
                 m_old = r.mx[i, h]
@@ -1908,11 +1855,12 @@
 
             return 0
 
-        lax.fori_loop(0, 2, part, 0)
+        lax.fori_loop(0, chunks, part, 0)
 
     def end(self):
         r = self.r
-        for i in range(2):
+
+        def one(i, _):
             parts = []
             for h in range(self.heads):
                 total = r.acc[i, h, 64:65, :]
@@ -1921,69 +1869,43 @@
             joined = join_heads(parts)
             r.o[i] = joined.astype(jnp.bfloat16)
             r.keep[i] = joined
-
-
-def label_spans(place, r):
-    ids = range(8)
-    shards = place.shards
-    blocks = r.labels_all[...].reshape(2, shards, 8, 128)
-    ends = []
-    for row in range(2):
-        here = blocks[row]
-        ends.append([jnp.sum(jnp.logical_and(here >= 0, here <= k).astype(jnp.int32)) for k in ids])
-    dense = (ends[0][0] < shards * TQ).astype(jnp.int32)
-    for row in range(2):
-        for i in range(2):
-            group = 2 * place.row + i
-            chunk = r.labels_all[tuple([row] + [bit(group * place.rest_size + place.rest, m) for m in bits_of(shards)])]
-            line = jnp.concatenate([chunk[0:1], chunk[1:2]], axis=1)
-            begin, end = jnp.zeros((1, TQ), jnp.int32), jnp.zeros((1, TQ), jnp.int32)
-            for k in ids:
-                begin = jnp.where(line == k, ends[row][k - 1] if k else 0, begin)
-                end = jnp.where(line == k, ends[row][k], end)
-            r.span[row, i, 0:1] = begin
-            r.span[row, i, 1:2] = end
-            first = (group * place.rest_size + place.rest) * TQ
-            r.bounds[row, i, 0] = jnp.min(begin) // TK
-            r.bounds[row, i, 1] = (jnp.max(end) + TK - 1) // TK
-            r.bounds[row, i, 2] = first // TK - 1 + place.rest % 2
-            r.bounds[row, i, 3] = (jnp.max(begin) + TK - 1) // TK
-            r.bounds[row, i, 4] = jnp.min(end) // TK
-            r.bounds[row, i, 5] = place.rest % 2
-            r.bounds[row, i, 6] = dense
-    return dense
+            return 0
+
+        lax.fori_loop(0, GROUPS, one, 0)
 
 
 def front_kernel(shards, r):
     place = Place(shards)
     tokens = r.kv.shape[1]
     y, core = bit(place.rest, 2), place.rest % 2
-    core_to, across, row_to = place.other_rest(1), place.other_rest(2), place.other_row()
-    met = hail(line_and_row(place) + [core_to, across])
-    dims = [("row", 1)] + [("blk", m) for m in bits_of(shards)]
-    lab_index = [place.row] + [bit(place.blk, m) for _, m in dims[1:]]
+    core_to, across = place.other_rest(1), place.other_rest(2)
+    met = hail([place.other_group(step) for step in (1, 2, 3)] + [core_to, across])
+    masks = bits_of(shards)
+    lab_index = [bit(place.blk, m) for m in masks]
 
     def lab_copy(stage):
-        index = tuple(slice(None) if p < stage else lab_index[p] for p in range(len(dims)))
-        axis, mask = dims[stage]
-        target = row_to if axis == "row" else (place.dp, flipped(place.blk, mask))
+        index = tuple(slice(None) if p < stage else lab_index[p] for p in range(len(masks)))
         there = r.labels_all.at[index]
-        return remote(there, there, r.lab_send.at[stage], r.lab_recv.at[stage], target)
+        return remote(there, there, r.lab_send.at[stage], r.lab_recv.at[stage], (place.dp, flipped(place.blk, masks[stage])))
+
+    def label_stage(stage):
+        lab_copy(stage).wait()
+        if stage + 1 < len(masks):
+            lab_copy(stage + 1).start()
 
     def held(dz, off, core_off):
-        row = 1 - place.row if off & 1 else place.row
-        rest = flipped(place.rest, 2) if off & 2 else place.rest
+        rest = flipped(place.rest, 2) if off else place.rest
         rest = flipped(rest, 1) if core_off else rest
         start = pl.multiple_of(place.chunk((place.group + dz) % GROUPS, rest) * tokens, tokens)
-        return r.kv_all.at[row, pl.ds(start, tokens)]
+        return r.kv_all.at[pl.ds(start, tokens)]
 
     def sem_of(dz, off, core_off):
-        return r.kv_recv.at[(core_off * 4 + off) * GROUPS + dz]
+        return r.kv_recv.at[(core_off * 2 + off) * GROUPS + dz]
 
     waits = []
 
-    def send(src, dz, off, core_off, target):
-        copy = remote(src, held(dz, off & 3, 0), r.kv_send.at[len(waits)], sem_of(*core_off), target)
+    def send(src, dz, off, came, target):
+        copy = remote(src, held(dz, off, 0), r.kv_send.at[len(waits)], sem_of(*came), target)
         copy.start()
         waits.append(copy)
 
@@ -1992,76 +1914,69 @@
         remote(here, here, r.kv_send.at[0], sem_of(dz, off, core_off), core_to).wait_recv()
 
     def pass_on(dz, off):
-        src = r.kv.at[place.group] if dz == 0 and off == 0 else held(dz, off, 0)
-        if not (dz == 0 and off == 0):
+        mine = dz == 0 and off == 0
+        if not mine:
             arrived(dz, off)
-        order = (0, 1) if dz % 2 == 0 else (1, 0)
-        last = max([order.index(p) for p in range(2) if off >> p & 1], default=-1)
-        for p in order[last + 1 :]:
-            send(src, dz, off, (dz, off | 1 << p, 0), across if p else row_to)
+        src = r.kv.at[place.group] if mine else held(dz, off, 0)
+        if not off:
+            send(src, dz, off, (dz, 1, 0), across)
         send(src, dz, off, (dz, off, 1), core_to)
+
+    def along(step):
+        copy = remote(r.kv.at[(place.group + step) % GROUPS], held(0, 0, 0), r.z_send.at[step], sem_of((GROUPS - step) % GROUPS, 0, 0), place.other_group(step))
+        copy.start()
+        return copy
+
+    work = RowForward(place, r)
+
+    def tile(dz, off):
+        arrived(dz, off, 1)
+        work.tile((place.group + dz) % GROUPS * 2 + (1 - y if off else y), GROUPS)
 
     r.labels_all[tuple(lab_index)] = r.label[...]
     await_all(met)
     lab_copy(0).start()
     own = pltpu.make_async_copy(r.kv.at[place.group], held(0, 0, 0), r.own_sem)
     own.start()
-
-    def along(step):
-        copy = remote(r.kv.at[(place.group + step) % GROUPS], held(0, 0, 0), r.z_send.at[step], sem_of((GROUPS - step) % GROUPS, 0, 0), place.other_group(step))
-        copy.start()
-        return copy
-
-    def label_stage(stage):
-        lab_copy(stage).wait()
-        if stage + 1 < len(dims):
-            lab_copy(stage + 1).start()
-
-    work = DenseForward(place, r)
-
-    def tile(dz, off_y):
-        for off in (2 * off_y, 2 * off_y + 1):
-            arrived(dz, off, 1)
-        work.tile((place.group + dz) % GROUPS, 1 - y if off_y else y)
-
+    queries = Line(place, r.q, r.q_all, r.q_send, r.q_recv)
+    queries.keep().start()
+    queries.start()
     first = [along(1), along(3)]
     pass_on(0, 0)
     make_bias(r.table, core, r.near, (0,))
     label_stage(0)
     pass_on(0, 1)
-    pass_on(0, 2)
     make_bias(r.table, core, r.near, (1,))
     label_stage(1)
+    work.clear()
+    label_stage(2)
+    label_stage(3)
+    blocks = r.labels_all[...].reshape(shards, 8, 128)
+    for n in range(shards):
+        line = jnp.concatenate([blocks[n, 0:1], blocks[n, 1:2]], axis=1)
+        r.kl[n * tokens : n * tokens + tokens, :] = label_features(line, True)
+    for z in range(GROUPS):
+        chunk = r.labels_all[tuple([z // 2, z % 2] + [bit(place.rest, m) for m in bits_of(place.rest_size)])]
+        line = jnp.concatenate([chunk[0:1], chunk[1:2]], axis=1)
+        r.ql[z] = label_features(line, False) * jnp.bfloat16(NEG)
+    queries.wait_all()
+    for z in range(GROUPS):
+        work.queries(z)
+    own.wait()
     for copy in first:
         copy.wait_send()
-    spread_heads(place, r.q, r.q_all, r.q_send, r.q_recv)
+    last = along(2)
+    tile(0, 0)
     pass_on(1, 0)
-    label_stage(2)
     pass_on(3, 0)
-    label_stage(3)
-    pass_on(0, 3)
-    spread_heads_gone(place, r.q, r.q_all, r.q_send, r.q_recv)
-    last = along(2)
-    label_stage(4)
-    dense = label_spans(place, r)
+    tile(0, 1)
     pass_on(1, 1)
-    pass_on(1, 2)
-    spread_heads_come(r.q, r.q_all, r.q_recv)
-    own.wait()
-    work.prepare(dense)
+    tile(1, 0)
     pass_on(3, 1)
-    pass_on(3, 2)
-    tile(0, 0)
-    pass_on(1, 3)
-    tile(0, 1)
-    pass_on(3, 3)
-    tile(1, 0)
+    tile(3, 0)
     pass_on(2, 0)
     tile(1, 1)
     pass_on(2, 1)
-    pass_on(2, 2)
-    tile(3, 0)
-    pass_on(2, 3)
     tile(3, 1)
     tile(2, 0)
     tile(2, 1)
@@ -2074,20 +1989,19 @@
 def front(shards, table, q_packed, kv_parts, label):
     tokens, width = kv_parts.shape[1:]
     heads = width // 128
-    nbits = 1 + len(bits_of(shards))
+    nbits = len(bits_of(shards))
     sem, f32, low = pltpu.SemaphoreType.DMA, jnp.float32, jnp.bfloat16
-    half = q_packed.shape[1:]
+    mem = lambda shape, dtype=low: pltpu.VMEM(shape, dtype)
+    packed = q_packed.shape
     ins = dict(table=Held(table, pltpu.SMEM), q=q_packed, kv=kv_parts, label=label)
     outs = dict(
-        q_all=((2, 2) + half, low), kv_all=((2, shards * tokens, width), low), bounds=((2, 2, 7), jnp.int32, pltpu.SMEM),
-        span=((2, 2, 2, TQ), jnp.int32), near=((heads, 2, TK, TQ), low),
-        o=((2,) + half, low), keep=((2,) + half, f32), lse=((2, heads, 1, TQ), f32),
+        q_all=(packed, low), kv_all=((shards * tokens, width), low), kl=((shards * tokens, 128), low), ql=((GROUPS, tokens, 128), low),
+        near=((heads, 2, TK, TQ), low), o=(packed, low), keep=(packed, f32), lse=((GROUPS, heads, 1, TQ), f32),
     )
     scratch = dict(
-        labels_all=pltpu.VMEM((2,) * nbits + label.shape, label.dtype),
-        qp=pltpu.VMEM((2, heads, TQ, 128), low), acc=pltpu.VMEM((2, heads, 80, TQ), f32),
-        mx=pltpu.VMEM((2, heads, 1, TQ), f32), keys=pltpu.VMEM((TK, width), low), vt=pltpu.VMEM((heads, 80, TK), low),
-        q_send=sem((4,)), q_recv=sem((4,)), kv_send=sem((28,)), z_send=sem((GROUPS,)), kv_recv=sem((32,)), own_sem=sem,
+        labels_all=mem((2,) * nbits + label.shape, label.dtype),
+        qp=mem((GROUPS, heads, TQ, 256)), acc=mem((GROUPS, heads, 80, TQ), f32), mx=mem((GROUPS, heads, 1, TQ), f32), vt=mem((heads, 80, TK)),
+        q_send=sem((4,)), q_recv=sem((4,)), kv_send=sem((12,)), z_send=sem((GROUPS,)), kv_recv=sem((16,)), own_sem=sem,
         lab_send=sem((nbits,)), lab_recv=sem((nbits,)),
     )
     return call(functools.partial(front_kernel, shards), 7, ins, outs, scratch)
@@ -2095,22 +2009,26 @@
 
 def middle_kernel(shards, r):
     place = Place(shards)
-    met = hail(line_and_row(place) + [place.other_rest(1)])
+    met = hail([place.other_group(step) for step in (1, 2, 3)] + [place.other_rest(1)])
     pairs = ((r.wo_hbm, r.wo), (r.wg_hbm, r.wg), (r.wu_hbm, r.wu), (r.wd_hbm, r.wd))
     fetches = [pltpu.make_async_copy(src, dst, r.w_sem.at[k]) for k, (src, dst) in enumerate(pairs)]
     for copy in fetches:
         copy.start()
     await_all(met)
-    return_heads(place, r.o, r.o_home, r.o_send, r.o_recv)
+    home = Line(place, r.o, r.o_home, r.o_send, r.o_recv)
+    home.keep().start()
+    home.start()
     for copy in fetches:
         copy.wait()
-    return_heads_wait(place, r.o, r.o_home, r.o_send, r.o_recv)
+    home.wait_all()
     feed_kernel(r.o_home, r.hidden, r.ct, r.gain, r.wo, r.wg, r.wu, r.wd, r.block_out, r.dres, r.da, r.dgain,
                 r.n2, r.att, r.act, r.dg, r.du, r.db, r.acc, r.dn2)
-    spread_heads(place, r.da, r.do, r.q_send, r.q_recv)
-    feed_weights(place, r.n2, r.att, r.act, r.dg, r.du, r.ct, r.db, r.keep_a, r.send_a, r.keep_b, r.send_b, r.keep_c, r.send_c,
+    away = Line(place, r.da, r.do, r.q_send, r.q_recv)
+    away.keep().start()
+    away.start()
+    feed_weights(place, r.n2, r.att, r.act, r.dg, r.du, r.ct, r.db, r.sums,
                  r.core_send, r.core_recv, r.gate, r.up, r.down, r.out, r.wide_out, r.slim_out, r.wide_in, r.slim_in)
-    spread_heads_wait(place, r.da, r.do, r.q_send, r.q_recv)
+    away.wait_all()
 
 
 def middle(shards, o_packed, hidden, ct, gain, wo, wg, wu, wd):
@@ -2118,15 +2036,13 @@
     ff = wg.shape[1]
     per, per_ff = width // 32, ff // 32
     sem, low, f32 = pltpu.SemaphoreType.DMA, jnp.bfloat16, jnp.float32
-    half = o_packed.shape[2:]
+    half = o_packed.shape[1:]
     wide_cols = ff + width // 2
     first = (wide_cols // 256 + 1) * 128
     ins = dict(o=o_packed, hidden=hidden, ct=ct, gain=gain, wo_hbm=Held(wo, pl.ANY), wg_hbm=Held(wg, pl.ANY), wu_hbm=Held(wu, pl.ANY), wd_hbm=Held(wd, pl.ANY))
     outs = dict(
-        block_out=((tokens, width), low), dres=((tokens, width), f32), dgain=((1, width), f32), do=((2, 2) + half, low),
-        keep_a=((8, 2 * per, first), low), send_a=((8, 2 * per, first), low),
-        keep_b=((8, 2 * per, wide_cols - first), low), send_b=((8, 2 * per, wide_cols - first), low),
-        keep_c=((8, per_ff, width), low), send_c=((8, per_ff, width), low),
+        block_out=((tokens, width), low), dres=((tokens, width), f32), dgain=((1, width), f32), do=((GROUPS,) + half, low),
+        sums=[((16, 2 * per, first), low), ((16, 2 * per, wide_cols - first), low), ((16, per_ff, width), low)],
     )
     mem = lambda shape, dtype=low: pltpu.VMEM(shape, dtype)
     scratch = dict(
@@ -2195,10 +2111,7 @@
     table = lax.dynamic_slice_in_dim(rel_bias.astype(jnp.float32).T, group * heads, heads, 0)
     if devices == 32:
         got = front(shards, table, q_packed, kv_parts, label_block)
-        bounds, span, q_all, kv_all, near_bias = got.bounds, got.span, got.q_all, got.kv_all, got.near
-        o_packed, o_kept, log_total = attention(
-            bounds, table, q_all, kv_all, span, (near_bias, got.o, got.keep, got.lse)
-        )
+        o_packed = got.o
     else:
         q_all, kv_all, labels_all = gather_all(shards, q_packed, kv_parts, label_block)
         labels_all = labels_all.reshape(2, shards, 8, 128)[:, :, : tokens // 128].reshape(2, shards * tokens)
@@ -2233,21 +2146,14 @@
     ct = cotangent[0]
     if devices == 32:
         mid = middle(shards, o_packed, hidden, ct, gain2, w_out, w_gate, w_up, w_down)
-        block_out, d_res, d_gain2, do_all = mid.block_out, mid.dres, mid.dgain, mid.do
-        swap = lambda part, axis, mask: lax.ppermute(part, axis, [(i, i ^ mask) for i in range(lax.axis_size(axis))])
-        came = [swap(mid.send_a, "dp", 1), swap(mid.send_b, "blk", 2), swap(mid.send_c, "blk", 4)]
-        dq_other, dkv_other, near_other, side_other, deltas = attention_back(
-            True, bounds, table, q_all, do_all, o_kept, kv_all, near_bias, span, log_total
-        )
+        block_out, d_res, d_gain2 = mid.block_out, mid.dres, mid.dgain
         last = back_and_last(
             shape,
-            [mid.keep_a, mid.keep_b, mid.keep_c],
-            came,
+            mid.sums,
             dict(
-                bounds=Held(bounds, pltpu.SMEM), table=Held(table, pltpu.SMEM), q=q_all, do=do_all, delta=deltas, kv_hbm=Held(kv_all, pl.ANY),
-                bias=near_bias, lse=log_total, dqs=dq_other,
-                dkvs_hbm=Held(dkv_other.reshape((GROUPS, 2, 2) + kv_parts.shape[1:]), pl.ANY), nears_hbm=Held(near_other, pl.ANY),
-                sides=side_other, hidden=hidden, dres=d_res, n1=n1, x=x, before=before, after=after,
+                table=Held(table, pltpu.SMEM), q=got.q_all, do=mid.do, keep=got.keep, kv_hbm=Held(got.kv_all, pl.ANY),
+                kl_hbm=Held(got.kl, pl.ANY), ql=got.ql, bias=got.near, lse=got.lse,
+                hidden=hidden, dres=d_res, n1=n1, x=x, before=before, after=after,
                 labels=labels, y=y, score=score_row, gain=gain1, wq=w_query, wk=w_key, wv=w_value, dgain2=d_gain2, share=share,
             ),
         )

time: 298 us -> 255 us (0.86)
  Pallas kernels: 266 us -> 234 us
  starting transfers between devices: 12.2 us -> 3.65 us
    pallas_call x2 -> x0, Pallas kernels: 28.5 us -> none  [the longest x1 16.5 us: attention_back(): pl.pallas_call(functools.partial(bwd_kernel, alone), out_shape=(jax.Shape...]
    ppermute x3 -> x0, starting transfers between devices: 8.52 us -> none  [body(): lax.ppermute(part, axis, [(i, i ^ mask) for i in range(lax.axis_size(axis...]
    pallas_call x3, Pallas kernels: 229 us -> 226 us  [call(): pl.pallas_call(run, out_shape=tuple((jax.ShapeDtypeStruct(entry[0], entry...]
  transfers between devices with their start and end apart: 5 -> 2, of which waited for: 2 -> 0; matrix products, arithmetic and copies ran while one was open for 2% -> 3% of each run, Pallas kernels for 6% -> 0%
where the time goes in v6:
time: 255 us; the launch traced here: 252 us
  Pallas kernels  234 us (92%)
  local copies, waits for them, and re-layouts  9.68 us (4%)
  starting transfers between devices  3.65 us (1%)
  other arithmetic  2.71 us (1%)
    pallas_call x3, Pallas kernels, call(): pl.pallas_call(run, out_shape=tuple((jax.ShapeDtypeStruct(entry[0], entry...  226 us
    pallas_call x1, Pallas kernels, pool_and_project(): pl.pallas_call(functools.partial(pool_kernel, shards, scale), out_shape=(...  6.08 us
  transfers between devices with their start and end apart: 2, of which 0 were waited for; matrix products, arithmetic and copies ran while one was open for 3% of the time, Pallas kernels for 0%

profile of v6, /device:TPU:0, one launch (start us, length us, event | category | flops | bytes accessed | tf_op | source)
XLA Modules:
  0.0 251.6 jit_solution(2490020924903221309)
XLA Ops:
  0.6 0.7 add_convert_fusion
  1.3 0.1 fusion.8
  1.4 0.7 slice_bitcast_fusion.1
  2.2 2.4 collective-permute-start
  4.6 1.3 collective-permute-start.1
  5.9 1.3 convert_bitcast_fusion.refs_3_.refs_21_
  7.2 0.9 slice.65
  8.1 1.3 broadcast_in_dim.21.refs_1_
  9.3 1.3 broadcast_in_dim.24.score_ref.refs_19_
  10.6 1.3 broadcast_in_dim.25.gain_ref.refs_9_
  11.9 0.6 pad.18.refs_1_
  12.5 0.0 collective-permute-done.1.after_ref.refs_0_
  12.5 0.0 copy-start.2
  12.5 0.0 collective-permute-done.before_ref.refs_1_
  12.5 0.0 copy-start.1
  12.5 0.1 fusion.6
  12.6 0.1 reshape.51
  12.7 0.1 copy.28
  12.8 0.1 fusion.7
  12.9 0.6 pad_add_fusion.lab_ref.refs_14_
  13.5 0.0 copy-done.2
  13.5 0.0 copy-done.1
  13.5 6.1 %pool_and_project.1 = (f32[256,768]{1,0:T(8,128)}, bf16[256,768]{1,0:T(8,128)(2,1)}, f32[8,256]{1,0:T(8,128)}, f32[1,128]{1,0:T(1,128)}, bf16[4,384,128]{2,1,0:T(8,128)(2,1)}, /*index=5*/bf16[4,256,384]{2,1,0:T(8,128)(2,1)}) custom-call(bf16[512,768]{1,0:T(8,128)(2,1)} %bitcast.24, bf16[3,768]{1,0:T(4,128)(2,1)} %copy-done.1, bf16[3,768]{1,0:T(4,128)(2,1)} %copy-done.2, ...), custom_call_target="tpu_custom_call" | custom-call | tf_op jit(solution)/shard_map/pool_and_project/pallas_call | solution.py:1140
  19.6 68.4 %front_kernel.1 = (f32[4,384,128]{2,1,0:T(8,128)}, bf16[4096,128]{1,0:T(8,128)(2,1)}, bf16[4096,384]{1,0:T(8,128)(2,1)}, f32[4,3,1,256]{3,2,1,0:T(1,128)}, bf16[...) custom-call(bf16[4,256,384]{2,1,0:T(8,128)(2,1)} %get-tuple-element., ...), custom_call_target="tpu_custom_call" | custom-call | tf_op jit(solution)/shard_map/front_kernel/pallas_call | solution.py:1440
  88.0 35.8 %middle_kernel.1 = (bf16[256,768]{1,0:T(8,128)(2,1)}, f32[1,768]{1,0:T(1,128)}, bf16[4,384,128]{2,1,0:T(8,128)(2,1)}, f32[256,768]{1,0:T(8,128)}, bf16[16,48,128...) custom-call(bf16[256,768]{1,0:T(8,128)(2,1)} %bitcast.30, ...), custom_call_target="tpu_custom_call" | custom-call | tf_op jit(solution)/shard_map/middle_kernel/pallas_call | solution.py:1440
  123.8 121.4 %back_kernel.1 = (f32[2,16,768]{2,1,0:T(8,128)}, bf16[512,768]{1,0:T(8,128)(2,1)}, f32[32,128]{1,0:T(8,128)}, f32[2,8,768]{2,1,0:T(8,128)}, f32[48,1280]{1,0:T(8...) custom-call(bf16[3,768]{1,0:T(4,128)(2,1)} %copy-done.2, ...), custom_call_target="tpu_custom_call" | custom-call | tf_op jit(solution)/shard_map/back_kernel/pallas_call | solution.py:1440
  245.2 0.0 copy-start
  245.2 2.8 %finish.1 = (bf16[512,768]{1,0:T(8,128)(2,1)}, f32[768]{0:T(1024)}, f32[768]{0:T(1024)}, f32[768]{0:T(1024)}, f32[16,128]{1,0:T(8,128)}, /*index=5*/f32[24,768]{...) custom-call(bf16[512,768]{1,0:T(8,128)(2,1)} %get-tuple-element.78.g, ...), custom_call_target="tpu_custom_call" | custom-call | tf_op jit(solution)/shard_map/finish/pallas_call | solution.py:1397
  247.9 1.3 slice_bitcast_fusion
  249.2 1.2 slice_bitcast_fusion.5
  250.4 0.0 copy-done
  250.4 0.7 copy.30
  (8 shorter events, 0.1 us)
Async XLA Ops:
  2.2 10.3 %collective-permute-start = (bf16[3,768]{1,0:T(4,128)(2,1)S(1)}, bf16[3,768]{1,0:T(4,128)(2,1)S(1)}, u32[]{:S(2)}, u32[]{:S(2)}) collective-permute-start(bf16[3,768]{1,0:T(4,128)(2,1)S(1)} %pad_maximum_fusion), channel_id=1, source_target_pairs={{0,1},{1,2},{2,3},{3,4},{4,5},{5,6},{6,7},{7,8},{8,9},{9,10},{10,1... | collective-permute-start | bytes 13832 | tf_op jit(solution)/shard_map/ppermute | solution.py:2067
  4.6 7.9 %collective-permute-start.1 = (bf16[3,768]{1,0:T(4,128)(2,1)S(1)}, bf16[3,768]{1,0:T(4,128)(2,1)S(1)}, u32[]{:S(2)}, u32[]{:S(2)}) collective-permute-start(bf16[3,768]{1,0:T(4,128)(2,1)S(1)} %pad_maximum_fusion.1), channel_id=1, source_target_pairs={{1,0},{2,1},{3,2},{4,3},{5,4},{6,5},{7,6},{8,7},{9,8},{10,9},{11,1... | collective-permute-start | bytes 13832 | tf_op jit(solution)/shard_map/ppermute | solution.py:2067
  12.5 1.1 copy-start.2
  12.5 1.1 copy-start.1
  245.2 5.3 %copy-start = (bf16[256,768]{1,0:T(8,128)(2,1)S(1)}, bf16[256,768]{1,0:T(8,128)(2,1)}, u32[]{:S(2)}) copy-start(bf16[256,768]{1,0:T(8,128)(2,1)} %get-tuple-element.61) | copy-start | bytes 1179652
